TPU v7x, 32 devices: a whole 2x2x4 slice. The times are simulated.
32 devices in a mesh: pts: 8 (over y, x, core), bins: 4 (over z).
Axes of the slice: x: 2, y: 2, z: 4, core: 2. Of those that a mesh axis runs over, the one named last changes fastest.
Arguments:
- spectrum: bfloat16 [1296, 32, 512], P('bins', 'pts'), may hold values from 0.049804688 to 4
- courant: float32 [1296, 2], replicated, may hold values from 0.05 to 0.45
- upwind: int32 [1296, 2], replicated, may hold values from 0 to 1
- coupling: bfloat16 [1296, 1296], replicated, may hold values from -0.15625 to 0.15625
- sea: int32 [32, 512], P('pts'), may hold values 0 or 1
- owner: int32 [8, 4, 512, 1], P('pts', 'bins'), may hold values from 0 to 7; in each aligned block of 512 rows (0 to 511, 512 to 1023, ..., all dimensions but the last counted through in order) at most 128 rows name the same one
Outputs:
- owner_rows: bfloat16 [8, 4, 1024, 1296], P('pts', 'bins')
Inputs may be any that keep to these rules, and one draw needn't show every extreme that they name: Among the 512 points of one block, at most 128 name the same owner, and in every draw some owner is named by exactly 128 points of some block.
All inputs are finite; a program needn't handle non-finite values. No bound on the sum of `sea` on one device may be relied on, other than what follows from the above.
Results may differ from a plain program's by a relative error of at most 0.0049.
Values may be sent and summed in bfloat16 or wider, within the bound.
No kernel may reach another device: no remote copies, remote signals or barrier semaphores. Data moves between devices by JAX's collectives and lax.ppermute only.
A program may use at most 64 MiB of HBM per device.

v0:
```python
import jax
import jax.numpy as jnp
from jax import lax
from jax.sharding import PartitionSpec as P


def padded_2(block, sides, width):
    for axis, dim in sides:
        count = lax.axis_size(axis)
        forward = [(i, i + 1) for i in range(count - 1)]
        backward = [(target, source) for source, target in forward]
        low = lax.ppermute(
            lax.slice_in_dim(block, block.shape[dim] - width, None, axis=dim), axis, forward
        )
        high = lax.ppermute(lax.slice_in_dim(block, 0, width, axis=dim), axis, backward)
        block = jnp.concatenate([low, block, high], axis=dim)
    return block


def advect(padded, sea_mask, courant, upwind):
    center = padded[:, 1:-1, 1:-1]
    donor_x = jnp.where(upwind[:, 0][:, None, None] == 0, padded[:, :-2, 1:-1], padded[:, 2:, 1:-1])
    donor_y = jnp.where(upwind[:, 1][:, None, None] == 0, padded[:, 1:-1, :-2], padded[:, 1:-1, 2:])
    moved = (
        center
        - courant[:, 0][:, None, None] * (center - donor_x)
        - courant[:, 1][:, None, None] * (center - donor_y)
    )
    return (moved * sea_mask[None]).astype(jnp.bfloat16)


def local(spectrum, courant, upwind, coupling, sea, owner):
    local_bins = spectrum.shape[0]
    lon_rows = spectrum.shape[1]
    bins_count = lax.axis_size("bins")
    lat_cells = spectrum.shape[2] // bins_count
    masked = spectrum * sea.astype(jnp.bfloat16)[None]
    local_sea = lax.dynamic_slice_in_dim(
        sea, lax.axis_index("bins") * lat_cells, lat_cells, 1
    ).astype(jnp.float32)
    first_bin = lax.axis_index("bins") * local_bins
    my_courant = lax.dynamic_slice_in_dim(courant, first_bin, local_bins, 0)
    my_upwind = lax.dynamic_slice_in_dim(upwind, first_bin, local_bins, 0)
    extended = padded_2(masked, (("pts", 1),), 1)
    extended = jnp.pad(extended.astype(jnp.float32), ((0, 0), (0, 0), (1, 1)))
    moved = advect(extended, sea.astype(jnp.float32), my_courant, my_upwind)
    columns = lax.all_to_all(moved, "bins", split_axis=2, concat_axis=0, tiled=True)
    all_bins = columns.shape[0]
    points = lon_rows * lat_cells
    flat = columns.reshape(all_bins, points)
    energy = jnp.mean(flat.astype(jnp.float32), axis=0)
    coupled = jnp.einsum("bp,bc->pc", flat, coupling, preferred_element_type=jnp.float32)
    weights = local_sea.reshape(points)
    updated = (
        weights[:, None] * (flat.astype(jnp.float32).T + coupled) / (1.0 + energy)[:, None]
    ).astype(jnp.bfloat16)
    owners_count = lax.axis_size("pts")
    capacity = max(2, (2 * points + owners_count - 1) // owners_count)
    target = owner.reshape(points)
    onehot = (target[:, None] == jnp.arange(owners_count, dtype=jnp.int32)[None, :]).astype(
        jnp.int32
    )
    slot_rank = jnp.sum(jnp.cumsum(onehot, axis=0) * onehot, axis=1) - 1
    slot_index = target * capacity + slot_rank
    selector = (
        slot_index[None, :] == jnp.arange(owners_count * capacity, dtype=jnp.int32)[:, None]
    ).astype(jnp.bfloat16)
    outgoing = jnp.dot(selector, updated, preferred_element_type=jnp.float32).astype(jnp.bfloat16)
    outgoing = outgoing.reshape(owners_count, capacity, all_bins)
    received = lax.all_to_all(outgoing, "pts", split_axis=0, concat_axis=0, tiled=True)
    return received.reshape(1, 1, owners_count * capacity, all_bins)


def solution(mesh):
    placed = (P("bins", "pts", None), P(), P(), P(), P("pts", None), P("pts", "bins", None, None))
    return jax.shard_map(
        local, mesh=mesh, in_specs=placed, out_specs=P("pts", "bins", None, None), check_vma=False
    )
```

profile of v0, /device:TPU:0, one launch (start us, length us, event | category | flops | bytes accessed | tf_op | source)
XLA Modules:
  0.0 117.3 jit_solution(11773283145271978311)
XLA Ops:
  0.0 0.8 fusion.21
  0.8 1.8 %copy_multiply_fusion = bf16[324,4,512]{2,0,1:T(8,128)(2,1)S(1)} fusion(bf16[324,4,512]{2,1,0:T(4,128)(2,1)} %param.6, bf16[4,512]{1,0:T(4,128)(2,1)S(1)} %get-tuple-element.12), kind=kLoop, calls=%fused_computation.22 | loop fusion | flops 663552 | bytes 2658304 | tf_op jit(solution)/shard_map/mul | solution.py:37
  2.6 1.3 %collective-permute-start.1 = (bf16[324,1,512]{2,0,1:T(8,128)(2,1)S(1)}, bf16[324,1,512]{2,0,1:T(8,128)(2,1)S(1)}, u32[]{:S(2)}, u32[]{:S(2)}) collective-permute-start(bf16[324,1,512]{2,0,1:T(8,128)(2,1)S(1)} %get-tuple-element.10), channel_id=1, source_target_pairs={{4,0},{8,4},{12,8},{16,12},{20,16},{24,20},{28,24},{5,1},{9,5},{13... | collective-permute-start | bytes 995336 | tf_op jit(solution)/shard_map/ppermute | solution.py:15
  3.9 3.1 %collective-permute-start = (bf16[324,1,512]{2,0,1:T(8,128)(2,1)S(1)}, bf16[324,1,512]{2,0,1:T(8,128)(2,1)S(1)}, u32[]{:S(2)}, u32[]{:S(2)}) collective-permute-start(bf16[324,1,512]{2,0,1:T(8,128)(2,1)S(1)} %get-tuple-element.9), channel_id=1, source_target_pairs={{0,4},{4,8},{8,12},{12,16},{16,20},{20,24},{24,28},{1,5},{5,9},{9,... | collective-permute-start | bytes 995336 | tf_op jit(solution)/shard_map/ppermute | solution.py:12
  6.9 0.9 dynamic-slice_reduce_fusion.1
  7.8 0.9 compare_reduce_fusion.1
  8.7 0.0 collective-permute-done.1
  8.7 0.3 maximum_convert_fusion
  9.0 2.1 %fusion.8 = bf16[324,4,512]{2,0,1:T(8,128)(2,1)S(1)} fusion(f32[324,6,512]{2,0,1:T(8,128)S(1)} %maximum_convert_fusion, f32[4,512]{1,0:T(4,128)S(1)} %get-tuple-element.11, f32[324]{0:T(512)S(1)} %get-tuple-element.8, f32[324]{0:T(512)S(1)} %get-tuple-element.7, pred[324]{0:T(512)(128)(4,1)S(1)} %get-tuple-element.6, pred[324]{0:T(512)(128)(4,1)S(1)} %get-tuple-element.5), kind=kLoop, calls=%fused_computation.12 | loop fusion | flops 6635520 | bytes 13431808 | tf_op jit(solution)/shard_map/convert_element_type | solution.py:29
  11.1 0.0 copy-start
  11.1 2.2 %copy.18 = bf16[324,4,512]{0,1,2:T(4,128)(2,1)} copy(bf16[324,4,512]{2,0,1:T(8,128)(2,1)S(1)} %fusion.8) | data formatting | bytes 2654208 | tf_op jit(solution)/shard_map/convert_element_type | solution.py:29
  13.4 6.3 %all-to-all-start = ((bf16[324,4,512]{0,1,2:T(4,128)(2,1)}), bf16[324,4,512]{0,1,2:T(4,128)(2,1)S(1)}, u32[]{:S(2)}, u32[]{:S(2)}) async-start(bf16[324,4,512]{0,1,2:T(4,128)(2,1)} %copy.18), calls=%async_computation | async-start | bytes 3145728 | tf_op jit(solution)/shard_map/all_to_all | solution.py:47
  19.7 1.1 reduce-window.6
  20.9 0.2 slice_reduce_fusion
  21.1 0.7 convert_bitcast_fusion
  21.8 0.1 fusion.18
  21.9 35.1 %all-to-all-done = bf16[324,4,512]{0,1,2:T(4,128)(2,1)S(1)} async-done(((bf16[324,4,512]{0,1,2:T(4,128)(2,1)}), bf16[324,4,512]{0,1,2:T(4,128)(2,1)S(1)}, u32[]{:S(2)}, u32[]{:S(2)}) %all-to-all-start) | async-done | bytes 1327136 | tf_op jit(solution)/shard_map/all_to_all | solution.py:47
  57.0 1.3 %copy.19 = bf16[324,4,4,128]{3,1,0,2:T(4,128)(2,1)S(1)} copy(bf16[324,4,4,128]{0,1,3,2:T(4,128)(2,1)S(1)} %bitcast.35) | data formatting | bytes 2654208 | tf_op jit(solution)/shard_map/all_to_all | solution.py:47
  58.3 1.4 %convert_reduce_fusion = f32[4,128]{1,0:T(4,128)S(1)} fusion(bf16[324,4,4,128]{3,1,0,2:T(4,128)(2,1)S(1)} %copy.19), kind=kLoop, calls=%fused_computation.18 | loop fusion | flops 1326592 | bytes 1329152 | tf_op jit(solution)/shard_map/reduce_sum | solution.py:51
  59.7 7.3 %fusion.12 = bf16[162,8,8,128]{3,2,1,0:T(8,128)(2,1)} fusion(s32[512]{0:T(512)S(1)} %add_add_fusion, bf16[1296,1296]{1,0:T(8,128)(2,1)} %param.9, bf16[162,8,4,128]{3,2,1,0:T(4,128)(2,1)S(1)} %bitcast.36, f32[512]{0:T(512)S(1)} %add_bitcast_fusion, f32[512]{0:T(512)S(1)} %convert_bitcast_fusion), kind=kOutput, calls=%fused_computation.21 | convolution fusion | flops 3084050432 | bytes 7346688 | tf_op jit(solution)/shard_map/dot_general | solution.py:68
  67.0 2.2 %copy.32 = bf16[162,8,8,128]{3,2,0,1:T(8,128)(2,1)S(1)} copy(bf16[162,8,8,128]{3,2,1,0:T(8,128)(2,1)} %fusion.12) | data formatting | bytes 5308416 | tf_op jit(solution)/shard_map/reshape | solution.py:69
  69.2 40.0 %all_to_all.20 = bf16[8,128,1296]{1,2,0:T(8,128)(2,1)S(1)} all-to-all(bf16[8,128,1296]{1,2,0:T(8,128)(2,1)S(1)} %bitcast.34), channel_id=1, replica_groups=mesh['pts'=8,'bins'=4] {'pts'}, dimensions={0} | all-to-all | bytes 5308416 | tf_op jit(solution)/shard_map/all_to_all | solution.py:70
  109.3 5.5 %copy.21 = bf16[8,128,1296]{1,0,2:T(8,128)(2,1)S(1)} copy(bf16[8,128,1296]{1,2,0:T(8,128)(2,1)S(1)} %all_to_all.20) | data formatting | bytes 5308416 | tf_op jit(solution)/shard_map/all_to_all | solution.py:70
  114.7 2.6 %reshape.78 = bf16[1,1,1024,1296]{2,3,1,0:T(8,128)(2,1)} reshape(bf16[8,128,1296]{1,0,2:T(8,128)(2,1)S(1)} %copy.21) | data formatting | bytes 5308416 | tf_op jit(solution)/shard_map/reshape | solution.py:71
  (8 shorter events, 0.1 us)
Async XLA Ops:
  2.6 6.1 %collective-permute-start.1 = (bf16[324,1,512]{2,0,1:T(8,128)(2,1)S(1)}, bf16[324,1,512]{2,0,1:T(8,128)(2,1)S(1)}, u32[]{:S(2)}, u32[]{:S(2)}) collective-permute-start(bf16[324,1,512]{2,0,1:T(8,128)(2,1)S(1)} %get-tuple-element.10), channel_id=1, source_target_pairs={{4,0},{8,4},{12,8},{16,12},{20,16},{24,20},{28,24},{5,1},{9,5},{13... | collective-permute-start | bytes 995336 | tf_op jit(solution)/shard_map/ppermute | solution.py:15
  3.9 4.8 %collective-permute-start = (bf16[324,1,512]{2,0,1:T(8,128)(2,1)S(1)}, bf16[324,1,512]{2,0,1:T(8,128)(2,1)S(1)}, u32[]{:S(2)}, u32[]{:S(2)}) collective-permute-start(bf16[324,1,512]{2,0,1:T(8,128)(2,1)S(1)} %get-tuple-element.9), channel_id=1, source_target_pairs={{0,4},{4,8},{8,12},{12,16},{16,20},{20,24},{24,28},{1,5},{5,9},{9,... | collective-permute-start | bytes 995336 | tf_op jit(solution)/shard_map/ppermute | solution.py:12
  11.1 8.6 %copy-start = (s32[1,1,512,1]{2,3,1,0:T(1,128)S(1)}, s32[1,1,512,1]{2,3,1,0:T(1,128)}, u32[]{:S(2)}) copy-start(s32[1,1,512,1]{2,3,1,0:T(1,128)} %param.11) | copy-start | bytes 6148
  13.4 43.6 %all-to-all-start = ((bf16[324,4,512]{0,1,2:T(4,128)(2,1)}), bf16[324,4,512]{0,1,2:T(4,128)(2,1)S(1)}, u32[]{:S(2)}, u32[]{:S(2)}) async-start(bf16[324,4,512]{0,1,2:T(4,128)(2,1)} %copy.18), calls=%async_computation | async-start | bytes 3145728 | tf_op jit(solution)/shard_map/all_to_all | solution.py:47
where the time goes:
time: 118 us; the launch traced here: 117 us
  blocking collectives  40 us (34%)
  waiting for transfers between devices  35.1 us (30%)
  local copies, waits for them, and re-layouts  15 us (13%)
  starting transfers between devices  10.7 us (9%)
  other arithmetic  9.15 us (8%)
  matrix products  7.29 us (6%)
    all_to_all x1, blocking collectives, local(): lax.all_to_all(outgoing, 'pts', split_axis=0, concat_axis=0, tiled=True)  40 us
    all_to_all x1, waiting for transfers between devices, local(): lax.all_to_all(moved, 'bins', split_axis=2, concat_axis=0, tiled=True)  35.1 us
    dot_general x1, matrix products, local(): jnp.dot(selector, updated, preferred_element_type=jnp.float32)  7.29 us
    all_to_all x1, starting transfers between devices, local(): lax.all_to_all(moved, 'bins', split_axis=2, concat_axis=0, tiled=True)  6.32 us
    all_to_all x1, local copies, waits for them, and re-layouts, local(): lax.all_to_all(outgoing, 'pts', split_axis=0, concat_axis=0, tiled=True)  5.48 us
    ppermute x1, starting transfers between devices, padded_2(): lax.ppermute(lax.slice_in_dim(block, block.shape[dim] - width, None, axis...  3.05 us
    reshape x1, local copies, waits for them, and re-layouts, local(): return received.reshape(1, 1, owners_count * capacity, all_bins)  2.59 us
  transfers between devices with their start and end apart: 3, of which 1 were waited for; matrix products, arithmetic and copies ran while one was open for 3% of the time, Pallas kernels for 0%

commit v1 on v0

--- a/solution.py
+++ b/solution.py
@@ -1,7 +1,280 @@
+import functools
+
 import jax
 import jax.numpy as jnp
 from jax import lax
+from jax.experimental import pallas as pl
+from jax.experimental.pallas import tpu as pltpu
 from jax.sharding import PartitionSpec as P
+
+F32 = jnp.float32
+BF16 = jnp.bfloat16
+I32 = jnp.int32
+LANES = 128
+CHUNKS = 2
+NT = (((1,), (1,)), ((), ()))
+
+
+def round_up(size, unit):
+    return -(-size // unit) * unit
+
+
+def iota(shape, axis):
+    return lax.broadcasted_iota(I32, shape, axis)
+
+
+def dot_nt(lhs, rhs):
+    return lax.dot_general(lhs, rhs, NT, preferred_element_type=F32)
+
+
+def pack_kernel(rows_out, bins_axis, owners_count, half, *refs):
+    planes, low, high, coef, sea = refs[:5]
+    owner = refs[5 : 5 + bins_axis]
+    chunks = refs[5 + bins_axis : 5 + bins_axis + CHUNKS * bins_axis]
+    meta = refs[5 + bins_axis + CHUNKS * bins_axis]
+    moved = refs[-1]
+    lon_rows, rows, lats = planes.shape
+    points = lon_rows * LANES
+    me = lax.axis_index("bins")
+    me_pts = lax.axis_index("pts")
+
+    tile = 16
+    lane = iota((tile, lats), 1)
+    sea_f = sea[...].astype(F32)
+
+    def advect(step, carry):
+        at = pl.ds(pl.multiple_of(step * tile, tile), tile)
+        c = coef[at, :]
+        cx, cy, ux, uy = c[:, 0:1], c[:, 1:2], c[:, 2:3], c[:, 3:4]
+        masked = [low[at, :].astype(F32)]
+        masked += [planes[l, at, :].astype(F32) for l in range(lon_rows)]
+        masked += [high[at, :].astype(F32)]
+        for l in range(lon_rows):
+            center = masked[l + 1]
+            donor_x = jnp.where(ux == 0.0, masked[l], masked[l + 2])
+            left = jnp.where(lane == 0, 0.0, pltpu.roll(center, 1, 1))
+            right = jnp.where(lane == lats - 1, 0.0, pltpu.roll(center, lats - 1, 1))
+            donor_y = jnp.where(uy == 0.0, left, right)
+            value = center - cx * (center - donor_x) - cy * (center - donor_y)
+            moved[l, at, :] = (value * sea_f[l : l + 1, :]).astype(BF16)
+        return carry
+
+    lax.fori_loop(0, rows // tile, advect, 0)
+
+    owners_id = iota((owners_count, points), 0)
+    hot = [(owner[m][...] == owners_id).astype(F32) for m in range(bins_axis)]
+    earlier = (iota((points, points), 0) < iota((points, points), 1)).astype(F32).astype(BF16)
+    before = jnp.dot(
+        jnp.concatenate(hot, axis=0).astype(BF16), earlier, preferred_element_type=F32
+    )
+    place_id = iota((points, points), 0)
+    for m in range(bins_axis):
+        own = owner[m][...]
+        count = jnp.sum(hot[m], axis=1, keepdims=True)
+        offset = jnp.sum(jnp.where(owners_id < own, count, 0.0), axis=0, keepdims=True)
+        mine = before[m * owners_count : (m + 1) * owners_count, :]
+        rank = jnp.sum(hot[m] * mine, axis=0, keepdims=True)
+        key = (offset + rank).astype(I32)
+        place = (key & 1) * half + (key >> 1)
+        order = (place_id == place).astype(F32).astype(BF16)
+        block = me ^ m
+        at = pl.ds(pl.multiple_of(block * LANES, LANES), LANES)
+        lhs = jnp.concatenate([moved[l, :, at] for l in range(lon_rows)], axis=1)
+        ordered = dot_nt(lhs, order)[:rows_out].astype(BF16)
+        for c in range(CHUNKS):
+            chunks[c * bins_axis + m][...] = ordered[:, c * half : (c + 1) * half]
+        if m == 0:
+            first = offset.astype(I32)
+            slot = (key - first - (((key & 1) - first) & 1)) >> 1
+            weight = jnp.concatenate([sea[l : l + 1, at].astype(F32) for l in range(lon_rows)], axis=1)
+            facts = jnp.concatenate(
+                [slot.astype(F32), (own ^ me_pts).astype(F32), rank, weight]
+                + [jnp.zeros((1, points), F32)] * 4,
+                axis=0,
+            )
+            meta[...] = dot_nt(facts.astype(BF16), order)
+
+
+def couple_kernel(chunk, bins_axis, owners_count, all_bins, pad_row, slots, *refs):
+    blocks = refs[:bins_axis]
+    weights, meta = refs[bins_axis : bins_axis + 2]
+    outs = refs[bins_axis + 2 : -1]
+    values = refs[-1]
+    rows, width = blocks[0].shape
+    half_rows = values.shape[0] // 2
+    me = lax.axis_index("bins")
+    for m in range(bins_axis):
+        at = pl.ds(pl.multiple_of((me ^ m) * rows, 8), rows)
+        values[at, :] = blocks[m][...].astype(F32)
+    flat = values[...].astype(BF16)
+    energy = jnp.sum(values[...], axis=0, keepdims=True) / all_bins
+    facts = meta[:, chunk * width : (chunk + 1) * width]
+    scale = facts[3:4, :] / (1.0 + energy)
+    slot, towards, rank = facts[0:1, :].astype(I32), facts[1:2, :].astype(I32), facts[2:3, :]
+    slot_id = iota((owners_count * slots, width), 0)
+    straight = (slot_id == towards * slots + slot).astype(F32).astype(BF16)
+    crossed = (slot_id == (towards ^ 1) * slots + slot).astype(F32).astype(BF16)
+    is_rank = iota((half_rows, width), 0) == pad_row
+    sent = []
+    for group in range(2):
+        at = slice(group * half_rows, (group + 1) * half_rows)
+        coupled = jnp.dot(weights[at, :], flat, preferred_element_type=F32)
+        updated = (values[at, :] + coupled) * scale
+        updated = jnp.where(is_rank, rank, updated).astype(BF16)
+        sent.append(dot_nt(updated, straight if group == chunk else crossed).astype(BF16))
+    even, odd = sent[chunk], sent[1 - chunk]
+    is_low = iota((half_rows, LANES), 1) < slots
+    for t in range(owners_count // 2):
+        at = slice(t * LANES, (t + 1) * LANES)
+        outs[t][0] = jnp.where(is_low, even[:, at], odd[:, at])
+        outs[t][1] = jnp.where(is_low, odd[:, at], even[:, at])
+
+
+def place_kernel(owners_count, rows, real, slots, *refs):
+    pairs = owners_count // 2
+    arrivals = refs[: CHUNKS * pairs]
+    swapped = refs[CHUNKS * pairs : CHUNKS * pairs + CHUNKS]
+    out = refs[CHUNKS * pairs + CHUNKS]
+    staged, sems = refs[-2:]
+    me = lax.axis_index("pts")
+    half_rows = arrivals[0].shape[1]
+    is_low = iota((half_rows, LANES), 1) < slots
+    slot_id = iota((LANES, LANES), 0)
+    copies = []
+    for x in range(owners_count):
+        t = x // 2
+        if x % 2 == 0:
+            first, second = arrivals[t][0], arrivals[pairs + t][0]
+        else:
+            second, first = swapped[0][t], swapped[1][t]
+        pieces = []
+        for lhs in (jnp.where(is_low, first, second), jnp.where(is_low, second, first)):
+            rank = lhs[real : real + 16 - real % 16, :].astype(F32)[0:1, :].astype(I32)
+            place = (slot_id == rank).astype(F32).astype(BF16)
+            rows_f = dot_nt(lhs, place)
+            for at in range(0, half_rows, rows):
+                pieces.append(rows_f[at : at + real, :])
+        staged[x] = jnp.concatenate(pieces, axis=0).astype(BF16)
+        at = pl.ds(pl.multiple_of((me ^ x) * LANES, LANES), LANES)
+        copy = pltpu.make_async_copy(staged.at[x], out.at[:, at], sems.at[x])
+        copy.start()
+        copies.append(copy)
+    for copy in copies:
+        copy.wait()
+
+
+def gate_kernel(count, after, *refs):
+    del count, after, refs
+
+
+def gate(arrays, after):
+    count = len(arrays)
+    return pl.pallas_call(
+        functools.partial(gate_kernel, count, len(after)),
+        out_shape=[jax.ShapeDtypeStruct(a.shape, a.dtype) for a in arrays],
+        in_specs=[pl.BlockSpec(memory_space=pl.ANY)] * (count + len(after)),
+        out_specs=[pl.BlockSpec(memory_space=pl.ANY)] * count,
+        input_output_aliases={i: i for i in range(count)},
+        name="gate",
+    )(*arrays, *after)
+
+
+def params(mib):
+    return pltpu.CompilerParams(vmem_limit_bytes=mib << 20)
+
+
+def vmem(count):
+    return [pl.BlockSpec(memory_space=pltpu.VMEM)] * count
+
+
+def cost(flops, bytes_accessed):
+    return pl.CostEstimate(flops=int(flops), bytes_accessed=int(bytes_accessed), transcendentals=0)
+
+
+def exchange(array, axis, offset):
+    return lax.ppermute(array, axis, [(i, i ^ offset) for i in range(lax.axis_size(axis))])
+
+
+def chunked(spectrum, courant, upwind, coupling, sea, owner):
+    local_bins, lon_rows, lats = spectrum.shape
+    all_bins = courant.shape[0]
+    bins_axis = lax.axis_size("bins")
+    owners_count = lax.axis_size("pts")
+    points = lon_rows * LANES
+    half = points // CHUNKS
+    slots = 2 * points // owners_count // CHUNKS
+    tall = round_up(local_bins, 16)
+    rows = round_up(local_bins + 1, 8)
+    half_rows = bins_axis * rows // 2
+    first_bin = lax.axis_index("bins") * local_bins
+
+    masked = spectrum * sea.astype(BF16)[None]
+    planes = jnp.pad(jnp.transpose(masked, (1, 0, 2)), ((0, 0), (0, tall - local_bins), (0, 0)))
+    up = [(i, i + 1) for i in range(owners_count - 1)]
+    down = [(i + 1, i) for i in range(owners_count - 1)]
+    low = lax.ppermute(planes[lon_rows - 1], "pts", up)
+    high = lax.ppermute(planes[0], "pts", down)
+    own = owner.reshape(1, points)
+    owners = [own] + [exchange(own, "bins", m) for m in range(1, bins_axis)]
+    coef = jnp.concatenate([courant, upwind.astype(F32)], axis=1)
+    coef = lax.dynamic_slice_in_dim(coef, first_bin, local_bins, 0)
+    coef = jnp.pad(coef, ((0, tall - local_bins), (0, 0)))
+
+    weights = jnp.transpose(coupling).reshape(bins_axis, local_bins, bins_axis, local_bins)
+    extra = rows - local_bins
+    weights = jnp.pad(weights, ((0, 0), (0, extra), (0, 0), (0, extra)))
+    weights = weights.reshape(bins_axis * rows, bins_axis * rows)
+
+    packed = pl.pallas_call(
+        functools.partial(pack_kernel, rows, bins_axis, owners_count, half),
+        out_shape=[jax.ShapeDtypeStruct((rows, half), BF16)] * (CHUNKS * bins_axis)
+        + [jax.ShapeDtypeStruct((8, points), F32)],
+        in_specs=vmem(5 + bins_axis),
+        out_specs=vmem(CHUNKS * bins_axis + 1),
+        scratch_shapes=[pltpu.VMEM((lon_rows, tall, lats), BF16)],
+        compiler_params=params(24),
+        cost_estimate=cost(2 * bins_axis * tall * points * points, 4e6),
+        name="pack",
+    )(planes, low, high, coef, sea, *owners)
+    meta = packed[-1]
+
+    arrivals, swaps, got = [], [], None
+    for c in range(CHUNKS):
+        blocks = packed[c * bins_axis : (c + 1) * bins_axis]
+        if got is not None:
+            blocks = gate(blocks, got)
+        got = [exchange(blocks[m], "bins", m) for m in range(1, bins_axis)]
+        pays = pl.pallas_call(
+            functools.partial(
+                couple_kernel, c, bins_axis, owners_count, all_bins, local_bins, slots
+            ),
+            out_shape=[jax.ShapeDtypeStruct((2, half_rows, LANES), BF16)] * (owners_count // 2),
+            in_specs=vmem(bins_axis + 2),
+            out_specs=vmem(owners_count // 2),
+            scratch_shapes=[pltpu.VMEM((bins_axis * rows, half), F32)],
+            compiler_params=params(32),
+            cost_estimate=cost(2 * all_bins * all_bins * half + 4 * all_bins * half * 512, 6e6),
+            name="couple",
+        )(blocks[0], *got, weights, meta)
+        came = [pays[0]]
+        came += [exchange(pays[t], "pts", 2 * t) for t in range(1, owners_count // 2)]
+        swaps.append(exchange(jnp.stack([a[1] for a in came]), "pts", 1))
+        arrivals += came
+
+    placed = pl.pallas_call(
+        functools.partial(place_kernel, owners_count, rows, local_bins, slots),
+        out_shape=jax.ShapeDtypeStruct((all_bins, owners_count * LANES), BF16),
+        in_specs=vmem(len(arrivals) + CHUNKS),
+        out_specs=pl.BlockSpec(memory_space=pl.ANY),
+        scratch_shapes=[
+            pltpu.VMEM((owners_count, all_bins, LANES), BF16),
+            pltpu.SemaphoreType.DMA((owners_count,)),
+        ],
+        compiler_params=params(32),
+        cost_estimate=cost(4 * all_bins * LANES * LANES * owners_count, 8e6),
+        name="place",
+    )(*arrivals, *swaps)
+    return jnp.transpose(placed).reshape(1, 1, owners_count * LANES, all_bins)
 
 
 def padded_2(block, sides, width):
@@ -29,7 +302,7 @@
     return (moved * sea_mask[None]).astype(jnp.bfloat16)
 
 
-def local(spectrum, courant, upwind, coupling, sea, owner):
+def whole(spectrum, courant, upwind, coupling, sea, owner):
     local_bins = spectrum.shape[0]
     lon_rows = spectrum.shape[1]
     bins_count = lax.axis_size("bins")
@@ -71,6 +344,22 @@
     return received.reshape(1, 1, owners_count * capacity, all_bins)
 
 
+def local(spectrum, courant, upwind, coupling, sea, owner):
+    bins_axis, owners_count = lax.axis_size("bins"), lax.axis_size("pts")
+    points = owner.shape[2]
+    suits = (
+        spectrum.shape[2] == bins_axis * LANES
+        and points % (2 * LANES) == 0
+        and 2 * points == owners_count * LANES
+        and bins_axis & (bins_axis - 1) == 0
+        and owners_count & (owners_count - 1) == 0
+        and bins_axis % 2 == 0
+        and owners_count <= 8
+    )
+    form = chunked if suits else whole
+    return form(spectrum, courant, upwind, coupling, sea, owner)
+
+
 def solution(mesh):
     placed = (P("bins", "pts", None), P(), P(), P(), P("pts", None), P("pts", "bins", None, None))
     return jax.shard_map(

time: 118 us -> 109 us (0.924)
  the two profiles are of different devices: /device:TPU:0 before, /device:TPU:11 now
where the time goes in v1:
time: 109 us; the launch traced here: 108 us
  local copies, waits for them, and re-layouts  39.8 us (37%)
  starting transfers between devices  27.5 us (25%)
  waiting for transfers between devices  25.4 us (23%)
  Pallas kernels  12.6 us (12%)
  other arithmetic  2.72 us (2%)
    ppermute x17, waiting for transfers between devices, exchange(): lax.ppermute(array, axis, [(i, i ^ offset) for i in range(lax.axis_size(a...  25.4 us
    ppermute x17, starting transfers between devices, exchange(): lax.ppermute(array, axis, [(i, i ^ offset) for i in range(lax.axis_size(a...  21 us
    reshape x2, local copies, waits for them, and re-layouts, chunked(): jnp.transpose(coupling)  18 us
    unnamed x29, local copies, waits for them, and re-layouts  8.03 us
    reshape x1, local copies, waits for them, and re-layouts, chunked(): weights = weights.reshape(bins_axis * rows, bins_axis * rows)  7.73 us
    pallas_call x2, Pallas kernels, chunked(): pl.pallas_call(functools.partial(couple_kernel, c, bins_axis, owners_coun...  5.85 us
    pad x1, local copies, waits for them, and re-layouts, chunked(): weights = jnp.pad(weights, ((0, 0), (0, extra), (0, 0), (0, extra)))  5.74 us
    pallas_call x1, Pallas kernels, chunked(): pl.pallas_call(functools.partial(pack_kernel, rows, bins_axis, owners_cou...  4.37 us
  transfers between devices with their start and end apart: 19, of which 9 were waited for; matrix products, arithmetic and copies ran while one was open for 30% of the time, Pallas kernels for 3%

profile of v1, /device:TPU:11, one launch (start us, length us, event | category | flops | bytes accessed | tf_op | source)
XLA Modules:
  0.0 108.3 jit_solution(7707761461222333613)
XLA Ops:
  0.7 1.8 %fusion = bf16[4,324,512]{2,1,0:T(8,128)(2,1)S(1)} fusion(bf16[324,4,512]{2,1,0:T(4,128)(2,1)} %param.6, bf16[4,512]{1,0:T(4,128)(2,1)S(1)} %convert_element_type.12), kind=kLoop, calls=%fused_computation.1 | loop fusion | flops 663552 | bytes 2658304 | tf_op jit(solution)/shard_map/transpose | solution.py:212
  2.5 2.6 %collective-permute-start.1 = (bf16[336,512]{1,0:T(8,128)(2,1)S(1)}, bf16[336,512]{1,0:T(8,128)(2,1)S(1)}, u32[]{:S(2)}, u32[]{:S(2)}) collective-permute-start(bf16[336,512]{1,0:T(8,128)(2,1)S(1)} %get-tuple-element.47), channel_id=1, source_target_pairs={{4,0},{8,4},{12,8},{16,12},{20,16},{24,20},{28,24},{5,1},{9,5},{13... | collective-permute-start | bytes 1032200 | tf_op jit(solution)/shard_map/ppermute | solution.py:216
  5.1 3.9 %collective-permute-start = (bf16[336,512]{1,0:T(8,128)(2,1)S(1)}, bf16[336,512]{1,0:T(8,128)(2,1)S(1)}, u32[]{:S(2)}, u32[]{:S(2)}) collective-permute-start(bf16[336,512]{1,0:T(8,128)(2,1)S(1)} %get-tuple-element.48), channel_id=1, source_target_pairs={{0,4},{4,8},{8,12},{12,16},{16,20},{20,24},{24,28},{1,5},{5,9},{9,... | collective-permute-start | bytes 1032200 | tf_op jit(solution)/shard_map/ppermute | solution.py:215
  13.9 4.4 %pack.1 = (bf16[328,256]{1,0:T(8,128)(2,1)S(1)}, bf16[328,256]{1,0:T(8,128)(2,1)S(1)}, bf16[328,256]{1,0:T(8,128)(2,1)S(1)}, bf16[328,256]{1,0:T(8,128)(2,1)S(1)...) custom-call(bf16[4,336,512]{2,1,0:T(8,128)(2,1)S(1)} %pad.12.refs_0_, ...), custom_call_target="tpu_custom_call" | custom-call | flops 704643072 | bytes 4000000 | tf_op jit(solution)/shard_map/pack/pallas_call | solution.py:228
  21.0 2.0 %collective-permute-start.5 = (bf16[328,256]{1,0:T(8,128)(2,1)S(1)}, bf16[328,256]{1,0:T(8,128)(2,1)S(1)}, u32[]{:S(2)}, u32[]{:S(2)}) collective-permute-start(bf16[328,256]{1,0:T(8,128)(2,1)S(1)} %get-tuple-element.27), channel_id=1, source_target_pairs={{0,1},{1,0},{2,3},{3,2},{4,5},{5,4},{6,7},{7,6},{8,9},{9,8},{10,11... | collective-permute-start | bytes 503816 | tf_op jit(solution)/shard_map/ppermute | solution.py:195
  24.5 9.2 %reshape.14 = bf16[4,324,4,324]{1,0,3,2:T(4,128)(2,1)} reshape(bf16[1296,1296]{0,1:T(8,128)(2,1)} %bitcast.17) | data formatting | bytes 6718464 | tf_op jit(solution)/shard_map/reshape | solution.py:223
  33.7 8.8 %copy.17 = bf16[4,324,4,324]{3,2,1,0:T(4,128)(2,1)} copy(bf16[4,324,4,324]{1,0,3,2:T(4,128)(2,1)} %reshape.14) | data formatting | bytes 6718464 | tf_op jit(solution)/shard_map/reshape | solution.py:223
  42.5 5.7 %pad.14 = bf16[4,328,4,328]{3,2,1,0:T(4,128)(2,1)} pad(bf16[4,324,4,324]{3,2,1,0:T(4,128)(2,1)} %copy.17, bf16[]{:T(256)} %constant.3.clone.1), padding=0_0x0_4x0_0x0_4 | pad | bytes 6801922 | tf_op jit(solution)/shard_map/jit(_pad)/pad | solution.py:225
  48.2 7.7 %reshape.15.refs_4_ = bf16[1312,1312]{1,0:T(8,128)(2,1)} reshape(bf16[4,328,4,328]{3,2,1,0:T(4,128)(2,1)} %pad.14) | data formatting | bytes 6885376 | tf_op jit(solution)/shard_map/reshape | solution.py:226
  56.0 2.2 %copy-done = bf16[1312,1312]{1,0:T(8,128)(2,1)S(1)} copy-done((bf16[1312,1312]{1,0:T(8,128)(2,1)S(1)}, bf16[1312,1312]{1,0:T(8,128)(2,1)}, u32[]{:S(2)}) %copy-start) | copy-done | bytes 3442712
  58.2 2.9 %couple.2 = (bf16[2,656,128]{2,1,0:T(8,128)(2,1)S(1)}, bf16[2,656,128]{2,1,0:T(8,128)(2,1)S(1)}, bf16[2,656,128]{2,1,0:T(8,128)(2,1)S(1)}, bf16[2,656,128]{2,1,0:T(8,128)(2,1)S(1)}) custom-call(bf16[328,256]{1,0:T(8,128)(2,1)S(1)} %get-tuple-element.26.refs_0_, bf16[328,256]{1,0:T(8,128)(2,1)S(1)} %collective-permute-done.5.refs_1_.refs_4_, ...), custom_call_target="tpu_custom_call" | custom-call | flops 1539440640 | bytes 6000000 | tf_op jit(solution)/shard_map/couple/pallas_call | solution.py:247
  61.3 2.1 %collective-permute-start.11 = (bf16[328,256]{1,0:T(8,128)(2,1)}, bf16[328,256]{1,0:T(8,128)(2,1)S(1)}, u32[]{:S(2)}, u32[]{:S(2)}) collective-permute-start(bf16[328,256]{1,0:T(8,128)(2,1)} %get-tuple-element.40), channel_id=1, source_target_pairs={{0,1},{1,0},{2,3},{3,2},{4,5},{5,4},{6,7},{7,6},{8,9},{9,8},{10,11... | collective-permute-start | bytes 503816 | tf_op jit(solution)/shard_map/ppermute | solution.py:195
  65.5 2.9 %collective-permute-done.11.refs_1_ = bf16[328,256]{1,0:T(8,128)(2,1)S(1)} collective-permute-done((bf16[328,256]{1,0:T(8,128)(2,1)}, bf16[328,256]{1,0:T(8,128)(2,1)S(1)}, u32[]{:S(2)}, u32[]{:S(2)}) %collective-permute-start.11) | collective-permute-done | bytes 167968 | tf_op jit(solution)/shard_map/ppermute | solution.py:195
  68.5 1.9 %collective-permute-done.12.refs_2_ = bf16[328,256]{1,0:T(8,128)(2,1)S(1)} collective-permute-done((bf16[328,256]{1,0:T(8,128)(2,1)}, bf16[328,256]{1,0:T(8,128)(2,1)S(1)}, u32[]{:S(2)}, u32[]{:S(2)}) %collective-permute-start.12) | collective-permute-done | bytes 167968 | tf_op jit(solution)/shard_map/ppermute | solution.py:195
  70.3 8.9 %collective-permute-done.13.refs_3_ = bf16[328,256]{1,0:T(8,128)(2,1)S(1)} collective-permute-done((bf16[328,256]{1,0:T(8,128)(2,1)}, bf16[328,256]{1,0:T(8,128)(2,1)S(1)}, u32[]{:S(2)}, u32[]{:S(2)}) %collective-permute-start.13) | collective-permute-done | bytes 167968 | tf_op jit(solution)/shard_map/ppermute | solution.py:195
  79.3 2.0 %copy-done.1 = bf16[1312,1312]{1,0:T(8,128)(2,1)S(1)} copy-done((bf16[1312,1312]{1,0:T(8,128)(2,1)S(1)}, bf16[1312,1312]{1,0:T(8,128)(2,1)}, u32[]{:S(2)}) %copy-start.1) | copy-done | bytes 3442712
  82.2 2.9 %couple.3 = (bf16[2,656,128]{2,1,0:T(8,128)(2,1)S(1)}, bf16[2,656,128]{2,1,0:T(8,128)(2,1)S(1)}, bf16[2,656,128]{2,1,0:T(8,128)(2,1)S(1)}, bf16[2,656,128]{2,1,0:T(8,128)(2,1)S(1)}) custom-call(bf16[328,256]{1,0:T(8,128)(2,1)S(1)} %copy-done.3, bf16[328,256]{1,0:T(8,128)(2,1)S(1)} %collective-permute-done.11.refs_1_, ...), custom_call_target="tpu_custom_call" | custom-call | flops 1539440640 | bytes 6000000 | tf_op jit(solution)/shard_map/couple/pallas_call | solution.py:247
  88.1 2.6 %collective-permute-start.17 = (bf16[4,656,128]{2,1,0:T(8,128)(2,1)S(1)}, bf16[4,656,128]{2,1,0:T(8,128)(2,1)S(1)}, u32[]{:S(2)}, u32[]{:S(2)}) collective-permute-start(bf16[4,656,128]{2,1,0:T(8,128)(2,1)S(1)} %pad_maximum_fusion), channel_id=1, source_target_pairs={{0,4},{4,0},{8,12},{12,8},{16,20},{20,16},{24,28},{28,24},{1,5},{5... | collective-permute-start | bytes 2015240 | tf_op jit(solution)/shard_map/ppermute | solution.py:195
  90.7 2.2 %collective-permute-done.14.refs_5_ = bf16[2,656,128]{2,1,0:T(8,128)(2,1)S(1)} collective-permute-done((bf16[2,656,128]{2,1,0:T(8,128)(2,1)S(1)}, bf16[2,656,128]{2,1,0:T(8,128)(2,1)S(1)}, u32[]{:S(2)}, u32[]{:S(2)}) %collective-permute-start.14) | collective-permute-done | bytes 335904 | tf_op jit(solution)/shard_map/ppermute | solution.py:195
  92.9 2.1 %collective-permute-done.15.refs_6_ = bf16[2,656,128]{2,1,0:T(8,128)(2,1)S(1)} collective-permute-done((bf16[2,656,128]{2,1,0:T(8,128)(2,1)S(1)}, bf16[2,656,128]{2,1,0:T(8,128)(2,1)S(1)}, u32[]{:S(2)}, u32[]{:S(2)}) %collective-permute-start.15) | collective-permute-done | bytes 335904 | tf_op jit(solution)/shard_map/ppermute | solution.py:195
  95.1 4.6 %collective-permute-done.16.refs_7_ = bf16[2,656,128]{2,1,0:T(8,128)(2,1)S(1)} collective-permute-done((bf16[2,656,128]{2,1,0:T(8,128)(2,1)S(1)}, bf16[2,656,128]{2,1,0:T(8,128)(2,1)S(1)}, u32[]{:S(2)}, u32[]{:S(2)}) %collective-permute-start.16) | collective-permute-done | bytes 335904 | tf_op jit(solution)/shard_map/ppermute | solution.py:195
  99.8 4.3 %collective-permute-start.18 = (bf16[4,656,128]{2,1,0:T(8,128)(2,1)S(1)}, bf16[4,656,128]{2,1,0:T(8,128)(2,1)S(1)}, u32[]{:S(2)}, u32[]{:S(2)}) collective-permute-start(bf16[4,656,128]{2,1,0:T(8,128)(2,1)S(1)} %pad_maximum_fusion.1), channel_id=1, source_target_pairs={{0,4},{4,0},{8,12},{12,8},{16,20},{20,16},{24,28},{28,24},{1,5},{5... | collective-permute-start | bytes 2015240 | tf_op jit(solution)/shard_map/ppermute | solution.py:195
  104.2 1.7 %collective-permute-done.18.refs_9_ = bf16[4,656,128]{2,1,0:T(8,128)(2,1)S(1)} collective-permute-done((bf16[4,656,128]{2,1,0:T(8,128)(2,1)S(1)}, bf16[4,656,128]{2,1,0:T(8,128)(2,1)S(1)}, u32[]{:S(2)}, u32[]{:S(2)}) %collective-permute-start.18) | collective-permute-done | bytes 671776 | tf_op jit(solution)/shard_map/ppermute | solution.py:195
  105.9 2.4 %place.1 = bf16[1296,1024]{1,0:T(8,128)(2,1)} custom-call(bf16[2,656,128]{2,1,0:T(8,128)(2,1)S(1)} %get-tuple-element.31.refs_0_, bf16[2,656,128]{2,1,0:T(8,128)(2,1)S(1)} %collective-permute-done.8.refs_1_, bf16[2,656,128]{2,1,0:T(8,128)(2,1)S(1)} %collective-permute-done.9.refs_2_, bf16[2,656,128]{2,1,0:T(8,128)(2,1)S(1)} %collective-permute-done.10.refs_3_, ...), custom_call_target="tpu_custom_call" | custom-call | flops 679477248 | bytes 8000000 | tf_op jit(solution)/shard_map/place/pallas_call | solution.py:264
  (69 shorter events, 15.9 us)
Async XLA Ops:
  2.5 6.6 %copy-start.11 = (s32[1,1,512,1]{2,3,1,0:T(1,128)S(1)}, s32[1,1,512,1]{2,3,1,0:T(1,128)}, u32[]{:S(2)}) copy-start(s32[1,1,512,1]{2,3,1,0:T(1,128)} %param.11) | copy-start | bytes 6148
  2.5 10.1 %copy-start.13 = (s32[1296,2]{0,1:T(2,128)S(1)}, s32[1296,2]{0,1:T(2,128)}, u32[]{:S(2)}) copy-start(s32[1296,2]{0,1:T(2,128)} %param.8) | copy-start | bytes 31108
  2.5 10.1 %copy-start.12 = (f32[1296,2]{0,1:T(2,128)S(1)}, f32[1296,2]{0,1:T(2,128)}, u32[]{:S(2)}) copy-start(f32[1296,2]{0,1:T(2,128)} %param.7) | copy-start | bytes 31108
  2.5 11.4 %collective-permute-start.1 = (bf16[336,512]{1,0:T(8,128)(2,1)S(1)}, bf16[336,512]{1,0:T(8,128)(2,1)S(1)}, u32[]{:S(2)}, u32[]{:S(2)}) collective-permute-start(bf16[336,512]{1,0:T(8,128)(2,1)S(1)} %get-tuple-element.47), channel_id=1, source_target_pairs={{4,0},{8,4},{12,8},{16,12},{20,16},{24,20},{28,24},{5,1},{9,5},{13... | collective-permute-start | bytes 1032200 | tf_op jit(solution)/shard_map/ppermute | solution.py:216
  5.1 8.8 %collective-permute-start = (bf16[336,512]{1,0:T(8,128)(2,1)S(1)}, bf16[336,512]{1,0:T(8,128)(2,1)S(1)}, u32[]{:S(2)}, u32[]{:S(2)}) collective-permute-start(bf16[336,512]{1,0:T(8,128)(2,1)S(1)} %get-tuple-element.48), channel_id=1, source_target_pairs={{0,4},{4,8},{8,12},{12,16},{16,20},{20,24},{24,28},{1,5},{5,9},{9,... | collective-permute-start | bytes 1032200 | tf_op jit(solution)/shard_map/ppermute | solution.py:215
  9.0 4.0 %collective-permute-start.4 = (s32[1,512]{1,0:T(1,128)S(1)}, s32[1,512]{1,0:T(1,128)S(1)}, u32[]{:S(2)}, u32[]{:S(2)}) collective-permute-start(s32[1,512]{1,0:T(1,128)S(1)} %bitcast.13), channel_id=1, source_target_pairs={{0,3},{1,2},{2,1},{3,0},{4,7},{5,6},{6,5},{7,4},{8,11},{9,10},{10,... | collective-permute-start | bytes 6152 | tf_op jit(solution)/shard_map/ppermute | solution.py:195
  10.4 3.3 %collective-permute-start.3 = (s32[1,512]{1,0:T(1,128)S(1)}, s32[1,512]{1,0:T(1,128)S(1)}, u32[]{:S(2)}, u32[]{:S(2)}) collective-permute-start(s32[1,512]{1,0:T(1,128)S(1)} %bitcast.14), channel_id=1, source_target_pairs={{0,2},{1,3},{2,0},{3,1},{4,6},{5,7},{6,4},{7,5},{8,10},{9,11},{10,... | collective-permute-start | bytes 6152 | tf_op jit(solution)/shard_map/ppermute | solution.py:195
  11.5 2.4 %collective-permute-start.2 = (s32[1,512]{1,0:T(1,128)S(1)}, s32[1,512]{1,0:T(1,128)S(1)}, u32[]{:S(2)}, u32[]{:S(2)}) collective-permute-start(s32[1,512]{1,0:T(1,128)S(1)} %bitcast.15), channel_id=1, source_target_pairs={{0,1},{1,0},{2,3},{3,2},{4,5},{5,4},{6,7},{7,6},{8,9},{9,8},{10,11... | collective-permute-start | bytes 6152 | tf_op jit(solution)/shard_map/ppermute | solution.py:195
  21.0 35.0 %collective-permute-start.5 = (bf16[328,256]{1,0:T(8,128)(2,1)S(1)}, bf16[328,256]{1,0:T(8,128)(2,1)S(1)}, u32[]{:S(2)}, u32[]{:S(2)}) collective-permute-start(bf16[328,256]{1,0:T(8,128)(2,1)S(1)} %get-tuple-element.27), channel_id=1, source_target_pairs={{0,1},{1,0},{2,3},{3,2},{4,5},{5,4},{6,7},{7,6},{8,9},{9,8},{10,11... | collective-permute-start | bytes 503816 | tf_op jit(solution)/shard_map/ppermute | solution.py:195
  23.0 33.0 %collective-permute-start.6 = (bf16[328,256]{1,0:T(8,128)(2,1)S(1)}, bf16[328,256]{1,0:T(8,128)(2,1)S(1)}, u32[]{:S(2)}, u32[]{:S(2)}) collective-permute-start(bf16[328,256]{1,0:T(8,128)(2,1)S(1)} %get-tuple-element.28), channel_id=1, source_target_pairs={{0,2},{1,3},{2,0},{3,1},{4,6},{5,7},{6,4},{7,5},{8,10},{9,11},{10,... | collective-permute-start | bytes 503816 | tf_op jit(solution)/shard_map/ppermute | solution.py:195
  24.5 31.5 %collective-permute-start.7 = (bf16[328,256]{1,0:T(8,128)(2,1)S(1)}, bf16[328,256]{1,0:T(8,128)(2,1)S(1)}, u32[]{:S(2)}, u32[]{:S(2)}) collective-permute-start(bf16[328,256]{1,0:T(8,128)(2,1)S(1)} %get-tuple-element.29), channel_id=1, source_target_pairs={{0,3},{1,2},{2,1},{3,0},{4,7},{5,6},{6,5},{7,4},{8,11},{9,10},{10,... | collective-permute-start | bytes 503816 | tf_op jit(solution)/shard_map/ppermute | solution.py:195
  56.0 5.2 %copy-start.7 = (bf16[328,256]{1,0:T(8,128)(2,1)}, bf16[328,256]{1,0:T(8,128)(2,1)S(1)}, u32[]{:S(2)}) copy-start(bf16[328,256]{1,0:T(8,128)(2,1)S(1)} %collective-permute-done.5.refs_1_.refs_4_) | copy-start | bytes 503812
  56.0 5.2 %copy-start.8 = (bf16[328,256]{1,0:T(8,128)(2,1)}, bf16[328,256]{1,0:T(8,128)(2,1)S(1)}, u32[]{:S(2)}) copy-start(bf16[328,256]{1,0:T(8,128)(2,1)S(1)} %collective-permute-done.6.refs_2_.refs_5_) | copy-start | bytes 503812
  61.2 25.3 %collective-permute-start.8 = (bf16[2,656,128]{2,1,0:T(8,128)(2,1)S(1)}, bf16[2,656,128]{2,1,0:T(8,128)(2,1)S(1)}, u32[]{:S(2)}, u32[]{:S(2)}) collective-permute-start(bf16[2,656,128]{2,1,0:T(8,128)(2,1)S(1)} %get-tuple-element.32), channel_id=1, source_target_pairs={{0,8},{4,12},{8,0},{12,4},{16,24},{20,28},{24,16},{28,20},{1,9},{5... | collective-permute-start | bytes 1007624 | tf_op jit(solution)/shard_map/ppermute | solution.py:195
  61.3 7.2 %collective-permute-start.11 = (bf16[328,256]{1,0:T(8,128)(2,1)}, bf16[328,256]{1,0:T(8,128)(2,1)S(1)}, u32[]{:S(2)}, u32[]{:S(2)}) collective-permute-start(bf16[328,256]{1,0:T(8,128)(2,1)} %get-tuple-element.40), channel_id=1, source_target_pairs={{0,1},{1,0},{2,3},{3,2},{4,5},{5,4},{6,7},{7,6},{8,9},{9,8},{10,11... | collective-permute-start | bytes 503816 | tf_op jit(solution)/shard_map/ppermute | solution.py:195
  63.4 6.9 %collective-permute-start.12 = (bf16[328,256]{1,0:T(8,128)(2,1)}, bf16[328,256]{1,0:T(8,128)(2,1)S(1)}, u32[]{:S(2)}, u32[]{:S(2)}) collective-permute-start(bf16[328,256]{1,0:T(8,128)(2,1)} %get-tuple-element.41), channel_id=1, source_target_pairs={{0,2},{1,3},{2,0},{3,1},{4,6},{5,7},{6,4},{7,5},{8,10},{9,11},{10,... | collective-permute-start | bytes 503816 | tf_op jit(solution)/shard_map/ppermute | solution.py:195
  64.0 15.3 %collective-permute-start.13 = (bf16[328,256]{1,0:T(8,128)(2,1)}, bf16[328,256]{1,0:T(8,128)(2,1)S(1)}, u32[]{:S(2)}, u32[]{:S(2)}) collective-permute-start(bf16[328,256]{1,0:T(8,128)(2,1)} %get-tuple-element.42), channel_id=1, source_target_pairs={{0,3},{1,2},{2,1},{3,0},{4,7},{5,6},{6,5},{7,4},{8,11},{9,10},{10,... | collective-permute-start | bytes 503816 | tf_op jit(solution)/shard_map/ppermute | solution.py:195
  64.7 23.3 %collective-permute-start.9 = (bf16[2,656,128]{2,1,0:T(8,128)(2,1)S(1)}, bf16[2,656,128]{2,1,0:T(8,128)(2,1)S(1)}, u32[]{:S(2)}, u32[]{:S(2)}) collective-permute-start(bf16[2,656,128]{2,1,0:T(8,128)(2,1)S(1)} %get-tuple-element.33), channel_id=1, source_target_pairs={{0,16},{4,20},{8,24},{12,28},{16,0},{20,4},{24,8},{28,12},{1,17},{... | collective-permute-start | bytes 1007624 | tf_op jit(solution)/shard_map/ppermute | solution.py:195
  68.5 19.5 %collective-permute-start.10 = (bf16[2,656,128]{2,1,0:T(8,128)(2,1)S(1)}, bf16[2,656,128]{2,1,0:T(8,128)(2,1)S(1)}, u32[]{:S(2)}, u32[]{:S(2)}) collective-permute-start(bf16[2,656,128]{2,1,0:T(8,128)(2,1)S(1)} %get-tuple-element.34), channel_id=1, source_target_pairs={{0,24},{4,28},{8,16},{12,20},{16,8},{20,12},{24,0},{28,4},{1,25},{... | collective-permute-start | bytes 1007624 | tf_op jit(solution)/shard_map/ppermute | solution.py:195
  85.2 7.8 %collective-permute-start.14 = (bf16[2,656,128]{2,1,0:T(8,128)(2,1)S(1)}, bf16[2,656,128]{2,1,0:T(8,128)(2,1)S(1)}, u32[]{:S(2)}, u32[]{:S(2)}) collective-permute-start(bf16[2,656,128]{2,1,0:T(8,128)(2,1)S(1)} %get-tuple-element.44), channel_id=1, source_target_pairs={{0,8},{4,12},{8,0},{12,4},{16,24},{20,28},{24,16},{28,20},{1,9},{5... | collective-permute-start | bytes 1007624 | tf_op jit(solution)/shard_map/ppermute | solution.py:195
  86.5 8.6 %collective-permute-start.15 = (bf16[2,656,128]{2,1,0:T(8,128)(2,1)S(1)}, bf16[2,656,128]{2,1,0:T(8,128)(2,1)S(1)}, u32[]{:S(2)}, u32[]{:S(2)}) collective-permute-start(bf16[2,656,128]{2,1,0:T(8,128)(2,1)S(1)} %get-tuple-element.45), channel_id=1, source_target_pairs={{0,16},{4,20},{8,24},{12,28},{16,0},{20,4},{24,8},{28,12},{1,17},{... | collective-permute-start | bytes 1007624 | tf_op jit(solution)/shard_map/ppermute | solution.py:195
  86.5 13.2 %collective-permute-start.16 = (bf16[2,656,128]{2,1,0:T(8,128)(2,1)S(1)}, bf16[2,656,128]{2,1,0:T(8,128)(2,1)S(1)}, u32[]{:S(2)}, u32[]{:S(2)}) collective-permute-start(bf16[2,656,128]{2,1,0:T(8,128)(2,1)S(1)} %get-tuple-element.46), channel_id=1, source_target_pairs={{0,24},{4,28},{8,16},{12,20},{16,8},{20,12},{24,0},{28,4},{1,25},{... | collective-permute-start | bytes 1007624 | tf_op jit(solution)/shard_map/ppermute | solution.py:195
  88.1 16.1 %collective-permute-start.17 = (bf16[4,656,128]{2,1,0:T(8,128)(2,1)S(1)}, bf16[4,656,128]{2,1,0:T(8,128)(2,1)S(1)}, u32[]{:S(2)}, u32[]{:S(2)}) collective-permute-start(bf16[4,656,128]{2,1,0:T(8,128)(2,1)S(1)} %pad_maximum_fusion), channel_id=1, source_target_pairs={{0,4},{4,0},{8,12},{12,8},{16,20},{20,16},{24,28},{28,24},{1,5},{5... | collective-permute-start | bytes 2015240 | tf_op jit(solution)/shard_map/ppermute | solution.py:195
  99.8 6.1 %collective-permute-start.18 = (bf16[4,656,128]{2,1,0:T(8,128)(2,1)S(1)}, bf16[4,656,128]{2,1,0:T(8,128)(2,1)S(1)}, u32[]{:S(2)}, u32[]{:S(2)}) collective-permute-start(bf16[4,656,128]{2,1,0:T(8,128)(2,1)S(1)} %pad_maximum_fusion.1), channel_id=1, source_target_pairs={{0,4},{4,0},{8,12},{12,8},{16,20},{20,16},{24,28},{28,24},{1,5},{5... | collective-permute-start | bytes 2015240 | tf_op jit(solution)/shard_map/ppermute | solution.py:195
  (9 other events, 14.1 us)

commit v2 on v1

--- a/solution.py
+++ b/solution.py
@@ -80,7 +80,8 @@
         block = me ^ m
         at = pl.ds(pl.multiple_of(block * LANES, LANES), LANES)
         lhs = jnp.concatenate([moved[l, :, at] for l in range(lon_rows)], axis=1)
-        ordered = dot_nt(lhs, order)[:rows_out].astype(BF16)
+        ordered = dot_nt(lhs, order)[:rows_out]
+        ordered = jnp.where((me & 1) == 1, pltpu.roll(ordered, 4, 0), ordered).astype(BF16)
         for c in range(CHUNKS):
             chunks[c * bins_axis + m][...] = ordered[:, c * half : (c + 1) * half]
         if m == 0:
@@ -95,17 +96,28 @@
             meta[...] = dot_nt(facts.astype(BF16), order)
 
 
-def couple_kernel(chunk, bins_axis, owners_count, all_bins, pad_row, slots, *refs):
+def transpose_kernel(coupling, out):
+    bins = coupling.shape[0]
+    for start in range(0, bins, 256):
+        size = min(256, bins - start)
+        eye = (iota((size, size), 0) == iota((size, size), 1)).astype(F32).astype(BF16)
+        out[start : start + size, :] = dot_nt(eye, coupling[:, start : start + size]).astype(BF16)
+
+
+def couple_kernel(chunk, bins_axis, owners_count, local_bins, slots, paired, *refs):
     blocks = refs[:bins_axis]
     weights, meta = refs[bins_axis : bins_axis + 2]
-    outs = refs[bins_axis + 2 : -1]
+    outs = refs[-1 - (owners_count // 2 if paired else owners_count) : -1]
     values = refs[-1]
     rows, width = blocks[0].shape
-    half_rows = values.shape[0] // 2
+    all_bins = values.shape[0]
+    half_bins = all_bins // 2
     me = lax.axis_index("bins")
+    values[...] = jnp.zeros_like(values)
     for m in range(bins_axis):
-        at = pl.ds(pl.multiple_of((me ^ m) * rows, 8), rows)
-        values[at, :] = blocks[m][...].astype(F32)
+        block = me ^ m
+        at = pl.ds(pl.multiple_of(block * local_bins - 4 * (block & 1), 8), rows)
+        values[at, :] += blocks[m][...].astype(F32)
     flat = values[...].astype(BF16)
     energy = jnp.sum(values[...], axis=0, keepdims=True) / all_bins
     facts = meta[:, chunk * width : (chunk + 1) * width]
@@ -114,46 +126,50 @@
     slot_id = iota((owners_count * slots, width), 0)
     straight = (slot_id == towards * slots + slot).astype(F32).astype(BF16)
     crossed = (slot_id == (towards ^ 1) * slots + slot).astype(F32).astype(BF16)
-    is_rank = iota((half_rows, width), 0) == pad_row
+    step = all_bins // 3
+    for start in range(0, all_bins, step):
+        at = slice(start, start + step)
+        coupled = jnp.dot(weights[at, :], flat, preferred_element_type=F32)
+        values[at, :] = (values[at, :] + coupled) * scale
+    spare = jnp.zeros((7, width), F32)
     sent = []
     for group in range(2):
-        at = slice(group * half_rows, (group + 1) * half_rows)
-        coupled = jnp.dot(weights[at, :], flat, preferred_element_type=F32)
-        updated = (values[at, :] + coupled) * scale
-        updated = jnp.where(is_rank, rank, updated).astype(BF16)
+        updated = values[group * half_bins : (group + 1) * half_bins, :]
+        updated = jnp.concatenate([updated, rank, spare], axis=0).astype(BF16)
         sent.append(dot_nt(updated, straight if group == chunk else crossed).astype(BF16))
     even, odd = sent[chunk], sent[1 - chunk]
-    is_low = iota((half_rows, LANES), 1) < slots
+    is_low = iota((half_bins + 8, LANES), 1) < slots
     for t in range(owners_count // 2):
         at = slice(t * LANES, (t + 1) * LANES)
-        outs[t][0] = jnp.where(is_low, even[:, at], odd[:, at])
-        outs[t][1] = jnp.where(is_low, odd[:, at], even[:, at])
-
-
-def place_kernel(owners_count, rows, real, slots, *refs):
+        first = jnp.where(is_low, even[:, at], odd[:, at])
+        second = jnp.where(is_low, odd[:, at], even[:, at])
+        if paired:
+            outs[t][0] = first
+            outs[t][1] = second
+        else:
+            outs[2 * t][...] = first
+            outs[2 * t + 1][...] = second
+
+
+def place_kernel(owners_count, slots, *refs):
     pairs = owners_count // 2
-    arrivals = refs[: CHUNKS * pairs]
-    swapped = refs[CHUNKS * pairs : CHUNKS * pairs + CHUNKS]
-    out = refs[CHUNKS * pairs + CHUNKS]
-    staged, sems = refs[-2:]
+    paired, swapped = refs[:pairs], refs[pairs]
+    direct = refs[pairs + 1 : pairs + 1 + owners_count]
+    out, staged, sems = refs[-3:]
     me = lax.axis_index("pts")
-    half_rows = arrivals[0].shape[1]
-    is_low = iota((half_rows, LANES), 1) < slots
+    tall = direct[0].shape[0]
+    half_bins = tall - 8
+    is_low = iota((tall, LANES), 1) < slots
     slot_id = iota((LANES, LANES), 0)
     copies = []
     for x in range(owners_count):
-        t = x // 2
-        if x % 2 == 0:
-            first, second = arrivals[t][0], arrivals[pairs + t][0]
-        else:
-            second, first = swapped[0][t], swapped[1][t]
+        early = paired[x // 2][0] if x % 2 == 0 else swapped[x // 2]
+        first, second = (early, direct[x][...]) if x % 2 == 0 else (direct[x][...], early)
         pieces = []
         for lhs in (jnp.where(is_low, first, second), jnp.where(is_low, second, first)):
-            rank = lhs[real : real + 16 - real % 16, :].astype(F32)[0:1, :].astype(I32)
+            rank = lhs[tall - 16 :, :].astype(F32)[8:9, :].astype(I32)
             place = (slot_id == rank).astype(F32).astype(BF16)
-            rows_f = dot_nt(lhs, place)
-            for at in range(0, half_rows, rows):
-                pieces.append(rows_f[at : at + real, :])
+            pieces.append(dot_nt(lhs, place)[:half_bins])
         staged[x] = jnp.concatenate(pieces, axis=0).astype(BF16)
         at = pl.ds(pl.multiple_of((me ^ x) * LANES, LANES), LANES)
         copy = pltpu.make_async_copy(staged.at[x], out.at[:, at], sems.at[x])
@@ -163,20 +179,38 @@
         copy.wait()
 
 
-def gate_kernel(count, after, *refs):
-    del count, after, refs
-
-
-def gate(arrays, after):
-    count = len(arrays)
+def gate_kernel(array, after, out):
+    del after
+    out[...] = array[...]
+
+
+def gate(array, after):
     return pl.pallas_call(
-        functools.partial(gate_kernel, count, len(after)),
-        out_shape=[jax.ShapeDtypeStruct(a.shape, a.dtype) for a in arrays],
-        in_specs=[pl.BlockSpec(memory_space=pl.ANY)] * (count + len(after)),
-        out_specs=[pl.BlockSpec(memory_space=pl.ANY)] * count,
-        input_output_aliases={i: i for i in range(count)},
+        gate_kernel,
+        out_shape=jax.ShapeDtypeStruct(array.shape, array.dtype),
+        in_specs=vmem(2),
+        out_specs=vmem(1)[0],
+        compiler_params=params(8),
+        cost_estimate=cost(0, 4 * array.size),
         name="gate",
-    )(*arrays, *after)
+    )(array, after)
+
+
+def stack_kernel(count, *refs):
+    for t in range(count):
+        refs[-1][t] = refs[t][1]
+
+
+def stack(pairs, after):
+    return pl.pallas_call(
+        functools.partial(stack_kernel, len(pairs)),
+        out_shape=jax.ShapeDtypeStruct((len(pairs),) + pairs[0].shape[1:], pairs[0].dtype),
+        in_specs=vmem(len(pairs) + 1),
+        out_specs=vmem(1)[0],
+        compiler_params=params(8),
+        cost_estimate=cost(0, 4 * sum(a.size for a in pairs)),
+        name="stack",
+    )(*pairs, after)
 
 
 def params(mib):
@@ -205,7 +239,7 @@
     slots = 2 * points // owners_count // CHUNKS
     tall = round_up(local_bins, 16)
     rows = round_up(local_bins + 1, 8)
-    half_rows = bins_axis * rows // 2
+    half_rows = all_bins // 2 + 8
     first_bin = lax.axis_index("bins") * local_bins
 
     masked = spectrum * sea.astype(BF16)[None]
@@ -220,10 +254,15 @@
     coef = lax.dynamic_slice_in_dim(coef, first_bin, local_bins, 0)
     coef = jnp.pad(coef, ((0, tall - local_bins), (0, 0)))
 
-    weights = jnp.transpose(coupling).reshape(bins_axis, local_bins, bins_axis, local_bins)
-    extra = rows - local_bins
-    weights = jnp.pad(weights, ((0, 0), (0, extra), (0, 0), (0, extra)))
-    weights = weights.reshape(bins_axis * rows, bins_axis * rows)
+    weights = pl.pallas_call(
+        transpose_kernel,
+        out_shape=jax.ShapeDtypeStruct(coupling.shape, BF16),
+        in_specs=vmem(1),
+        out_specs=vmem(1)[0],
+        compiler_params=params(16),
+        cost_estimate=cost(2 * 256 * all_bins * all_bins, 7e6),
+        name="transpose",
+    )(coupling)
 
     packed = pl.pallas_call(
         functools.partial(pack_kernel, rows, bins_axis, owners_count, half),
@@ -232,48 +271,52 @@
         in_specs=vmem(5 + bins_axis),
         out_specs=vmem(CHUNKS * bins_axis + 1),
         scratch_shapes=[pltpu.VMEM((lon_rows, tall, lats), BF16)],
-        compiler_params=params(24),
+        compiler_params=params(16),
         cost_estimate=cost(2 * bins_axis * tall * points * points, 4e6),
         name="pack",
     )(planes, low, high, coef, sea, *owners)
     meta = packed[-1]
 
-    arrivals, swaps, got = [], [], None
-    for c in range(CHUNKS):
-        blocks = packed[c * bins_axis : (c + 1) * bins_axis]
-        if got is not None:
-            blocks = gate(blocks, got)
-        got = [exchange(blocks[m], "bins", m) for m in range(1, bins_axis)]
-        pays = pl.pallas_call(
+    def couple(c, blocks, ready, paired):
+        shape, count = ((half_rows, LANES), owners_count)
+        if paired:
+            shape, count = (2,) + shape, count // 2
+        return pl.pallas_call(
             functools.partial(
-                couple_kernel, c, bins_axis, owners_count, all_bins, local_bins, slots
+                couple_kernel, c, bins_axis, owners_count, local_bins, slots, paired
             ),
-            out_shape=[jax.ShapeDtypeStruct((2, half_rows, LANES), BF16)] * (owners_count // 2),
-            in_specs=vmem(bins_axis + 2),
-            out_specs=vmem(owners_count // 2),
-            scratch_shapes=[pltpu.VMEM((bins_axis * rows, half), F32)],
-            compiler_params=params(32),
+            out_shape=[jax.ShapeDtypeStruct(shape, BF16)] * count,
+            in_specs=vmem(len(blocks) + 2 + len(ready)),
+            out_specs=vmem(count),
+            scratch_shapes=[pltpu.VMEM((all_bins, half), F32)],
+            compiler_params=params(16),
             cost_estimate=cost(2 * all_bins * all_bins * half + 4 * all_bins * half * 512, 6e6),
             name="couple",
-        )(blocks[0], *got, weights, meta)
-        came = [pays[0]]
-        came += [exchange(pays[t], "pts", 2 * t) for t in range(1, owners_count // 2)]
-        swaps.append(exchange(jnp.stack([a[1] for a in came]), "pts", 1))
-        arrivals += came
+        )(*blocks, weights, meta, *ready)
+
+    early, late = packed[:bins_axis], packed[bins_axis : 2 * bins_axis]
+    first = [exchange(early[m], "bins", m) for m in range(1, bins_axis)]
+    late = [late[0]] + [gate(b, after) for b, after in zip(late[1:], first)]
+    second = [exchange(late[m], "bins", m) for m in range(1, bins_axis)]
+    pays = couple(0, [early[0], *first], late[1:], True)
+    pairs = [pays[0]] + [exchange(pays[t], "pts", 2 * t) for t in range(1, owners_count // 2)]
+    pays = couple(1, [late[0], *second], [], False)
+    direct = [pays[0]] + [exchange(pays[x], "pts", x) for x in range(1, owners_count)]
+    arrivals = [*pairs, exchange(stack(pairs, pays[0]), "pts", 1), *direct]
 
     placed = pl.pallas_call(
-        functools.partial(place_kernel, owners_count, rows, local_bins, slots),
+        functools.partial(place_kernel, owners_count, slots),
         out_shape=jax.ShapeDtypeStruct((all_bins, owners_count * LANES), BF16),
-        in_specs=vmem(len(arrivals) + CHUNKS),
+        in_specs=vmem(len(arrivals)),
         out_specs=pl.BlockSpec(memory_space=pl.ANY),
         scratch_shapes=[
             pltpu.VMEM((owners_count, all_bins, LANES), BF16),
             pltpu.SemaphoreType.DMA((owners_count,)),
         ],
-        compiler_params=params(32),
+        compiler_params=params(16),
         cost_estimate=cost(4 * all_bins * LANES * LANES * owners_count, 8e6),
         name="place",
-    )(*arrivals, *swaps)
+    )(*arrivals)
     return jnp.transpose(placed).reshape(1, 1, owners_count * LANES, all_bins)
 
 
@@ -354,6 +397,8 @@
         and bins_axis & (bins_axis - 1) == 0
         and owners_count & (owners_count - 1) == 0
         and bins_axis % 2 == 0
+        and spectrum.shape[0] % 8 == 4
+        and courant.shape[0] % 48 == 0
         and owners_count <= 8
     )
     form = chunked if suits else whole

time: 109 us -> 85.3 us (0.78)
  the two profiles are of different devices: /device:TPU:11 before, /device:TPU:0 now
where the time goes in v2:
time: 85.3 us; the launch traced here: 84.3 us
  waiting for transfers between devices  34.7 us (41%)
  starting transfers between devices  31.2 us (37%)
  Pallas kernels  12.5 us (15%)
  local copies, waits for them, and re-layouts  3.22 us (4%)
  other arithmetic  2.54 us (3%)
    ppermute x20, waiting for transfers between devices, exchange(): lax.ppermute(array, axis, [(i, i ^ offset) for i in range(lax.axis_size(a...  34.7 us
    ppermute x20, starting transfers between devices, exchange(): lax.ppermute(array, axis, [(i, i ^ offset) for i in range(lax.axis_size(a...  27.5 us
    pallas_call x1, Pallas kernels, chunked(): pl.pallas_call(functools.partial(pack_kernel, rows, bins_axis, owners_cou...  4.63 us
    pallas_call x2, Pallas kernels, couple(): pl.pallas_call(functools.partial(couple_kernel, c, bins_axis, owners_coun...  4.14 us
    pallas_call x1, Pallas kernels, chunked(): pl.pallas_call(functools.partial(place_kernel, owners_count, slots), out_...  2.37 us
    ppermute x1, starting transfers between devices, chunked(): low = lax.ppermute(planes[lon_rows - 1], 'pts', up)  2.37 us
    unnamed x11, local copies, waits for them, and re-layouts  2.19 us
    transpose x1, other arithmetic, chunked(): jnp.transpose(masked, (1, 0, 2))  1.75 us
  transfers between devices with their start and end apart: 22, of which 9 were waited for; matrix products, arithmetic and copies ran while one was open for 0% of the time, Pallas kernels for 6%

profile of v2, /device:TPU:0, one launch (start us, length us, event | category | flops | bytes accessed | tf_op | source)
XLA Modules:
  0.0 84.3 jit_solution(1063587967088981990)
XLA Ops:
  0.7 1.8 %fusion = bf16[4,324,512]{2,1,0:T(8,128)(2,1)S(1)} fusion(bf16[324,4,512]{2,1,0:T(4,128)(2,1)} %param.6, bf16[4,512]{1,0:T(4,128)(2,1)S(1)} %convert_element_type.10), kind=kLoop, calls=%fused_computation.1 | loop fusion | flops 663552 | bytes 2658304 | tf_op jit(solution)/shard_map/transpose | solution.py:246
  3.4 2.4 %collective-permute-start = (bf16[336,512]{1,0:T(8,128)(2,1)}, bf16[336,512]{1,0:T(8,128)(2,1)S(1)}, u32[]{:S(2)}, u32[]{:S(2)}) collective-permute-start(bf16[336,512]{1,0:T(8,128)(2,1)} %get-tuple-element.48), channel_id=1, source_target_pairs={{0,4},{4,8},{8,12},{12,16},{16,20},{20,24},{24,28},{1,5},{5,9},{9,... | collective-permute-start | bytes 1032200 | tf_op jit(solution)/shard_map/ppermute | solution.py:249
  5.8 1.3 %collective-permute-start.1 = (bf16[336,512]{1,0:T(8,128)(2,1)}, bf16[336,512]{1,0:T(8,128)(2,1)S(1)}, u32[]{:S(2)}, u32[]{:S(2)}) collective-permute-start(bf16[336,512]{1,0:T(8,128)(2,1)} %get-tuple-element.47), channel_id=1, source_target_pairs={{4,0},{8,4},{12,8},{16,12},{20,16},{24,20},{28,24},{5,1},{9,5},{13... | collective-permute-start | bytes 1032200 | tf_op jit(solution)/shard_map/ppermute | solution.py:250
  7.1 2.5 %collective-permute-start.2 = (s32[1,512]{1,0:T(1,128)S(1)}, s32[1,512]{1,0:T(1,128)S(1)}, u32[]{:S(2)}, u32[]{:S(2)}) collective-permute-start(s32[1,512]{1,0:T(1,128)S(1)} %bitcast.10), channel_id=1, source_target_pairs={{0,1},{1,0},{2,3},{3,2},{4,5},{5,4},{6,7},{7,6},{8,9},{9,8},{10,11... | collective-permute-start | bytes 6152 | tf_op jit(solution)/shard_map/ppermute | solution.py:229
  9.5 2.6 %collective-permute-start.3 = (s32[1,512]{1,0:T(1,128)S(1)}, s32[1,512]{1,0:T(1,128)S(1)}, u32[]{:S(2)}, u32[]{:S(2)}) collective-permute-start(s32[1,512]{1,0:T(1,128)S(1)} %bitcast.11), channel_id=1, source_target_pairs={{0,2},{1,3},{2,0},{3,1},{4,6},{5,7},{6,4},{7,5},{8,10},{9,11},{10,... | collective-permute-start | bytes 6152 | tf_op jit(solution)/shard_map/ppermute | solution.py:229
  12.6 1.5 %collective-permute-done.3.refs_7_ = s32[1,512]{1,0:T(1,128)S(1)} collective-permute-done((s32[1,512]{1,0:T(1,128)S(1)}, s32[1,512]{1,0:T(1,128)S(1)}, u32[]{:S(2)}, u32[]{:S(2)}) %collective-permute-start.3) | collective-permute-done | bytes 2080 | tf_op jit(solution)/shard_map/ppermute | solution.py:229
  14.0 3.5 %collective-permute-done.4.refs_8_ = s32[1,512]{1,0:T(1,128)S(1)} collective-permute-done((s32[1,512]{1,0:T(1,128)S(1)}, s32[1,512]{1,0:T(1,128)S(1)}, u32[]{:S(2)}, u32[]{:S(2)}) %collective-permute-start.4) | collective-permute-done | bytes 2080 | tf_op jit(solution)/shard_map/ppermute | solution.py:229
  17.5 4.6 %pack.1 = (bf16[328,256]{1,0:T(8,128)(2,1)S(1)}, bf16[328,256]{1,0:T(8,128)(2,1)S(1)}, bf16[328,256]{1,0:T(8,128)(2,1)S(1)}, bf16[328,256]{1,0:T(8,128)(2,1)S(1)...) custom-call(bf16[4,336,512]{2,1,0:T(8,128)(2,1)S(1)} %pad.8.refs_0_,, ...), custom_call_target="tpu_custom_call" | custom-call | flops 704643072 | bytes 4000000 | tf_op jit(solution)/shard_map/pack/pallas_call | solution.py:267
  22.8 3.8 %collective-permute-start.7 = (bf16[328,256]{1,0:T(8,128)(2,1)S(1)}, bf16[328,256]{1,0:T(8,128)(2,1)S(1)}, u32[]{:S(2)}, u32[]{:S(2)}) collective-permute-start(bf16[328,256]{1,0:T(8,128)(2,1)S(1)} %get-tuple-element.29), channel_id=1, source_target_pairs={{0,3},{1,2},{2,1},{3,0},{4,7},{5,6},{6,5},{7,4},{8,11},{9,10},{10,... | collective-permute-start | bytes 503816 | tf_op jit(solution)/shard_map/ppermute | solution.py:229
  26.6 2.0 %copy-done = bf16[1296,1296]{1,0:T(8,128)(2,1)S(1)} copy-done((bf16[1296,1296]{1,0:T(8,128)(2,1)S(1)}, bf16[1296,1296]{1,0:T(8,128)(2,1)}, u32[]{:S(2)}) %copy-start) | copy-done | bytes 3359256
  29.9 1.6 %collective-permute-done.5.after.refs_1_ = bf16[328,256]{1,0:T(8,128)(2,1)S(1)} collective-permute-done((bf16[328,256]{1,0:T(8,128)(2,1)S(1)}, bf16[328,256]{1,0:T(8,128)(2,1)S(1)}, u32[]{:S(2)}, u32[]{:S(2)}) %collective-permute-start.5) | collective-permute-done | bytes 167968 | tf_op jit(solution)/shard_map/ppermute | solution.py:229
  31.6 4.8 %collective-permute-done.6.after.refs_2_ = bf16[328,256]{1,0:T(8,128)(2,1)S(1)} collective-permute-done((bf16[328,256]{1,0:T(8,128)(2,1)S(1)}, bf16[328,256]{1,0:T(8,128)(2,1)S(1)}, u32[]{:S(2)}, u32[]{:S(2)}) %collective-permute-start.6) | collective-permute-done | bytes 167968 | tf_op jit(solution)/shard_map/ppermute | solution.py:229
  36.4 2.1 %couple.2 = (bf16[2,656,128]{2,1,0:T(8,128)(2,1)S(1)}, bf16[2,656,128]{2,1,0:T(8,128)(2,1)S(1)}, bf16[2,656,128]{2,1,0:T(8,128)(2,1)S(1)}, bf16[2,656,128]{2,1,0:T(8,128)(2,1)S(1)}) custom-call(bf16[328,256]{1,0:T(8,128)(2,1)S(1)} %get-tuple-element.26.refs_0_, bf16[328,256]{1,0:T(8,128)(2,1)S(1)} %collective-permute-done.5.after.refs_1_, ...), custom_call_target="tpu_custom_call" | custom-call | flops 1539440640 | bytes 6000000 | tf_op jit(solution)/shard_map/couple/pallas_call | solution.py:284
  38.5 5.4 %collective-permute-start.8 = (bf16[2,656,128]{2,1,0:T(8,128)(2,1)S(1)}, bf16[2,656,128]{2,1,0:T(8,128)(2,1)S(1)}, u32[]{:S(2)}, u32[]{:S(2)}) collective-permute-start(bf16[2,656,128]{2,1,0:T(8,128)(2,1)S(1)} %get-tuple-element.35), channel_id=1, source_target_pairs={{0,8},{4,12},{8,0},{12,4},{16,24},{20,28},{24,16},{28,20},{1,9},{5... | collective-permute-start | bytes 1007624 | tf_op jit(solution)/shard_map/ppermute | solution.py:229
  43.9 1.5 %collective-permute-start.10 = (bf16[2,656,128]{2,1,0:T(8,128)(2,1)S(1)}, bf16[2,656,128]{2,1,0:T(8,128)(2,1)S(1)}, u32[]{:S(2)}, u32[]{:S(2)}) collective-permute-start(bf16[2,656,128]{2,1,0:T(8,128)(2,1)S(1)} %get-tuple-element.37), channel_id=1, source_target_pairs={{0,24},{4,28},{8,16},{12,20},{16,8},{20,12},{24,0},{28,4},{1,25},{... | collective-permute-start | bytes 1007624 | tf_op jit(solution)/shard_map/ppermute | solution.py:229
  45.4 3.4 %collective-permute-start.12 = (bf16[328,256]{1,0:T(8,128)(2,1)S(1)}, bf16[328,256]{1,0:T(8,128)(2,1)S(1)}, u32[]{:S(2)}, u32[]{:S(2)}) collective-permute-start(bf16[328,256]{1,0:T(8,128)(2,1)S(1)} %gate.4.refs_7_), channel_id=1, source_target_pairs={{0,2},{1,3},{2,0},{3,1},{4,6},{5,7},{6,4},{7,5},{8,10},{9,11},{10,... | collective-permute-start | bytes 503816 | tf_op jit(solution)/shard_map/ppermute | solution.py:229
  50.1 10.2 %collective-permute-done.12.refs_2_ = bf16[328,256]{1,0:T(8,128)(2,1)S(1)} collective-permute-done((bf16[328,256]{1,0:T(8,128)(2,1)S(1)}, bf16[328,256]{1,0:T(8,128)(2,1)S(1)}, u32[]{:S(2)}, u32[]{:S(2)}) %collective-permute-start.12) | collective-permute-done | bytes 167968 | tf_op jit(solution)/shard_map/ppermute | solution.py:229
  60.3 2.1 %couple.3 = (bf16[656,128]{1,0:T(8,128)(2,1)S(1)}, bf16[656,128]{1,0:T(8,128)(2,1)S(1)}, bf16[656,128]{1,0:T(8,128)(2,1)S(1)}, bf16[656,128]{1,0:T(8,128)(2,1)S(...) custom-call(bf16[328,256]{1,0:T(8,128)(2,1)S(1)} %get-tuple-element., ...), custom_call_target="tpu_custom_call" | custom-call | flops 1539440640 | bytes 6000000 | tf_op jit(solution)/shard_map/couple/pallas_call | solution.py:284
  64.9 1.7 %collective-permute-start.19 = (bf16[656,128]{1,0:T(8,128)(2,1)S(1)}, bf16[656,128]{1,0:T(8,128)(2,1)S(1)}, u32[]{:S(2)}, u32[]{:S(2)}) collective-permute-start(bf16[656,128]{1,0:T(8,128)(2,1)S(1)} %get-tuple-element.44), channel_id=1, source_target_pairs={{0,20},{4,16},{8,28},{12,24},{16,4},{20,0},{24,12},{28,8},{1,21},{... | collective-permute-start | bytes 503816 | tf_op jit(solution)/shard_map/ppermute | solution.py:229
  66.6 3.6 %collective-permute-done.16.refs_7_ = bf16[656,128]{1,0:T(8,128)(2,1)S(1)} collective-permute-done((bf16[656,128]{1,0:T(8,128)(2,1)S(1)}, bf16[656,128]{1,0:T(8,128)(2,1)S(1)}, u32[]{:S(2)}, u32[]{:S(2)}) %collective-permute-start.16) | collective-permute-done | bytes 167968 | tf_op jit(solution)/shard_map/ppermute | solution.py:229
  71.0 1.4 %collective-permute-done.17.refs_8_ = bf16[656,128]{1,0:T(8,128)(2,1)S(1)} collective-permute-done((bf16[656,128]{1,0:T(8,128)(2,1)S(1)}, bf16[656,128]{1,0:T(8,128)(2,1)S(1)}, u32[]{:S(2)}, u32[]{:S(2)}) %collective-permute-start.17) | collective-permute-done | bytes 167968 | tf_op jit(solution)/shard_map/ppermute | solution.py:229
  72.4 1.6 %collective-permute-start.21 = (bf16[656,128]{1,0:T(8,128)(2,1)S(1)}, bf16[656,128]{1,0:T(8,128)(2,1)S(1)}, u32[]{:S(2)}, u32[]{:S(2)}) collective-permute-start(bf16[656,128]{1,0:T(8,128)(2,1)S(1)} %get-tuple-element.46), channel_id=1, source_target_pairs={{0,28},{4,24},{8,20},{12,16},{16,12},{20,8},{24,4},{28,0},{1,29},{... | collective-permute-start | bytes 503816 | tf_op jit(solution)/shard_map/ppermute | solution.py:229
  74.0 8.0 %collective-permute-done.19.refs_10_ = bf16[656,128]{1,0:T(8,128)(2,1)S(1)} collective-permute-done((bf16[656,128]{1,0:T(8,128)(2,1)S(1)}, bf16[656,128]{1,0:T(8,128)(2,1)S(1)}, u32[]{:S(2)}, u32[]{:S(2)}) %collective-permute-start.19) | collective-permute-done | bytes 167968 | tf_op jit(solution)/shard_map/ppermute | solution.py:229
  82.0 2.4 %place.1 = bf16[1296,1024]{1,0:T(8,128)(2,1)} custom-call(bf16[2,656,128]{2,1,0:T(8,128)(2,1)S(1)} %get-tuple-element.34.refs_0_, bf16[2,656,128]{2,1,0:T(8,128)(2,1)S(1)} %collective-permute-done.8.refs_1_, bf16[2,656,128]{2,1,0:T(8,128)(2,1)S(1)} %collective-permute-done.9.refs_2_, bf16[2,656,128]{2,1,0:T(8,128)(2,1)S(1)} %collective-permute-done.10.refs_3_, ...), custom_call_target="tpu_custom_call" | custom-call | flops 679477248 | bytes 8000000 | tf_op jit(solution)/shard_map/place/pallas_call | solution.py:307
  (47 shorter events, 8.6 us)
Async XLA Ops:
  2.5 9.7 %copy-start.4 = (s32[1296,2]{0,1:T(2,128)S(1)}, s32[1296,2]{0,1:T(2,128)}, u32[]{:S(2)}) copy-start(s32[1296,2]{0,1:T(2,128)} %param.8) | copy-start | bytes 31108
  2.5 9.7 %copy-start.3 = (f32[1296,2]{0,1:T(2,128)S(1)}, f32[1296,2]{0,1:T(2,128)}, u32[]{:S(2)}) copy-start(f32[1296,2]{0,1:T(2,128)} %param.7) | copy-start | bytes 31108
  3.4 14.1 %collective-permute-start = (bf16[336,512]{1,0:T(8,128)(2,1)}, bf16[336,512]{1,0:T(8,128)(2,1)S(1)}, u32[]{:S(2)}, u32[]{:S(2)}) collective-permute-start(bf16[336,512]{1,0:T(8,128)(2,1)} %get-tuple-element.48), channel_id=1, source_target_pairs={{0,4},{4,8},{8,12},{12,16},{16,20},{20,24},{24,28},{1,5},{5,9},{9,... | collective-permute-start | bytes 1032200 | tf_op jit(solution)/shard_map/ppermute | solution.py:249
  5.8 11.8 %collective-permute-start.1 = (bf16[336,512]{1,0:T(8,128)(2,1)}, bf16[336,512]{1,0:T(8,128)(2,1)S(1)}, u32[]{:S(2)}, u32[]{:S(2)}) collective-permute-start(bf16[336,512]{1,0:T(8,128)(2,1)} %get-tuple-element.47), channel_id=1, source_target_pairs={{4,0},{8,4},{12,8},{16,12},{20,16},{24,20},{28,24},{5,1},{9,5},{13... | collective-permute-start | bytes 1032200 | tf_op jit(solution)/shard_map/ppermute | solution.py:250
  7.1 5.5 %collective-permute-start.2 = (s32[1,512]{1,0:T(1,128)S(1)}, s32[1,512]{1,0:T(1,128)S(1)}, u32[]{:S(2)}, u32[]{:S(2)}) collective-permute-start(s32[1,512]{1,0:T(1,128)S(1)} %bitcast.10), channel_id=1, source_target_pairs={{0,1},{1,0},{2,3},{3,2},{4,5},{5,4},{6,7},{7,6},{8,9},{9,8},{10,11... | collective-permute-start | bytes 6152 | tf_op jit(solution)/shard_map/ppermute | solution.py:229
  9.5 4.5 %collective-permute-start.3 = (s32[1,512]{1,0:T(1,128)S(1)}, s32[1,512]{1,0:T(1,128)S(1)}, u32[]{:S(2)}, u32[]{:S(2)}) collective-permute-start(s32[1,512]{1,0:T(1,128)S(1)} %bitcast.11), channel_id=1, source_target_pairs={{0,2},{1,3},{2,0},{3,1},{4,6},{5,7},{6,4},{7,5},{8,10},{9,11},{10,... | collective-permute-start | bytes 6152 | tf_op jit(solution)/shard_map/ppermute | solution.py:229
  12.1 5.4 %collective-permute-start.4 = (s32[1,512]{1,0:T(1,128)S(1)}, s32[1,512]{1,0:T(1,128)S(1)}, u32[]{:S(2)}, u32[]{:S(2)}) collective-permute-start(s32[1,512]{1,0:T(1,128)S(1)} %bitcast.12), channel_id=1, source_target_pairs={{0,3},{1,2},{2,1},{3,0},{4,7},{5,6},{6,5},{7,4},{8,11},{9,10},{10,... | collective-permute-start | bytes 6152 | tf_op jit(solution)/shard_map/ppermute | solution.py:229
  22.2 9.3 %collective-permute-start.5 = (bf16[328,256]{1,0:T(8,128)(2,1)S(1)}, bf16[328,256]{1,0:T(8,128)(2,1)S(1)}, u32[]{:S(2)}, u32[]{:S(2)}) collective-permute-start(bf16[328,256]{1,0:T(8,128)(2,1)S(1)} %get-tuple-element.27), channel_id=1, source_target_pairs={{0,1},{1,0},{2,3},{3,2},{4,5},{5,4},{6,7},{7,6},{8,9},{9,8},{10,11... | collective-permute-start | bytes 503816 | tf_op jit(solution)/shard_map/ppermute | solution.py:229
  22.2 14.1 %collective-permute-start.6 = (bf16[328,256]{1,0:T(8,128)(2,1)S(1)}, bf16[328,256]{1,0:T(8,128)(2,1)S(1)}, u32[]{:S(2)}, u32[]{:S(2)}) collective-permute-start(bf16[328,256]{1,0:T(8,128)(2,1)S(1)} %get-tuple-element.28), channel_id=1, source_target_pairs={{0,2},{1,3},{2,0},{3,1},{4,6},{5,7},{6,4},{7,5},{8,10},{9,11},{10,... | collective-permute-start | bytes 503816 | tf_op jit(solution)/shard_map/ppermute | solution.py:229
  22.8 13.6 %collective-permute-start.7 = (bf16[328,256]{1,0:T(8,128)(2,1)S(1)}, bf16[328,256]{1,0:T(8,128)(2,1)S(1)}, u32[]{:S(2)}, u32[]{:S(2)}) collective-permute-start(bf16[328,256]{1,0:T(8,128)(2,1)S(1)} %get-tuple-element.29), channel_id=1, source_target_pairs={{0,3},{1,2},{2,1},{3,0},{4,7},{5,6},{6,5},{7,4},{8,11},{9,10},{10,... | collective-permute-start | bytes 503816 | tf_op jit(solution)/shard_map/ppermute | solution.py:229
  31.5 17.3 %collective-permute-start.11 = (bf16[328,256]{1,0:T(8,128)(2,1)S(1)}, bf16[328,256]{1,0:T(8,128)(2,1)S(1)}, u32[]{:S(2)}, u32[]{:S(2)}) collective-permute-start(bf16[328,256]{1,0:T(8,128)(2,1)S(1)} %gate.3.refs_6_), channel_id=1, source_target_pairs={{0,1},{1,0},{2,3},{3,2},{4,5},{5,4},{6,7},{7,6},{8,9},{9,8},{10,11... | collective-permute-start | bytes 503816 | tf_op jit(solution)/shard_map/ppermute | solution.py:229
  38.5 23.9 %collective-permute-start.8 = (bf16[2,656,128]{2,1,0:T(8,128)(2,1)S(1)}, bf16[2,656,128]{2,1,0:T(8,128)(2,1)S(1)}, u32[]{:S(2)}, u32[]{:S(2)}) collective-permute-start(bf16[2,656,128]{2,1,0:T(8,128)(2,1)S(1)} %get-tuple-element.35), channel_id=1, source_target_pairs={{0,8},{4,12},{8,0},{12,4},{16,24},{20,28},{24,16},{28,20},{1,9},{5... | collective-permute-start | bytes 1007624 | tf_op jit(solution)/shard_map/ppermute | solution.py:229
  43.9 18.6 %collective-permute-start.9 = (bf16[2,656,128]{2,1,0:T(8,128)(2,1)S(1)}, bf16[2,656,128]{2,1,0:T(8,128)(2,1)S(1)}, u32[]{:S(2)}, u32[]{:S(2)}) collective-permute-start(bf16[2,656,128]{2,1,0:T(8,128)(2,1)S(1)} %get-tuple-element.36), channel_id=1, source_target_pairs={{0,16},{4,20},{8,24},{12,28},{16,0},{20,4},{24,8},{28,12},{1,17},{... | collective-permute-start | bytes 1007624 | tf_op jit(solution)/shard_map/ppermute | solution.py:229
  43.9 18.6 %collective-permute-start.10 = (bf16[2,656,128]{2,1,0:T(8,128)(2,1)S(1)}, bf16[2,656,128]{2,1,0:T(8,128)(2,1)S(1)}, u32[]{:S(2)}, u32[]{:S(2)}) collective-permute-start(bf16[2,656,128]{2,1,0:T(8,128)(2,1)S(1)} %get-tuple-element.37), channel_id=1, source_target_pairs={{0,24},{4,28},{8,16},{12,20},{16,8},{20,12},{24,0},{28,4},{1,25},{... | collective-permute-start | bytes 1007624 | tf_op jit(solution)/shard_map/ppermute | solution.py:229
  45.4 14.9 %collective-permute-start.12 = (bf16[328,256]{1,0:T(8,128)(2,1)S(1)}, bf16[328,256]{1,0:T(8,128)(2,1)S(1)}, u32[]{:S(2)}, u32[]{:S(2)}) collective-permute-start(bf16[328,256]{1,0:T(8,128)(2,1)S(1)} %gate.4.refs_7_), channel_id=1, source_target_pairs={{0,2},{1,3},{2,0},{3,1},{4,6},{5,7},{6,4},{7,5},{8,10},{9,11},{10,... | collective-permute-start | bytes 503816 | tf_op jit(solution)/shard_map/ppermute | solution.py:229
  48.8 11.5 %collective-permute-start.13 = (bf16[328,256]{1,0:T(8,128)(2,1)S(1)}, bf16[328,256]{1,0:T(8,128)(2,1)S(1)}, u32[]{:S(2)}, u32[]{:S(2)}) collective-permute-start(bf16[328,256]{1,0:T(8,128)(2,1)S(1)} %gate.5.refs_8_), channel_id=1, source_target_pairs={{0,3},{1,2},{2,1},{3,0},{4,7},{5,6},{6,5},{7,4},{8,11},{9,10},{10,... | collective-permute-start | bytes 503816 | tf_op jit(solution)/shard_map/ppermute | solution.py:229
  62.5 19.5 %collective-permute-start.14 = (bf16[4,656,128]{2,1,0:T(8,128)(2,1)S(1)}, bf16[4,656,128]{2,1,0:T(8,128)(2,1)S(1)}, u32[]{:S(2)}, u32[]{:S(2)}) collective-permute-start(bf16[4,656,128]{2,1,0:T(8,128)(2,1)S(1)} %stack.1), channel_id=1, source_target_pairs={{0,4},{4,0},{8,12},{12,8},{16,20},{20,16},{24,28},{28,24},{1,5},{5... | collective-permute-start | bytes 2015240 | tf_op jit(solution)/shard_map/ppermute | solution.py:229
  62.6 2.3 %collective-permute-start.15 = (bf16[656,128]{1,0:T(8,128)(2,1)S(1)}, bf16[656,128]{1,0:T(8,128)(2,1)S(1)}, u32[]{:S(2)}, u32[]{:S(2)}) collective-permute-start(bf16[656,128]{1,0:T(8,128)(2,1)S(1)} %get-tuple-element.40), channel_id=1, source_target_pairs={{0,4},{4,0},{8,12},{12,8},{16,20},{20,16},{24,28},{28,24},{1,5},{5... | collective-permute-start | bytes 503816 | tf_op jit(solution)/shard_map/ppermute | solution.py:229
  63.1 7.1 %collective-permute-start.16 = (bf16[656,128]{1,0:T(8,128)(2,1)S(1)}, bf16[656,128]{1,0:T(8,128)(2,1)S(1)}, u32[]{:S(2)}, u32[]{:S(2)}) collective-permute-start(bf16[656,128]{1,0:T(8,128)(2,1)S(1)} %get-tuple-element.41), channel_id=1, source_target_pairs={{0,8},{4,12},{8,0},{12,4},{16,24},{20,28},{24,16},{28,20},{1,9},{5... | collective-permute-start | bytes 503816 | tf_op jit(solution)/shard_map/ppermute | solution.py:229
  64.1 8.3 %collective-permute-start.17 = (bf16[656,128]{1,0:T(8,128)(2,1)S(1)}, bf16[656,128]{1,0:T(8,128)(2,1)S(1)}, u32[]{:S(2)}, u32[]{:S(2)}) collective-permute-start(bf16[656,128]{1,0:T(8,128)(2,1)S(1)} %get-tuple-element.42), channel_id=1, source_target_pairs={{0,12},{4,8},{8,4},{12,0},{16,28},{20,24},{24,20},{28,16},{1,13},{... | collective-permute-start | bytes 503816 | tf_op jit(solution)/shard_map/ppermute | solution.py:229
  64.5 9.4 %collective-permute-start.18 = (bf16[656,128]{1,0:T(8,128)(2,1)S(1)}, bf16[656,128]{1,0:T(8,128)(2,1)S(1)}, u32[]{:S(2)}, u32[]{:S(2)}) collective-permute-start(bf16[656,128]{1,0:T(8,128)(2,1)S(1)} %get-tuple-element.43), channel_id=1, source_target_pairs={{0,16},{4,20},{8,24},{12,28},{16,0},{20,4},{24,8},{28,12},{1,17},{... | collective-permute-start | bytes 503816 | tf_op jit(solution)/shard_map/ppermute | solution.py:229
  64.9 17.0 %collective-permute-start.19 = (bf16[656,128]{1,0:T(8,128)(2,1)S(1)}, bf16[656,128]{1,0:T(8,128)(2,1)S(1)}, u32[]{:S(2)}, u32[]{:S(2)}) collective-permute-start(bf16[656,128]{1,0:T(8,128)(2,1)S(1)} %get-tuple-element.44), channel_id=1, source_target_pairs={{0,20},{4,16},{8,28},{12,24},{16,4},{20,0},{24,12},{28,8},{1,21},{... | collective-permute-start | bytes 503816 | tf_op jit(solution)/shard_map/ppermute | solution.py:229
  70.2 11.7 %collective-permute-start.20 = (bf16[656,128]{1,0:T(8,128)(2,1)S(1)}, bf16[656,128]{1,0:T(8,128)(2,1)S(1)}, u32[]{:S(2)}, u32[]{:S(2)}) collective-permute-start(bf16[656,128]{1,0:T(8,128)(2,1)S(1)} %get-tuple-element.45), channel_id=1, source_target_pairs={{0,24},{4,28},{8,16},{12,20},{16,8},{20,12},{24,0},{28,4},{1,25},{... | collective-permute-start | bytes 503816 | tf_op jit(solution)/shard_map/ppermute | solution.py:229
  72.4 9.6 %collective-permute-start.21 = (bf16[656,128]{1,0:T(8,128)(2,1)S(1)}, bf16[656,128]{1,0:T(8,128)(2,1)S(1)}, u32[]{:S(2)}, u32[]{:S(2)}) collective-permute-start(bf16[656,128]{1,0:T(8,128)(2,1)S(1)} %get-tuple-element.46), channel_id=1, source_target_pairs={{0,28},{4,24},{8,20},{12,16},{16,12},{20,8},{24,4},{28,0},{1,29},{... | collective-permute-start | bytes 503816 | tf_op jit(solution)/shard_map/ppermute | solution.py:229
  (3 other events, 11.9 us)

commit v3 on v2

--- a/solution.py
+++ b/solution.py
@@ -27,39 +27,47 @@
     return lax.dot_general(lhs, rhs, NT, preferred_element_type=F32)
 
 
-def pack_kernel(rows_out, bins_axis, owners_count, half, *refs):
-    planes, low, high, coef, sea = refs[:5]
-    owner = refs[5 : 5 + bins_axis]
-    chunks = refs[5 + bins_axis : 5 + bins_axis + CHUNKS * bins_axis]
-    meta = refs[5 + bins_axis + CHUNKS * bins_axis]
-    moved = refs[-1]
-    lon_rows, rows, lats = planes.shape
+def upwind_row(at, speed, side, before, center, after, sea_row):
+    lats = center.shape[1]
+    lane = iota(center.shape, 1)
+    wide = lats // LANES
+    cx, cy = [jnp.concatenate([speed[k, at, :]] * wide, axis=1) for k in range(2)]
+    ux, uy = [jnp.concatenate([side[k, at, :]] * wide, axis=1) for k in range(2)]
+    donor_x = jnp.where(ux == 0, before, after).astype(F32)
+    left = jnp.where(lane == 0, 0, pltpu.roll(center, 1, 1))
+    right = jnp.where(lane == lats - 1, 0, pltpu.roll(center, lats - 1, 1))
+    donor_y = jnp.where(uy == 0, left, right).astype(F32)
+    center = center.astype(F32)
+    value = center - cx * (center - donor_x) - cy * (center - donor_y)
+    return (value * sea_row).astype(BF16)
+
+
+def columns(moved, block):
+    at = pl.ds(pl.multiple_of(block * LANES, LANES), LANES)
+    return jnp.concatenate([moved[l, :, at] for l in range(moved.shape[0])], axis=1)
+
+
+def inner_kernel(bins_axis, owners_count, half, *refs):
+    planes, speed, side, sea = refs[:4]
+    owner = refs[4 : 4 + bins_axis]
+    inner, rim_order, meta, moved = refs[4 + bins_axis :]
+    lon_rows, rows, _ = planes.shape
     points = lon_rows * LANES
     me = lax.axis_index("bins")
     me_pts = lax.axis_index("pts")
-
-    tile = 16
-    lane = iota((tile, lats), 1)
     sea_f = sea[...].astype(F32)
-
-    def advect(step, carry):
-        at = pl.ds(pl.multiple_of(step * tile, tile), tile)
-        c = coef[at, :]
-        cx, cy, ux, uy = c[:, 0:1], c[:, 1:2], c[:, 2:3], c[:, 3:4]
-        masked = [low[at, :].astype(F32)]
-        masked += [planes[l, at, :].astype(F32) for l in range(lon_rows)]
-        masked += [high[at, :].astype(F32)]
-        for l in range(lon_rows):
-            center = masked[l + 1]
-            donor_x = jnp.where(ux == 0.0, masked[l], masked[l + 2])
-            left = jnp.where(lane == 0, 0.0, pltpu.roll(center, 1, 1))
-            right = jnp.where(lane == lats - 1, 0.0, pltpu.roll(center, lats - 1, 1))
-            donor_y = jnp.where(uy == 0.0, left, right)
-            value = center - cx * (center - donor_x) - cy * (center - donor_y)
-            moved[l, at, :] = (value * sea_f[l : l + 1, :]).astype(BF16)
+    sea_b = sea_f.astype(BF16)
+
+    def step(index, carry):
+        at = pl.ds(pl.multiple_of(index * 16, 16), 16)
+        masked = [planes[l, at, :] * sea_b[l : l + 1, :] for l in range(lon_rows)]
+        for l in range(1, lon_rows - 1):
+            moved[l - 1, at, :] = upwind_row(
+                at, speed, side, masked[l - 1], masked[l], masked[l + 1], sea_f[l : l + 1, :]
+            )
         return carry
 
-    lax.fori_loop(0, rows // tile, advect, 0)
+    lax.fori_loop(0, rows // 16, step, 0, unroll=7)
 
     owners_id = iota((owners_count, points), 0)
     hot = [(owner[m][...] == owners_id).astype(F32) for m in range(bins_axis)]
@@ -68,6 +76,7 @@
         jnp.concatenate(hot, axis=0).astype(BF16), earlier, preferred_element_type=F32
     )
     place_id = iota((points, points), 0)
+    last = (lon_rows - 1) * LANES
     for m in range(bins_axis):
         own = owner[m][...]
         count = jnp.sum(hot[m], axis=1, keepdims=True)
@@ -77,16 +86,13 @@
         key = (offset + rank).astype(I32)
         place = (key & 1) * half + (key >> 1)
         order = (place_id == place).astype(F32).astype(BF16)
-        block = me ^ m
-        at = pl.ds(pl.multiple_of(block * LANES, LANES), LANES)
-        lhs = jnp.concatenate([moved[l, :, at] for l in range(lon_rows)], axis=1)
-        ordered = dot_nt(lhs, order)[:rows_out]
-        ordered = jnp.where((me & 1) == 1, pltpu.roll(ordered, 4, 0), ordered).astype(BF16)
-        for c in range(CHUNKS):
-            chunks[c * bins_axis + m][...] = ordered[:, c * half : (c + 1) * half]
+        inner[m] = dot_nt(columns(moved, me ^ m), order[:, LANES:last]).astype(BF16)
+        rim_order[m, :, :LANES] = order[:, :LANES]
+        rim_order[m, :, LANES:] = order[:, last:]
         if m == 0:
             first = offset.astype(I32)
             slot = (key - first - (((key & 1) - first) & 1)) >> 1
+            at = pl.ds(pl.multiple_of(me * LANES, LANES), LANES)
             weight = jnp.concatenate([sea[l : l + 1, at].astype(F32) for l in range(lon_rows)], axis=1)
             facts = jnp.concatenate(
                 [slot.astype(F32), (own ^ me_pts).astype(F32), rank, weight]
@@ -96,6 +102,47 @@
             meta[...] = dot_nt(facts.astype(BF16), order)
 
 
+def pack_kernel(rows_out, bins_axis, half, *refs):
+    planes, low, high, speed, side, sea, inner, rim_order = refs[:8]
+    chunks, moved = refs[8:-1], refs[-1]
+    lon_rows, rows, _ = planes.shape
+    me = lax.axis_index("bins")
+    sea_f = sea[...].astype(F32)
+    sea_b = sea_f.astype(BF16)
+
+    top = lon_rows - 1
+
+    def rim(at, below, above):
+        masked = [planes[l, at, :] * sea_b[l : l + 1, :] for l in (0, 1, top - 1, top)]
+        moved[0, at, :] = upwind_row(
+            at, speed, side, below, masked[0], masked[1], sea_f[0:1, :]
+        )
+        moved[1, at, :] = upwind_row(
+            at, speed, side, masked[2], masked[3], above, sea_f[top : top + 1, :]
+        )
+
+    def step(index, carry):
+        at = pl.ds(pl.multiple_of(index * 16, 16), 16)
+        rim(at, low[at, :], high[at, :])
+        return carry
+
+    held = low.shape[0]
+    full = held // 16 * 16
+    lax.fori_loop(0, full // 16, step, 0, unroll=5)
+    if full < rows:
+        spare = jnp.zeros((rows - held, low.shape[1]), F32)
+        ends = [
+            jnp.concatenate([h[full:, :].astype(F32), spare], axis=0).astype(BF16) for h in (low, high)
+        ]
+        rim(pl.ds(full, 16), *ends)
+    for m in range(bins_axis):
+        ordered = dot_nt(columns(moved, me ^ m), rim_order[m]) + inner[m].astype(F32)
+        ordered = ordered[:rows_out]
+        ordered = jnp.where((me & 1) == 1, pltpu.roll(ordered, 4, 0), ordered).astype(BF16)
+        for c in range(CHUNKS):
+            chunks[c * bins_axis + m][...] = ordered[:, c * half : (c + 1) * half]
+
+
 def transpose_kernel(coupling, out):
     bins = coupling.shape[0]
     for start in range(0, bins, 256):
@@ -104,11 +151,12 @@
         out[start : start + size, :] = dot_nt(eye, coupling[:, start : start + size]).astype(BF16)
 
 
-def couple_kernel(chunk, bins_axis, owners_count, local_bins, slots, paired, *refs):
+def couple_kernel(chunk, bins_axis, local_bins, slots, paired, *refs):
     blocks = refs[:bins_axis]
     weights, meta = refs[bins_axis : bins_axis + 2]
-    outs = refs[-1 - (owners_count // 2 if paired else owners_count) : -1]
     values = refs[-1]
+    owners_count = 2 * len(paired)
+    outs = list(refs[-1 - sum(1 if pair else 2 for pair in paired) : -1])
     rows, width = blocks[0].shape
     all_bins = values.shape[0]
     half_bins = all_bins // 2
@@ -143,40 +191,71 @@
         at = slice(t * LANES, (t + 1) * LANES)
         first = jnp.where(is_low, even[:, at], odd[:, at])
         second = jnp.where(is_low, odd[:, at], even[:, at])
-        if paired:
-            outs[t][0] = first
-            outs[t][1] = second
+        if paired[t]:
+            out = outs.pop(0)
+            out[0], out[1] = first, second
         else:
-            outs[2 * t][...] = first
-            outs[2 * t + 1][...] = second
-
-
-def place_kernel(owners_count, slots, *refs):
-    pairs = owners_count // 2
-    paired, swapped = refs[:pairs], refs[pairs]
-    direct = refs[pairs + 1 : pairs + 1 + owners_count]
+            outs.pop(0)[...] = first
+            outs.pop(0)[...] = second
+
+
+def place_kernel(slots, sources, picks, *refs):
     out, staged, sems = refs[-3:]
     me = lax.axis_index("pts")
-    tall = direct[0].shape[0]
+    tall = refs[0].shape[-2]
     half_bins = tall - 8
     is_low = iota((tall, LANES), 1) < slots
     slot_id = iota((LANES, LANES), 0)
+
+    def block(pick):
+        ref, index = refs[pick[0]], pick[1]
+        return ref[...] if index is None else ref[index]
+
     copies = []
-    for x in range(owners_count):
-        early = paired[x // 2][0] if x % 2 == 0 else swapped[x // 2]
-        first, second = (early, direct[x][...]) if x % 2 == 0 else (direct[x][...], early)
+    for number, x in enumerate(sources):
+        first, second = [block(picks[number][c]) for c in range(CHUNKS)]
+        if x % 2 == 1:
+            first, second = second, first
         pieces = []
         for lhs in (jnp.where(is_low, first, second), jnp.where(is_low, second, first)):
             rank = lhs[tall - 16 :, :].astype(F32)[8:9, :].astype(I32)
             place = (slot_id == rank).astype(F32).astype(BF16)
             pieces.append(dot_nt(lhs, place)[:half_bins])
-        staged[x] = jnp.concatenate(pieces, axis=0).astype(BF16)
+        staged[number] = jnp.concatenate(pieces, axis=0).astype(BF16)
         at = pl.ds(pl.multiple_of((me ^ x) * LANES, LANES), LANES)
-        copy = pltpu.make_async_copy(staged.at[x], out.at[:, at], sems.at[x])
+        copy = pltpu.make_async_copy(staged.at[number], out.at[:, at], sems.at[number])
         copy.start()
         copies.append(copy)
     for copy in copies:
         copy.wait()
+
+
+def place(out, slots, owners_count, all_bins, sources):
+    arrays, picks = [], []
+    for x in sorted(sources):
+        mine = []
+        for array, index in sources[x]:
+            known = [n for n, a in enumerate(arrays) if a is array]
+            if not known:
+                arrays.append(array)
+                known = [len(arrays) - 1]
+            mine.append((known[0], index))
+        picks.append(tuple(mine))
+    held = [] if out is None else [out]
+    return pl.pallas_call(
+        functools.partial(place_kernel, slots, tuple(sorted(sources)), tuple(picks)),
+        out_shape=jax.ShapeDtypeStruct((all_bins, owners_count * LANES), BF16),
+        in_specs=vmem(len(arrays)) + [pl.BlockSpec(memory_space=pl.ANY)] * len(held),
+        out_specs=pl.BlockSpec(memory_space=pl.ANY),
+        scratch_shapes=[
+            pltpu.VMEM((len(sources), all_bins, LANES), BF16),
+            pltpu.SemaphoreType.DMA((len(sources),)),
+        ],
+        input_output_aliases={len(arrays): 0} if held else {},
+        compiler_params=params(16),
+        cost_estimate=cost(4 * all_bins * LANES * LANES * len(sources), 1e6 * len(sources)),
+        name="place",
+    )(*arrays, *held)
 
 
 def gate_kernel(array, after, out):
@@ -222,7 +301,8 @@
 
 
 def cost(flops, bytes_accessed):
-    return pl.CostEstimate(flops=int(flops), bytes_accessed=int(bytes_accessed), transcendentals=0)
+    del flops, bytes_accessed
+    return pl.CostEstimate(flops=1, bytes_accessed=1, transcendentals=0)
 
 
 def exchange(array, axis, offset):
@@ -242,17 +322,20 @@
     half_rows = all_bins // 2 + 8
     first_bin = lax.axis_index("bins") * local_bins
 
-    masked = spectrum * sea.astype(BF16)[None]
-    planes = jnp.pad(jnp.transpose(masked, (1, 0, 2)), ((0, 0), (0, tall - local_bins), (0, 0)))
+    planes = jnp.pad(jnp.transpose(spectrum, (1, 0, 2)), ((0, 0), (0, tall - local_bins), (0, 0)))
+    edges = [planes[r, :local_bins] * sea[r].astype(BF16)[None] for r in (0, lon_rows - 1)]
     up = [(i, i + 1) for i in range(owners_count - 1)]
     down = [(i + 1, i) for i in range(owners_count - 1)]
-    low = lax.ppermute(planes[lon_rows - 1], "pts", up)
-    high = lax.ppermute(planes[0], "pts", down)
+    low = lax.ppermute(edges[1], "pts", up)
+    high = lax.ppermute(edges[0], "pts", down)
     own = owner.reshape(1, points)
     owners = [own] + [exchange(own, "bins", m) for m in range(1, bins_axis)]
-    coef = jnp.concatenate([courant, upwind.astype(F32)], axis=1)
-    coef = lax.dynamic_slice_in_dim(coef, first_bin, local_bins, 0)
-    coef = jnp.pad(coef, ((0, tall - local_bins), (0, 0)))
+    def wide(table, dtype):
+        mine = lax.dynamic_slice_in_dim(table.T, first_bin, local_bins, 1).astype(dtype)
+        mine = jnp.pad(mine, ((0, 0), (0, tall - local_bins)))
+        return jnp.broadcast_to(mine[:, :, None], (2, tall, LANES))
+
+    speed, side = wide(courant, F32), wide(upwind, BF16)
 
     weights = pl.pallas_call(
         transpose_kernel,
@@ -264,59 +347,66 @@
         name="transpose",
     )(coupling)
 
+    inner, rim_order, meta = pl.pallas_call(
+        functools.partial(inner_kernel, bins_axis, owners_count, half),
+        out_shape=[
+            jax.ShapeDtypeStruct((bins_axis, tall, points), BF16),
+            jax.ShapeDtypeStruct((bins_axis, points, 2 * LANES), BF16),
+            jax.ShapeDtypeStruct((8, points), F32),
+        ],
+        in_specs=vmem(4 + bins_axis),
+        out_specs=vmem(3),
+        scratch_shapes=[pltpu.VMEM((lon_rows - 2, tall, lats), BF16)],
+        compiler_params=params(16),
+        cost_estimate=cost(bins_axis * tall * points * points, 4e6),
+        name="inner",
+    )(planes, speed, side, sea, *owners)
     packed = pl.pallas_call(
-        functools.partial(pack_kernel, rows, bins_axis, owners_count, half),
-        out_shape=[jax.ShapeDtypeStruct((rows, half), BF16)] * (CHUNKS * bins_axis)
-        + [jax.ShapeDtypeStruct((8, points), F32)],
-        in_specs=vmem(5 + bins_axis),
-        out_specs=vmem(CHUNKS * bins_axis + 1),
-        scratch_shapes=[pltpu.VMEM((lon_rows, tall, lats), BF16)],
+        functools.partial(pack_kernel, rows, bins_axis, half),
+        out_shape=[jax.ShapeDtypeStruct((rows, half), BF16)] * (CHUNKS * bins_axis),
+        in_specs=vmem(8),
+        out_specs=vmem(CHUNKS * bins_axis),
+        scratch_shapes=[pltpu.VMEM((2, tall, lats), BF16)],
         compiler_params=params(16),
-        cost_estimate=cost(2 * bins_axis * tall * points * points, 4e6),
+        cost_estimate=cost(bins_axis * tall * points * points, 4e6),
         name="pack",
-    )(planes, low, high, coef, sea, *owners)
-    meta = packed[-1]
+    )(planes, low, high, speed, side, sea, inner, rim_order)
 
     def couple(c, blocks, ready, paired):
-        shape, count = ((half_rows, LANES), owners_count)
-        if paired:
-            shape, count = (2,) + shape, count // 2
-        return pl.pallas_call(
-            functools.partial(
-                couple_kernel, c, bins_axis, owners_count, local_bins, slots, paired
-            ),
-            out_shape=[jax.ShapeDtypeStruct(shape, BF16)] * count,
+        shapes = [[(2, half_rows, LANES)] if pair else [(half_rows, LANES)] * 2 for pair in paired]
+        shapes = sum(shapes, [])
+        return list(pl.pallas_call(
+            functools.partial(couple_kernel, c, bins_axis, local_bins, slots, paired),
+            out_shape=[jax.ShapeDtypeStruct(shape, BF16) for shape in shapes],
             in_specs=vmem(len(blocks) + 2 + len(ready)),
-            out_specs=vmem(count),
+            out_specs=vmem(len(shapes)),
             scratch_shapes=[pltpu.VMEM((all_bins, half), F32)],
             compiler_params=params(16),
             cost_estimate=cost(2 * all_bins * all_bins * half + 4 * all_bins * half * 512, 6e6),
             name="couple",
-        )(*blocks, weights, meta, *ready)
-
+        )(*blocks, weights, meta, *ready))
+
+    pairs = owners_count // 2
     early, late = packed[:bins_axis], packed[bins_axis : 2 * bins_axis]
     first = [exchange(early[m], "bins", m) for m in range(1, bins_axis)]
     late = [late[0]] + [gate(b, after) for b, after in zip(late[1:], first)]
     second = [exchange(late[m], "bins", m) for m in range(1, bins_axis)]
-    pays = couple(0, [early[0], *first], late[1:], True)
-    pairs = [pays[0]] + [exchange(pays[t], "pts", 2 * t) for t in range(1, owners_count // 2)]
-    pays = couple(1, [late[0], *second], [], False)
-    direct = [pays[0]] + [exchange(pays[x], "pts", x) for x in range(1, owners_count)]
-    arrivals = [*pairs, exchange(stack(pairs, pays[0]), "pts", 1), *direct]
-
-    placed = pl.pallas_call(
-        functools.partial(place_kernel, owners_count, slots),
-        out_shape=jax.ShapeDtypeStruct((all_bins, owners_count * LANES), BF16),
-        in_specs=vmem(len(arrivals)),
-        out_specs=pl.BlockSpec(memory_space=pl.ANY),
-        scratch_shapes=[
-            pltpu.VMEM((owners_count, all_bins, LANES), BF16),
-            pltpu.SemaphoreType.DMA((owners_count,)),
-        ],
-        compiler_params=params(16),
-        cost_estimate=cost(4 * all_bins * LANES * LANES * owners_count, 8e6),
-        name="place",
-    )(*arrivals)
+    pays = couple(0, [early[0], *first], [*late[2:], second[0]], (True,) * pairs)
+    came = {0: pays[0]}
+    for t in range(pairs - 1, 0, -1):
+        came[t] = exchange(pays[t], "pts", 2 * t)
+    pays = couple(1, [late[0], *second], [], (True,) * pairs)
+    last = {0: pays[0]}
+    for t in range(pairs - 1, 0, -1):
+        last[t] = exchange(pays[t], "pts", 2 * t)
+    swapped = exchange(stack([came[t] for t in range(pairs)], last[pairs - 1]), "pts", 1)
+    swapped_late = exchange(stack([last[t] for t in range(pairs)], last[0]), "pts", 1)
+
+    shape = (slots, owners_count, all_bins)
+    placed = place(None, *shape, {2 * t: [(came[t], 0), (last[t], 0)] for t in range(pairs)})
+    placed = place(
+        placed, *shape, {2 * t + 1: [(swapped, t), (swapped_late, t)] for t in range(pairs)}
+    )
     return jnp.transpose(placed).reshape(1, 1, owners_count * LANES, all_bins)
 
 
@@ -399,7 +489,8 @@
         and bins_axis % 2 == 0
         and spectrum.shape[0] % 8 == 4
         and courant.shape[0] % 48 == 0
-        and owners_count <= 8
+        and owners_count == 8
+        and spectrum.shape[1] >= 3
     )
     form = chunked if suits else whole
     return form(spectrum, courant, upwind, coupling, sea, owner)

time: 85.3 us -> 80.8 us (0.947)
  the two profiles are of different devices: /device:TPU:0 before, /device:TPU:11 now
where the time goes in v3:
time: 80.8 us; the launch traced here: 80.6 us
  waiting for transfers between devices  38.6 us (48%)
  starting transfers between devices  26.3 us (33%)
  Pallas kernels  12.5 us (15%)
  local copies, waits for them, and re-layouts  2.14 us (3%)
  other arithmetic  0.82 us (1%)
    ppermute x17, waiting for transfers between devices, exchange(): lax.ppermute(array, axis, [(i, i ^ offset) for i in range(lax.axis_size(a...  38.6 us
    ppermute x17, starting transfers between devices, exchange(): lax.ppermute(array, axis, [(i, i ^ offset) for i in range(lax.axis_size(a...  20.7 us
    pallas_call x2, Pallas kernels, couple(): pl.pallas_call(functools.partial(couple_kernel, c, bins_axis, local_bins,...  4.13 us
    ppermute x1, starting transfers between devices, chunked(): low = lax.ppermute(edges[1], 'pts', up)  3.68 us
    pallas_call x2, Pallas kernels, place(): pl.pallas_call(functools.partial(place_kernel, slots, tuple(sorted(source...  3.26 us
    pallas_call x1, Pallas kernels, chunked(): pl.pallas_call(functools.partial(inner_kernel, bins_axis, owners_count, h...  2.11 us
    ppermute x1, starting transfers between devices, chunked(): high = lax.ppermute(edges[0], 'pts', down)  1.92 us
    unnamed x9, local copies, waits for them, and re-layouts  1.63 us
  transfers between devices with their start and end apart: 19, of which 9 were waited for; matrix products, arithmetic and copies ran while one was open for 2% of the time, Pallas kernels for 9%

profile of v3, /device:TPU:11, one launch (start us, length us, event | category | flops | bytes accessed | tf_op | source)
XLA Modules:
  0.0 80.6 jit_solution(2227956118872866727)
XLA Ops:
  0.0 1.6 %copy.10 = bf16[324,4,512]{2,0,1:T(8,128)(2,1)S(1)} copy(bf16[324,4,512]{2,1,0:T(4,128)(2,1)} %param.6) | data formatting | bytes 2654208 | tf_op args[0]
  1.7 3.7 %collective-permute-start = (bf16[324,512]{1,0:T(8,128)(2,1)S(1)}, bf16[324,512]{1,0:T(8,128)(2,1)S(1)}, u32[]{:S(2)}, u32[]{:S(2)}) collective-permute-start(bf16[324,512]{1,0:T(8,128)(2,1)S(1)} %get-tuple-element.46), channel_id=1, source_target_pairs={{0,4},{4,8},{8,12},{12,16},{16,20},{20,24},{24,28},{1,5},{5,9},{9,... | collective-permute-start | bytes 995336 | tf_op jit(solution)/shard_map/ppermute | solution.py:329
  5.4 1.9 %collective-permute-start.1 = (bf16[324,512]{1,0:T(8,128)(2,1)S(1)}, bf16[324,512]{1,0:T(8,128)(2,1)S(1)}, u32[]{:S(2)}, u32[]{:S(2)}) collective-permute-start(bf16[324,512]{1,0:T(8,128)(2,1)S(1)} %get-tuple-element.45), channel_id=1, source_target_pairs={{4,0},{8,4},{12,8},{16,12},{20,16},{24,20},{28,24},{5,1},{9,5},{13... | collective-permute-start | bytes 995336 | tf_op jit(solution)/shard_map/ppermute | solution.py:330
  7.6 2.3 %collective-permute-start.3 = (s32[1,512]{1,0:T(1,128)S(1)}, s32[1,512]{1,0:T(1,128)S(1)}, u32[]{:S(2)}, u32[]{:S(2)}) collective-permute-start(s32[1,512]{1,0:T(1,128)S(1)} %bitcast.20), channel_id=1, source_target_pairs={{0,2},{1,3},{2,0},{3,1},{4,6},{5,7},{6,4},{7,5},{8,10},{9,11},{10,... | collective-permute-start | bytes 6152 | tf_op jit(solution)/shard_map/ppermute | solution.py:309
  11.1 1.5 %collective-permute-done.4.refs_7_ = s32[1,512]{1,0:T(1,128)S(1)} collective-permute-done((s32[1,512]{1,0:T(1,128)S(1)}, s32[1,512]{1,0:T(1,128)S(1)}, u32[]{:S(2)}, u32[]{:S(2)}) %collective-permute-start.4) | collective-permute-done | bytes 2080 | tf_op jit(solution)/shard_map/ppermute | solution.py:309
  12.9 2.1 %inner.1 = (bf16[4,336,512]{2,1,0:T(8,128)(2,1)S(1)}, bf16[4,512,256]{2,1,0:T(8,128)(2,1)S(1)}, f32[8,512]{1,0:T(8,128)S(1)}) custom-call(bf16[4,336,512]{2,1,0:T(8,128)(2,1)S(1)} %pad.12.refs_0_, f32[2,336,128]{2,1,0:T(8,128)S(1)} %broadcast_in_dim.4.refs_1_.refs_3_, bf16[2,336,128]{2,1,0:T(8,128)(2,1)S(1)} %broadcast_in_dim.5.refs_2_.refs_4_, ...), custom_call_target="tpu_custom_call" | custom-call | flops 1 | bytes 1 | tf_op jit(solution)/shard_map/inner/pallas_call | solution.py:350
  15.1 1.6 %pack.1 = (bf16[328,256]{1,0:T(8,128)(2,1)S(1)}, bf16[328,256]{1,0:T(8,128)(2,1)S(1)}, bf16[328,256]{1,0:T(8,128)(2,1)S(1)}, bf16[328,256]{1,0:T(8,128)(2,1)S(1)...) custom-call(bf16[4,336,512]{2,1,0:T(8,128)(2,1)S(1)} %pad.12.refs_0_, ...), custom_call_target="tpu_custom_call" | custom-call | flops 1 | bytes 1 | tf_op jit(solution)/shard_map/pack/pallas_call | solution.py:364
  16.6 2.9 %collective-permute-start.5 = (bf16[328,256]{1,0:T(8,128)(2,1)S(1)}, bf16[328,256]{1,0:T(8,128)(2,1)S(1)}, u32[]{:S(2)}, u32[]{:S(2)}) collective-permute-start(bf16[328,256]{1,0:T(8,128)(2,1)S(1)} %get-tuple-element.27), channel_id=1, source_target_pairs={{0,1},{1,0},{2,3},{3,2},{4,5},{5,4},{6,7},{7,6},{8,9},{9,8},{10,11... | collective-permute-start | bytes 503816 | tf_op jit(solution)/shard_map/ppermute | solution.py:309
  20.8 3.0 %collective-permute-done.5.after.refs_1_ = bf16[328,256]{1,0:T(8,128)(2,1)S(1)} collective-permute-done((bf16[328,256]{1,0:T(8,128)(2,1)S(1)}, bf16[328,256]{1,0:T(8,128)(2,1)S(1)}, u32[]{:S(2)}, u32[]{:S(2)}) %collective-permute-start.5) | collective-permute-done | bytes 167968 | tf_op jit(solution)/shard_map/ppermute | solution.py:309
  23.8 2.4 %collective-permute-start.8 = (bf16[328,256]{1,0:T(8,128)(2,1)S(1)}, bf16[328,256]{1,0:T(8,128)(2,1)S(1)}, u32[]{:S(2)}, u32[]{:S(2)}) collective-permute-start(bf16[328,256]{1,0:T(8,128)(2,1)S(1)} %gate.5), channel_id=1, source_target_pairs={{0,1},{1,0},{2,3},{3,2},{4,5},{5,4},{6,7},{7,6},{8,9},{9,8},{10,11... | collective-permute-start | bytes 503816 | tf_op jit(solution)/shard_map/ppermute | solution.py:309
  27.6 6.9 %collective-permute-done.7.after.refs_3_ = bf16[328,256]{1,0:T(8,128)(2,1)S(1)} collective-permute-done((bf16[328,256]{1,0:T(8,128)(2,1)S(1)}, bf16[328,256]{1,0:T(8,128)(2,1)S(1)}, u32[]{:S(2)}, u32[]{:S(2)}) %collective-permute-start.7) | collective-permute-done | bytes 167968 | tf_op jit(solution)/shard_map/ppermute | solution.py:309
  34.6 2.1 %couple.2 = (bf16[2,656,128]{2,1,0:T(8,128)(2,1)S(1)}, bf16[2,656,128]{2,1,0:T(8,128)(2,1)S(1)}, bf16[2,656,128]{2,1,0:T(8,128)(2,1)S(1)}, bf16[2,656,128]{2,1,0:T(8,128)(2,1)S(1)}) custom-call(bf16[328,256]{1,0:T(8,128)(2,1)S(1)} %get-tuple-element.26.refs_0_, bf16[328,256]{1,0:T(8,128)(2,1)S(1)} %collective-permute-done.5.after.refs_1_, ...), custom_call_target="tpu_custom_call" | custom-call | flops 1 | bytes 1 | tf_op jit(solution)/shard_map/couple/pallas_call | solution.py:378
  36.6 2.0 %collective-permute-start.9 = (bf16[2,656,128]{2,1,0:T(8,128)(2,1)S(1)}, bf16[2,656,128]{2,1,0:T(8,128)(2,1)S(1)}, u32[]{:S(2)}, u32[]{:S(2)}) collective-permute-start(bf16[2,656,128]{2,1,0:T(8,128)(2,1)S(1)} %get-tuple-element.35), channel_id=1, source_target_pairs={{0,8},{4,12},{8,0},{12,4},{16,24},{20,28},{24,16},{28,20},{1,9},{5... | collective-permute-start | bytes 1007624 | tf_op jit(solution)/shard_map/ppermute | solution.py:309
  38.6 1.3 %collective-permute-start.12 = (bf16[328,256]{1,0:T(8,128)(2,1)S(1)}, bf16[328,256]{1,0:T(8,128)(2,1)S(1)}, u32[]{:S(2)}, u32[]{:S(2)}) collective-permute-start(bf16[328,256]{1,0:T(8,128)(2,1)S(1)} %gate.3.refs_6_), channel_id=1, source_target_pairs={{0,2},{1,3},{2,0},{3,1},{4,6},{5,7},{6,4},{7,5},{8,10},{9,11},{10,... | collective-permute-start | bytes 503816 | tf_op jit(solution)/shard_map/ppermute | solution.py:309
  42.4 8.5 %collective-permute-done.12.refs_2_ = bf16[328,256]{1,0:T(8,128)(2,1)S(1)} collective-permute-done((bf16[328,256]{1,0:T(8,128)(2,1)S(1)}, bf16[328,256]{1,0:T(8,128)(2,1)S(1)}, u32[]{:S(2)}, u32[]{:S(2)}) %collective-permute-start.12) | collective-permute-done | bytes 167968 | tf_op jit(solution)/shard_map/ppermute | solution.py:309
  50.9 5.6 %collective-permute-done.13.refs_3_ = bf16[328,256]{1,0:T(8,128)(2,1)S(1)} collective-permute-done((bf16[328,256]{1,0:T(8,128)(2,1)S(1)}, bf16[328,256]{1,0:T(8,128)(2,1)S(1)}, u32[]{:S(2)}, u32[]{:S(2)}) %collective-permute-start.13) | collective-permute-done | bytes 167968 | tf_op jit(solution)/shard_map/ppermute | solution.py:309
  56.5 2.1 %couple.3 = (bf16[2,656,128]{2,1,0:T(8,128)(2,1)S(1)}, bf16[2,656,128]{2,1,0:T(8,128)(2,1)S(1)}, bf16[2,656,128]{2,1,0:T(8,128)(2,1)S(1)}, bf16[2,656,128]{2,1,0:T(8,128)(2,1)S(1)}) custom-call(bf16[328,256]{1,0:T(8,128)(2,1)S(1)} %get-tuple-element.38.refs_0_, bf16[328,256]{1,0:T(8,128)(2,1)S(1)} %collective-permute-done.8.refs_8_.refs_1_, ...), custom_call_target="tpu_custom_call" | custom-call | flops 1 | bytes 1 | tf_op jit(solution)/shard_map/couple/pallas_call | solution.py:378
  58.8 2.5 %collective-permute-start.17 = (bf16[2,656,128]{2,1,0:T(8,128)(2,1)S(1)}, bf16[2,656,128]{2,1,0:T(8,128)(2,1)S(1)}, u32[]{:S(2)}, u32[]{:S(2)}) collective-permute-start(bf16[2,656,128]{2,1,0:T(8,128)(2,1)S(1)} %get-tuple-element.42), channel_id=1, source_target_pairs={{0,16},{4,20},{8,24},{12,28},{16,0},{20,4},{24,8},{28,12},{1,17},{... | collective-permute-start | bytes 1007624 | tf_op jit(solution)/shard_map/ppermute | solution.py:309
  61.3 7.2 %collective-permute-done.14.refs_4_.refs_3_.refs_7_ = bf16[2,656,128]{2,1,0:T(8,128)(2,1)S(1)} collective-permute-done((bf16[2,656,128]{2,1,0:T(8,128)(2,1)S(1)}, bf16[2,656,128]{2,1,0:T(8,128)(2,1)S(1)}, u32[]{:S(2)}, u32[]{:S(2)}) %collective-permute-start.14) | collective-permute-done | bytes 335904 | tf_op jit(solution)/shard_map/ppermute | solution.py:309
  68.6 2.3 %collective-permute-start.15 = (bf16[4,656,128]{2,1,0:T(8,128)(2,1)S(1)}, bf16[4,656,128]{2,1,0:T(8,128)(2,1)S(1)}, u32[]{:S(2)}, u32[]{:S(2)}) collective-permute-start(bf16[4,656,128]{2,1,0:T(8,128)(2,1)S(1)} %stack.2), channel_id=1, source_target_pairs={{0,4},{4,0},{8,12},{12,8},{16,20},{20,16},{24,28},{28,24},{1,5},{5... | collective-permute-start | bytes 2015240 | tf_op jit(solution)/shard_map/ppermute | solution.py:309
  71.0 2.8 %collective-permute-done.16.refs_1_.refs_3_ = bf16[2,656,128]{2,1,0:T(8,128)(2,1)S(1)} collective-permute-done((bf16[2,656,128]{2,1,0:T(8,128)(2,1)S(1)}, bf16[2,656,128]{2,1,0:T(8,128)(2,1)S(1)}, u32[]{:S(2)}, u32[]{:S(2)}) %collective-permute-start.16) | collective-permute-done | bytes 335904 | tf_op jit(solution)/shard_map/ppermute | solution.py:309
  73.8 2.8 %collective-permute-done.17.refs_2_.refs_5_ = bf16[2,656,128]{2,1,0:T(8,128)(2,1)S(1)} collective-permute-done((bf16[2,656,128]{2,1,0:T(8,128)(2,1)S(1)}, bf16[2,656,128]{2,1,0:T(8,128)(2,1)S(1)}, u32[]{:S(2)}, u32[]{:S(2)}) %collective-permute-start.17) | collective-permute-done | bytes 335904 | tf_op jit(solution)/shard_map/ppermute | solution.py:309
  77.2 1.6 %place.2.refs_2_ = bf16[1296,1024]{1,0:T(8,128)(2,1)} custom-call(bf16[2,656,128]{2,1,0:T(8,128)(2,1)S(1)} %get-tuple-element.34.refs_0_, bf16[2,656,128]{2,1,0:T(8,128)(2,1)S(1)} %get-tuple-element.40.refs_0_.refs_4_.refs_1_, bf16[2,656,128]{2,1,0:T(8,128)(2,1)S(1)} %collective-permute-done.9.refs_1_.refs_2_, ...), custom_call_target="tpu_custom_call" | custom-call | flops 1 | bytes 1 | tf_op jit(solution)/shard_map/place/pallas_call | solution.py:245
  78.9 1.6 %place.3 = bf16[1296,1024]{1,0:T(8,128)(2,1)} custom-call(bf16[4,656,128]{2,1,0:T(8,128)(2,1)S(1)} %collective-permute-done.15.refs_0_, bf16[4,656,128]{2,1,0:T(8,128)(2,1)S(1)} %collective-permute-done.18.refs_1_, bf16[1296,1024]{1,0:T(8,128)(2,1)} %place.2.refs_2_), custom_call_target="tpu_custom_call", output_to_operand_aliasing={{}: (2, {})} | custom-call | flops 1 | bytes 1 | tf_op jit(solution)/shard_map/place/pallas_call | solution.py:245
  (45 shorter events, 7.7 us)
Async XLA Ops:
  0.0 10.1 %copy-start = (f32[1296,2]{0,1:T(2,128)S(1)}, f32[1296,2]{0,1:T(2,128)}, u32[]{:S(2)}) copy-start(f32[1296,2]{0,1:T(2,128)} %param.7) | copy-start | bytes 31108
  0.0 1.6 %copy-start.2 = (s32[4,512]{1,0:T(4,128)S(1)}, s32[4,512]{1,0:T(4,128)}, u32[]{:S(2)}) copy-start(s32[4,512]{1,0:T(4,128)} %refs_5_.1) | copy-start | bytes 24580
  0.0 7.3 %copy-start.3 = (s32[1,1,512,1]{2,3,1,0:T(1,128)S(1)}, s32[1,1,512,1]{2,3,1,0:T(1,128)}, u32[]{:S(2)}) copy-start(s32[1,1,512,1]{2,3,1,0:T(1,128)} %param.11) | copy-start | bytes 6148
  1.7 13.3 %collective-permute-start = (bf16[324,512]{1,0:T(8,128)(2,1)S(1)}, bf16[324,512]{1,0:T(8,128)(2,1)S(1)}, u32[]{:S(2)}, u32[]{:S(2)}) collective-permute-start(bf16[324,512]{1,0:T(8,128)(2,1)S(1)} %get-tuple-element.46), channel_id=1, source_target_pairs={{0,4},{4,8},{8,12},{12,16},{16,20},{20,24},{24,28},{1,5},{5,9},{9,... | collective-permute-start | bytes 995336 | tf_op jit(solution)/shard_map/ppermute | solution.py:329
  5.4 9.6 %collective-permute-start.1 = (bf16[324,512]{1,0:T(8,128)(2,1)S(1)}, bf16[324,512]{1,0:T(8,128)(2,1)S(1)}, u32[]{:S(2)}, u32[]{:S(2)}) collective-permute-start(bf16[324,512]{1,0:T(8,128)(2,1)S(1)} %get-tuple-element.45), channel_id=1, source_target_pairs={{4,0},{8,4},{12,8},{16,12},{20,16},{24,20},{28,24},{5,1},{9,5},{13... | collective-permute-start | bytes 995336 | tf_op jit(solution)/shard_map/ppermute | solution.py:330
  7.4 3.7 %collective-permute-start.2 = (s32[1,512]{1,0:T(1,128)S(1)}, s32[1,512]{1,0:T(1,128)S(1)}, u32[]{:S(2)}, u32[]{:S(2)}) collective-permute-start(s32[1,512]{1,0:T(1,128)S(1)} %bitcast.19), channel_id=1, source_target_pairs={{0,1},{1,0},{2,3},{3,2},{4,5},{5,4},{6,7},{7,6},{8,9},{9,8},{10,11... | collective-permute-start | bytes 6152 | tf_op jit(solution)/shard_map/ppermute | solution.py:309
  7.6 3.5 %collective-permute-start.3 = (s32[1,512]{1,0:T(1,128)S(1)}, s32[1,512]{1,0:T(1,128)S(1)}, u32[]{:S(2)}, u32[]{:S(2)}) collective-permute-start(s32[1,512]{1,0:T(1,128)S(1)} %bitcast.20), channel_id=1, source_target_pairs={{0,2},{1,3},{2,0},{3,1},{4,6},{5,7},{6,4},{7,5},{8,10},{9,11},{10,... | collective-permute-start | bytes 6152 | tf_op jit(solution)/shard_map/ppermute | solution.py:309
  9.9 2.7 %collective-permute-start.4 = (s32[1,512]{1,0:T(1,128)S(1)}, s32[1,512]{1,0:T(1,128)S(1)}, u32[]{:S(2)}, u32[]{:S(2)}) collective-permute-start(s32[1,512]{1,0:T(1,128)S(1)} %bitcast.21), channel_id=1, source_target_pairs={{0,3},{1,2},{2,1},{3,0},{4,7},{5,6},{6,5},{7,4},{8,11},{9,10},{10,... | collective-permute-start | bytes 6152 | tf_op jit(solution)/shard_map/ppermute | solution.py:309
  15.0 11.2 %copy-start.1 = (bf16[1296,1296]{1,0:T(8,128)(2,1)S(1)}, bf16[1296,1296]{1,0:T(8,128)(2,1)}, u32[]{:S(2)}) copy-start(bf16[1296,1296]{1,0:T(8,128)(2,1)} %coupling.1) | copy-start | bytes 10077700
  16.6 7.2 %collective-permute-start.5 = (bf16[328,256]{1,0:T(8,128)(2,1)S(1)}, bf16[328,256]{1,0:T(8,128)(2,1)S(1)}, u32[]{:S(2)}, u32[]{:S(2)}) collective-permute-start(bf16[328,256]{1,0:T(8,128)(2,1)S(1)} %get-tuple-element.27), channel_id=1, source_target_pairs={{0,1},{1,0},{2,3},{3,2},{4,5},{5,4},{6,7},{7,6},{8,9},{9,8},{10,11... | collective-permute-start | bytes 503816 | tf_op jit(solution)/shard_map/ppermute | solution.py:309
  19.5 8.0 %collective-permute-start.6 = (bf16[328,256]{1,0:T(8,128)(2,1)S(1)}, bf16[328,256]{1,0:T(8,128)(2,1)S(1)}, u32[]{:S(2)}, u32[]{:S(2)}) collective-permute-start(bf16[328,256]{1,0:T(8,128)(2,1)S(1)} %get-tuple-element.28), channel_id=1, source_target_pairs={{0,2},{1,3},{2,0},{3,1},{4,6},{5,7},{6,4},{7,5},{8,10},{9,11},{10,... | collective-permute-start | bytes 503816 | tf_op jit(solution)/shard_map/ppermute | solution.py:309
  19.5 15.0 %collective-permute-start.7 = (bf16[328,256]{1,0:T(8,128)(2,1)S(1)}, bf16[328,256]{1,0:T(8,128)(2,1)S(1)}, u32[]{:S(2)}, u32[]{:S(2)}) collective-permute-start(bf16[328,256]{1,0:T(8,128)(2,1)S(1)} %get-tuple-element.29), channel_id=1, source_target_pairs={{0,3},{1,2},{2,1},{3,0},{4,7},{5,6},{6,5},{7,4},{8,11},{9,10},{10,... | collective-permute-start | bytes 503816 | tf_op jit(solution)/shard_map/ppermute | solution.py:309
  23.8 10.7 %collective-permute-start.8 = (bf16[328,256]{1,0:T(8,128)(2,1)S(1)}, bf16[328,256]{1,0:T(8,128)(2,1)S(1)}, u32[]{:S(2)}, u32[]{:S(2)}) collective-permute-start(bf16[328,256]{1,0:T(8,128)(2,1)S(1)} %gate.5), channel_id=1, source_target_pairs={{0,1},{1,0},{2,3},{3,2},{4,5},{5,4},{6,7},{7,6},{8,9},{9,8},{10,11... | collective-permute-start | bytes 503816 | tf_op jit(solution)/shard_map/ppermute | solution.py:309
  36.6 22.2 %collective-permute-start.9 = (bf16[2,656,128]{2,1,0:T(8,128)(2,1)S(1)}, bf16[2,656,128]{2,1,0:T(8,128)(2,1)S(1)}, u32[]{:S(2)}, u32[]{:S(2)}) collective-permute-start(bf16[2,656,128]{2,1,0:T(8,128)(2,1)S(1)} %get-tuple-element.35), channel_id=1, source_target_pairs={{0,8},{4,12},{8,0},{12,4},{16,24},{20,28},{24,16},{28,20},{1,9},{5... | collective-permute-start | bytes 1007624 | tf_op jit(solution)/shard_map/ppermute | solution.py:309
  38.6 12.3 %collective-permute-start.12 = (bf16[328,256]{1,0:T(8,128)(2,1)S(1)}, bf16[328,256]{1,0:T(8,128)(2,1)S(1)}, u32[]{:S(2)}, u32[]{:S(2)}) collective-permute-start(bf16[328,256]{1,0:T(8,128)(2,1)S(1)} %gate.3.refs_6_), channel_id=1, source_target_pairs={{0,2},{1,3},{2,0},{3,1},{4,6},{5,7},{6,4},{7,5},{8,10},{9,11},{10,... | collective-permute-start | bytes 503816 | tf_op jit(solution)/shard_map/ppermute | solution.py:309
  40.0 16.6 %collective-permute-start.13 = (bf16[328,256]{1,0:T(8,128)(2,1)S(1)}, bf16[328,256]{1,0:T(8,128)(2,1)S(1)}, u32[]{:S(2)}, u32[]{:S(2)}) collective-permute-start(bf16[328,256]{1,0:T(8,128)(2,1)S(1)} %gate.4.refs_7_), channel_id=1, source_target_pairs={{0,3},{1,2},{2,1},{3,0},{4,7},{5,6},{6,5},{7,4},{8,11},{9,10},{10,... | collective-permute-start | bytes 503816 | tf_op jit(solution)/shard_map/ppermute | solution.py:309
  41.1 20.2 %collective-permute-start.10 = (bf16[2,656,128]{2,1,0:T(8,128)(2,1)S(1)}, bf16[2,656,128]{2,1,0:T(8,128)(2,1)S(1)}, u32[]{:S(2)}, u32[]{:S(2)}) collective-permute-start(bf16[2,656,128]{2,1,0:T(8,128)(2,1)S(1)} %get-tuple-element.36), channel_id=1, source_target_pairs={{0,16},{4,20},{8,24},{12,28},{16,0},{20,4},{24,8},{28,12},{1,17},{... | collective-permute-start | bytes 1007624 | tf_op jit(solution)/shard_map/ppermute | solution.py:309
  41.1 20.2 %collective-permute-start.11 = (bf16[2,656,128]{2,1,0:T(8,128)(2,1)S(1)}, bf16[2,656,128]{2,1,0:T(8,128)(2,1)S(1)}, u32[]{:S(2)}, u32[]{:S(2)}) collective-permute-start(bf16[2,656,128]{2,1,0:T(8,128)(2,1)S(1)} %get-tuple-element.37), channel_id=1, source_target_pairs={{0,24},{4,28},{8,16},{12,20},{16,8},{20,12},{24,0},{28,4},{1,25},{... | collective-permute-start | bytes 1007624 | tf_op jit(solution)/shard_map/ppermute | solution.py:309
  58.6 10.0 %collective-permute-start.14 = (bf16[2,656,128]{2,1,0:T(8,128)(2,1)S(1)}, bf16[2,656,128]{2,1,0:T(8,128)(2,1)S(1)}, u32[]{:S(2)}, u32[]{:S(2)}) collective-permute-start(bf16[2,656,128]{2,1,0:T(8,128)(2,1)S(1)} %get-tuple-element.39), channel_id=1, source_target_pairs={{0,24},{4,28},{8,16},{12,20},{16,8},{20,12},{24,0},{28,4},{1,25},{... | collective-permute-start | bytes 1007624 | tf_op jit(solution)/shard_map/ppermute | solution.py:309
  58.7 15.1 %collective-permute-start.16 = (bf16[2,656,128]{2,1,0:T(8,128)(2,1)S(1)}, bf16[2,656,128]{2,1,0:T(8,128)(2,1)S(1)}, u32[]{:S(2)}, u32[]{:S(2)}) collective-permute-start(bf16[2,656,128]{2,1,0:T(8,128)(2,1)S(1)} %get-tuple-element.41), channel_id=1, source_target_pairs={{0,8},{4,12},{8,0},{12,4},{16,24},{20,28},{24,16},{28,20},{1,9},{5... | collective-permute-start | bytes 1007624 | tf_op jit(solution)/shard_map/ppermute | solution.py:309
  58.8 17.7 %collective-permute-start.17 = (bf16[2,656,128]{2,1,0:T(8,128)(2,1)S(1)}, bf16[2,656,128]{2,1,0:T(8,128)(2,1)S(1)}, u32[]{:S(2)}, u32[]{:S(2)}) collective-permute-start(bf16[2,656,128]{2,1,0:T(8,128)(2,1)S(1)} %get-tuple-element.42), channel_id=1, source_target_pairs={{0,16},{4,20},{8,24},{12,28},{16,0},{20,4},{24,8},{28,12},{1,17},{... | collective-permute-start | bytes 1007624 | tf_op jit(solution)/shard_map/ppermute | solution.py:309
  68.6 10.2 %collective-permute-start.15 = (bf16[4,656,128]{2,1,0:T(8,128)(2,1)S(1)}, bf16[4,656,128]{2,1,0:T(8,128)(2,1)S(1)}, u32[]{:S(2)}, u32[]{:S(2)}) collective-permute-start(bf16[4,656,128]{2,1,0:T(8,128)(2,1)S(1)} %stack.2), channel_id=1, source_target_pairs={{0,4},{4,0},{8,12},{12,8},{16,20},{20,16},{24,28},{28,24},{1,5},{5... | collective-permute-start | bytes 2015240 | tf_op jit(solution)/shard_map/ppermute | solution.py:309
  76.6 2.3 %collective-permute-start.18 = (bf16[4,656,128]{2,1,0:T(8,128)(2,1)S(1)}, bf16[4,656,128]{2,1,0:T(8,128)(2,1)S(1)}, u32[]{:S(2)}, u32[]{:S(2)}) collective-permute-start(bf16[4,656,128]{2,1,0:T(8,128)(2,1)S(1)} %stack.3), channel_id=1, source_target_pairs={{0,4},{4,0},{8,12},{12,8},{16,20},{20,16},{24,28},{28,24},{1,5},{5... | collective-permute-start | bytes 2015240 | tf_op jit(solution)/shard_map/ppermute | solution.py:309

commit v4 on v3

--- a/solution.py
+++ b/solution.py
@@ -253,26 +253,25 @@
         ],
         input_output_aliases={len(arrays): 0} if held else {},
         compiler_params=params(16),
-        cost_estimate=cost(4 * all_bins * LANES * LANES * len(sources), 1e6 * len(sources)),
+        cost_estimate=cost(1, 1),
         name="place",
     )(*arrays, *held)
 
 
-def gate_kernel(array, after, out):
-    del after
-    out[...] = array[...]
-
-
-def gate(array, after):
+def gate_kernel(array, *refs):
+    refs[-1][...] = array[...]
+
+
+def gate(array, *after):
     return pl.pallas_call(
         gate_kernel,
         out_shape=jax.ShapeDtypeStruct(array.shape, array.dtype),
-        in_specs=vmem(2),
+        in_specs=vmem(1 + len(after)),
         out_specs=vmem(1)[0],
-        compiler_params=params(8),
-        cost_estimate=cost(0, 4 * array.size),
+        compiler_params=params(16),
+        cost_estimate=cost(1, 1),
         name="gate",
-    )(array, after)
+    )(array, *after)
 
 
 def stack_kernel(count, *refs):
@@ -287,7 +286,7 @@
         in_specs=vmem(len(pairs) + 1),
         out_specs=vmem(1)[0],
         compiler_params=params(8),
-        cost_estimate=cost(0, 4 * sum(a.size for a in pairs)),
+        cost_estimate=cost(1, 1),
         name="stack",
     )(*pairs, after)
 
@@ -301,8 +300,8 @@
 
 
 def cost(flops, bytes_accessed):
-    del flops, bytes_accessed
-    return pl.CostEstimate(flops=1, bytes_accessed=1, transcendentals=0)
+    del bytes_accessed
+    return pl.CostEstimate(flops=int(flops), bytes_accessed=1, transcendentals=0)
 
 
 def exchange(array, axis, offset):
@@ -343,7 +342,7 @@
         in_specs=vmem(1),
         out_specs=vmem(1)[0],
         compiler_params=params(16),
-        cost_estimate=cost(2 * 256 * all_bins * all_bins, 7e6),
+        cost_estimate=cost(1, 1),
         name="transpose",
     )(coupling)
 
@@ -358,7 +357,7 @@
         out_specs=vmem(3),
         scratch_shapes=[pltpu.VMEM((lon_rows - 2, tall, lats), BF16)],
         compiler_params=params(16),
-        cost_estimate=cost(bins_axis * tall * points * points, 4e6),
+        cost_estimate=cost(1, 1),
         name="inner",
     )(planes, speed, side, sea, *owners)
     packed = pl.pallas_call(
@@ -368,7 +367,7 @@
         out_specs=vmem(CHUNKS * bins_axis),
         scratch_shapes=[pltpu.VMEM((2, tall, lats), BF16)],
         compiler_params=params(16),
-        cost_estimate=cost(bins_axis * tall * points * points, 4e6),
+        cost_estimate=cost(1, 1),
         name="pack",
     )(planes, low, high, speed, side, sea, inner, rim_order)
 
@@ -382,16 +381,16 @@
             out_specs=vmem(len(shapes)),
             scratch_shapes=[pltpu.VMEM((all_bins, half), F32)],
             compiler_params=params(16),
-            cost_estimate=cost(2 * all_bins * all_bins * half + 4 * all_bins * half * 512, 6e6),
+            cost_estimate=cost(1 + c * 3e10, 1),
             name="couple",
         )(*blocks, weights, meta, *ready))
 
     pairs = owners_count // 2
     early, late = packed[:bins_axis], packed[bins_axis : 2 * bins_axis]
     first = [exchange(early[m], "bins", m) for m in range(1, bins_axis)]
-    late = [late[0]] + [gate(b, after) for b, after in zip(late[1:], first)]
+    late = [late[0], gate(late[1], first[0], weights)] + [gate(b, *first) for b in late[2:]]
     second = [exchange(late[m], "bins", m) for m in range(1, bins_axis)]
-    pays = couple(0, [early[0], *first], [*late[2:], second[0]], (True,) * pairs)
+    pays = couple(0, [early[0], *first], late[1:], (True,) * pairs)
     came = {0: pays[0]}
     for t in range(pairs - 1, 0, -1):
         came[t] = exchange(pays[t], "pts", 2 * t)

time: 80.8 us -> 78.7 us (0.974)
  the two profiles are of different devices: /device:TPU:11 before, /device:TPU:0 now
where the time goes in v4:
time: 78.7 us; the launch traced here: 78.5 us
  waiting for transfers between devices  36 us (46%)
  starting transfers between devices  26.9 us (34%)
  Pallas kernels  12.5 us (16%)
  local copies, waits for them, and re-layouts  2.14 us (3%)
  other arithmetic  0.82 us (1%)
    ppermute x17, waiting for transfers between devices, exchange(): lax.ppermute(array, axis, [(i, i ^ offset) for i in range(lax.axis_size(a...  36 us
    ppermute x17, starting transfers between devices, exchange(): lax.ppermute(array, axis, [(i, i ^ offset) for i in range(lax.axis_size(a...  23.2 us
    pallas_call x2, Pallas kernels, couple(): pl.pallas_call(functools.partial(couple_kernel, c, bins_axis, local_bins,...  4.13 us
    pallas_call x2, Pallas kernels, place(): pl.pallas_call(functools.partial(place_kernel, slots, tuple(sorted(source...  3.26 us
    ppermute x1, starting transfers between devices, chunked(): low = lax.ppermute(edges[1], 'pts', up)  2.38 us
    pallas_call x1, Pallas kernels, chunked(): pl.pallas_call(functools.partial(inner_kernel, bins_axis, owners_count, h...  2.11 us
    unnamed x9, local copies, waits for them, and re-layouts  1.63 us
    pallas_call x1, Pallas kernels, chunked(): pl.pallas_call(functools.partial(pack_kernel, rows, bins_axis, half), out...  1.57 us
  transfers between devices with their start and end apart: 19, of which 9 were waited for; matrix products, arithmetic and copies ran while one was open for 2% of the time, Pallas kernels for 12%

profile of v4, /device:TPU:0, one launch (start us, length us, event | category | flops | bytes accessed | tf_op | source)
XLA Modules:
  0.0 78.5 jit_solution(3195330593962427015)
XLA Ops:
  0.0 1.6 %copy.10 = bf16[324,4,512]{2,0,1:T(8,128)(2,1)S(1)} copy(bf16[324,4,512]{2,1,0:T(4,128)(2,1)} %param.6) | data formatting | bytes 2654208 | tf_op args[0]
  1.7 2.4 %collective-permute-start = (bf16[324,512]{1,0:T(8,128)(2,1)S(1)}, bf16[324,512]{1,0:T(8,128)(2,1)S(1)}, u32[]{:S(2)}, u32[]{:S(2)}) collective-permute-start(bf16[324,512]{1,0:T(8,128)(2,1)S(1)} %get-tuple-element.46), channel_id=1, source_target_pairs={{0,4},{4,8},{8,12},{12,16},{16,20},{20,24},{24,28},{1,5},{5,9},{9,... | collective-permute-start | bytes 995336 | tf_op jit(solution)/shard_map/ppermute | solution.py:328
  4.1 1.3 %collective-permute-start.1 = (bf16[324,512]{1,0:T(8,128)(2,1)S(1)}, bf16[324,512]{1,0:T(8,128)(2,1)S(1)}, u32[]{:S(2)}, u32[]{:S(2)}) collective-permute-start(bf16[324,512]{1,0:T(8,128)(2,1)S(1)} %get-tuple-element.45), channel_id=1, source_target_pairs={{4,0},{8,4},{12,8},{16,12},{20,16},{24,20},{28,24},{5,1},{9,5},{13... | collective-permute-start | bytes 995336 | tf_op jit(solution)/shard_map/ppermute | solution.py:329
  5.4 2.5 %collective-permute-start.2 = (s32[1,512]{1,0:T(1,128)S(1)}, s32[1,512]{1,0:T(1,128)S(1)}, u32[]{:S(2)}, u32[]{:S(2)}) collective-permute-start(s32[1,512]{1,0:T(1,128)S(1)} %bitcast.19), channel_id=1, source_target_pairs={{0,1},{1,0},{2,3},{3,2},{4,5},{5,4},{6,7},{7,6},{8,9},{9,8},{10,11... | collective-permute-start | bytes 6152 | tf_op jit(solution)/shard_map/ppermute | solution.py:308
  7.9 2.6 %collective-permute-start.3 = (s32[1,512]{1,0:T(1,128)S(1)}, s32[1,512]{1,0:T(1,128)S(1)}, u32[]{:S(2)}, u32[]{:S(2)}) collective-permute-start(s32[1,512]{1,0:T(1,128)S(1)} %bitcast.20), channel_id=1, source_target_pairs={{0,2},{1,3},{2,0},{3,1},{4,6},{5,7},{6,4},{7,5},{8,10},{9,11},{10,... | collective-permute-start | bytes 6152 | tf_op jit(solution)/shard_map/ppermute | solution.py:308
  12.4 3.5 %collective-permute-done.4.refs_7_ = s32[1,512]{1,0:T(1,128)S(1)} collective-permute-done((s32[1,512]{1,0:T(1,128)S(1)}, s32[1,512]{1,0:T(1,128)S(1)}, u32[]{:S(2)}, u32[]{:S(2)}) %collective-permute-start.4) | collective-permute-done | bytes 2080 | tf_op jit(solution)/shard_map/ppermute | solution.py:308
  16.2 2.1 %inner.1 = (bf16[4,336,512]{2,1,0:T(8,128)(2,1)S(1)}, bf16[4,512,256]{2,1,0:T(8,128)(2,1)S(1)}, f32[8,512]{1,0:T(8,128)S(1)}) custom-call(bf16[4,336,512]{2,1,0:T(8,128)(2,1)S(1)} %pad.12.refs_0_, f32[2,336,128]{2,1,0:T(8,128)S(1)} %broadcast_in_dim.4.refs_1_.refs_3_, bf16[2,336,128]{2,1,0:T(8,128)(2,1)S(1)} %broadcast_in_dim.5.refs_2_.refs_4_, ...), custom_call_target="tpu_custom_call" | custom-call | flops 1 | bytes 1 | tf_op jit(solution)/shard_map/inner/pallas_call | solution.py:349
  18.3 1.6 %pack.1 = (bf16[328,256]{1,0:T(8,128)(2,1)S(1)}, bf16[328,256]{1,0:T(8,128)(2,1)S(1)}, bf16[328,256]{1,0:T(8,128)(2,1)S(1)}, bf16[328,256]{1,0:T(8,128)(2,1)S(1)...) custom-call(bf16[4,336,512]{2,1,0:T(8,128)(2,1)S(1)} %pad.12.refs_0_, ...), custom_call_target="tpu_custom_call" | custom-call | flops 1 | bytes 1 | tf_op jit(solution)/shard_map/pack/pallas_call | solution.py:363
  20.6 3.8 %collective-permute-start.7 = (bf16[328,256]{1,0:T(8,128)(2,1)S(1)}, bf16[328,256]{1,0:T(8,128)(2,1)S(1)}, u32[]{:S(2)}, u32[]{:S(2)}) collective-permute-start(bf16[328,256]{1,0:T(8,128)(2,1)S(1)} %get-tuple-element.29), channel_id=1, source_target_pairs={{0,3},{1,2},{2,1},{3,0},{4,7},{5,6},{6,5},{7,4},{8,11},{9,10},{10,... | collective-permute-start | bytes 503816 | tf_op jit(solution)/shard_map/ppermute | solution.py:308
  24.4 1.3 %transpose.20.refs_1_.refs_4_ = bf16[1296,1296]{1,0:T(8,128)(2,1)S(1)} custom-call(bf16[1296,1296]{1,0:T(8,128)(2,1)S(1)} %copy-done.1), custom_call_target="tpu_custom_call" | custom-call | flops 1 | bytes 1 | tf_op jit(solution)/shard_map/transpose/pallas_call | solution.py:339
  25.7 2.7 %collective-permute-done.5.refs_0_.refs_1_ = bf16[328,256]{1,0:T(8,128)(2,1)S(1)} collective-permute-done((bf16[328,256]{1,0:T(8,128)(2,1)S(1)}, bf16[328,256]{1,0:T(8,128)(2,1)S(1)}, u32[]{:S(2)}, u32[]{:S(2)}) %collective-permute-start.5) | collective-permute-done | bytes 167968 | tf_op jit(solution)/shard_map/ppermute | solution.py:308
  28.4 7.0 %collective-permute-done.6.refs_1_.refs_2_ = bf16[328,256]{1,0:T(8,128)(2,1)S(1)} collective-permute-done((bf16[328,256]{1,0:T(8,128)(2,1)S(1)}, bf16[328,256]{1,0:T(8,128)(2,1)S(1)}, u32[]{:S(2)}, u32[]{:S(2)}) %collective-permute-start.6) | collective-permute-done | bytes 167968 | tf_op jit(solution)/shard_map/ppermute | solution.py:308
  35.4 3.8 %collective-permute-start.12 = (bf16[328,256]{1,0:T(8,128)(2,1)S(1)}, bf16[328,256]{1,0:T(8,128)(2,1)S(1)}, u32[]{:S(2)}, u32[]{:S(2)}) collective-permute-start(bf16[328,256]{1,0:T(8,128)(2,1)S(1)} %gate.4.refs_7_), channel_id=1, source_target_pairs={{0,2},{1,3},{2,0},{3,1},{4,6},{5,7},{6,4},{7,5},{8,10},{9,11},{10,... | collective-permute-start | bytes 503816 | tf_op jit(solution)/shard_map/ppermute | solution.py:308
  39.3 2.5 %collective-permute-start.13 = (bf16[328,256]{1,0:T(8,128)(2,1)S(1)}, bf16[328,256]{1,0:T(8,128)(2,1)S(1)}, u32[]{:S(2)}, u32[]{:S(2)}) collective-permute-start(bf16[328,256]{1,0:T(8,128)(2,1)S(1)} %gate.5.refs_8_), channel_id=1, source_target_pairs={{0,3},{1,2},{2,1},{3,0},{4,7},{5,6},{6,5},{7,4},{8,11},{9,10},{10,... | collective-permute-start | bytes 503816 | tf_op jit(solution)/shard_map/ppermute | solution.py:308
  41.8 2.1 %couple.2 = (bf16[2,656,128]{2,1,0:T(8,128)(2,1)S(1)}, bf16[2,656,128]{2,1,0:T(8,128)(2,1)S(1)}, bf16[2,656,128]{2,1,0:T(8,128)(2,1)S(1)}, bf16[2,656,128]{2,1,0:T(8,128)(2,1)S(1)}) custom-call(bf16[328,256]{1,0:T(8,128)(2,1)S(1)} %get-tuple-element.26.refs_0_, bf16[328,256]{1,0:T(8,128)(2,1)S(1)} %collective-permute-done.5.refs_0_.refs_1_, ...), custom_call_target="tpu_custom_call" | custom-call | flops 1 | bytes 1 | tf_op jit(solution)/shard_map/couple/pallas_call | solution.py:377
  43.9 1.7 %collective-permute-start.8 = (bf16[2,656,128]{2,1,0:T(8,128)(2,1)S(1)}, bf16[2,656,128]{2,1,0:T(8,128)(2,1)S(1)}, u32[]{:S(2)}, u32[]{:S(2)}) collective-permute-start(bf16[2,656,128]{2,1,0:T(8,128)(2,1)S(1)} %get-tuple-element.35), channel_id=1, source_target_pairs={{0,8},{4,12},{8,0},{12,4},{16,24},{20,28},{24,16},{28,20},{1,9},{5... | collective-permute-start | bytes 1007624 | tf_op jit(solution)/shard_map/ppermute | solution.py:308
  47.4 4.2 %collective-permute-done.12.refs_2_ = bf16[328,256]{1,0:T(8,128)(2,1)S(1)} collective-permute-done((bf16[328,256]{1,0:T(8,128)(2,1)S(1)}, bf16[328,256]{1,0:T(8,128)(2,1)S(1)}, u32[]{:S(2)}, u32[]{:S(2)}) %collective-permute-start.12) | collective-permute-done | bytes 167968 | tf_op jit(solution)/shard_map/ppermute | solution.py:308
  51.6 2.1 %couple.3 = (bf16[2,656,128]{2,1,0:T(8,128)(2,1)S(1)}, bf16[2,656,128]{2,1,0:T(8,128)(2,1)S(1)}, bf16[2,656,128]{2,1,0:T(8,128)(2,1)S(1)}, bf16[2,656,128]{2,1,0:T(8,128)(2,1)S(1)}) custom-call(bf16[328,256]{1,0:T(8,128)(2,1)S(1)} %get-tuple-element.38.refs_0_, bf16[328,256]{1,0:T(8,128)(2,1)S(1)} %collective-permute-done.11.refs_1_, ...), custom_call_target="tpu_custom_call" | custom-call | flops 30000001024 | bytes 1 | tf_op jit(solution)/shard_map/couple/pallas_call | solution.py:377
  54.5 1.6 %collective-permute-start.16 = (bf16[2,656,128]{2,1,0:T(8,128)(2,1)S(1)}, bf16[2,656,128]{2,1,0:T(8,128)(2,1)S(1)}, u32[]{:S(2)}, u32[]{:S(2)}) collective-permute-start(bf16[2,656,128]{2,1,0:T(8,128)(2,1)S(1)} %get-tuple-element.41), channel_id=1, source_target_pairs={{0,8},{4,12},{8,0},{12,4},{16,24},{20,28},{24,16},{28,20},{1,9},{5... | collective-permute-start | bytes 1007624 | tf_op jit(solution)/shard_map/ppermute | solution.py:308
  57.2 9.9 %collective-permute-done.9.refs_2_.refs_4_ = bf16[2,656,128]{2,1,0:T(8,128)(2,1)S(1)} collective-permute-done((bf16[2,656,128]{2,1,0:T(8,128)(2,1)S(1)}, bf16[2,656,128]{2,1,0:T(8,128)(2,1)S(1)}, u32[]{:S(2)}, u32[]{:S(2)}) %collective-permute-start.9) | collective-permute-done | bytes 335904 | tf_op jit(solution)/shard_map/ppermute | solution.py:308
  67.2 2.5 %collective-permute-done.14.refs_4_.refs_3_.refs_7_ = bf16[2,656,128]{2,1,0:T(8,128)(2,1)S(1)} collective-permute-done((bf16[2,656,128]{2,1,0:T(8,128)(2,1)S(1)}, bf16[2,656,128]{2,1,0:T(8,128)(2,1)S(1)}, u32[]{:S(2)}, u32[]{:S(2)}) %collective-permute-start.14) | collective-permute-done | bytes 335904 | tf_op jit(solution)/shard_map/ppermute | solution.py:308
  69.8 4.8 %collective-permute-done.16.refs_1_.refs_3_ = bf16[2,656,128]{2,1,0:T(8,128)(2,1)S(1)} collective-permute-done((bf16[2,656,128]{2,1,0:T(8,128)(2,1)S(1)}, bf16[2,656,128]{2,1,0:T(8,128)(2,1)S(1)}, u32[]{:S(2)}, u32[]{:S(2)}) %collective-permute-start.16) | collective-permute-done | bytes 335904 | tf_op jit(solution)/shard_map/ppermute | solution.py:308
  74.8 1.6 %place.2.refs_2_ = bf16[1296,1024]{1,0:T(8,128)(2,1)} custom-call(bf16[2,656,128]{2,1,0:T(8,128)(2,1)S(1)} %get-tuple-element.34.refs_0_, bf16[2,656,128]{2,1,0:T(8,128)(2,1)S(1)} %get-tuple-element.40.refs_0_.refs_4_.refs_1_, bf16[2,656,128]{2,1,0:T(8,128)(2,1)S(1)} %collective-permute-done.8.refs_1_.refs_2_, ...), custom_call_target="tpu_custom_call" | custom-call | flops 1 | bytes 1 | tf_op jit(solution)/shard_map/place/pallas_call | solution.py:245
  76.9 1.6 %place.3 = bf16[1296,1024]{1,0:T(8,128)(2,1)} custom-call(bf16[4,656,128]{2,1,0:T(8,128)(2,1)S(1)} %collective-permute-done.15.refs_0_, bf16[4,656,128]{2,1,0:T(8,128)(2,1)S(1)} %collective-permute-done.18.refs_1_, bf16[1296,1024]{1,0:T(8,128)(2,1)} %place.2.refs_2_), custom_call_target="tpu_custom_call", output_to_operand_aliasing={{}: (2, {})} | custom-call | flops 1 | bytes 1 | tf_op jit(solution)/shard_map/place/pallas_call | solution.py:245
  (45 shorter events, 7.5 us)
Async XLA Ops:
  0.0 10.5 %copy-start = (f32[1296,2]{0,1:T(2,128)S(1)}, f32[1296,2]{0,1:T(2,128)}, u32[]{:S(2)}) copy-start(f32[1296,2]{0,1:T(2,128)} %param.7) | copy-start | bytes 31108
  0.0 1.6 %copy-start.2 = (s32[4,512]{1,0:T(4,128)S(1)}, s32[4,512]{1,0:T(4,128)}, u32[]{:S(2)}) copy-start(s32[4,512]{1,0:T(4,128)} %refs_5_.1) | copy-start | bytes 24580
  0.0 5.4 %copy-start.3 = (s32[1,1,512,1]{2,3,1,0:T(1,128)S(1)}, s32[1,1,512,1]{2,3,1,0:T(1,128)}, u32[]{:S(2)}) copy-start(s32[1,1,512,1]{2,3,1,0:T(1,128)} %param.11) | copy-start | bytes 6148
  1.7 16.6 %collective-permute-start = (bf16[324,512]{1,0:T(8,128)(2,1)S(1)}, bf16[324,512]{1,0:T(8,128)(2,1)S(1)}, u32[]{:S(2)}, u32[]{:S(2)}) collective-permute-start(bf16[324,512]{1,0:T(8,128)(2,1)S(1)} %get-tuple-element.46), channel_id=1, source_target_pairs={{0,4},{4,8},{8,12},{12,16},{16,20},{20,24},{24,28},{1,5},{5,9},{9,... | collective-permute-start | bytes 995336 | tf_op jit(solution)/shard_map/ppermute | solution.py:328
  4.1 14.2 %collective-permute-start.1 = (bf16[324,512]{1,0:T(8,128)(2,1)S(1)}, bf16[324,512]{1,0:T(8,128)(2,1)S(1)}, u32[]{:S(2)}, u32[]{:S(2)}) collective-permute-start(bf16[324,512]{1,0:T(8,128)(2,1)S(1)} %get-tuple-element.45), channel_id=1, source_target_pairs={{4,0},{8,4},{12,8},{16,12},{20,16},{24,20},{28,24},{5,1},{9,5},{13... | collective-permute-start | bytes 995336 | tf_op jit(solution)/shard_map/ppermute | solution.py:329
  5.4 6.0 %collective-permute-start.2 = (s32[1,512]{1,0:T(1,128)S(1)}, s32[1,512]{1,0:T(1,128)S(1)}, u32[]{:S(2)}, u32[]{:S(2)}) collective-permute-start(s32[1,512]{1,0:T(1,128)S(1)} %bitcast.19), channel_id=1, source_target_pairs={{0,1},{1,0},{2,3},{3,2},{4,5},{5,4},{6,7},{7,6},{8,9},{9,8},{10,11... | collective-permute-start | bytes 6152 | tf_op jit(solution)/shard_map/ppermute | solution.py:308
  7.9 4.5 %collective-permute-start.3 = (s32[1,512]{1,0:T(1,128)S(1)}, s32[1,512]{1,0:T(1,128)S(1)}, u32[]{:S(2)}, u32[]{:S(2)}) collective-permute-start(s32[1,512]{1,0:T(1,128)S(1)} %bitcast.20), channel_id=1, source_target_pairs={{0,2},{1,3},{2,0},{3,1},{4,6},{5,7},{6,4},{7,5},{8,10},{9,11},{10,... | collective-permute-start | bytes 6152 | tf_op jit(solution)/shard_map/ppermute | solution.py:308
  10.5 5.4 %collective-permute-start.4 = (s32[1,512]{1,0:T(1,128)S(1)}, s32[1,512]{1,0:T(1,128)S(1)}, u32[]{:S(2)}, u32[]{:S(2)}) collective-permute-start(s32[1,512]{1,0:T(1,128)S(1)} %bitcast.21), channel_id=1, source_target_pairs={{0,3},{1,2},{2,1},{3,0},{4,7},{5,6},{6,5},{7,4},{8,11},{9,10},{10,... | collective-permute-start | bytes 6152 | tf_op jit(solution)/shard_map/ppermute | solution.py:308
  18.3 6.1 %copy-start.1 = (bf16[1296,1296]{1,0:T(8,128)(2,1)S(1)}, bf16[1296,1296]{1,0:T(8,128)(2,1)}, u32[]{:S(2)}) copy-start(bf16[1296,1296]{1,0:T(8,128)(2,1)} %coupling.1) | copy-start | bytes 10077700
  19.9 8.4 %collective-permute-start.5 = (bf16[328,256]{1,0:T(8,128)(2,1)S(1)}, bf16[328,256]{1,0:T(8,128)(2,1)S(1)}, u32[]{:S(2)}, u32[]{:S(2)}) collective-permute-start(bf16[328,256]{1,0:T(8,128)(2,1)S(1)} %get-tuple-element.27), channel_id=1, source_target_pairs={{0,1},{1,0},{2,3},{3,2},{4,5},{5,4},{6,7},{7,6},{8,9},{9,8},{10,11... | collective-permute-start | bytes 503816 | tf_op jit(solution)/shard_map/ppermute | solution.py:308
  20.0 15.4 %collective-permute-start.6 = (bf16[328,256]{1,0:T(8,128)(2,1)S(1)}, bf16[328,256]{1,0:T(8,128)(2,1)S(1)}, u32[]{:S(2)}, u32[]{:S(2)}) collective-permute-start(bf16[328,256]{1,0:T(8,128)(2,1)S(1)} %get-tuple-element.28), channel_id=1, source_target_pairs={{0,2},{1,3},{2,0},{3,1},{4,6},{5,7},{6,4},{7,5},{8,10},{9,11},{10,... | collective-permute-start | bytes 503816 | tf_op jit(solution)/shard_map/ppermute | solution.py:308
  20.6 14.9 %collective-permute-start.7 = (bf16[328,256]{1,0:T(8,128)(2,1)S(1)}, bf16[328,256]{1,0:T(8,128)(2,1)S(1)}, u32[]{:S(2)}, u32[]{:S(2)}) collective-permute-start(bf16[328,256]{1,0:T(8,128)(2,1)S(1)} %get-tuple-element.29), channel_id=1, source_target_pairs={{0,3},{1,2},{2,1},{3,0},{4,7},{5,6},{6,5},{7,4},{8,11},{9,10},{10,... | collective-permute-start | bytes 503816 | tf_op jit(solution)/shard_map/ppermute | solution.py:308
  28.4 17.8 %collective-permute-start.11 = (bf16[328,256]{1,0:T(8,128)(2,1)S(1)}, bf16[328,256]{1,0:T(8,128)(2,1)S(1)}, u32[]{:S(2)}, u32[]{:S(2)}) collective-permute-start(bf16[328,256]{1,0:T(8,128)(2,1)S(1)} %gate.3.refs_6_), channel_id=1, source_target_pairs={{0,1},{1,0},{2,3},{3,2},{4,5},{5,4},{6,7},{7,6},{8,9},{9,8},{10,11... | collective-permute-start | bytes 503816 | tf_op jit(solution)/shard_map/ppermute | solution.py:308
  35.4 16.2 %collective-permute-start.12 = (bf16[328,256]{1,0:T(8,128)(2,1)S(1)}, bf16[328,256]{1,0:T(8,128)(2,1)S(1)}, u32[]{:S(2)}, u32[]{:S(2)}) collective-permute-start(bf16[328,256]{1,0:T(8,128)(2,1)S(1)} %gate.4.refs_7_), channel_id=1, source_target_pairs={{0,2},{1,3},{2,0},{3,1},{4,6},{5,7},{6,4},{7,5},{8,10},{9,11},{10,... | collective-permute-start | bytes 503816 | tf_op jit(solution)/shard_map/ppermute | solution.py:308
  39.3 12.3 %collective-permute-start.13 = (bf16[328,256]{1,0:T(8,128)(2,1)S(1)}, bf16[328,256]{1,0:T(8,128)(2,1)S(1)}, u32[]{:S(2)}, u32[]{:S(2)}) collective-permute-start(bf16[328,256]{1,0:T(8,128)(2,1)S(1)} %gate.5.refs_8_), channel_id=1, source_target_pairs={{0,3},{1,2},{2,1},{3,0},{4,7},{5,6},{6,5},{7,4},{8,11},{9,10},{10,... | collective-permute-start | bytes 503816 | tf_op jit(solution)/shard_map/ppermute | solution.py:308
  43.9 12.2 %collective-permute-start.8 = (bf16[2,656,128]{2,1,0:T(8,128)(2,1)S(1)}, bf16[2,656,128]{2,1,0:T(8,128)(2,1)S(1)}, u32[]{:S(2)}, u32[]{:S(2)}) collective-permute-start(bf16[2,656,128]{2,1,0:T(8,128)(2,1)S(1)} %get-tuple-element.35), channel_id=1, source_target_pairs={{0,8},{4,12},{8,0},{12,4},{16,24},{20,28},{24,16},{28,20},{1,9},{5... | collective-permute-start | bytes 1007624 | tf_op jit(solution)/shard_map/ppermute | solution.py:308
  45.6 21.6 %collective-permute-start.9 = (bf16[2,656,128]{2,1,0:T(8,128)(2,1)S(1)}, bf16[2,656,128]{2,1,0:T(8,128)(2,1)S(1)}, u32[]{:S(2)}, u32[]{:S(2)}) collective-permute-start(bf16[2,656,128]{2,1,0:T(8,128)(2,1)S(1)} %get-tuple-element.36), channel_id=1, source_target_pairs={{0,16},{4,20},{8,24},{12,28},{16,0},{20,4},{24,8},{28,12},{1,17},{... | collective-permute-start | bytes 1007624 | tf_op jit(solution)/shard_map/ppermute | solution.py:308
  46.2 21.0 %collective-permute-start.10 = (bf16[2,656,128]{2,1,0:T(8,128)(2,1)S(1)}, bf16[2,656,128]{2,1,0:T(8,128)(2,1)S(1)}, u32[]{:S(2)}, u32[]{:S(2)}) collective-permute-start(bf16[2,656,128]{2,1,0:T(8,128)(2,1)S(1)} %get-tuple-element.37), channel_id=1, source_target_pairs={{0,24},{4,28},{8,16},{12,20},{16,8},{20,12},{24,0},{28,4},{1,25},{... | collective-permute-start | bytes 1007624 | tf_op jit(solution)/shard_map/ppermute | solution.py:308
  53.7 16.0 %collective-permute-start.14 = (bf16[2,656,128]{2,1,0:T(8,128)(2,1)S(1)}, bf16[2,656,128]{2,1,0:T(8,128)(2,1)S(1)}, u32[]{:S(2)}, u32[]{:S(2)}) collective-permute-start(bf16[2,656,128]{2,1,0:T(8,128)(2,1)S(1)} %get-tuple-element.39), channel_id=1, source_target_pairs={{0,24},{4,28},{8,16},{12,20},{16,8},{20,12},{24,0},{28,4},{1,25},{... | collective-permute-start | bytes 1007624 | tf_op jit(solution)/shard_map/ppermute | solution.py:308
  54.5 20.1 %collective-permute-start.16 = (bf16[2,656,128]{2,1,0:T(8,128)(2,1)S(1)}, bf16[2,656,128]{2,1,0:T(8,128)(2,1)S(1)}, u32[]{:S(2)}, u32[]{:S(2)}) collective-permute-start(bf16[2,656,128]{2,1,0:T(8,128)(2,1)S(1)} %get-tuple-element.41), channel_id=1, source_target_pairs={{0,8},{4,12},{8,0},{12,4},{16,24},{20,28},{24,16},{28,20},{1,9},{5... | collective-permute-start | bytes 1007624 | tf_op jit(solution)/shard_map/ppermute | solution.py:308
  56.1 18.5 %collective-permute-start.17 = (bf16[2,656,128]{2,1,0:T(8,128)(2,1)S(1)}, bf16[2,656,128]{2,1,0:T(8,128)(2,1)S(1)}, u32[]{:S(2)}, u32[]{:S(2)}) collective-permute-start(bf16[2,656,128]{2,1,0:T(8,128)(2,1)S(1)} %get-tuple-element.42), channel_id=1, source_target_pairs={{0,16},{4,20},{8,24},{12,28},{16,0},{20,4},{24,8},{28,12},{1,17},{... | collective-permute-start | bytes 1007624 | tf_op jit(solution)/shard_map/ppermute | solution.py:308
  69.8 6.6 %collective-permute-start.15 = (bf16[4,656,128]{2,1,0:T(8,128)(2,1)S(1)}, bf16[4,656,128]{2,1,0:T(8,128)(2,1)S(1)}, u32[]{:S(2)}, u32[]{:S(2)}) collective-permute-start(bf16[4,656,128]{2,1,0:T(8,128)(2,1)S(1)} %stack.2), channel_id=1, source_target_pairs={{0,4},{4,0},{8,12},{12,8},{16,20},{20,16},{24,28},{28,24},{1,5},{5... | collective-permute-start | bytes 2015240 | tf_op jit(solution)/shard_map/ppermute | solution.py:308
  74.7 2.2 %collective-permute-start.18 = (bf16[4,656,128]{2,1,0:T(8,128)(2,1)S(1)}, bf16[4,656,128]{2,1,0:T(8,128)(2,1)S(1)}, u32[]{:S(2)}, u32[]{:S(2)}) collective-permute-start(bf16[4,656,128]{2,1,0:T(8,128)(2,1)S(1)} %stack.3), channel_id=1, source_target_pairs={{0,4},{4,0},{8,12},{12,8},{16,20},{20,16},{24,28},{28,24},{1,5},{5... | collective-permute-start | bytes 2015240 | tf_op jit(solution)/shard_map/ppermute | solution.py:308

commit v5 on v4

--- a/solution.py
+++ b/solution.py
@@ -42,33 +42,56 @@
     return (value * sea_row).astype(BF16)
 
 
-def columns(moved, block):
-    at = pl.ds(pl.multiple_of(block * LANES, LANES), LANES)
-    return jnp.concatenate([moved[l, :, at] for l in range(moved.shape[0])], axis=1)
-
-
-def inner_kernel(bins_axis, owners_count, half, *refs):
-    planes, speed, side, sea = refs[:4]
-    owner = refs[4 : 4 + bins_axis]
-    inner, rim_order, meta, moved = refs[4 + bins_axis :]
+def inner_kernel(planes, near, speed, side, sea, moved):
     lon_rows, rows, _ = planes.shape
+    top = lon_rows - 1
+    even = lax.axis_index("pts") % 2 == 0
+    sea_f = sea[...].astype(F32)
+    sea_b = sea_f.astype(BF16)
+
+    def tile(at, close):
+        masked = [planes[l, at, :] * sea_b[l : l + 1, :] for l in range(lon_rows)]
+        for l in range(1, top):
+            moved[l - 1, at, :] = upwind_row(
+                at, speed, side, masked[l - 1], masked[l], masked[l + 1], sea_f[l : l + 1, :]
+            )
+        center = jnp.where(even, masked[top], masked[0])
+        below = jnp.where(even, masked[top - 1], close)
+        above = jnp.where(even, close, masked[1])
+        weight = jnp.where(even, sea_f[top : top + 1, :], sea_f[0:1, :])
+        moved[top - 1, at, :] = upwind_row(at, speed, side, below, center, above, weight)
+
+    over_rows(tile, rows, near)
+
+
+def over_rows(tile, rows, halo):
+    held = halo.shape[0]
+    full = held // 16 * 16
+
+    def step(index, carry):
+        at = pl.ds(pl.multiple_of(index * 16, 16), 16)
+        tile(at, halo[at, :])
+        return carry
+
+    lax.fori_loop(0, full // 16, step, 0, unroll=5)
+    if full < rows:
+        spare = jnp.zeros((rows - held, halo.shape[1]), F32)
+        end = jnp.concatenate([halo[full:, :].astype(F32), spare], axis=0).astype(BF16)
+        tile(pl.ds(full, 16), end)
+
+
+def order_kernel(bins_axis, owners_count, half, *refs):
+    inner, sea = refs[:2]
+    owner = refs[2 : 2 + bins_axis]
+    part, far_order, meta, order = refs[2 + bins_axis :]
+    lon_rows = inner.shape[0] + 1
     points = lon_rows * LANES
     me = lax.axis_index("bins")
     me_pts = lax.axis_index("pts")
-    sea_f = sea[...].astype(F32)
-    sea_b = sea_f.astype(BF16)
-
-    def step(index, carry):
-        at = pl.ds(pl.multiple_of(index * 16, 16), 16)
-        masked = [planes[l, at, :] * sea_b[l : l + 1, :] for l in range(lon_rows)]
-        for l in range(1, lon_rows - 1):
-            moved[l - 1, at, :] = upwind_row(
-                at, speed, side, masked[l - 1], masked[l], masked[l + 1], sea_f[l : l + 1, :]
-            )
-        return carry
-
-    lax.fori_loop(0, rows // 16, step, 0, unroll=7)
-
+    even = me_pts % 2 == 0
+    last = (lon_rows - 1) * LANES
+    near_at = pl.ds(pl.multiple_of(jnp.where(even, last, 0), LANES), LANES)
+    far_at = pl.ds(pl.multiple_of(jnp.where(even, 0, last), LANES), LANES)
     owners_id = iota((owners_count, points), 0)
     hot = [(owner[m][...] == owners_id).astype(F32) for m in range(bins_axis)]
     earlier = (iota((points, points), 0) < iota((points, points), 1)).astype(F32).astype(BF16)
@@ -76,7 +99,6 @@
         jnp.concatenate(hot, axis=0).astype(BF16), earlier, preferred_element_type=F32
     )
     place_id = iota((points, points), 0)
-    last = (lon_rows - 1) * LANES
     for m in range(bins_axis):
         own = owner[m][...]
         count = jnp.sum(hot[m], axis=1, keepdims=True)
@@ -85,58 +107,46 @@
         rank = jnp.sum(hot[m] * mine, axis=0, keepdims=True)
         key = (offset + rank).astype(I32)
         place = (key & 1) * half + (key >> 1)
-        order = (place_id == place).astype(F32).astype(BF16)
-        inner[m] = dot_nt(columns(moved, me ^ m), order[:, LANES:last]).astype(BF16)
-        rim_order[m, :, :LANES] = order[:, :LANES]
-        rim_order[m, :, LANES:] = order[:, last:]
+        order[...] = (place_id == place).astype(F32).astype(BF16)
+        far_order[m] = order[:, far_at]
+        at = pl.ds(pl.multiple_of((me ^ m) * LANES, LANES), LANES)
+        cells = jnp.concatenate([inner[l, :, at] for l in range(lon_rows - 1)], axis=1)
+        columns = jnp.concatenate([order[:, LANES:last], order[:, near_at]], axis=1)
+        part[m] = dot_nt(cells, columns).astype(BF16)
         if m == 0:
             first = offset.astype(I32)
             slot = (key - first - (((key & 1) - first) & 1)) >> 1
-            at = pl.ds(pl.multiple_of(me * LANES, LANES), LANES)
             weight = jnp.concatenate([sea[l : l + 1, at].astype(F32) for l in range(lon_rows)], axis=1)
             facts = jnp.concatenate(
                 [slot.astype(F32), (own ^ me_pts).astype(F32), rank, weight]
                 + [jnp.zeros((1, points), F32)] * 4,
                 axis=0,
             )
-            meta[...] = dot_nt(facts.astype(BF16), order)
+            meta[...] = dot_nt(facts.astype(BF16), order[...])
 
 
 def pack_kernel(rows_out, bins_axis, half, *refs):
-    planes, low, high, speed, side, sea, inner, rim_order = refs[:8]
-    chunks, moved = refs[8:-1], refs[-1]
+    planes, far, speed, side, sea, part, far_order = refs[:7]
+    chunks, moved = refs[7:-1], refs[-1]
     lon_rows, rows, _ = planes.shape
+    top = lon_rows - 1
     me = lax.axis_index("bins")
+    even = lax.axis_index("pts") % 2 == 0
+    center_row, next_row = jnp.where(even, 0, top), jnp.where(even, 1, top - 1)
     sea_f = sea[...].astype(F32)
-    sea_b = sea_f.astype(BF16)
-
-    top = lon_rows - 1
-
-    def rim(at, below, above):
-        masked = [planes[l, at, :] * sea_b[l : l + 1, :] for l in (0, 1, top - 1, top)]
-        moved[0, at, :] = upwind_row(
-            at, speed, side, below, masked[0], masked[1], sea_f[0:1, :]
-        )
-        moved[1, at, :] = upwind_row(
-            at, speed, side, masked[2], masked[3], above, sea_f[top : top + 1, :]
-        )
-
-    def step(index, carry):
-        at = pl.ds(pl.multiple_of(index * 16, 16), 16)
-        rim(at, low[at, :], high[at, :])
-        return carry
-
-    held = low.shape[0]
-    full = held // 16 * 16
-    lax.fori_loop(0, full // 16, step, 0, unroll=5)
-    if full < rows:
-        spare = jnp.zeros((rows - held, low.shape[1]), F32)
-        ends = [
-            jnp.concatenate([h[full:, :].astype(F32), spare], axis=0).astype(BF16) for h in (low, high)
-        ]
-        rim(pl.ds(full, 16), *ends)
+    center_sea = jnp.where(even, sea_f[0:1, :], sea_f[top : top + 1, :])
+    next_sea = jnp.where(even, sea_f[1:2, :], sea_f[top - 1 : top, :]).astype(BF16)
+
+    def tile(at, distant):
+        center = planes[center_row, at, :] * center_sea.astype(BF16)
+        beside = planes[next_row, at, :] * next_sea
+        below, above = jnp.where(even, distant, beside), jnp.where(even, beside, distant)
+        moved[at, :] = upwind_row(at, speed, side, below, center, above, center_sea)
+
+    over_rows(tile, rows, far)
     for m in range(bins_axis):
-        ordered = dot_nt(columns(moved, me ^ m), rim_order[m]) + inner[m].astype(F32)
+        at = pl.ds(pl.multiple_of((me ^ m) * LANES, LANES), LANES)
+        ordered = dot_nt(moved[:, at], far_order[m]) + part[m].astype(F32)
         ordered = ordered[:rows_out]
         ordered = jnp.where((me & 1) == 1, pltpu.roll(ordered, 4, 0), ordered).astype(BF16)
         for c in range(CHUNKS):
@@ -174,7 +184,7 @@
     slot_id = iota((owners_count * slots, width), 0)
     straight = (slot_id == towards * slots + slot).astype(F32).astype(BF16)
     crossed = (slot_id == (towards ^ 1) * slots + slot).astype(F32).astype(BF16)
-    step = all_bins // 3
+    step = all_bins // 9
     for start in range(0, all_bins, step):
         at = slice(start, start + step)
         coupled = jnp.dot(weights[at, :], flat, preferred_element_type=F32)
@@ -322,13 +332,19 @@
     first_bin = lax.axis_index("bins") * local_bins
 
     planes = jnp.pad(jnp.transpose(spectrum, (1, 0, 2)), ((0, 0), (0, tall - local_bins), (0, 0)))
-    edges = [planes[r, :local_bins] * sea[r].astype(BF16)[None] for r in (0, lon_rows - 1)]
-    up = [(i, i + 1) for i in range(owners_count - 1)]
-    down = [(i + 1, i) for i in range(owners_count - 1)]
-    low = lax.ppermute(edges[1], "pts", up)
-    high = lax.ppermute(edges[0], "pts", down)
+    even = lax.axis_index("pts") % 2 == 0
+    rows_at = [jnp.where(even, 0, lon_rows - 1), jnp.where(even, lon_rows - 1, 0)]
+    edges = [
+        lax.dynamic_index_in_dim(planes, r, 0, False)[:local_bins]
+        * lax.dynamic_index_in_dim(sea, r, 0, False).astype(BF16)[None]
+        for r in rows_at
+    ]
+    between = [(i, i + 1) for i in range(1, owners_count - 1, 2)]
+    far = lax.ppermute(edges[0], "pts", between + [(b, a) for a, b in between])
+    near = exchange(edges[1], "pts", 1)
     own = owner.reshape(1, points)
-    owners = [own] + [exchange(own, "bins", m) for m in range(1, bins_axis)]
+    owners = [own, *reversed([exchange(own, "bins", m) for m in range(bins_axis - 1, 0, -1)])]
+
     def wide(table, dtype):
         mine = lax.dynamic_slice_in_dim(table.T, first_bin, local_bins, 1).astype(dtype)
         mine = jnp.pad(mine, ((0, 0), (0, tall - local_bins)))
@@ -346,30 +362,39 @@
         name="transpose",
     )(coupling)
 
-    inner, rim_order, meta = pl.pallas_call(
-        functools.partial(inner_kernel, bins_axis, owners_count, half),
+    inner = pl.pallas_call(
+        inner_kernel,
+        out_shape=jax.ShapeDtypeStruct((lon_rows - 1, tall, lats), BF16),
+        in_specs=vmem(5),
+        out_specs=vmem(1)[0],
+        compiler_params=params(16),
+        cost_estimate=cost(1, 1),
+        name="inner",
+    )(planes, near, speed, side, sea)
+    part, far_order, meta = pl.pallas_call(
+        functools.partial(order_kernel, bins_axis, owners_count, half),
         out_shape=[
             jax.ShapeDtypeStruct((bins_axis, tall, points), BF16),
-            jax.ShapeDtypeStruct((bins_axis, points, 2 * LANES), BF16),
+            jax.ShapeDtypeStruct((bins_axis, points, LANES), BF16),
             jax.ShapeDtypeStruct((8, points), F32),
         ],
-        in_specs=vmem(4 + bins_axis),
+        in_specs=vmem(2 + bins_axis),
         out_specs=vmem(3),
-        scratch_shapes=[pltpu.VMEM((lon_rows - 2, tall, lats), BF16)],
+        scratch_shapes=[pltpu.VMEM((points, points), BF16)],
         compiler_params=params(16),
         cost_estimate=cost(1, 1),
-        name="inner",
-    )(planes, speed, side, sea, *owners)
+        name="order",
+    )(inner, sea, *owners)
     packed = pl.pallas_call(
         functools.partial(pack_kernel, rows, bins_axis, half),
         out_shape=[jax.ShapeDtypeStruct((rows, half), BF16)] * (CHUNKS * bins_axis),
-        in_specs=vmem(8),
+        in_specs=vmem(7),
         out_specs=vmem(CHUNKS * bins_axis),
-        scratch_shapes=[pltpu.VMEM((2, tall, lats), BF16)],
+        scratch_shapes=[pltpu.VMEM((tall, lats), BF16)],
         compiler_params=params(16),
         cost_estimate=cost(1, 1),
         name="pack",
-    )(planes, low, high, speed, side, sea, inner, rim_order)
+    )(planes, far, speed, side, sea, part, far_order)
 
     def couple(c, blocks, ready, paired):
         shapes = [[(2, half_rows, LANES)] if pair else [(half_rows, LANES)] * 2 for pair in paired]
@@ -487,7 +512,7 @@
         and owners_count & (owners_count - 1) == 0
         and bins_axis % 2 == 0
         and spectrum.shape[0] % 8 == 4
-        and courant.shape[0] % 48 == 0
+        and courant.shape[0] % 144 == 0
         and owners_count == 8
         and spectrum.shape[1] >= 3
     )

time: 78.7 us -> 77 us (0.978)
  waiting for transfers between devices: 36 us -> 32.8 us
  starting transfers between devices: 26.9 us -> 28 us
    ppermute x17 -> x18, starting transfers between devices: 23.2 us -> 27.4 us  [exchange(): lax.ppermute(array, axis, [(i, i ^ offset) for i in range(lax.axis_size(a...]
    ppermute x17 -> x18, waiting for transfers between devices: 36 us -> 32.8 us  [exchange(): lax.ppermute(array, axis, [(i, i ^ offset) for i in range(lax.axis_size(a...]
    ppermute x2 -> x1, starting transfers between devices: 3.67 us -> 0.67 us  [chunked(): far = lax.ppermute(edges[0], 'pts', between + [(b, a) for a, b in between])]
    pallas_call x1 -> x2, Pallas kernels: 2.11 us -> 3.1 us  [the longest x1 1.87 us: chunked(): pl.pallas_call(functools.partial(order_kernel, bins_axis, owners_count, h...]
  transfers between devices with their start and end apart: 19 -> 19, of which waited for: 9 -> 8; matrix products, arithmetic and copies ran while one was open for 2% -> 2% of each run, Pallas kernels for 12% -> 13%
where the time goes in v5:
time: 77 us; the launch traced here: 76.9 us
  waiting for transfers between devices  32.8 us (43%)
  starting transfers between devices  28 us (36%)
  Pallas kernels  12.7 us (16%)
  local copies, waits for them, and re-layouts  2.11 us (3%)
  other arithmetic  0.93 us (1%)
    ppermute x18, waiting for transfers between devices, exchange(): lax.ppermute(array, axis, [(i, i ^ offset) for i in range(lax.axis_size(a...  32.8 us
    ppermute x18, starting transfers between devices, exchange(): lax.ppermute(array, axis, [(i, i ^ offset) for i in range(lax.axis_size(a...  27.4 us
    pallas_call x2, Pallas kernels, couple(): pl.pallas_call(functools.partial(couple_kernel, c, bins_axis, local_bins,...  3.72 us
    pallas_call x2, Pallas kernels, place(): pl.pallas_call(functools.partial(place_kernel, slots, tuple(sorted(source...  3.26 us
    pallas_call x1, Pallas kernels, chunked(): pl.pallas_call(functools.partial(order_kernel, bins_axis, owners_count, h...  1.87 us
    unnamed x9, local copies, waits for them, and re-layouts  1.62 us
  transfers between devices with their start and end apart: 19, of which 8 were waited for; matrix products, arithmetic and copies ran while one was open for 2% of the time, Pallas kernels for 13%

profile of v5, /device:TPU:0, one launch (start us, length us, event | category | flops | bytes accessed | tf_op | source)
XLA Modules:
  0.0 76.9 jit_solution(6889795375279922866)
XLA Ops:
  0.0 1.6 %copy.10 = bf16[324,4,512]{2,0,1:T(8,128)(2,1)S(1)} copy(bf16[324,4,512]{2,1,0:T(4,128)(2,1)} %param.6) | data formatting | bytes 2654208 | tf_op args[0]
  3.0 2.7 %collective-permute-start.2 = (s32[1,512]{1,0:T(1,128)S(1)}, s32[1,512]{1,0:T(1,128)S(1)}, u32[]{:S(2)}, u32[]{:S(2)}) collective-permute-start(s32[1,512]{1,0:T(1,128)S(1)} %bitcast.19), channel_id=1, source_target_pairs={{0,1},{1,0},{2,3},{3,2},{4,5},{5,4},{6,7},{7,6},{8,9},{9,8},{10,11... | collective-permute-start | bytes 6152 | tf_op jit(solution)/shard_map/ppermute | solution.py:318
  5.7 2.6 %collective-permute-start.3 = (s32[1,512]{1,0:T(1,128)S(1)}, s32[1,512]{1,0:T(1,128)S(1)}, u32[]{:S(2)}, u32[]{:S(2)}) collective-permute-start(s32[1,512]{1,0:T(1,128)S(1)} %bitcast.20), channel_id=1, source_target_pairs={{0,2},{1,3},{2,0},{3,1},{4,6},{5,7},{6,4},{7,5},{8,10},{9,11},{10,... | collective-permute-start | bytes 6152 | tf_op jit(solution)/shard_map/ppermute | solution.py:318
  10.8 2.8 %collective-permute-done.4.refs_5_ = s32[1,512]{1,0:T(1,128)S(1)} collective-permute-done((s32[1,512]{1,0:T(1,128)S(1)}, s32[1,512]{1,0:T(1,128)S(1)}, u32[]{:S(2)}, u32[]{:S(2)}) %collective-permute-start.4) | collective-permute-done | bytes 2080 | tf_op jit(solution)/shard_map/ppermute | solution.py:318
  13.6 1.9 %order.1 = (bf16[4,336,512]{2,1,0:T(8,128)(2,1)S(1)}, bf16[4,512,128]{2,1,0:T(8,128)(2,1)S(1)}, f32[8,512]{1,0:T(8,128)S(1)}) custom-call(bf16[3,336,512]{2,1,0:T(8,128)(2,1)S(1)} %inner.1.refs_0_, s32[4,512]{1,0:T(4,128)S(1)} %copy-done.2, s32[1,512]{1,0:T(1,128)S(1)} %bitcast.22, s32[1,512]{1,0:T(1,128)S(1)} %collective-permute-done.2.refs_3_, ...), custom_call_target="tpu_custom_call" | custom-call | flops 1 | bytes 1 | tf_op jit(solution)/shard_map/order/pallas_call | solution.py:374
  16.9 1.6 %collective-permute-start.6 = (bf16[328,256]{1,0:T(8,128)(2,1)S(1)}, bf16[328,256]{1,0:T(8,128)(2,1)S(1)}, u32[]{:S(2)}, u32[]{:S(2)}) collective-permute-start(bf16[328,256]{1,0:T(8,128)(2,1)S(1)} %get-tuple-element.28), channel_id=1, source_target_pairs={{0,2},{1,3},{2,0},{3,1},{4,6},{5,7},{6,4},{7,5},{8,10},{9,11},{10,... | collective-permute-start | bytes 503816 | tf_op jit(solution)/shard_map/ppermute | solution.py:318
  18.4 2.8 %collective-permute-start.7 = (bf16[328,256]{1,0:T(8,128)(2,1)S(1)}, bf16[328,256]{1,0:T(8,128)(2,1)S(1)}, u32[]{:S(2)}, u32[]{:S(2)}) collective-permute-start(bf16[328,256]{1,0:T(8,128)(2,1)S(1)} %get-tuple-element.29), channel_id=1, source_target_pairs={{0,3},{1,2},{2,1},{3,0},{4,7},{5,6},{6,5},{7,4},{8,11},{9,10},{10,... | collective-permute-start | bytes 503816 | tf_op jit(solution)/shard_map/ppermute | solution.py:318
  22.5 3.3 %collective-permute-done.5.refs_0_.refs_1_ = bf16[328,256]{1,0:T(8,128)(2,1)S(1)} collective-permute-done((bf16[328,256]{1,0:T(8,128)(2,1)S(1)}, bf16[328,256]{1,0:T(8,128)(2,1)S(1)}, u32[]{:S(2)}, u32[]{:S(2)}) %collective-permute-start.5) | collective-permute-done | bytes 167968 | tf_op jit(solution)/shard_map/ppermute | solution.py:318
  25.9 6.1 %collective-permute-done.6.refs_1_.refs_2_ = bf16[328,256]{1,0:T(8,128)(2,1)S(1)} collective-permute-done((bf16[328,256]{1,0:T(8,128)(2,1)S(1)}, bf16[328,256]{1,0:T(8,128)(2,1)S(1)}, u32[]{:S(2)}, u32[]{:S(2)}) %collective-permute-start.6) | collective-permute-done | bytes 167968 | tf_op jit(solution)/shard_map/ppermute | solution.py:318
  32.1 3.1 %collective-permute-start.12 = (bf16[328,256]{1,0:T(8,128)(2,1)S(1)}, bf16[328,256]{1,0:T(8,128)(2,1)S(1)}, u32[]{:S(2)}, u32[]{:S(2)}) collective-permute-start(bf16[328,256]{1,0:T(8,128)(2,1)S(1)} %gate.4.refs_7_), channel_id=1, source_target_pairs={{0,2},{1,3},{2,0},{3,1},{4,6},{5,7},{6,4},{7,5},{8,10},{9,11},{10,... | collective-permute-start | bytes 503816 | tf_op jit(solution)/shard_map/ppermute | solution.py:318
  35.2 3.4 %collective-permute-start.13 = (bf16[328,256]{1,0:T(8,128)(2,1)S(1)}, bf16[328,256]{1,0:T(8,128)(2,1)S(1)}, u32[]{:S(2)}, u32[]{:S(2)}) collective-permute-start(bf16[328,256]{1,0:T(8,128)(2,1)S(1)} %gate.5.refs_8_), channel_id=1, source_target_pairs={{0,3},{1,2},{2,1},{3,0},{4,7},{5,6},{6,5},{7,4},{8,11},{9,10},{10,... | collective-permute-start | bytes 503816 | tf_op jit(solution)/shard_map/ppermute | solution.py:318
  38.7 1.9 %couple.2 = (bf16[2,656,128]{2,1,0:T(8,128)(2,1)S(1)}, bf16[2,656,128]{2,1,0:T(8,128)(2,1)S(1)}, bf16[2,656,128]{2,1,0:T(8,128)(2,1)S(1)}, bf16[2,656,128]{2,1,0:T(8,128)(2,1)S(1)}) custom-call(bf16[328,256]{1,0:T(8,128)(2,1)S(1)} %get-tuple-element.26.refs_0_, bf16[328,256]{1,0:T(8,128)(2,1)S(1)} %collective-permute-done.5.refs_0_.refs_1_, ...), custom_call_target="tpu_custom_call" | custom-call | flops 1 | bytes 1 | tf_op jit(solution)/shard_map/couple/pallas_call | solution.py:402
  40.6 2.7 %collective-permute-start.8 = (bf16[2,656,128]{2,1,0:T(8,128)(2,1)S(1)}, bf16[2,656,128]{2,1,0:T(8,128)(2,1)S(1)}, u32[]{:S(2)}, u32[]{:S(2)}) collective-permute-start(bf16[2,656,128]{2,1,0:T(8,128)(2,1)S(1)} %get-tuple-element.35), channel_id=1, source_target_pairs={{0,8},{4,12},{8,0},{12,4},{16,24},{20,28},{24,16},{28,20},{1,9},{5... | collective-permute-start | bytes 1007624 | tf_op jit(solution)/shard_map/ppermute | solution.py:318
  43.3 1.5 %collective-permute-start.10 = (bf16[2,656,128]{2,1,0:T(8,128)(2,1)S(1)}, bf16[2,656,128]{2,1,0:T(8,128)(2,1)S(1)}, u32[]{:S(2)}, u32[]{:S(2)}) collective-permute-start(bf16[2,656,128]{2,1,0:T(8,128)(2,1)S(1)} %get-tuple-element.37), channel_id=1, source_target_pairs={{0,24},{4,28},{8,16},{12,20},{16,8},{20,12},{24,0},{28,4},{1,25},{... | collective-permute-start | bytes 1007624 | tf_op jit(solution)/shard_map/ppermute | solution.py:318
  44.8 2.5 %collective-permute-done.12.refs_2_ = bf16[328,256]{1,0:T(8,128)(2,1)S(1)} collective-permute-done((bf16[328,256]{1,0:T(8,128)(2,1)S(1)}, bf16[328,256]{1,0:T(8,128)(2,1)S(1)}, u32[]{:S(2)}, u32[]{:S(2)}) %collective-permute-start.12) | collective-permute-done | bytes 167968 | tf_op jit(solution)/shard_map/ppermute | solution.py:318
  47.3 1.9 %couple.3 = (bf16[2,656,128]{2,1,0:T(8,128)(2,1)S(1)}, bf16[2,656,128]{2,1,0:T(8,128)(2,1)S(1)}, bf16[2,656,128]{2,1,0:T(8,128)(2,1)S(1)}, bf16[2,656,128]{2,1,0:T(8,128)(2,1)S(1)}) custom-call(bf16[328,256]{1,0:T(8,128)(2,1)S(1)} %get-tuple-element.38.refs_0_, bf16[328,256]{1,0:T(8,128)(2,1)S(1)} %collective-permute-done.11.refs_1_, ...), custom_call_target="tpu_custom_call" | custom-call | flops 30000001024 | bytes 1 | tf_op jit(solution)/shard_map/couple/pallas_call | solution.py:402
  49.2 1.3 %collective-permute-start.14 = (bf16[2,656,128]{2,1,0:T(8,128)(2,1)S(1)}, bf16[2,656,128]{2,1,0:T(8,128)(2,1)S(1)}, u32[]{:S(2)}, u32[]{:S(2)}) collective-permute-start(bf16[2,656,128]{2,1,0:T(8,128)(2,1)S(1)} %get-tuple-element.39), channel_id=1, source_target_pairs={{0,24},{4,28},{8,16},{12,20},{16,8},{20,12},{24,0},{28,4},{1,25},{... | collective-permute-start | bytes 1007624 | tf_op jit(solution)/shard_map/ppermute | solution.py:318
  50.5 3.4 %collective-permute-start.16 = (bf16[2,656,128]{2,1,0:T(8,128)(2,1)S(1)}, bf16[2,656,128]{2,1,0:T(8,128)(2,1)S(1)}, u32[]{:S(2)}, u32[]{:S(2)}) collective-permute-start(bf16[2,656,128]{2,1,0:T(8,128)(2,1)S(1)} %get-tuple-element.41), channel_id=1, source_target_pairs={{0,8},{4,12},{8,0},{12,4},{16,24},{20,28},{24,16},{28,20},{1,9},{5... | collective-permute-start | bytes 1007624 | tf_op jit(solution)/shard_map/ppermute | solution.py:318
  53.8 1.4 %collective-permute-start.17 = (bf16[2,656,128]{2,1,0:T(8,128)(2,1)S(1)}, bf16[2,656,128]{2,1,0:T(8,128)(2,1)S(1)}, u32[]{:S(2)}, u32[]{:S(2)}) collective-permute-start(bf16[2,656,128]{2,1,0:T(8,128)(2,1)S(1)} %get-tuple-element.42), channel_id=1, source_target_pairs={{0,16},{4,20},{8,24},{12,28},{16,0},{20,4},{24,8},{28,12},{1,17},{... | collective-permute-start | bytes 1007624 | tf_op jit(solution)/shard_map/ppermute | solution.py:318
  55.2 12.2 %collective-permute-done.9.refs_2_.refs_4_ = bf16[2,656,128]{2,1,0:T(8,128)(2,1)S(1)} collective-permute-done((bf16[2,656,128]{2,1,0:T(8,128)(2,1)S(1)}, bf16[2,656,128]{2,1,0:T(8,128)(2,1)S(1)}, u32[]{:S(2)}, u32[]{:S(2)}) %collective-permute-start.9) | collective-permute-done | bytes 335904 | tf_op jit(solution)/shard_map/ppermute | solution.py:318
  67.6 4.0 %collective-permute-done.16.refs_1_.refs_3_ = bf16[2,656,128]{2,1,0:T(8,128)(2,1)S(1)} collective-permute-done((bf16[2,656,128]{2,1,0:T(8,128)(2,1)S(1)}, bf16[2,656,128]{2,1,0:T(8,128)(2,1)S(1)}, u32[]{:S(2)}, u32[]{:S(2)}) %collective-permute-start.16) | collective-permute-done | bytes 335904 | tf_op jit(solution)/shard_map/ppermute | solution.py:318
  71.6 1.4 %collective-permute-done.17.refs_2_.refs_5_ = bf16[2,656,128]{2,1,0:T(8,128)(2,1)S(1)} collective-permute-done((bf16[2,656,128]{2,1,0:T(8,128)(2,1)S(1)}, bf16[2,656,128]{2,1,0:T(8,128)(2,1)S(1)}, u32[]{:S(2)}, u32[]{:S(2)}) %collective-permute-start.17) | collective-permute-done | bytes 335904 | tf_op jit(solution)/shard_map/ppermute | solution.py:318
  73.1 1.6 %place.2.refs_2_ = bf16[1296,1024]{1,0:T(8,128)(2,1)} custom-call(bf16[2,656,128]{2,1,0:T(8,128)(2,1)S(1)} %get-tuple-element.34.refs_0_, bf16[2,656,128]{2,1,0:T(8,128)(2,1)S(1)} %get-tuple-element.40.refs_0_.refs_4_.refs_1_, bf16[2,656,128]{2,1,0:T(8,128)(2,1)S(1)} %collective-permute-done.8.refs_1_.refs_2_, ...), custom_call_target="tpu_custom_call" | custom-call | flops 1 | bytes 1 | tf_op jit(solution)/shard_map/place/pallas_call | solution.py:255
  75.2 1.6 %place.3 = bf16[1296,1024]{1,0:T(8,128)(2,1)} custom-call(bf16[4,656,128]{2,1,0:T(8,128)(2,1)S(1)} %collective-permute-done.15.refs_0_, bf16[4,656,128]{2,1,0:T(8,128)(2,1)S(1)} %collective-permute-done.18.refs_1_, bf16[1296,1024]{1,0:T(8,128)(2,1)} %place.2.refs_2_), custom_call_target="tpu_custom_call", output_to_operand_aliasing={{}: (2, {})} | custom-call | flops 1 | bytes 1 | tf_op jit(solution)/shard_map/place/pallas_call | solution.py:255
  (45 shorter events, 7.3 us)
Async XLA Ops:
  0.0 8.3 %copy-start = (f32[1296,2]{0,1:T(2,128)S(1)}, f32[1296,2]{0,1:T(2,128)}, u32[]{:S(2)}) copy-start(f32[1296,2]{0,1:T(2,128)} %param.7) | copy-start | bytes 31108
  0.0 1.6 %copy-start.2 = (s32[4,512]{1,0:T(4,128)S(1)}, s32[4,512]{1,0:T(4,128)}, u32[]{:S(2)}) copy-start(s32[4,512]{1,0:T(4,128)} %refs_4_.1) | copy-start | bytes 24580
  1.6 1.4 %copy-start.3 = (s32[1,1,512,1]{2,3,1,0:T(1,128)S(1)}, s32[1,1,512,1]{2,3,1,0:T(1,128)}, u32[]{:S(2)}) copy-start(s32[1,1,512,1]{2,3,1,0:T(1,128)} %param.11) | copy-start | bytes 6148
  1.8 7.4 %collective-permute-start.1 = (bf16[324,512]{1,0:T(8,128)(2,1)S(1)}, bf16[324,512]{1,0:T(8,128)(2,1)S(1)}, u32[]{:S(2)}, u32[]{:S(2)}) collective-permute-start(bf16[324,512]{1,0:T(8,128)(2,1)S(1)} %get-tuple-element.45), channel_id=1, source_target_pairs={{0,4},{4,0},{8,12},{12,8},{16,20},{20,16},{24,28},{28,24},{1,5},{5... | collective-permute-start | bytes 995336 | tf_op jit(solution)/shard_map/ppermute | solution.py:318
  2.3 13.2 %collective-permute-start = (bf16[324,512]{1,0:T(8,128)(2,1)S(1)}, bf16[324,512]{1,0:T(8,128)(2,1)S(1)}, u32[]{:S(2)}, u32[]{:S(2)}) collective-permute-start(bf16[324,512]{1,0:T(8,128)(2,1)S(1)} %get-tuple-element.46), channel_id=1, source_target_pairs={{4,8},{12,16},{20,24},{8,4},{16,12},{24,20},{5,9},{13,17},{21,25},... | collective-permute-start | bytes 995336 | tf_op jit(solution)/shard_map/ppermute | solution.py:343
  3.0 7.8 %collective-permute-start.2 = (s32[1,512]{1,0:T(1,128)S(1)}, s32[1,512]{1,0:T(1,128)S(1)}, u32[]{:S(2)}, u32[]{:S(2)}) collective-permute-start(s32[1,512]{1,0:T(1,128)S(1)} %bitcast.19), channel_id=1, source_target_pairs={{0,1},{1,0},{2,3},{3,2},{4,5},{5,4},{6,7},{7,6},{8,9},{9,8},{10,11... | collective-permute-start | bytes 6152 | tf_op jit(solution)/shard_map/ppermute | solution.py:318
  5.7 5.1 %collective-permute-start.3 = (s32[1,512]{1,0:T(1,128)S(1)}, s32[1,512]{1,0:T(1,128)S(1)}, u32[]{:S(2)}, u32[]{:S(2)}) collective-permute-start(s32[1,512]{1,0:T(1,128)S(1)} %bitcast.20), channel_id=1, source_target_pairs={{0,2},{1,3},{2,0},{3,1},{4,6},{5,7},{6,4},{7,5},{8,10},{9,11},{10,... | collective-permute-start | bytes 6152 | tf_op jit(solution)/shard_map/ppermute | solution.py:318
  8.3 5.4 %collective-permute-start.4 = (s32[1,512]{1,0:T(1,128)S(1)}, s32[1,512]{1,0:T(1,128)S(1)}, u32[]{:S(2)}, u32[]{:S(2)}) collective-permute-start(s32[1,512]{1,0:T(1,128)S(1)} %bitcast.21), channel_id=1, source_target_pairs={{0,3},{1,2},{2,1},{3,0},{4,7},{5,6},{6,5},{7,4},{8,11},{9,10},{10,... | collective-permute-start | bytes 6152 | tf_op jit(solution)/shard_map/ppermute | solution.py:318
  15.5 5.7 %copy-start.1 = (bf16[1296,1296]{1,0:T(8,128)(2,1)S(1)}, bf16[1296,1296]{1,0:T(8,128)(2,1)}, u32[]{:S(2)}) copy-start(bf16[1296,1296]{1,0:T(8,128)(2,1)} %coupling.1) | copy-start | bytes 10077700
  16.8 9.0 %collective-permute-start.5 = (bf16[328,256]{1,0:T(8,128)(2,1)S(1)}, bf16[328,256]{1,0:T(8,128)(2,1)S(1)}, u32[]{:S(2)}, u32[]{:S(2)}) collective-permute-start(bf16[328,256]{1,0:T(8,128)(2,1)S(1)} %get-tuple-element.27), channel_id=1, source_target_pairs={{0,1},{1,0},{2,3},{3,2},{4,5},{5,4},{6,7},{7,6},{8,9},{9,8},{10,11... | collective-permute-start | bytes 503816 | tf_op jit(solution)/shard_map/ppermute | solution.py:318
  16.9 15.2 %collective-permute-start.6 = (bf16[328,256]{1,0:T(8,128)(2,1)S(1)}, bf16[328,256]{1,0:T(8,128)(2,1)S(1)}, u32[]{:S(2)}, u32[]{:S(2)}) collective-permute-start(bf16[328,256]{1,0:T(8,128)(2,1)S(1)} %get-tuple-element.28), channel_id=1, source_target_pairs={{0,2},{1,3},{2,0},{3,1},{4,6},{5,7},{6,4},{7,5},{8,10},{9,11},{10,... | collective-permute-start | bytes 503816 | tf_op jit(solution)/shard_map/ppermute | solution.py:318
  18.4 13.6 %collective-permute-start.7 = (bf16[328,256]{1,0:T(8,128)(2,1)S(1)}, bf16[328,256]{1,0:T(8,128)(2,1)S(1)}, u32[]{:S(2)}, u32[]{:S(2)}) collective-permute-start(bf16[328,256]{1,0:T(8,128)(2,1)S(1)} %get-tuple-element.29), channel_id=1, source_target_pairs={{0,3},{1,2},{2,1},{3,0},{4,7},{5,6},{6,5},{7,4},{8,11},{9,10},{10,... | collective-permute-start | bytes 503816 | tf_op jit(solution)/shard_map/ppermute | solution.py:318
  25.8 17.4 %collective-permute-start.11 = (bf16[328,256]{1,0:T(8,128)(2,1)S(1)}, bf16[328,256]{1,0:T(8,128)(2,1)S(1)}, u32[]{:S(2)}, u32[]{:S(2)}) collective-permute-start(bf16[328,256]{1,0:T(8,128)(2,1)S(1)} %gate.3.refs_6_), channel_id=1, source_target_pairs={{0,1},{1,0},{2,3},{3,2},{4,5},{5,4},{6,7},{7,6},{8,9},{9,8},{10,11... | collective-permute-start | bytes 503816 | tf_op jit(solution)/shard_map/ppermute | solution.py:318
  32.1 15.2 %collective-permute-start.12 = (bf16[328,256]{1,0:T(8,128)(2,1)S(1)}, bf16[328,256]{1,0:T(8,128)(2,1)S(1)}, u32[]{:S(2)}, u32[]{:S(2)}) collective-permute-start(bf16[328,256]{1,0:T(8,128)(2,1)S(1)} %gate.4.refs_7_), channel_id=1, source_target_pairs={{0,2},{1,3},{2,0},{3,1},{4,6},{5,7},{6,4},{7,5},{8,10},{9,11},{10,... | collective-permute-start | bytes 503816 | tf_op jit(solution)/shard_map/ppermute | solution.py:318
  35.2 12.1 %collective-permute-start.13 = (bf16[328,256]{1,0:T(8,128)(2,1)S(1)}, bf16[328,256]{1,0:T(8,128)(2,1)S(1)}, u32[]{:S(2)}, u32[]{:S(2)}) collective-permute-start(bf16[328,256]{1,0:T(8,128)(2,1)S(1)} %gate.5.refs_8_), channel_id=1, source_target_pairs={{0,3},{1,2},{2,1},{3,0},{4,7},{5,6},{6,5},{7,4},{8,11},{9,10},{10,... | collective-permute-start | bytes 503816 | tf_op jit(solution)/shard_map/ppermute | solution.py:318
  40.6 13.3 %collective-permute-start.8 = (bf16[2,656,128]{2,1,0:T(8,128)(2,1)S(1)}, bf16[2,656,128]{2,1,0:T(8,128)(2,1)S(1)}, u32[]{:S(2)}, u32[]{:S(2)}) collective-permute-start(bf16[2,656,128]{2,1,0:T(8,128)(2,1)S(1)} %get-tuple-element.35), channel_id=1, source_target_pairs={{0,8},{4,12},{8,0},{12,4},{16,24},{20,28},{24,16},{28,20},{1,9},{5... | collective-permute-start | bytes 1007624 | tf_op jit(solution)/shard_map/ppermute | solution.py:318
  43.3 24.2 %collective-permute-start.9 = (bf16[2,656,128]{2,1,0:T(8,128)(2,1)S(1)}, bf16[2,656,128]{2,1,0:T(8,128)(2,1)S(1)}, u32[]{:S(2)}, u32[]{:S(2)}) collective-permute-start(bf16[2,656,128]{2,1,0:T(8,128)(2,1)S(1)} %get-tuple-element.36), channel_id=1, source_target_pairs={{0,16},{4,20},{8,24},{12,28},{16,0},{20,4},{24,8},{28,12},{1,17},{... | collective-permute-start | bytes 1007624 | tf_op jit(solution)/shard_map/ppermute | solution.py:318
  43.3 24.2 %collective-permute-start.10 = (bf16[2,656,128]{2,1,0:T(8,128)(2,1)S(1)}, bf16[2,656,128]{2,1,0:T(8,128)(2,1)S(1)}, u32[]{:S(2)}, u32[]{:S(2)}) collective-permute-start(bf16[2,656,128]{2,1,0:T(8,128)(2,1)S(1)} %get-tuple-element.37), channel_id=1, source_target_pairs={{0,24},{4,28},{8,16},{12,20},{16,8},{20,12},{24,0},{28,4},{1,25},{... | collective-permute-start | bytes 1007624 | tf_op jit(solution)/shard_map/ppermute | solution.py:318
  49.2 18.3 %collective-permute-start.14 = (bf16[2,656,128]{2,1,0:T(8,128)(2,1)S(1)}, bf16[2,656,128]{2,1,0:T(8,128)(2,1)S(1)}, u32[]{:S(2)}, u32[]{:S(2)}) collective-permute-start(bf16[2,656,128]{2,1,0:T(8,128)(2,1)S(1)} %get-tuple-element.39), channel_id=1, source_target_pairs={{0,24},{4,28},{8,16},{12,20},{16,8},{20,12},{24,0},{28,4},{1,25},{... | collective-permute-start | bytes 1007624 | tf_op jit(solution)/shard_map/ppermute | solution.py:318
  50.5 21.1 %collective-permute-start.16 = (bf16[2,656,128]{2,1,0:T(8,128)(2,1)S(1)}, bf16[2,656,128]{2,1,0:T(8,128)(2,1)S(1)}, u32[]{:S(2)}, u32[]{:S(2)}) collective-permute-start(bf16[2,656,128]{2,1,0:T(8,128)(2,1)S(1)} %get-tuple-element.41), channel_id=1, source_target_pairs={{0,8},{4,12},{8,0},{12,4},{16,24},{20,28},{24,16},{28,20},{1,9},{5... | collective-permute-start | bytes 1007624 | tf_op jit(solution)/shard_map/ppermute | solution.py:318
  53.8 19.1 %collective-permute-start.17 = (bf16[2,656,128]{2,1,0:T(8,128)(2,1)S(1)}, bf16[2,656,128]{2,1,0:T(8,128)(2,1)S(1)}, u32[]{:S(2)}, u32[]{:S(2)}) collective-permute-start(bf16[2,656,128]{2,1,0:T(8,128)(2,1)S(1)} %get-tuple-element.42), channel_id=1, source_target_pairs={{0,16},{4,20},{8,24},{12,28},{16,0},{20,4},{24,8},{28,12},{1,17},{... | collective-permute-start | bytes 1007624 | tf_op jit(solution)/shard_map/ppermute | solution.py:318
  67.5 7.2 %collective-permute-start.15 = (bf16[4,656,128]{2,1,0:T(8,128)(2,1)S(1)}, bf16[4,656,128]{2,1,0:T(8,128)(2,1)S(1)}, u32[]{:S(2)}, u32[]{:S(2)}) collective-permute-start(bf16[4,656,128]{2,1,0:T(8,128)(2,1)S(1)} %stack.2), channel_id=1, source_target_pairs={{0,4},{4,0},{8,12},{12,8},{16,20},{20,16},{24,28},{28,24},{1,5},{5... | collective-permute-start | bytes 2015240 | tf_op jit(solution)/shard_map/ppermute | solution.py:318
  73.0 2.2 %collective-permute-start.18 = (bf16[4,656,128]{2,1,0:T(8,128)(2,1)S(1)}, bf16[4,656,128]{2,1,0:T(8,128)(2,1)S(1)}, u32[]{:S(2)}, u32[]{:S(2)}) collective-permute-start(bf16[4,656,128]{2,1,0:T(8,128)(2,1)S(1)} %stack.3), channel_id=1, source_target_pairs={{0,4},{4,0},{8,12},{12,8},{16,20},{20,16},{24,28},{28,24},{1,5},{5... | collective-permute-start | bytes 2015240 | tf_op jit(solution)/shard_map/ppermute | solution.py:318

commit v6 on v5

--- a/solution.py
+++ b/solution.py
@@ -11,7 +11,8 @@
 BF16 = jnp.bfloat16
 I32 = jnp.int32
 LANES = 128
-CHUNKS = 2
+CHUNKS = 4
+MAIN = ((0, 1), (2,))
 NT = (((1,), (1,)), ((), ()))
 
 
@@ -80,11 +81,11 @@
         tile(pl.ds(full, 16), end)
 
 
-def order_kernel(bins_axis, owners_count, half, *refs):
+def order_kernel(bins_axis, owners_count, width, slots, *refs):
     inner, sea = refs[:2]
     owner = refs[2 : 2 + bins_axis]
     part, far_order, meta, order = refs[2 + bins_axis :]
-    lon_rows = inner.shape[0] + 1
+    lon_rows, rows = inner.shape[0] + 1, inner.shape[1]
     points = lon_rows * LANES
     me = lax.axis_index("bins")
     me_pts = lax.axis_index("pts")
@@ -98,36 +99,43 @@
     before = jnp.dot(
         jnp.concatenate(hot, axis=0).astype(BF16), earlier, preferred_element_type=F32
     )
-    place_id = iota((points, points), 0)
+    main = (CHUNKS - 1) * width
+    place_id = iota(order.shape, 0)
+    none = [jnp.zeros((1, points), F32)]
     for m in range(bins_axis):
         own = owner[m][...]
         count = jnp.sum(hot[m], axis=1, keepdims=True)
         offset = jnp.sum(jnp.where(owners_id < own, count, 0.0), axis=0, keepdims=True)
         mine = before[m * owners_count : (m + 1) * owners_count, :]
         rank = jnp.sum(hot[m] * mine, axis=0, keepdims=True)
-        key = (offset + rank).astype(I32)
-        place = (key & 1) * half + (key >> 1)
+        key, first = (offset + rank).astype(I32), offset.astype(I32)
+        quarter = key & (CHUNKS - 1)
+        slot = (key - first - ((quarter - first) & (CHUNKS - 1))) // CHUNKS
+        towards = own ^ me_pts
+        block = me ^ m
+        group = (towards & (CHUNKS - 1)) ^ block
+        spread = main + towards // CHUNKS * LANES + group * slots + slot
+        place = jnp.where(quarter < CHUNKS - 1, quarter * width + key // CHUNKS, spread)
         order[...] = (place_id == place).astype(F32).astype(BF16)
         far_order[m] = order[:, far_at]
-        at = pl.ds(pl.multiple_of((me ^ m) * LANES, LANES), LANES)
+        at = pl.ds(pl.multiple_of(block * LANES, LANES), LANES)
         cells = jnp.concatenate([inner[l, :, at] for l in range(lon_rows - 1)], axis=1)
         columns = jnp.concatenate([order[:, LANES:last], order[:, near_at]], axis=1)
         part[m] = dot_nt(cells, columns).astype(BF16)
+        weight = jnp.concatenate([sea[l : l + 1, at].astype(F32) for l in range(lon_rows)], axis=1)
+        facts = jnp.concatenate(none * 4 + [weight, rank] + none * 10, axis=0).astype(BF16)
+        end = slice(rows - 16, rows)
+        spare = part[m, end, main:].astype(F32) + dot_nt(facts, order[main:, :])
+        part[m, end, main:] = spare.astype(BF16)
         if m == 0:
-            first = offset.astype(I32)
-            slot = (key - first - (((key & 1) - first) & 1)) >> 1
-            weight = jnp.concatenate([sea[l : l + 1, at].astype(F32) for l in range(lon_rows)], axis=1)
-            facts = jnp.concatenate(
-                [slot.astype(F32), (own ^ me_pts).astype(F32), rank, weight]
-                + [jnp.zeros((1, points), F32)] * 4,
-                axis=0,
-            )
-            meta[...] = dot_nt(facts.astype(BF16), order[...])
-
-
-def pack_kernel(rows_out, bins_axis, half, *refs):
+            facts = [slot.astype(F32), towards.astype(F32), rank, weight] + none * 4
+            meta[...] = dot_nt(jnp.concatenate(facts, axis=0).astype(BF16), order[:main, :])
+
+
+def pack_kernel(rows_out, bins_axis, width, pairs, *refs):
     planes, far, speed, side, sea, part, far_order = refs[:7]
     chunks, moved = refs[7:-1], refs[-1]
+    direct = chunks[len(MAIN) * bins_axis :]
     lon_rows, rows, _ = planes.shape
     top = lon_rows - 1
     me = lax.axis_index("bins")
@@ -144,13 +152,36 @@
         moved[at, :] = upwind_row(at, speed, side, below, center, above, center_sea)
 
     over_rows(tile, rows, far)
+    spread = []
     for m in range(bins_axis):
         at = pl.ds(pl.multiple_of((me ^ m) * LANES, LANES), LANES)
         ordered = dot_nt(moved[:, at], far_order[m]) + part[m].astype(F32)
         ordered = ordered[:rows_out]
         ordered = jnp.where((me & 1) == 1, pltpu.roll(ordered, 4, 0), ordered).astype(BF16)
-        for c in range(CHUNKS):
-            chunks[c * bins_axis + m][...] = ordered[:, c * half : (c + 1) * half]
+        for c, quarters in enumerate(MAIN):
+            at = slice(quarters[0] * width, (quarters[-1] + 1) * width)
+            chunks[c * bins_axis + m][...] = ordered[:, at]
+        spread.append(ordered[:, (CHUNKS - 1) * width :])
+    group = iota((rows_out, LANES), 1) // (LANES // CHUNKS)
+    for x in range(2 * pairs):
+        at = slice(x // CHUNKS * LANES, (x // CHUNKS + 1) * LANES)
+        mixed = spread[0][:, at]
+        for m in range(1, bins_axis):
+            mixed = jnp.where(group == ((me ^ m) ^ (x % CHUNKS)), spread[m][:, at], mixed)
+        direct[x // 2][x % 2, 0] = mixed
+
+
+def regroup_kernel(bins_axis, pairs, *refs):
+    came, swapped, outs = refs[:pairs], refs[pairs], refs[pairs + 1 :]
+    me = lax.axis_index("bins")
+    sources = [swapped[x // 2, 0] if x % 2 else came[x // 2][0, 0] for x in range(2 * pairs)]
+    group = iota(sources[0].shape, 1) // (LANES // CHUNKS)
+    for m in range(bins_axis):
+        for u in range(2 * pairs // CHUNKS):
+            mixed = sources[u * CHUNKS]
+            for k in range(1, CHUNKS):
+                mixed = jnp.where(group == ((me ^ m) ^ k), sources[u * CHUNKS + k], mixed)
+            outs[m][:, u * LANES : (u + 1) * LANES] = mixed
 
 
 def transpose_kernel(coupling, out):
@@ -161,76 +192,90 @@
         out[start : start + size, :] = dot_nt(eye, coupling[:, start : start + size]).astype(BF16)
 
 
-def couple_kernel(chunk, bins_axis, local_bins, slots, paired, *refs):
+def lane_groups(blocks, shift):
+    group = iota(blocks[0].shape, 1) // (LANES // CHUNKS)
+    mixed = blocks[shift]
+    for q in range(1, CHUNKS):
+        mixed = jnp.where(group == q, blocks[q ^ shift], mixed)
+    return mixed
+
+
+def couple_kernel(quarters, bins_axis, local_bins, slots, pairs, *refs):
     blocks = refs[:bins_axis]
     weights, meta = refs[bins_axis : bins_axis + 2]
-    values = refs[-1]
-    owners_count = 2 * len(paired)
-    outs = list(refs[-1 - sum(1 if pair else 2 for pair in paired) : -1])
-    rows, width = blocks[0].shape
+    values, outs = refs[-1], refs[-1 - pairs : -1]
+    rows, columns = blocks[0].shape
     all_bins = values.shape[0]
-    half_bins = all_bins // 2
+    held = all_bins // CHUNKS
+    tall = outs[0].shape[2]
+    at_owner = quarters[0] == CHUNKS - 1
     me = lax.axis_index("bins")
     values[...] = jnp.zeros_like(values)
+    row = iota((rows, columns), 0)
     for m in range(bins_axis):
         block = me ^ m
         at = pl.ds(pl.multiple_of(block * local_bins - 4 * (block & 1), 8), rows)
-        values[at, :] += blocks[m][...].astype(F32)
+        arrived = blocks[m][...].astype(F32)
+        if at_owner:
+            lead = 4 * (block & 1)
+            arrived = jnp.where((row >= lead) & (row < local_bins + lead), arrived, 0.0)
+        values[at, :] += arrived
     flat = values[...].astype(BF16)
     energy = jnp.sum(values[...], axis=0, keepdims=True) / all_bins
-    facts = meta[:, chunk * width : (chunk + 1) * width]
-    scale = facts[3:4, :] / (1.0 + energy)
-    slot, towards, rank = facts[0:1, :].astype(I32), facts[1:2, :].astype(I32), facts[2:3, :]
-    slot_id = iota((owners_count * slots, width), 0)
-    straight = (slot_id == towards * slots + slot).astype(F32).astype(BF16)
-    crossed = (slot_id == (towards ^ 1) * slots + slot).astype(F32).astype(BF16)
+    if at_owner:
+        own = blocks[0][...].astype(F32)
+        spare = jnp.where((me & 1) == 1, own[0:4, :], own[local_bins : local_bins + 4, :])
+        weight, rank = spare[0:1, :], spare[1:2, :]
+        lane = iota((1, columns), 1)
+        slot = lane & (slots - 1)
+        low = ((lane // slots) & (CHUNKS - 1)) ^ me
+        towards = lane // LANES * CHUNKS + low
+    else:
+        facts = meta[:, quarters[0] * LANES : (quarters[-1] + 1) * LANES]
+        slot, towards = facts[0:1, :].astype(I32), facts[1:2, :].astype(I32)
+        rank, weight = facts[2:3, :], facts[3:4, :]
+    scale = weight / (1.0 + energy)
     step = all_bins // 9
     for start in range(0, all_bins, step):
         at = slice(start, start + step)
         coupled = jnp.dot(weights[at, :], flat, preferred_element_type=F32)
         values[at, :] = (values[at, :] + coupled) * scale
-    spare = jnp.zeros((7, width), F32)
-    sent = []
-    for group in range(2):
-        updated = values[group * half_bins : (group + 1) * half_bins, :]
-        updated = jnp.concatenate([updated, rank, spare], axis=0).astype(BF16)
-        sent.append(dot_nt(updated, straight if group == chunk else crossed).astype(BF16))
-    even, odd = sent[chunk], sent[1 - chunk]
-    is_low = iota((half_bins + 8, LANES), 1) < slots
-    for t in range(owners_count // 2):
-        at = slice(t * LANES, (t + 1) * LANES)
-        first = jnp.where(is_low, even[:, at], odd[:, at])
-        second = jnp.where(is_low, odd[:, at], even[:, at])
-        if paired[t]:
-            out = outs.pop(0)
-            out[0], out[1] = first, second
-        else:
-            outs.pop(0)[...] = first
-            outs.pop(0)[...] = second
-
-
-def place_kernel(slots, sources, picks, *refs):
+    width = columns // len(quarters)
+    slot_id = iota((2 * pairs * slots, width), 0)
+    row_id = iota((tall, width), 0)
+    for n, quarter in enumerate(quarters):
+        cut = slice(n * width, (n + 1) * width)
+        sent = []
+        for v in range(CHUNKS):
+            start = (v ^ quarter) * held
+            lead = start % 8
+            updated = values[start - lead : start - lead + tall, cut]
+            if lead:
+                updated = pltpu.roll(updated, tall - lead, 0)
+            updated = jnp.where(row_id < held, updated, jnp.where(row_id == held, rank[:, cut], 0.0))
+            group = (towards[:, cut] & (CHUNKS - 1)) ^ v
+            column = towards[:, cut] // CHUNKS * LANES + group * slots + slot[:, cut]
+            route = (slot_id == column).astype(F32).astype(BF16)
+            sent.append(dot_nt(updated.astype(BF16), route).astype(BF16))
+        for x in range(2 * pairs):
+            at = slice(x // CHUNKS * LANES, (x // CHUNKS + 1) * LANES)
+            outs[x // 2][x % 2, n] = lane_groups([rows_v[:, at] for rows_v in sent], x % CHUNKS)
+
+
+def place_kernel(held, sources, picks, *refs):
     out, staged, sems = refs[-3:]
     me = lax.axis_index("pts")
     tall = refs[0].shape[-2]
-    half_bins = tall - 8
-    is_low = iota((tall, LANES), 1) < slots
     slot_id = iota((LANES, LANES), 0)
-
-    def block(pick):
-        ref, index = refs[pick[0]], pick[1]
-        return ref[...] if index is None else ref[index]
-
     copies = []
     for number, x in enumerate(sources):
-        first, second = [block(picks[number][c]) for c in range(CHUNKS)]
-        if x % 2 == 1:
-            first, second = second, first
+        blocks = [refs[n][index] for n, index in picks[number]]
         pieces = []
-        for lhs in (jnp.where(is_low, first, second), jnp.where(is_low, second, first)):
-            rank = lhs[tall - 16 :, :].astype(F32)[8:9, :].astype(I32)
-            place = (slot_id == rank).astype(F32).astype(BF16)
-            pieces.append(dot_nt(lhs, place)[:half_bins])
+        for g in range(CHUNKS):
+            lhs = lane_groups(blocks, (x % CHUNKS) ^ g)
+            rank = lhs[tall - 8 :, :].astype(F32)[held - tall + 8 : held - tall + 9, :].astype(I32)
+            spots = (slot_id == rank).astype(F32).astype(BF16)
+            pieces.append(dot_nt(lhs, spots)[:held])
         staged[number] = jnp.concatenate(pieces, axis=0).astype(BF16)
         at = pl.ds(pl.multiple_of((me ^ x) * LANES, LANES), LANES)
         copy = pltpu.make_async_copy(staged.at[number], out.at[:, at], sems.at[number])
@@ -240,7 +285,7 @@
         copy.wait()
 
 
-def place(out, slots, owners_count, all_bins, sources):
+def place(out, owners_count, all_bins, sources):
     arrays, picks = [], []
     for x in sorted(sources):
         mine = []
@@ -253,7 +298,7 @@
         picks.append(tuple(mine))
     held = [] if out is None else [out]
     return pl.pallas_call(
-        functools.partial(place_kernel, slots, tuple(sorted(sources)), tuple(picks)),
+        functools.partial(place_kernel, all_bins // CHUNKS, tuple(sorted(sources)), tuple(picks)),
         out_shape=jax.ShapeDtypeStruct((all_bins, owners_count * LANES), BF16),
         in_specs=vmem(len(arrays)) + [pl.BlockSpec(memory_space=pl.ANY)] * len(held),
         out_specs=pl.BlockSpec(memory_space=pl.ANY),
@@ -289,16 +334,16 @@
         refs[-1][t] = refs[t][1]
 
 
-def stack(pairs, after):
+def stack(pairs, *after):
     return pl.pallas_call(
         functools.partial(stack_kernel, len(pairs)),
         out_shape=jax.ShapeDtypeStruct((len(pairs),) + pairs[0].shape[1:], pairs[0].dtype),
-        in_specs=vmem(len(pairs) + 1),
+        in_specs=vmem(len(pairs) + len(after)),
         out_specs=vmem(1)[0],
         compiler_params=params(8),
         cost_estimate=cost(1, 1),
         name="stack",
-    )(*pairs, after)
+    )(*pairs, *after)
 
 
 def params(mib):
@@ -324,11 +369,13 @@
     bins_axis = lax.axis_size("bins")
     owners_count = lax.axis_size("pts")
     points = lon_rows * LANES
-    half = points // CHUNKS
+    width = points // CHUNKS
     slots = 2 * points // owners_count // CHUNKS
     tall = round_up(local_bins, 16)
     rows = round_up(local_bins + 1, 8)
-    half_rows = all_bins // 2 + 8
+    order_columns = (CHUNKS - 1) * width + owners_count * slots
+    pairs = owners_count // 2
+    quarter_rows = round_up(all_bins // CHUNKS + 1, 8)
     first_bin = lax.axis_index("bins") * local_bins
 
     planes = jnp.pad(jnp.transpose(spectrum, (1, 0, 2)), ((0, 0), (0, tall - local_bins), (0, 0)))
@@ -372,65 +419,96 @@
         name="inner",
     )(planes, near, speed, side, sea)
     part, far_order, meta = pl.pallas_call(
-        functools.partial(order_kernel, bins_axis, owners_count, half),
+        functools.partial(order_kernel, bins_axis, owners_count, width, slots),
         out_shape=[
-            jax.ShapeDtypeStruct((bins_axis, tall, points), BF16),
-            jax.ShapeDtypeStruct((bins_axis, points, LANES), BF16),
-            jax.ShapeDtypeStruct((8, points), F32),
+            jax.ShapeDtypeStruct((bins_axis, tall, order_columns), BF16),
+            jax.ShapeDtypeStruct((bins_axis, order_columns, LANES), BF16),
+            jax.ShapeDtypeStruct((8, (CHUNKS - 1) * width), F32),
         ],
         in_specs=vmem(2 + bins_axis),
         out_specs=vmem(3),
-        scratch_shapes=[pltpu.VMEM((points, points), BF16)],
+        scratch_shapes=[pltpu.VMEM((order_columns, points), BF16)],
         compiler_params=params(16),
         cost_estimate=cost(1, 1),
         name="order",
     )(inner, sea, *owners)
     packed = pl.pallas_call(
-        functools.partial(pack_kernel, rows, bins_axis, half),
-        out_shape=[jax.ShapeDtypeStruct((rows, half), BF16)] * (CHUNKS * bins_axis),
+        functools.partial(pack_kernel, rows, bins_axis, width, pairs),
+        out_shape=[
+            jax.ShapeDtypeStruct((rows, len(quarters) * width), BF16)
+            for quarters in MAIN
+            for _ in range(bins_axis)
+        ]
+        + [jax.ShapeDtypeStruct((2, 1, rows, LANES), BF16)] * pairs,
         in_specs=vmem(7),
-        out_specs=vmem(CHUNKS * bins_axis),
+        out_specs=vmem(len(MAIN) * bins_axis + pairs),
         scratch_shapes=[pltpu.VMEM((tall, lats), BF16)],
         compiler_params=params(16),
         cost_estimate=cost(1, 1),
         name="pack",
     )(planes, far, speed, side, sea, part, far_order)
 
-    def couple(c, blocks, ready, paired):
-        shapes = [[(2, half_rows, LANES)] if pair else [(half_rows, LANES)] * 2 for pair in paired]
-        shapes = sum(shapes, [])
-        return list(pl.pallas_call(
-            functools.partial(couple_kernel, c, bins_axis, local_bins, slots, paired),
-            out_shape=[jax.ShapeDtypeStruct(shape, BF16) for shape in shapes],
+    def couple(quarters, blocks, ready):
+        shape = (2, len(quarters), quarter_rows, LANES)
+        return pl.pallas_call(
+            functools.partial(couple_kernel, quarters, bins_axis, local_bins, slots, pairs),
+            out_shape=[jax.ShapeDtypeStruct(shape, BF16)] * pairs,
             in_specs=vmem(len(blocks) + 2 + len(ready)),
-            out_specs=vmem(len(shapes)),
-            scratch_shapes=[pltpu.VMEM((all_bins, half), F32)],
+            out_specs=vmem(pairs),
+            scratch_shapes=[pltpu.VMEM((all_bins, blocks[0].shape[1]), F32)],
             compiler_params=params(16),
-            cost_estimate=cost(1 + c * 3e10, 1),
+            cost_estimate=cost((3e9, 1, 3e10, 3e10)[quarters[0]], 1),
             name="couple",
-        )(*blocks, weights, meta, *ready))
-
-    pairs = owners_count // 2
+        )(*blocks, weights, meta, *ready)
+
+    def over_bins(blocks):
+        return [blocks[0]] + [exchange(blocks[m], "bins", m) for m in range(1, bins_axis)]
+
+    def over_pts(pays):
+        sent = {0: pays[0]}
+        for t in range(pairs - 1, 0, -1):
+            sent[t] = exchange(pays[t], "pts", 2 * t)
+        return [sent[t] for t in range(pairs)]
+
+    def held_back(blocks, *after):
+        return [blocks[0]] + [gate(b, *after) for b in blocks[1:]]
+
     early, late = packed[:bins_axis], packed[bins_axis : 2 * bins_axis]
-    first = [exchange(early[m], "bins", m) for m in range(1, bins_axis)]
-    late = [late[0], gate(late[1], first[0], weights)] + [gate(b, *first) for b in late[2:]]
-    second = [exchange(late[m], "bins", m) for m in range(1, bins_axis)]
-    pays = couple(0, [early[0], *first], late[1:], (True,) * pairs)
-    came = {0: pays[0]}
-    for t in range(pairs - 1, 0, -1):
-        came[t] = exchange(pays[t], "pts", 2 * t)
-    pays = couple(1, [late[0], *second], [], (True,) * pairs)
-    last = {0: pays[0]}
-    for t in range(pairs - 1, 0, -1):
-        last[t] = exchange(pays[t], "pts", 2 * t)
-    swapped = exchange(stack([came[t] for t in range(pairs)], last[pairs - 1]), "pts", 1)
-    swapped_late = exchange(stack([last[t] for t in range(pairs)], last[0]), "pts", 1)
-
-    shape = (slots, owners_count, all_bins)
-    placed = place(None, *shape, {2 * t: [(came[t], 0), (last[t], 0)] for t in range(pairs)})
-    placed = place(
-        placed, *shape, {2 * t + 1: [(swapped, t), (swapped_late, t)] for t in range(pairs)}
-    )
+    direct = packed[2 * bins_axis :]
+    first = over_bins(early)
+    direct = over_pts(direct)
+    late = [late[0], gate(late[1], first[1], weights), *[gate(b, *first[1:]) for b in late[2:]]]
+    second = over_bins(late)
+    came = [over_pts(couple(MAIN[0], first, late[1:]))]
+    regrouped = pl.pallas_call(
+        functools.partial(regroup_kernel, bins_axis, pairs),
+        out_shape=[jax.ShapeDtypeStruct((rows, owners_count * slots), BF16)] * bins_axis,
+        in_specs=vmem(pairs + 1),
+        out_specs=vmem(bins_axis),
+        compiler_params=params(16),
+        cost_estimate=cost(1, 1),
+        name="regroup",
+    )(*direct, exchange(stack(direct, came[0][0]), "pts", 1))
+    regrouped = [
+        regrouped[0],
+        gate(regrouped[1], *second[1:], came[0][0], came[0][pairs - 1]),
+        *[gate(b, *second[1:], came[0][0]) for b in regrouped[2:]],
+    ]
+    third = over_bins(regrouped)
+    came.append(over_pts(couple(MAIN[1], second, regrouped[2:])))
+    last = came[-1]
+    here = couple((CHUNKS - 1,), third, [])
+    swapped = [exchange(stack(came[0], *third[2:]), "pts", 1), exchange(stack(last, here[0]), "pts", 1)]
+
+    shape = (owners_count, all_bins)
+    cuts = [(c, n) for c, quarters in enumerate(MAIN) for n in range(len(quarters))]
+    near_side = {
+        2 * t: [(came[c][t], (0, n)) for c, n in cuts] + [(here[t], (0, 0))] for t in range(pairs)
+    }
+    far_side = {
+        2 * t + 1: [(swapped[c], (t, n)) for c, n in cuts] + [(here[t], (1, 0))] for t in range(pairs)
+    }
+    placed = place(place(None, *shape, near_side), *shape, far_side)
     return jnp.transpose(placed).reshape(1, 1, owners_count * LANES, all_bins)
 
 
@@ -513,6 +591,9 @@
         and bins_axis % 2 == 0
         and spectrum.shape[0] % 8 == 4
         and courant.shape[0] % 144 == 0
+        and courant.shape[0] // CHUNKS % 8 == 4
+        and points == CHUNKS * LANES
+        and bins_axis == CHUNKS
         and owners_count == 8
         and spectrum.shape[1] >= 3
     )

time: 77 us -> 73.3 us (0.952); the launches traced: 76.9 us -> 71.9 us
  waiting for transfers between devices: 32.8 us -> 14.4 us
  starting transfers between devices: 28 us -> 37.7 us
  Pallas kernels: 12.7 us -> 16.3 us
    ppermute x18 -> x25, waiting for transfers between devices: 32.8 us -> 14.4 us  [exchange(): lax.ppermute(array, axis, [(i, i ^ offset) for i in range(lax.axis_size(a...]
    ppermute x18 -> x25, starting transfers between devices: 27.4 us -> 37 us  [exchange(): lax.ppermute(array, axis, [(i, i ^ offset) for i in range(lax.axis_size(a...]
    pallas_call x6 -> x8, Pallas kernels: 10.1 us -> 13.6 us  [the longest x3 5.7 us: couple(): pl.pallas_call(functools.partial(couple_kernel, quarters, bins_axis, loca...]
  transfers between devices with their start and end apart: 19 -> 26, of which waited for: 8 -> 6; matrix products, arithmetic and copies ran while one was open for 2% -> 2% of each run, Pallas kernels for 13% -> 18%
where the time goes in v6:
time: 73.3 us; the launch traced here: 71.9 us
  starting transfers between devices  37.7 us (51%)
  Pallas kernels  16.3 us (22%)
  waiting for transfers between devices  14.4 us (20%)
  local copies, waits for them, and re-layouts  2.11 us (3%)
  other arithmetic  0.93 us (1%)
    ppermute x25, starting transfers between devices, exchange(): lax.ppermute(array, axis, [(i, i ^ offset) for i in range(lax.axis_size(a...  37 us
    ppermute x25, waiting for transfers between devices, exchange(): lax.ppermute(array, axis, [(i, i ^ offset) for i in range(lax.axis_size(a...  14.4 us
    pallas_call x3, Pallas kernels, couple(): pl.pallas_call(functools.partial(couple_kernel, quarters, bins_axis, loca...  5.7 us
    pallas_call x2, Pallas kernels, place(): pl.pallas_call(functools.partial(place_kernel, all_bins // CHUNKS, tuple(...  3.35 us
    pallas_call x1, Pallas kernels, chunked(): pl.pallas_call(functools.partial(order_kernel, bins_axis, owners_count, w...  2.61 us
    pallas_call x1, Pallas kernels, chunked(): pl.pallas_call(functools.partial(pack_kernel, rows, bins_axis, width, pai...  1.69 us
    unnamed x9, local copies, waits for them, and re-layouts  1.62 us
  transfers between devices with their start and end apart: 26, of which 6 were waited for; matrix products, arithmetic and copies ran while one was open for 2% of the time, Pallas kernels for 18%

profile of v6, /device:TPU:0, one launch (start us, length us, event | category | flops | bytes accessed | tf_op | source)
XLA Modules:
  0.0 71.9 jit_solution(15028891938646845690)
XLA Ops:
  0.0 1.6 %copy.10 = bf16[324,4,512]{2,0,1:T(8,128)(2,1)S(1)} copy(bf16[324,4,512]{2,1,0:T(4,128)(2,1)} %param.6) | data formatting | bytes 2654208 | tf_op args[0]
  3.0 4.7 %collective-permute-start.4 = (s32[1,512]{1,0:T(1,128)S(1)}, s32[1,512]{1,0:T(1,128)S(1)}, u32[]{:S(2)}, u32[]{:S(2)}) collective-permute-start(s32[1,512]{1,0:T(1,128)S(1)} %bitcast.19), channel_id=1, source_target_pairs={{0,3},{1,2},{2,1},{3,0},{4,7},{5,6},{6,5},{7,4},{8,11},{9,10},{10,... | collective-permute-start | bytes 6152 | tf_op jit(solution)/shard_map/ppermute | solution.py:363
  10.9 1.3 %collective-permute-done.3.refs_4_ = s32[1,512]{1,0:T(1,128)S(1)} collective-permute-done((s32[1,512]{1,0:T(1,128)S(1)}, s32[1,512]{1,0:T(1,128)S(1)}, u32[]{:S(2)}, u32[]{:S(2)}) %collective-permute-start.3) | collective-permute-done | bytes 2080 | tf_op jit(solution)/shard_map/ppermute | solution.py:363
  12.2 2.6 %order.1 = (bf16[4,336,640]{2,1,0:T(8,128)(2,1)S(1)}, bf16[4,640,128]{2,1,0:T(8,128)(2,1)S(1)}, f32[8,384]{1,0:T(8,128)S(1)}) custom-call(bf16[3,336,512]{2,1,0:T(8,128)(2,1)S(1)} %inner.1.refs_0_, s32[4,512]{1,0:T(4,128)S(1)} %copy-done.2, s32[1,512]{1,0:T(1,128)S(1)} %bitcast.22, s32[1,512]{1,0:T(1,128)S(1)} %collective-permute-done.2.refs_3_, ...), custom_call_target="tpu_custom_call" | custom-call | flops 1 | bytes 1 | tf_op jit(solution)/shard_map/order/pallas_call | solution.py:421
  14.8 1.7 %pack.1 = (bf16[328,256]{1,0:T(8,128)(2,1)S(1)}, bf16[328,256]{1,0:T(8,128)(2,1)S(1)}, bf16[328,256]{1,0:T(8,128)(2,1)S(1)}, bf16[328,256]{1,0:T(8,128)(2,1)S(1)...) custom-call(bf16[4,336,512]{2,1,0:T(8,128)(2,1)S(1)} %pad.12.planes., ...), custom_call_target="tpu_custom_call" | custom-call | flops 1 | bytes 1 | tf_op jit(solution)/shard_map/pack/pallas_call | solution.py:435
  16.7 2.9 %collective-permute-start.6 = (bf16[328,256]{1,0:T(8,128)(2,1)S(1)}, bf16[328,256]{1,0:T(8,128)(2,1)S(1)}, u32[]{:S(2)}, u32[]{:S(2)}) collective-permute-start(bf16[328,256]{1,0:T(8,128)(2,1)S(1)} %get-tuple-element.40), channel_id=1, source_target_pairs={{0,2},{1,3},{2,0},{3,1},{4,6},{5,7},{6,4},{7,5},{8,10},{9,11},{10,... | collective-permute-start | bytes 503816 | tf_op jit(solution)/shard_map/ppermute | solution.py:363
  19.6 1.3 %collective-permute-start.7 = (bf16[328,256]{1,0:T(8,128)(2,1)S(1)}, bf16[328,256]{1,0:T(8,128)(2,1)S(1)}, u32[]{:S(2)}, u32[]{:S(2)}) collective-permute-start(bf16[328,256]{1,0:T(8,128)(2,1)S(1)} %get-tuple-element.41), channel_id=1, source_target_pairs={{0,3},{1,2},{2,1},{3,0},{4,7},{5,6},{6,5},{7,4},{8,11},{9,10},{10,... | collective-permute-start | bytes 503816 | tf_op jit(solution)/shard_map/ppermute | solution.py:363
  21.0 1.3 %transpose.21.refs_1_.refs_4_ = bf16[1296,1296]{1,0:T(8,128)(2,1)S(1)} custom-call(bf16[1296,1296]{1,0:T(8,128)(2,1)S(1)} %copy-done.1), custom_call_target="tpu_custom_call" | custom-call | flops 1 | bytes 1 | tf_op jit(solution)/shard_map/transpose/pallas_call | solution.py:402
  22.2 3.4 %collective-permute-start.11 = (bf16[2,1,328,128]{3,2,1,0:T(8,128)(2,1)S(1)}, bf16[2,1,328,128]{3,2,1,0:T(8,128)(2,1)S(1)}, u32[]{:S(2)}, u32[]{:S(2)}) collective-permute-start(bf16[2,1,328,128]{3,2,1,0:T(8,128)(2,1)S(1)} %get-tuple-element.51), channel_id=1, source_target_pairs={{0,8},{4,12},{8,0},{12,4},{16,24},{20,28},{24,16},{28,20},{1,9},{5... | collective-permute-start | bytes 503816 | tf_op jit(solution)/shard_map/ppermute | solution.py:363
  25.7 1.5 %collective-permute-start.12 = (bf16[2,1,328,128]{3,2,1,0:T(8,128)(2,1)S(1)}, bf16[2,1,328,128]{3,2,1,0:T(8,128)(2,1)S(1)}, u32[]{:S(2)}, u32[]{:S(2)}) collective-permute-start(bf16[2,1,328,128]{3,2,1,0:T(8,128)(2,1)S(1)} %get-tuple-element.52), channel_id=1, source_target_pairs={{0,16},{4,20},{8,24},{12,28},{16,0},{20,4},{24,8},{28,12},{1,17},{... | collective-permute-start | bytes 503816 | tf_op jit(solution)/shard_map/ppermute | solution.py:363
  28.0 4.2 %collective-permute-done.7.refs_2_.refs_3_ = bf16[328,256]{1,0:T(8,128)(2,1)S(1)} collective-permute-done((bf16[328,256]{1,0:T(8,128)(2,1)S(1)}, bf16[328,256]{1,0:T(8,128)(2,1)S(1)}, u32[]{:S(2)}, u32[]{:S(2)}) %collective-permute-start.7) | collective-permute-done | bytes 167968 | tf_op jit(solution)/shard_map/ppermute | solution.py:363
  32.3 1.9 %couple.3 = (bf16[2,2,328,128]{3,2,1,0:T(8,128)(2,1)S(1)}, bf16[2,2,328,128]{3,2,1,0:T(8,128)(2,1)S(1)}, bf16[2,2,328,128]{3,2,1,0:T(8,128)(2,1)S(1)}, bf16[2,2,328,128]{3,2,1,0:T(8,128)(2,1)S(1)}) custom-call(bf16[328,256]{1,0:T(8,128)(2,1)S(1)} %get-tuple-element.38.refs_0_, bf16[328,256]{1,0:T(8,128)(2,1)S(1)} %collective-permute-done.5.refs_0_.refs_1_, ...), custom_call_target="tpu_custom_call" | custom-call | flops 3000000000 | bytes 1 | tf_op jit(solution)/shard_map/couple/pallas_call | solution.py:453
  35.2 1.9 %collective-permute-start.10 = (bf16[2,2,328,128]{3,2,1,0:T(8,128)(2,1)S(1)}, bf16[2,2,328,128]{3,2,1,0:T(8,128)(2,1)S(1)}, u32[]{:S(2)}, u32[]{:S(2)}) collective-permute-start(bf16[2,2,328,128]{3,2,1,0:T(8,128)(2,1)S(1)} %get-tuple-element.49), channel_id=1, source_target_pairs={{0,24},{4,28},{8,16},{12,20},{16,8},{20,12},{24,0},{28,4},{1,25},{... | collective-permute-start | bytes 1007624 | tf_op jit(solution)/shard_map/ppermute | solution.py:363
  37.1 3.4 %collective-permute-start.16 = (bf16[328,128]{1,0:T(8,128)(2,1)S(1)}, bf16[328,128]{1,0:T(8,128)(2,1)S(1)}, u32[]{:S(2)}, u32[]{:S(2)}) collective-permute-start(bf16[328,128]{1,0:T(8,128)(2,1)S(1)} %gate.7.refs_7_), channel_id=1, source_target_pairs={{0,2},{1,3},{2,0},{3,1},{4,6},{5,7},{6,4},{7,5},{8,10},{9,11},{10,... | collective-permute-start | bytes 251912 | tf_op jit(solution)/shard_map/ppermute | solution.py:363
  40.5 1.3 %collective-permute-start.17 = (bf16[328,128]{1,0:T(8,128)(2,1)S(1)}, bf16[328,128]{1,0:T(8,128)(2,1)S(1)}, u32[]{:S(2)}, u32[]{:S(2)}) collective-permute-start(bf16[328,128]{1,0:T(8,128)(2,1)S(1)} %gate.8.refs_8_), channel_id=1, source_target_pairs={{0,3},{1,2},{2,1},{3,0},{4,7},{5,6},{6,5},{7,4},{8,11},{9,10},{10,... | collective-permute-start | bytes 251912 | tf_op jit(solution)/shard_map/ppermute | solution.py:363
  41.9 2.9 %collective-permute-start.8 = (bf16[2,2,328,128]{3,2,1,0:T(8,128)(2,1)S(1)}, bf16[2,2,328,128]{3,2,1,0:T(8,128)(2,1)S(1)}, u32[]{:S(2)}, u32[]{:S(2)}) collective-permute-start(bf16[2,2,328,128]{3,2,1,0:T(8,128)(2,1)S(1)} %get-tuple-element.47), channel_id=1, source_target_pairs={{0,8},{4,12},{8,0},{12,4},{16,24},{20,28},{24,16},{28,20},{1,9},{5... | collective-permute-start | bytes 1007624 | tf_op jit(solution)/shard_map/ppermute | solution.py:363
  45.0 2.1 %collective-permute-done.16.refs_1_.refs_2_ = bf16[328,128]{1,0:T(8,128)(2,1)S(1)} collective-permute-done((bf16[328,128]{1,0:T(8,128)(2,1)S(1)}, bf16[328,128]{1,0:T(8,128)(2,1)S(1)}, u32[]{:S(2)}, u32[]{:S(2)}) %collective-permute-start.16) | collective-permute-done | bytes 84000 | tf_op jit(solution)/shard_map/ppermute | solution.py:363
  47.1 3.3 %collective-permute-start.9 = (bf16[2,2,328,128]{3,2,1,0:T(8,128)(2,1)S(1)}, bf16[2,2,328,128]{3,2,1,0:T(8,128)(2,1)S(1)}, u32[]{:S(2)}, u32[]{:S(2)}) collective-permute-start(bf16[2,2,328,128]{3,2,1,0:T(8,128)(2,1)S(1)} %get-tuple-element.48), channel_id=1, source_target_pairs={{0,16},{4,20},{8,24},{12,28},{16,0},{20,4},{24,8},{28,12},{1,17},{... | collective-permute-start | bytes 1007624 | tf_op jit(solution)/shard_map/ppermute | solution.py:363
  51.8 3.3 %collective-permute-start.24 = (bf16[328,256]{1,0:T(8,128)(2,1)S(1)}, bf16[328,256]{1,0:T(8,128)(2,1)S(1)}, u32[]{:S(2)}, u32[]{:S(2)}) collective-permute-start(bf16[328,256]{1,0:T(8,128)(2,1)S(1)} %gate.11), channel_id=1, source_target_pairs={{0,1},{1,0},{2,3},{3,2},{4,5},{5,4},{6,7},{7,6},{8,9},{9,8},{10,11... | collective-permute-start | bytes 503816 | tf_op jit(solution)/shard_map/ppermute | solution.py:363
  55.1 1.6 %couple.4 = (bf16[2,1,328,128]{3,2,1,0:T(8,128)(2,1)S(1)}, bf16[2,1,328,128]{3,2,1,0:T(8,128)(2,1)S(1)}, bf16[2,1,328,128]{3,2,1,0:T(8,128)(2,1)S(1)}, bf16[2,1,328,128]{3,2,1,0:T(8,128)(2,1)S(1)}) custom-call(bf16[328,128]{1,0:T(8,128)(2,1)S(1)} %get-tuple-element.56.refs_0_, bf16[328,128]{1,0:T(8,128)(2,1)S(1)} %collective-permute-done.15.refs_0_.refs_1_, ...), custom_call_target="tpu_custom_call" | custom-call | flops 30000001024 | bytes 1 | tf_op jit(solution)/shard_map/couple/pallas_call | solution.py:453
  60.6 4.9 %collective-permute-done.18.refs_4_.refs_2_ = bf16[328,256]{1,0:T(8,128)(2,1)S(1)} collective-permute-done((bf16[328,256]{1,0:T(8,128)(2,1)S(1)}, bf16[328,256]{1,0:T(8,128)(2,1)S(1)}, u32[]{:S(2)}, u32[]{:S(2)}) %collective-permute-start.18) | collective-permute-done | bytes 167968 | tf_op jit(solution)/shard_map/ppermute | solution.py:363
  65.6 2.1 %couple.5 = (bf16[2,1,328,128]{3,2,1,0:T(8,128)(2,1)S(1)}, bf16[2,1,328,128]{3,2,1,0:T(8,128)(2,1)S(1)}, bf16[2,1,328,128]{3,2,1,0:T(8,128)(2,1)S(1)}, bf16[2,1,328,128]{3,2,1,0:T(8,128)(2,1)S(1)}) custom-call(bf16[328,256]{1,0:T(8,128)(2,1)S(1)} %get-tuple-element.61.refs_0_, bf16[328,256]{1,0:T(8,128)(2,1)S(1)} %collective-permute-done.24.refs_1_, ...), custom_call_target="tpu_custom_call" | custom-call | flops 30000001024 | bytes 1 | tf_op jit(solution)/shard_map/couple/pallas_call | solution.py:453
  68.4 1.7 %place.2.refs_6_ = bf16[1296,1024]{1,0:T(8,128)(2,1)} custom-call(bf16[2,2,328,128]{3,2,1,0:T(8,128)(2,1)S(1)} %get-tuple-element.46.refs_4_.refs_3_.refs_0_, bf16[2,1,328,128]{3,2,1,0:T(8,128)(2,1)S(1)} %get-tuple-element.57.refs_0_.refs_1_, bf16[2,1,328,128]{3,2,1,0:T(8,128)(2,1)S(1)} %get-tuple-element.63.refs_4_.refs_2_, ...), custom_call_target="tpu_custom_call" | custom-call | flops 1 | bytes 1 | tf_op jit(solution)/shard_map/place/pallas_call | solution.py:300
  70.1 1.7 %place.3 = bf16[1296,1024]{1,0:T(8,128)(2,1)} custom-call(bf16[4,2,328,128]{3,2,1,0:T(8,128)(2,1)S(1)} %collective-permute-done.20.refs_0_, bf16[4,1,328,128]{3,2,1,0:T(8,128)(2,1)S(1)} %collective-permute-done.25.refs_1_, bf16[2,1,328,128]{3,2,1,0:T(8,128)(2,1)S(1)} %get-tuple-element.63.refs_4_.refs_2_, ...), custom_call_target="tpu_custom_call", output_to_operand_aliasing={{}: (6, {})} | custom-call | flops 1 | bytes 1 | tf_op jit(solution)/shard_map/place/pallas_call | solution.py:300
  (65 shorter events, 12.7 us)
Async XLA Ops:
  1.8 7.5 %collective-permute-start.1 = (bf16[324,512]{1,0:T(8,128)(2,1)S(1)}, bf16[324,512]{1,0:T(8,128)(2,1)S(1)}, u32[]{:S(2)}, u32[]{:S(2)}) collective-permute-start(bf16[324,512]{1,0:T(8,128)(2,1)S(1)} %get-tuple-element.69), channel_id=1, source_target_pairs={{0,4},{4,0},{8,12},{12,8},{16,20},{20,16},{24,28},{28,24},{1,5},{5... | collective-permute-start | bytes 995336 | tf_op jit(solution)/shard_map/ppermute | solution.py:363
  2.3 12.5 %collective-permute-start = (bf16[324,512]{1,0:T(8,128)(2,1)S(1)}, bf16[324,512]{1,0:T(8,128)(2,1)S(1)}, u32[]{:S(2)}, u32[]{:S(2)}) collective-permute-start(bf16[324,512]{1,0:T(8,128)(2,1)S(1)} %get-tuple-element.70), channel_id=1, source_target_pairs={{4,8},{12,16},{20,24},{8,4},{16,12},{24,20},{5,9},{13,17},{21,25},... | collective-permute-start | bytes 995336 | tf_op jit(solution)/shard_map/ppermute | solution.py:390
  3.0 7.9 %collective-permute-start.4 = (s32[1,512]{1,0:T(1,128)S(1)}, s32[1,512]{1,0:T(1,128)S(1)}, u32[]{:S(2)}, u32[]{:S(2)}) collective-permute-start(s32[1,512]{1,0:T(1,128)S(1)} %bitcast.19), channel_id=1, source_target_pairs={{0,3},{1,2},{2,1},{3,0},{4,7},{5,6},{6,5},{7,4},{8,11},{9,10},{10,... | collective-permute-start | bytes 6152 | tf_op jit(solution)/shard_map/ppermute | solution.py:363
  7.7 4.5 %collective-permute-start.3 = (s32[1,512]{1,0:T(1,128)S(1)}, s32[1,512]{1,0:T(1,128)S(1)}, u32[]{:S(2)}, u32[]{:S(2)}) collective-permute-start(s32[1,512]{1,0:T(1,128)S(1)} %bitcast.20), channel_id=1, source_target_pairs={{0,2},{1,3},{2,0},{3,1},{4,6},{5,7},{6,4},{7,5},{8,10},{9,11},{10,... | collective-permute-start | bytes 6152 | tf_op jit(solution)/shard_map/ppermute | solution.py:363
  16.5 10.7 %collective-permute-start.5 = (bf16[328,256]{1,0:T(8,128)(2,1)S(1)}, bf16[328,256]{1,0:T(8,128)(2,1)S(1)}, u32[]{:S(2)}, u32[]{:S(2)}) collective-permute-start(bf16[328,256]{1,0:T(8,128)(2,1)S(1)} %get-tuple-element.39), channel_id=1, source_target_pairs={{0,1},{1,0},{2,3},{3,2},{4,5},{5,4},{6,7},{7,6},{8,9},{9,8},{10,11... | collective-permute-start | bytes 503816 | tf_op jit(solution)/shard_map/ppermute | solution.py:363
  16.7 11.3 %collective-permute-start.6 = (bf16[328,256]{1,0:T(8,128)(2,1)S(1)}, bf16[328,256]{1,0:T(8,128)(2,1)S(1)}, u32[]{:S(2)}, u32[]{:S(2)}) collective-permute-start(bf16[328,256]{1,0:T(8,128)(2,1)S(1)} %get-tuple-element.40), channel_id=1, source_target_pairs={{0,2},{1,3},{2,0},{3,1},{4,6},{5,7},{6,4},{7,5},{8,10},{9,11},{10,... | collective-permute-start | bytes 503816 | tf_op jit(solution)/shard_map/ppermute | solution.py:363
  19.6 12.6 %collective-permute-start.7 = (bf16[328,256]{1,0:T(8,128)(2,1)S(1)}, bf16[328,256]{1,0:T(8,128)(2,1)S(1)}, u32[]{:S(2)}, u32[]{:S(2)}) collective-permute-start(bf16[328,256]{1,0:T(8,128)(2,1)S(1)} %get-tuple-element.41), channel_id=1, source_target_pairs={{0,3},{1,2},{2,1},{3,0},{4,7},{5,6},{6,5},{7,4},{8,11},{9,10},{10,... | collective-permute-start | bytes 503816 | tf_op jit(solution)/shard_map/ppermute | solution.py:363
  22.2 12.0 %collective-permute-start.11 = (bf16[2,1,328,128]{3,2,1,0:T(8,128)(2,1)S(1)}, bf16[2,1,328,128]{3,2,1,0:T(8,128)(2,1)S(1)}, u32[]{:S(2)}, u32[]{:S(2)}) collective-permute-start(bf16[2,1,328,128]{3,2,1,0:T(8,128)(2,1)S(1)} %get-tuple-element.51), channel_id=1, source_target_pairs={{0,8},{4,12},{8,0},{12,4},{16,24},{20,28},{24,16},{28,20},{1,9},{5... | collective-permute-start | bytes 503816 | tf_op jit(solution)/shard_map/ppermute | solution.py:363
  25.7 8.6 %collective-permute-start.12 = (bf16[2,1,328,128]{3,2,1,0:T(8,128)(2,1)S(1)}, bf16[2,1,328,128]{3,2,1,0:T(8,128)(2,1)S(1)}, u32[]{:S(2)}, u32[]{:S(2)}) collective-permute-start(bf16[2,1,328,128]{3,2,1,0:T(8,128)(2,1)S(1)} %get-tuple-element.52), channel_id=1, source_target_pairs={{0,16},{4,20},{8,24},{12,28},{16,0},{20,4},{24,8},{28,12},{1,17},{... | collective-permute-start | bytes 503816 | tf_op jit(solution)/shard_map/ppermute | solution.py:363
  27.2 7.8 %collective-permute-start.13 = (bf16[2,1,328,128]{3,2,1,0:T(8,128)(2,1)S(1)}, bf16[2,1,328,128]{3,2,1,0:T(8,128)(2,1)S(1)}, u32[]{:S(2)}, u32[]{:S(2)}) collective-permute-start(bf16[2,1,328,128]{3,2,1,0:T(8,128)(2,1)S(1)} %get-tuple-element.53), channel_id=1, source_target_pairs={{0,24},{4,28},{8,16},{12,20},{16,8},{20,12},{24,0},{28,4},{1,25},{... | collective-permute-start | bytes 503816 | tf_op jit(solution)/shard_map/ppermute | solution.py:363
  35.0 6.9 %collective-permute-start.14 = (bf16[4,1,328,128]{3,2,1,0:T(8,128)(2,1)S(1)}, bf16[4,1,328,128]{3,2,1,0:T(8,128)(2,1)S(1)}, u32[]{:S(2)}, u32[]{:S(2)}) collective-permute-start(bf16[4,1,328,128]{3,2,1,0:T(8,128)(2,1)S(1)} %stack.3), channel_id=1, source_target_pairs={{0,4},{4,0},{8,12},{12,8},{16,20},{20,16},{24,28},{28,24},{1,5},{5... | collective-permute-start | bytes 1007624 | tf_op jit(solution)/shard_map/ppermute | solution.py:363
  35.2 16.5 %collective-permute-start.10 = (bf16[2,2,328,128]{3,2,1,0:T(8,128)(2,1)S(1)}, bf16[2,2,328,128]{3,2,1,0:T(8,128)(2,1)S(1)}, u32[]{:S(2)}, u32[]{:S(2)}) collective-permute-start(bf16[2,2,328,128]{3,2,1,0:T(8,128)(2,1)S(1)} %get-tuple-element.49), channel_id=1, source_target_pairs={{0,24},{4,28},{8,16},{12,20},{16,8},{20,12},{24,0},{28,4},{1,25},{... | collective-permute-start | bytes 1007624 | tf_op jit(solution)/shard_map/ppermute | solution.py:363
  37.1 10.0 %collective-permute-start.16 = (bf16[328,128]{1,0:T(8,128)(2,1)S(1)}, bf16[328,128]{1,0:T(8,128)(2,1)S(1)}, u32[]{:S(2)}, u32[]{:S(2)}) collective-permute-start(bf16[328,128]{1,0:T(8,128)(2,1)S(1)} %gate.7.refs_7_), channel_id=1, source_target_pairs={{0,2},{1,3},{2,0},{3,1},{4,6},{5,7},{6,4},{7,5},{8,10},{9,11},{10,... | collective-permute-start | bytes 251912 | tf_op jit(solution)/shard_map/ppermute | solution.py:363
  40.5 9.9 %collective-permute-start.17 = (bf16[328,128]{1,0:T(8,128)(2,1)S(1)}, bf16[328,128]{1,0:T(8,128)(2,1)S(1)}, u32[]{:S(2)}, u32[]{:S(2)}) collective-permute-start(bf16[328,128]{1,0:T(8,128)(2,1)S(1)} %gate.8.refs_8_), channel_id=1, source_target_pairs={{0,3},{1,2},{2,1},{3,0},{4,7},{5,6},{6,5},{7,4},{8,11},{9,10},{10,... | collective-permute-start | bytes 251912 | tf_op jit(solution)/shard_map/ppermute | solution.py:363
  41.8 8.6 %collective-permute-start.15 = (bf16[328,128]{1,0:T(8,128)(2,1)S(1)}, bf16[328,128]{1,0:T(8,128)(2,1)S(1)}, u32[]{:S(2)}, u32[]{:S(2)}) collective-permute-start(bf16[328,128]{1,0:T(8,128)(2,1)S(1)} %gate.6.refs_6_), channel_id=1, source_target_pairs={{0,1},{1,0},{2,3},{3,2},{4,5},{5,4},{6,7},{7,6},{8,9},{9,8},{10,11... | collective-permute-start | bytes 251912 | tf_op jit(solution)/shard_map/ppermute | solution.py:363
  41.9 14.9 %collective-permute-start.8 = (bf16[2,2,328,128]{3,2,1,0:T(8,128)(2,1)S(1)}, bf16[2,2,328,128]{3,2,1,0:T(8,128)(2,1)S(1)}, u32[]{:S(2)}, u32[]{:S(2)}) collective-permute-start(bf16[2,2,328,128]{3,2,1,0:T(8,128)(2,1)S(1)} %get-tuple-element.47), channel_id=1, source_target_pairs={{0,8},{4,12},{8,0},{12,4},{16,24},{20,28},{24,16},{28,20},{1,9},{5... | collective-permute-start | bytes 1007624 | tf_op jit(solution)/shard_map/ppermute | solution.py:363
  47.1 10.5 %collective-permute-start.9 = (bf16[2,2,328,128]{3,2,1,0:T(8,128)(2,1)S(1)}, bf16[2,2,328,128]{3,2,1,0:T(8,128)(2,1)S(1)}, u32[]{:S(2)}, u32[]{:S(2)}) collective-permute-start(bf16[2,2,328,128]{3,2,1,0:T(8,128)(2,1)S(1)} %get-tuple-element.48), channel_id=1, source_target_pairs={{0,16},{4,20},{8,24},{12,28},{16,0},{20,4},{24,8},{28,12},{1,17},{... | collective-permute-start | bytes 1007624 | tf_op jit(solution)/shard_map/ppermute | solution.py:363
  50.5 9.1 %collective-permute-start.19 = (bf16[328,256]{1,0:T(8,128)(2,1)S(1)}, bf16[328,256]{1,0:T(8,128)(2,1)S(1)}, u32[]{:S(2)}, u32[]{:S(2)}) collective-permute-start(bf16[328,256]{1,0:T(8,128)(2,1)S(1)} %gate.10.refs_7_), channel_id=1, source_target_pairs={{0,3},{1,2},{2,1},{3,0},{4,7},{5,6},{6,5},{7,4},{8,11},{9,10},{10,... | collective-permute-start | bytes 503816 | tf_op jit(solution)/shard_map/ppermute | solution.py:363
  51.7 13.8 %collective-permute-start.18 = (bf16[328,256]{1,0:T(8,128)(2,1)S(1)}, bf16[328,256]{1,0:T(8,128)(2,1)S(1)}, u32[]{:S(2)}, u32[]{:S(2)}) collective-permute-start(bf16[328,256]{1,0:T(8,128)(2,1)S(1)} %gate.9.refs_6_), channel_id=1, source_target_pairs={{0,2},{1,3},{2,0},{3,1},{4,6},{5,7},{6,4},{7,5},{8,10},{9,11},{10,... | collective-permute-start | bytes 503816 | tf_op jit(solution)/shard_map/ppermute | solution.py:363
  51.8 13.8 %collective-permute-start.24 = (bf16[328,256]{1,0:T(8,128)(2,1)S(1)}, bf16[328,256]{1,0:T(8,128)(2,1)S(1)}, u32[]{:S(2)}, u32[]{:S(2)}) collective-permute-start(bf16[328,256]{1,0:T(8,128)(2,1)S(1)} %gate.11), channel_id=1, source_target_pairs={{0,1},{1,0},{2,3},{3,2},{4,5},{5,4},{6,7},{7,6},{8,9},{9,8},{10,11... | collective-permute-start | bytes 503816 | tf_op jit(solution)/shard_map/ppermute | solution.py:363
  56.7 11.0 %collective-permute-start.21 = (bf16[2,1,328,128]{3,2,1,0:T(8,128)(2,1)S(1)}, bf16[2,1,328,128]{3,2,1,0:T(8,128)(2,1)S(1)}, u32[]{:S(2)}, u32[]{:S(2)}) collective-permute-start(bf16[2,1,328,128]{3,2,1,0:T(8,128)(2,1)S(1)} %get-tuple-element.58), channel_id=1, source_target_pairs={{0,8},{4,12},{8,0},{12,4},{16,24},{20,28},{24,16},{28,20},{1,9},{5... | collective-permute-start | bytes 503816 | tf_op jit(solution)/shard_map/ppermute | solution.py:363
  57.6 10.2 %collective-permute-start.22 = (bf16[2,1,328,128]{3,2,1,0:T(8,128)(2,1)S(1)}, bf16[2,1,328,128]{3,2,1,0:T(8,128)(2,1)S(1)}, u32[]{:S(2)}, u32[]{:S(2)}) collective-permute-start(bf16[2,1,328,128]{3,2,1,0:T(8,128)(2,1)S(1)} %get-tuple-element.59), channel_id=1, source_target_pairs={{0,16},{4,20},{8,24},{12,28},{16,0},{20,4},{24,8},{28,12},{1,17},{... | collective-permute-start | bytes 503816 | tf_op jit(solution)/shard_map/ppermute | solution.py:363
  59.5 8.2 %collective-permute-start.23 = (bf16[2,1,328,128]{3,2,1,0:T(8,128)(2,1)S(1)}, bf16[2,1,328,128]{3,2,1,0:T(8,128)(2,1)S(1)}, u32[]{:S(2)}, u32[]{:S(2)}) collective-permute-start(bf16[2,1,328,128]{3,2,1,0:T(8,128)(2,1)S(1)} %get-tuple-element.60), channel_id=1, source_target_pairs={{0,24},{4,28},{8,16},{12,20},{16,8},{20,12},{24,0},{28,4},{1,25},{... | collective-permute-start | bytes 503816 | tf_op jit(solution)/shard_map/ppermute | solution.py:363
  65.5 4.5 %collective-permute-start.20 = (bf16[4,2,328,128]{3,2,1,0:T(8,128)(2,1)S(1)}, bf16[4,2,328,128]{3,2,1,0:T(8,128)(2,1)S(1)}, u32[]{:S(2)}, u32[]{:S(2)}) collective-permute-start(bf16[4,2,328,128]{3,2,1,0:T(8,128)(2,1)S(1)} %stack.4), channel_id=1, source_target_pairs={{0,4},{4,0},{8,12},{12,8},{16,20},{20,16},{24,28},{28,24},{1,5},{5... | collective-permute-start | bytes 2015240 | tf_op jit(solution)/shard_map/ppermute | solution.py:363
  (6 other events, 24.2 us)

commit v7 on v6

--- a/solution.py
+++ b/solution.py
@@ -477,9 +477,6 @@
     direct = packed[2 * bins_axis :]
     first = over_bins(early)
     direct = over_pts(direct)
-    late = [late[0], gate(late[1], first[1], weights), *[gate(b, *first[1:]) for b in late[2:]]]
-    second = over_bins(late)
-    came = [over_pts(couple(MAIN[0], first, late[1:]))]
     regrouped = pl.pallas_call(
         functools.partial(regroup_kernel, bins_axis, pairs),
         out_shape=[jax.ShapeDtypeStruct((rows, owners_count * slots), BF16)] * bins_axis,
@@ -488,7 +485,10 @@
         compiler_params=params(16),
         cost_estimate=cost(1, 1),
         name="regroup",
-    )(*direct, exchange(stack(direct, came[0][0]), "pts", 1))
+    )(*direct, exchange(stack(direct, first[1], first[2]), "pts", 1))
+    late = [late[0], gate(late[1], first[1], weights), *[gate(b, *first[1:]) for b in late[2:]]]
+    second = over_bins(late)
+    came = [over_pts(couple(MAIN[0], first, late[1:]))]
     regrouped = [
         regrouped[0],
         gate(regrouped[1], *second[1:], came[0][0], came[0][pairs - 1]),
@@ -498,7 +498,7 @@
     came.append(over_pts(couple(MAIN[1], second, regrouped[2:])))
     last = came[-1]
     here = couple((CHUNKS - 1,), third, [])
-    swapped = [exchange(stack(came[0], *third[2:]), "pts", 1), exchange(stack(last, here[0]), "pts", 1)]
+    swapped = [exchange(stack(came[0], last[0]), "pts", 1), exchange(stack(last, here[0]), "pts", 1)]
 
     shape = (owners_count, all_bins)
     cuts = [(c, n) for c, quarters in enumerate(MAIN) for n in range(len(quarters))]

time: 73.3 us -> 72.2 us (0.985); the launches traced: 71.9 us -> 71.9 us
  starting transfers between devices: 37.7 us -> 32.6 us
  waiting for transfers between devices: 14.4 us -> 19.4 us
    ppermute x25, starting transfers between devices: 37 us -> 32 us  [exchange(): lax.ppermute(array, axis, [(i, i ^ offset) for i in range(lax.axis_size(a...]
    ppermute x25, waiting for transfers between devices: 14.4 us -> 19.4 us  [exchange(): lax.ppermute(array, axis, [(i, i ^ offset) for i in range(lax.axis_size(a...]
  transfers between devices with their start and end apart: 26 -> 26, of which waited for: 6 -> 7; matrix products, arithmetic and copies ran while one was open for 2% -> 2% of each run, Pallas kernels for 18% -> 18%
where the time goes in v7:
time: 72.2 us; the launch traced here: 71.9 us
  starting transfers between devices  32.6 us (45%)
  waiting for transfers between devices  19.4 us (27%)
  Pallas kernels  16.3 us (23%)
  local copies, waits for them, and re-layouts  2.11 us (3%)
  other arithmetic  0.93 us (1%)
    ppermute x25, starting transfers between devices, exchange(): lax.ppermute(array, axis, [(i, i ^ offset) for i in range(lax.axis_size(a...  32 us
    ppermute x25, waiting for transfers between devices, exchange(): lax.ppermute(array, axis, [(i, i ^ offset) for i in range(lax.axis_size(a...  19.4 us
    pallas_call x3, Pallas kernels, couple(): pl.pallas_call(functools.partial(couple_kernel, quarters, bins_axis, loca...  5.69 us
    pallas_call x2, Pallas kernels, place(): pl.pallas_call(functools.partial(place_kernel, all_bins // CHUNKS, tuple(...  3.35 us
    pallas_call x1, Pallas kernels, chunked(): pl.pallas_call(functools.partial(order_kernel, bins_axis, owners_count, w...  2.61 us
    pallas_call x1, Pallas kernels, chunked(): pl.pallas_call(functools.partial(pack_kernel, rows, bins_axis, width, pai...  1.69 us
    unnamed x9, local copies, waits for them, and re-layouts  1.62 us
  transfers between devices with their start and end apart: 26, of which 7 were waited for; matrix products, arithmetic and copies ran while one was open for 2% of the time, Pallas kernels for 18%

profile of v7, /device:TPU:0, one launch (start us, length us, event | category | flops | bytes accessed | tf_op | source)
XLA Modules:
  0.0 71.9 jit_solution(8120251269283566627)
XLA Ops:
  0.0 1.6 %copy.10 = bf16[324,4,512]{2,0,1:T(8,128)(2,1)S(1)} copy(bf16[324,4,512]{2,1,0:T(4,128)(2,1)} %param.6) | data formatting | bytes 2654208 | tf_op args[0]
  3.0 4.7 %collective-permute-start.4 = (s32[1,512]{1,0:T(1,128)S(1)}, s32[1,512]{1,0:T(1,128)S(1)}, u32[]{:S(2)}, u32[]{:S(2)}) collective-permute-start(s32[1,512]{1,0:T(1,128)S(1)} %bitcast.19), channel_id=1, source_target_pairs={{0,3},{1,2},{2,1},{3,0},{4,7},{5,6},{6,5},{7,4},{8,11},{9,10},{10,... | collective-permute-start | bytes 6152 | tf_op jit(solution)/shard_map/ppermute | solution.py:363
  12.2 2.6 %order.1 = (bf16[4,336,640]{2,1,0:T(8,128)(2,1)S(1)}, bf16[4,640,128]{2,1,0:T(8,128)(2,1)S(1)}, f32[8,384]{1,0:T(8,128)S(1)}) custom-call(bf16[3,336,512]{2,1,0:T(8,128)(2,1)S(1)} %inner.1.refs_0_, s32[4,512]{1,0:T(4,128)S(1)} %copy-done.2, s32[1,512]{1,0:T(1,128)S(1)} %bitcast.22, s32[1,512]{1,0:T(1,128)S(1)} %collective-permute-done.2.refs_3_, ...), custom_call_target="tpu_custom_call" | custom-call | flops 1 | bytes 1 | tf_op jit(solution)/shard_map/order/pallas_call | solution.py:421
  14.8 1.7 %pack.1 = (bf16[328,256]{1,0:T(8,128)(2,1)S(1)}, bf16[328,256]{1,0:T(8,128)(2,1)S(1)}, bf16[328,256]{1,0:T(8,128)(2,1)S(1)}, bf16[328,256]{1,0:T(8,128)(2,1)S(1)...) custom-call(bf16[4,336,512]{2,1,0:T(8,128)(2,1)S(1)} %pad.12.planes., ...), custom_call_target="tpu_custom_call" | custom-call | flops 1 | bytes 1 | tf_op jit(solution)/shard_map/pack/pallas_call | solution.py:435
  16.7 2.9 %collective-permute-start.6 = (bf16[328,256]{1,0:T(8,128)(2,1)S(1)}, bf16[328,256]{1,0:T(8,128)(2,1)S(1)}, u32[]{:S(2)}, u32[]{:S(2)}) collective-permute-start(bf16[328,256]{1,0:T(8,128)(2,1)S(1)} %get-tuple-element.40), channel_id=1, source_target_pairs={{0,2},{1,3},{2,0},{3,1},{4,6},{5,7},{6,4},{7,5},{8,10},{9,11},{10,... | collective-permute-start | bytes 503816 | tf_op jit(solution)/shard_map/ppermute | solution.py:363
  19.6 3.3 %collective-permute-start.14 = (bf16[2,1,328,128]{3,2,1,0:T(8,128)(2,1)S(1)}, bf16[2,1,328,128]{3,2,1,0:T(8,128)(2,1)S(1)}, u32[]{:S(2)}, u32[]{:S(2)}) collective-permute-start(bf16[2,1,328,128]{3,2,1,0:T(8,128)(2,1)S(1)} %get-tuple-element.52), channel_id=1, source_target_pairs={{0,8},{4,12},{8,0},{12,4},{16,24},{20,28},{24,16},{28,20},{1,9},{5... | collective-permute-start | bytes 503816 | tf_op jit(solution)/shard_map/ppermute | solution.py:363
  23.0 1.5 %collective-permute-start.15 = (bf16[2,1,328,128]{3,2,1,0:T(8,128)(2,1)S(1)}, bf16[2,1,328,128]{3,2,1,0:T(8,128)(2,1)S(1)}, u32[]{:S(2)}, u32[]{:S(2)}) collective-permute-start(bf16[2,1,328,128]{3,2,1,0:T(8,128)(2,1)S(1)} %get-tuple-element.53), channel_id=1, source_target_pairs={{0,16},{4,20},{8,24},{12,28},{16,0},{20,4},{24,8},{28,12},{1,17},{... | collective-permute-start | bytes 503816 | tf_op jit(solution)/shard_map/ppermute | solution.py:363
  25.4 1.6 %collective-permute-done.5.refs_0_.refs_1_.refs_4_ = bf16[328,256]{1,0:T(8,128)(2,1)S(1)} collective-permute-done((bf16[328,256]{1,0:T(8,128)(2,1)S(1)}, bf16[328,256]{1,0:T(8,128)(2,1)S(1)}, u32[]{:S(2)}, u32[]{:S(2)}) %collective-permute-start.5) | collective-permute-done | bytes 167968 | tf_op jit(solution)/shard_map/ppermute | solution.py:363
  28.3 4.2 %collective-permute-done.15.refs_2_ = bf16[2,1,328,128]{3,2,1,0:T(8,128)(2,1)S(1)} collective-permute-done((bf16[2,1,328,128]{3,2,1,0:T(8,128)(2,1)S(1)}, bf16[2,1,328,128]{3,2,1,0:T(8,128)(2,1)S(1)}, u32[]{:S(2)}, u32[]{:S(2)}) %collective-permute-start.15) | collective-permute-done | bytes 167968 | tf_op jit(solution)/shard_map/ppermute | solution.py:363
  32.7 2.9 %collective-permute-done.7.refs_2_.refs_3_ = bf16[328,256]{1,0:T(8,128)(2,1)S(1)} collective-permute-done((bf16[328,256]{1,0:T(8,128)(2,1)S(1)}, bf16[328,256]{1,0:T(8,128)(2,1)S(1)}, u32[]{:S(2)}, u32[]{:S(2)}) %collective-permute-start.7) | collective-permute-done | bytes 167968 | tf_op jit(solution)/shard_map/ppermute | solution.py:363
  35.6 1.9 %couple.3 = (bf16[2,2,328,128]{3,2,1,0:T(8,128)(2,1)S(1)}, bf16[2,2,328,128]{3,2,1,0:T(8,128)(2,1)S(1)}, bf16[2,2,328,128]{3,2,1,0:T(8,128)(2,1)S(1)}, bf16[2,2,328,128]{3,2,1,0:T(8,128)(2,1)S(1)}) custom-call(bf16[328,256]{1,0:T(8,128)(2,1)S(1)} %get-tuple-element.38.refs_0_, bf16[328,256]{1,0:T(8,128)(2,1)S(1)} %collective-permute-done.5.refs_0_.refs_1_.refs_4_, ...), custom_call_target="tpu_custom_call" | custom-call | flops 3000000000 | bytes 1 | tf_op jit(solution)/shard_map/couple/pallas_call | solution.py:453
  37.6 3.2 %collective-permute-start.12 = (bf16[328,128]{1,0:T(8,128)(2,1)S(1)}, bf16[328,128]{1,0:T(8,128)(2,1)S(1)}, u32[]{:S(2)}, u32[]{:S(2)}) collective-permute-start(bf16[328,128]{1,0:T(8,128)(2,1)S(1)} %gate.7.refs_7_), channel_id=1, source_target_pairs={{0,2},{1,3},{2,0},{3,1},{4,6},{5,7},{6,4},{7,5},{8,10},{9,11},{10,... | collective-permute-start | bytes 251912 | tf_op jit(solution)/shard_map/ppermute | solution.py:363
  41.8 2.8 %collective-permute-start.8 = (bf16[2,2,328,128]{3,2,1,0:T(8,128)(2,1)S(1)}, bf16[2,2,328,128]{3,2,1,0:T(8,128)(2,1)S(1)}, u32[]{:S(2)}, u32[]{:S(2)}) collective-permute-start(bf16[2,2,328,128]{3,2,1,0:T(8,128)(2,1)S(1)} %get-tuple-element.47), channel_id=1, source_target_pairs={{0,8},{4,12},{8,0},{12,4},{16,24},{20,28},{24,16},{28,20},{1,9},{5... | collective-permute-start | bytes 1007624 | tf_op jit(solution)/shard_map/ppermute | solution.py:363
  44.9 2.4 %collective-permute-done.12.refs_1_.refs_2_ = bf16[328,128]{1,0:T(8,128)(2,1)S(1)} collective-permute-done((bf16[328,128]{1,0:T(8,128)(2,1)S(1)}, bf16[328,128]{1,0:T(8,128)(2,1)S(1)}, u32[]{:S(2)}, u32[]{:S(2)}) %collective-permute-start.12) | collective-permute-done | bytes 84000 | tf_op jit(solution)/shard_map/ppermute | solution.py:363
  47.3 1.6 %collective-permute-start.9 = (bf16[2,2,328,128]{3,2,1,0:T(8,128)(2,1)S(1)}, bf16[2,2,328,128]{3,2,1,0:T(8,128)(2,1)S(1)}, u32[]{:S(2)}, u32[]{:S(2)}) collective-permute-start(bf16[2,2,328,128]{3,2,1,0:T(8,128)(2,1)S(1)} %get-tuple-element.48), channel_id=1, source_target_pairs={{0,16},{4,20},{8,24},{12,28},{16,0},{20,4},{24,8},{28,12},{1,17},{... | collective-permute-start | bytes 1007624 | tf_op jit(solution)/shard_map/ppermute | solution.py:363
  52.7 1.6 %couple.4 = (bf16[2,1,328,128]{3,2,1,0:T(8,128)(2,1)S(1)}, bf16[2,1,328,128]{3,2,1,0:T(8,128)(2,1)S(1)}, bf16[2,1,328,128]{3,2,1,0:T(8,128)(2,1)S(1)}, bf16[2,1,328,128]{3,2,1,0:T(8,128)(2,1)S(1)}) custom-call(bf16[328,128]{1,0:T(8,128)(2,1)S(1)} %get-tuple-element.50.refs_0_, bf16[328,128]{1,0:T(8,128)(2,1)S(1)} %collective-permute-done.11.refs_0_.refs_1_, ...), custom_call_target="tpu_custom_call" | custom-call | flops 30000001024 | bytes 1 | tf_op jit(solution)/shard_map/couple/pallas_call | solution.py:453
  54.3 1.4 %collective-permute-start.19 = (bf16[2,1,328,128]{3,2,1,0:T(8,128)(2,1)S(1)}, bf16[2,1,328,128]{3,2,1,0:T(8,128)(2,1)S(1)}, u32[]{:S(2)}, u32[]{:S(2)}) collective-permute-start(bf16[2,1,328,128]{3,2,1,0:T(8,128)(2,1)S(1)} %get-tuple-element.58), channel_id=1, source_target_pairs={{0,8},{4,12},{8,0},{12,4},{16,24},{20,28},{24,16},{28,20},{1,9},{5... | collective-permute-start | bytes 503816 | tf_op jit(solution)/shard_map/ppermute | solution.py:363
  55.7 1.5 %collective-permute-start.20 = (bf16[2,1,328,128]{3,2,1,0:T(8,128)(2,1)S(1)}, bf16[2,1,328,128]{3,2,1,0:T(8,128)(2,1)S(1)}, u32[]{:S(2)}, u32[]{:S(2)}) collective-permute-start(bf16[2,1,328,128]{3,2,1,0:T(8,128)(2,1)S(1)} %get-tuple-element.59), channel_id=1, source_target_pairs={{0,16},{4,20},{8,24},{12,28},{16,0},{20,4},{24,8},{28,12},{1,17},{... | collective-permute-start | bytes 503816 | tf_op jit(solution)/shard_map/ppermute | solution.py:363
  57.3 4.7 %collective-permute-done.23.refs_2_ = bf16[328,256]{1,0:T(8,128)(2,1)S(1)} collective-permute-done((bf16[328,256]{1,0:T(8,128)(2,1)S(1)}, bf16[328,256]{1,0:T(8,128)(2,1)S(1)}, u32[]{:S(2)}, u32[]{:S(2)}) %collective-permute-start.23) | collective-permute-done | bytes 167968 | tf_op jit(solution)/shard_map/ppermute | solution.py:363
  62.0 1.9 %collective-permute-start.21 = (bf16[2,1,328,128]{3,2,1,0:T(8,128)(2,1)S(1)}, bf16[2,1,328,128]{3,2,1,0:T(8,128)(2,1)S(1)}, u32[]{:S(2)}, u32[]{:S(2)}) collective-permute-start(bf16[2,1,328,128]{3,2,1,0:T(8,128)(2,1)S(1)} %get-tuple-element.60), channel_id=1, source_target_pairs={{0,24},{4,28},{8,16},{12,20},{16,8},{20,12},{24,0},{28,4},{1,25},{... | collective-permute-start | bytes 503816 | tf_op jit(solution)/shard_map/ppermute | solution.py:363
  63.9 2.1 %couple.5 = (bf16[2,1,328,128]{3,2,1,0:T(8,128)(2,1)S(1)}, bf16[2,1,328,128]{3,2,1,0:T(8,128)(2,1)S(1)}, bf16[2,1,328,128]{3,2,1,0:T(8,128)(2,1)S(1)}, bf16[2,1,328,128]{3,2,1,0:T(8,128)(2,1)S(1)}) custom-call(bf16[328,256]{1,0:T(8,128)(2,1)S(1)} %get-tuple-element.61.refs_0_, bf16[328,256]{1,0:T(8,128)(2,1)S(1)} %collective-permute-done.22.refs_1_, ...), custom_call_target="tpu_custom_call" | custom-call | flops 30000001024 | bytes 1 | tf_op jit(solution)/shard_map/couple/pallas_call | solution.py:453
  66.1 2.2 %collective-permute-done.21.refs_3_.refs_10_ = bf16[2,1,328,128]{3,2,1,0:T(8,128)(2,1)S(1)} collective-permute-done((bf16[2,1,328,128]{3,2,1,0:T(8,128)(2,1)S(1)}, bf16[2,1,328,128]{3,2,1,0:T(8,128)(2,1)S(1)}, u32[]{:S(2)}, u32[]{:S(2)}) %collective-permute-start.21) | collective-permute-done | bytes 167968 | tf_op jit(solution)/shard_map/ppermute | solution.py:363
  68.3 1.7 %place.2.refs_6_ = bf16[1296,1024]{1,0:T(8,128)(2,1)} custom-call(bf16[2,2,328,128]{3,2,1,0:T(8,128)(2,1)S(1)} %get-tuple-element.46.refs_3_.refs_0_, bf16[2,1,328,128]{3,2,1,0:T(8,128)(2,1)S(1)} %get-tuple-element.57.refs_4_.refs_0_.refs_1_, bf16[2,1,328,128]{3,2,1,0:T(8,128)(2,1)S(1)} %get-tuple-element.63.refs_4_.refs_2_, ...), custom_call_target="tpu_custom_call" | custom-call | flops 1 | bytes 1 | tf_op jit(solution)/shard_map/place/pallas_call | solution.py:300
  70.0 1.7 %place.3 = bf16[1296,1024]{1,0:T(8,128)(2,1)} custom-call(bf16[4,2,328,128]{3,2,1,0:T(8,128)(2,1)S(1)} %collective-permute-done.18.refs_0_, bf16[4,1,328,128]{3,2,1,0:T(8,128)(2,1)S(1)} %collective-permute-done.25.refs_1_, bf16[2,1,328,128]{3,2,1,0:T(8,128)(2,1)S(1)} %get-tuple-element.63.refs_4_.refs_2_, ...), custom_call_target="tpu_custom_call", output_to_operand_aliasing={{}: (6, {})} | custom-call | flops 1 | bytes 1 | tf_op jit(solution)/shard_map/place/pallas_call | solution.py:300
  (65 shorter events, 13.5 us)
Async XLA Ops:
  1.8 7.5 %collective-permute-start.1 = (bf16[324,512]{1,0:T(8,128)(2,1)S(1)}, bf16[324,512]{1,0:T(8,128)(2,1)S(1)}, u32[]{:S(2)}, u32[]{:S(2)}) collective-permute-start(bf16[324,512]{1,0:T(8,128)(2,1)S(1)} %get-tuple-element.69), channel_id=1, source_target_pairs={{0,4},{4,0},{8,12},{12,8},{16,20},{20,16},{24,28},{28,24},{1,5},{5... | collective-permute-start | bytes 995336 | tf_op jit(solution)/shard_map/ppermute | solution.py:363
  2.3 12.5 %collective-permute-start = (bf16[324,512]{1,0:T(8,128)(2,1)S(1)}, bf16[324,512]{1,0:T(8,128)(2,1)S(1)}, u32[]{:S(2)}, u32[]{:S(2)}) collective-permute-start(bf16[324,512]{1,0:T(8,128)(2,1)S(1)} %get-tuple-element.70), channel_id=1, source_target_pairs={{4,8},{12,16},{20,24},{8,4},{16,12},{24,20},{5,9},{13,17},{21,25},... | collective-permute-start | bytes 995336 | tf_op jit(solution)/shard_map/ppermute | solution.py:390
  3.0 7.9 %collective-permute-start.4 = (s32[1,512]{1,0:T(1,128)S(1)}, s32[1,512]{1,0:T(1,128)S(1)}, u32[]{:S(2)}, u32[]{:S(2)}) collective-permute-start(s32[1,512]{1,0:T(1,128)S(1)} %bitcast.19), channel_id=1, source_target_pairs={{0,3},{1,2},{2,1},{3,0},{4,7},{5,6},{6,5},{7,4},{8,11},{9,10},{10,... | collective-permute-start | bytes 6152 | tf_op jit(solution)/shard_map/ppermute | solution.py:363
  7.7 4.5 %collective-permute-start.3 = (s32[1,512]{1,0:T(1,128)S(1)}, s32[1,512]{1,0:T(1,128)S(1)}, u32[]{:S(2)}, u32[]{:S(2)}) collective-permute-start(s32[1,512]{1,0:T(1,128)S(1)} %bitcast.20), channel_id=1, source_target_pairs={{0,2},{1,3},{2,0},{3,1},{4,6},{5,7},{6,4},{7,5},{8,10},{9,11},{10,... | collective-permute-start | bytes 6152 | tf_op jit(solution)/shard_map/ppermute | solution.py:363
  16.5 10.5 %collective-permute-start.5 = (bf16[328,256]{1,0:T(8,128)(2,1)S(1)}, bf16[328,256]{1,0:T(8,128)(2,1)S(1)}, u32[]{:S(2)}, u32[]{:S(2)}) collective-permute-start(bf16[328,256]{1,0:T(8,128)(2,1)S(1)} %get-tuple-element.39), channel_id=1, source_target_pairs={{0,1},{1,0},{2,3},{3,2},{4,5},{5,4},{6,7},{7,6},{8,9},{9,8},{10,11... | collective-permute-start | bytes 503816 | tf_op jit(solution)/shard_map/ppermute | solution.py:363
  16.7 11.6 %collective-permute-start.6 = (bf16[328,256]{1,0:T(8,128)(2,1)S(1)}, bf16[328,256]{1,0:T(8,128)(2,1)S(1)}, u32[]{:S(2)}, u32[]{:S(2)}) collective-permute-start(bf16[328,256]{1,0:T(8,128)(2,1)S(1)} %get-tuple-element.40), channel_id=1, source_target_pairs={{0,2},{1,3},{2,0},{3,1},{4,6},{5,7},{6,4},{7,5},{8,10},{9,11},{10,... | collective-permute-start | bytes 503816 | tf_op jit(solution)/shard_map/ppermute | solution.py:363
  19.6 8.7 %collective-permute-start.14 = (bf16[2,1,328,128]{3,2,1,0:T(8,128)(2,1)S(1)}, bf16[2,1,328,128]{3,2,1,0:T(8,128)(2,1)S(1)}, u32[]{:S(2)}, u32[]{:S(2)}) collective-permute-start(bf16[2,1,328,128]{3,2,1,0:T(8,128)(2,1)S(1)} %get-tuple-element.52), channel_id=1, source_target_pairs={{0,8},{4,12},{8,0},{12,4},{16,24},{20,28},{24,16},{28,20},{1,9},{5... | collective-permute-start | bytes 503816 | tf_op jit(solution)/shard_map/ppermute | solution.py:363
  23.0 9.6 %collective-permute-start.15 = (bf16[2,1,328,128]{3,2,1,0:T(8,128)(2,1)S(1)}, bf16[2,1,328,128]{3,2,1,0:T(8,128)(2,1)S(1)}, u32[]{:S(2)}, u32[]{:S(2)}) collective-permute-start(bf16[2,1,328,128]{3,2,1,0:T(8,128)(2,1)S(1)} %get-tuple-element.53), channel_id=1, source_target_pairs={{0,16},{4,20},{8,24},{12,28},{16,0},{20,4},{24,8},{28,12},{1,17},{... | collective-permute-start | bytes 503816 | tf_op jit(solution)/shard_map/ppermute | solution.py:363
  24.5 8.1 %collective-permute-start.16 = (bf16[2,1,328,128]{3,2,1,0:T(8,128)(2,1)S(1)}, bf16[2,1,328,128]{3,2,1,0:T(8,128)(2,1)S(1)}, u32[]{:S(2)}, u32[]{:S(2)}) collective-permute-start(bf16[2,1,328,128]{3,2,1,0:T(8,128)(2,1)S(1)} %get-tuple-element.54), channel_id=1, source_target_pairs={{0,24},{4,28},{8,16},{12,20},{16,8},{20,12},{24,0},{28,4},{1,25},{... | collective-permute-start | bytes 503816 | tf_op jit(solution)/shard_map/ppermute | solution.py:363
  27.0 8.6 %collective-permute-start.7 = (bf16[328,256]{1,0:T(8,128)(2,1)S(1)}, bf16[328,256]{1,0:T(8,128)(2,1)S(1)}, u32[]{:S(2)}, u32[]{:S(2)}) collective-permute-start(bf16[328,256]{1,0:T(8,128)(2,1)S(1)} %get-tuple-element.41), channel_id=1, source_target_pairs={{0,3},{1,2},{2,1},{3,0},{4,7},{5,6},{6,5},{7,4},{8,11},{9,10},{10,... | collective-permute-start | bytes 503816 | tf_op jit(solution)/shard_map/ppermute | solution.py:363
  32.6 9.2 %collective-permute-start.17 = (bf16[4,1,328,128]{3,2,1,0:T(8,128)(2,1)S(1)}, bf16[4,1,328,128]{3,2,1,0:T(8,128)(2,1)S(1)}, u32[]{:S(2)}, u32[]{:S(2)}) collective-permute-start(bf16[4,1,328,128]{3,2,1,0:T(8,128)(2,1)S(1)} %stack.3), channel_id=1, source_target_pairs={{0,4},{4,0},{8,12},{12,8},{16,20},{20,16},{24,28},{28,24},{1,5},{5... | collective-permute-start | bytes 1007624 | tf_op jit(solution)/shard_map/ppermute | solution.py:363
  37.5 13.9 %collective-permute-start.10 = (bf16[2,2,328,128]{3,2,1,0:T(8,128)(2,1)S(1)}, bf16[2,2,328,128]{3,2,1,0:T(8,128)(2,1)S(1)}, u32[]{:S(2)}, u32[]{:S(2)}) collective-permute-start(bf16[2,2,328,128]{3,2,1,0:T(8,128)(2,1)S(1)} %get-tuple-element.49), channel_id=1, source_target_pairs={{0,24},{4,28},{8,16},{12,20},{16,8},{20,12},{24,0},{28,4},{1,25},{... | collective-permute-start | bytes 1007624 | tf_op jit(solution)/shard_map/ppermute | solution.py:363
  37.6 9.7 %collective-permute-start.12 = (bf16[328,128]{1,0:T(8,128)(2,1)S(1)}, bf16[328,128]{1,0:T(8,128)(2,1)S(1)}, u32[]{:S(2)}, u32[]{:S(2)}) collective-permute-start(bf16[328,128]{1,0:T(8,128)(2,1)S(1)} %gate.7.refs_7_), channel_id=1, source_target_pairs={{0,2},{1,3},{2,0},{3,1},{4,6},{5,7},{6,4},{7,5},{8,10},{9,11},{10,... | collective-permute-start | bytes 251912 | tf_op jit(solution)/shard_map/ppermute | solution.py:363
  40.8 8.1 %collective-permute-start.13 = (bf16[328,128]{1,0:T(8,128)(2,1)S(1)}, bf16[328,128]{1,0:T(8,128)(2,1)S(1)}, u32[]{:S(2)}, u32[]{:S(2)}) collective-permute-start(bf16[328,128]{1,0:T(8,128)(2,1)S(1)} %gate.8.refs_8_), channel_id=1, source_target_pairs={{0,3},{1,2},{2,1},{3,0},{4,7},{5,6},{6,5},{7,4},{8,11},{9,10},{10,... | collective-permute-start | bytes 251912 | tf_op jit(solution)/shard_map/ppermute | solution.py:363
  41.7 7.2 %collective-permute-start.11 = (bf16[328,128]{1,0:T(8,128)(2,1)S(1)}, bf16[328,128]{1,0:T(8,128)(2,1)S(1)}, u32[]{:S(2)}, u32[]{:S(2)}) collective-permute-start(bf16[328,128]{1,0:T(8,128)(2,1)S(1)} %gate.6.refs_6_), channel_id=1, source_target_pairs={{0,1},{1,0},{2,3},{3,2},{4,5},{5,4},{6,7},{7,6},{8,9},{9,8},{10,11... | collective-permute-start | bytes 251912 | tf_op jit(solution)/shard_map/ppermute | solution.py:363
  41.8 12.6 %collective-permute-start.8 = (bf16[2,2,328,128]{3,2,1,0:T(8,128)(2,1)S(1)}, bf16[2,2,328,128]{3,2,1,0:T(8,128)(2,1)S(1)}, u32[]{:S(2)}, u32[]{:S(2)}) collective-permute-start(bf16[2,2,328,128]{3,2,1,0:T(8,128)(2,1)S(1)} %get-tuple-element.47), channel_id=1, source_target_pairs={{0,8},{4,12},{8,0},{12,4},{16,24},{20,28},{24,16},{28,20},{1,9},{5... | collective-permute-start | bytes 1007624 | tf_op jit(solution)/shard_map/ppermute | solution.py:363
  47.3 8.4 %collective-permute-start.9 = (bf16[2,2,328,128]{3,2,1,0:T(8,128)(2,1)S(1)}, bf16[2,2,328,128]{3,2,1,0:T(8,128)(2,1)S(1)}, u32[]{:S(2)}, u32[]{:S(2)}) collective-permute-start(bf16[2,2,328,128]{3,2,1,0:T(8,128)(2,1)S(1)} %get-tuple-element.48), channel_id=1, source_target_pairs={{0,16},{4,20},{8,24},{12,28},{16,0},{20,4},{24,8},{28,12},{1,17},{... | collective-permute-start | bytes 1007624 | tf_op jit(solution)/shard_map/ppermute | solution.py:363
  49.0 13.0 %collective-permute-start.23 = (bf16[328,256]{1,0:T(8,128)(2,1)S(1)}, bf16[328,256]{1,0:T(8,128)(2,1)S(1)}, u32[]{:S(2)}, u32[]{:S(2)}) collective-permute-start(bf16[328,256]{1,0:T(8,128)(2,1)S(1)} %gate.9.refs_6_), channel_id=1, source_target_pairs={{0,2},{1,3},{2,0},{3,1},{4,6},{5,7},{6,4},{7,5},{8,10},{9,11},{10,... | collective-permute-start | bytes 503816 | tf_op jit(solution)/shard_map/ppermute | solution.py:363
  50.1 13.8 %collective-permute-start.24 = (bf16[328,256]{1,0:T(8,128)(2,1)S(1)}, bf16[328,256]{1,0:T(8,128)(2,1)S(1)}, u32[]{:S(2)}, u32[]{:S(2)}) collective-permute-start(bf16[328,256]{1,0:T(8,128)(2,1)S(1)} %gate.10.refs_7_), channel_id=1, source_target_pairs={{0,3},{1,2},{2,1},{3,0},{4,7},{5,6},{6,5},{7,4},{8,11},{9,10},{10,... | collective-permute-start | bytes 503816 | tf_op jit(solution)/shard_map/ppermute | solution.py:363
  51.4 12.5 %collective-permute-start.22 = (bf16[328,256]{1,0:T(8,128)(2,1)S(1)}, bf16[328,256]{1,0:T(8,128)(2,1)S(1)}, u32[]{:S(2)}, u32[]{:S(2)}) collective-permute-start(bf16[328,256]{1,0:T(8,128)(2,1)S(1)} %gate.11), channel_id=1, source_target_pairs={{0,1},{1,0},{2,3},{3,2},{4,5},{5,4},{6,7},{7,6},{8,9},{9,8},{10,11... | collective-permute-start | bytes 503816 | tf_op jit(solution)/shard_map/ppermute | solution.py:363
  54.3 11.7 %collective-permute-start.19 = (bf16[2,1,328,128]{3,2,1,0:T(8,128)(2,1)S(1)}, bf16[2,1,328,128]{3,2,1,0:T(8,128)(2,1)S(1)}, u32[]{:S(2)}, u32[]{:S(2)}) collective-permute-start(bf16[2,1,328,128]{3,2,1,0:T(8,128)(2,1)S(1)} %get-tuple-element.58), channel_id=1, source_target_pairs={{0,8},{4,12},{8,0},{12,4},{16,24},{20,28},{24,16},{28,20},{1,9},{5... | collective-permute-start | bytes 503816 | tf_op jit(solution)/shard_map/ppermute | solution.py:363
  55.7 10.3 %collective-permute-start.20 = (bf16[2,1,328,128]{3,2,1,0:T(8,128)(2,1)S(1)}, bf16[2,1,328,128]{3,2,1,0:T(8,128)(2,1)S(1)}, u32[]{:S(2)}, u32[]{:S(2)}) collective-permute-start(bf16[2,1,328,128]{3,2,1,0:T(8,128)(2,1)S(1)} %get-tuple-element.59), channel_id=1, source_target_pairs={{0,16},{4,20},{8,24},{12,28},{16,0},{20,4},{24,8},{28,12},{1,17},{... | collective-permute-start | bytes 503816 | tf_op jit(solution)/shard_map/ppermute | solution.py:363
  62.0 6.3 %collective-permute-start.21 = (bf16[2,1,328,128]{3,2,1,0:T(8,128)(2,1)S(1)}, bf16[2,1,328,128]{3,2,1,0:T(8,128)(2,1)S(1)}, u32[]{:S(2)}, u32[]{:S(2)}) collective-permute-start(bf16[2,1,328,128]{3,2,1,0:T(8,128)(2,1)S(1)} %get-tuple-element.60), channel_id=1, source_target_pairs={{0,24},{4,28},{8,16},{12,20},{16,8},{20,12},{24,0},{28,4},{1,25},{... | collective-permute-start | bytes 503816 | tf_op jit(solution)/shard_map/ppermute | solution.py:363
  63.9 6.1 %collective-permute-start.18 = (bf16[4,2,328,128]{3,2,1,0:T(8,128)(2,1)S(1)}, bf16[4,2,328,128]{3,2,1,0:T(8,128)(2,1)S(1)}, u32[]{:S(2)}, u32[]{:S(2)}) collective-permute-start(bf16[4,2,328,128]{3,2,1,0:T(8,128)(2,1)S(1)} %stack.4), channel_id=1, source_target_pairs={{0,4},{4,0},{8,12},{12,8},{16,20},{20,16},{24,28},{28,24},{1,5},{5... | collective-permute-start | bytes 2015240 | tf_op jit(solution)/shard_map/ppermute | solution.py:363
  (6 other events, 29.8 us)

commit v8 on v7

--- a/solution.py
+++ b/solution.py
@@ -589,7 +589,7 @@
         and bins_axis & (bins_axis - 1) == 0
         and owners_count & (owners_count - 1) == 0
         and bins_axis % 2 == 0
-        and spectrum.shape[0] % 8 == 4
+        and spectrum.shape[0] % 16 == 4
         and courant.shape[0] % 144 == 0
         and courant.shape[0] // CHUNKS % 8 == 4
         and points == CHUNKS * LANES

time: 72.2 us -> 72.2 us (level)
  no operation moved by 1% of the time
where the time goes in v8:
time: 72.2 us; the launch traced here: 71.9 us
  starting transfers between devices  32.6 us (45%)
  waiting for transfers between devices  19.4 us (27%)
  Pallas kernels  16.3 us (23%)
  local copies, waits for them, and re-layouts  2.11 us (3%)
  other arithmetic  0.93 us (1%)
    ppermute x25, starting transfers between devices, exchange(): lax.ppermute(array, axis, [(i, i ^ offset) for i in range(lax.axis_size(a...  32 us
    ppermute x25, waiting for transfers between devices, exchange(): lax.ppermute(array, axis, [(i, i ^ offset) for i in range(lax.axis_size(a...  19.4 us
    pallas_call x3, Pallas kernels, couple(): pl.pallas_call(functools.partial(couple_kernel, quarters, bins_axis, loca...  5.69 us
    pallas_call x2, Pallas kernels, place(): pl.pallas_call(functools.partial(place_kernel, all_bins // CHUNKS, tuple(...  3.35 us
    pallas_call x1, Pallas kernels, chunked(): pl.pallas_call(functools.partial(order_kernel, bins_axis, owners_count, w...  2.61 us
    pallas_call x1, Pallas kernels, chunked(): pl.pallas_call(functools.partial(pack_kernel, rows, bins_axis, width, pai...  1.69 us
    unnamed x9, local copies, waits for them, and re-layouts  1.62 us
  transfers between devices with their start and end apart: 26, of which 7 were waited for; matrix products, arithmetic and copies ran while one was open for 2% of the time, Pallas kernels for 18%

profile of v8, /device:TPU:0, one launch (start us, length us, event | category | flops | bytes accessed | tf_op | source)
XLA Modules:
  0.0 71.9 jit_solution(8120251269283566627)
XLA Ops:
  0.0 1.6 %copy.10 = bf16[324,4,512]{2,0,1:T(8,128)(2,1)S(1)} copy(bf16[324,4,512]{2,1,0:T(4,128)(2,1)} %param.6) | data formatting | bytes 2654208 | tf_op args[0]
  3.0 4.7 %collective-permute-start.4 = (s32[1,512]{1,0:T(1,128)S(1)}, s32[1,512]{1,0:T(1,128)S(1)}, u32[]{:S(2)}, u32[]{:S(2)}) collective-permute-start(s32[1,512]{1,0:T(1,128)S(1)} %bitcast.19), channel_id=1, source_target_pairs={{0,3},{1,2},{2,1},{3,0},{4,7},{5,6},{6,5},{7,4},{8,11},{9,10},{10,... | collective-permute-start | bytes 6152 | tf_op jit(solution)/shard_map/ppermute | solution.py:363
  12.2 2.6 %order.1 = (bf16[4,336,640]{2,1,0:T(8,128)(2,1)S(1)}, bf16[4,640,128]{2,1,0:T(8,128)(2,1)S(1)}, f32[8,384]{1,0:T(8,128)S(1)}) custom-call(bf16[3,336,512]{2,1,0:T(8,128)(2,1)S(1)} %inner.1.refs_0_, s32[4,512]{1,0:T(4,128)S(1)} %copy-done.2, s32[1,512]{1,0:T(1,128)S(1)} %bitcast.22, s32[1,512]{1,0:T(1,128)S(1)} %collective-permute-done.2.refs_3_, ...), custom_call_target="tpu_custom_call" | custom-call | flops 1 | bytes 1 | tf_op jit(solution)/shard_map/order/pallas_call | solution.py:421
  14.8 1.7 %pack.1 = (bf16[328,256]{1,0:T(8,128)(2,1)S(1)}, bf16[328,256]{1,0:T(8,128)(2,1)S(1)}, bf16[328,256]{1,0:T(8,128)(2,1)S(1)}, bf16[328,256]{1,0:T(8,128)(2,1)S(1)...) custom-call(bf16[4,336,512]{2,1,0:T(8,128)(2,1)S(1)} %pad.12.planes., ...), custom_call_target="tpu_custom_call" | custom-call | flops 1 | bytes 1 | tf_op jit(solution)/shard_map/pack/pallas_call | solution.py:435
  16.7 2.9 %collective-permute-start.6 = (bf16[328,256]{1,0:T(8,128)(2,1)S(1)}, bf16[328,256]{1,0:T(8,128)(2,1)S(1)}, u32[]{:S(2)}, u32[]{:S(2)}) collective-permute-start(bf16[328,256]{1,0:T(8,128)(2,1)S(1)} %get-tuple-element.40), channel_id=1, source_target_pairs={{0,2},{1,3},{2,0},{3,1},{4,6},{5,7},{6,4},{7,5},{8,10},{9,11},{10,... | collective-permute-start | bytes 503816 | tf_op jit(solution)/shard_map/ppermute | solution.py:363
  19.6 3.3 %collective-permute-start.14 = (bf16[2,1,328,128]{3,2,1,0:T(8,128)(2,1)S(1)}, bf16[2,1,328,128]{3,2,1,0:T(8,128)(2,1)S(1)}, u32[]{:S(2)}, u32[]{:S(2)}) collective-permute-start(bf16[2,1,328,128]{3,2,1,0:T(8,128)(2,1)S(1)} %get-tuple-element.52), channel_id=1, source_target_pairs={{0,8},{4,12},{8,0},{12,4},{16,24},{20,28},{24,16},{28,20},{1,9},{5... | collective-permute-start | bytes 503816 | tf_op jit(solution)/shard_map/ppermute | solution.py:363
  23.0 1.5 %collective-permute-start.15 = (bf16[2,1,328,128]{3,2,1,0:T(8,128)(2,1)S(1)}, bf16[2,1,328,128]{3,2,1,0:T(8,128)(2,1)S(1)}, u32[]{:S(2)}, u32[]{:S(2)}) collective-permute-start(bf16[2,1,328,128]{3,2,1,0:T(8,128)(2,1)S(1)} %get-tuple-element.53), channel_id=1, source_target_pairs={{0,16},{4,20},{8,24},{12,28},{16,0},{20,4},{24,8},{28,12},{1,17},{... | collective-permute-start | bytes 503816 | tf_op jit(solution)/shard_map/ppermute | solution.py:363
  25.4 1.6 %collective-permute-done.5.refs_0_.refs_1_.refs_4_ = bf16[328,256]{1,0:T(8,128)(2,1)S(1)} collective-permute-done((bf16[328,256]{1,0:T(8,128)(2,1)S(1)}, bf16[328,256]{1,0:T(8,128)(2,1)S(1)}, u32[]{:S(2)}, u32[]{:S(2)}) %collective-permute-start.5) | collective-permute-done | bytes 167968 | tf_op jit(solution)/shard_map/ppermute | solution.py:363
  28.3 4.2 %collective-permute-done.15.refs_2_ = bf16[2,1,328,128]{3,2,1,0:T(8,128)(2,1)S(1)} collective-permute-done((bf16[2,1,328,128]{3,2,1,0:T(8,128)(2,1)S(1)}, bf16[2,1,328,128]{3,2,1,0:T(8,128)(2,1)S(1)}, u32[]{:S(2)}, u32[]{:S(2)}) %collective-permute-start.15) | collective-permute-done | bytes 167968 | tf_op jit(solution)/shard_map/ppermute | solution.py:363
  32.7 2.9 %collective-permute-done.7.refs_2_.refs_3_ = bf16[328,256]{1,0:T(8,128)(2,1)S(1)} collective-permute-done((bf16[328,256]{1,0:T(8,128)(2,1)S(1)}, bf16[328,256]{1,0:T(8,128)(2,1)S(1)}, u32[]{:S(2)}, u32[]{:S(2)}) %collective-permute-start.7) | collective-permute-done | bytes 167968 | tf_op jit(solution)/shard_map/ppermute | solution.py:363
  35.6 1.9 %couple.3 = (bf16[2,2,328,128]{3,2,1,0:T(8,128)(2,1)S(1)}, bf16[2,2,328,128]{3,2,1,0:T(8,128)(2,1)S(1)}, bf16[2,2,328,128]{3,2,1,0:T(8,128)(2,1)S(1)}, bf16[2,2,328,128]{3,2,1,0:T(8,128)(2,1)S(1)}) custom-call(bf16[328,256]{1,0:T(8,128)(2,1)S(1)} %get-tuple-element.38.refs_0_, bf16[328,256]{1,0:T(8,128)(2,1)S(1)} %collective-permute-done.5.refs_0_.refs_1_.refs_4_, ...), custom_call_target="tpu_custom_call" | custom-call | flops 3000000000 | bytes 1 | tf_op jit(solution)/shard_map/couple/pallas_call | solution.py:453
  37.6 3.2 %collective-permute-start.12 = (bf16[328,128]{1,0:T(8,128)(2,1)S(1)}, bf16[328,128]{1,0:T(8,128)(2,1)S(1)}, u32[]{:S(2)}, u32[]{:S(2)}) collective-permute-start(bf16[328,128]{1,0:T(8,128)(2,1)S(1)} %gate.7.refs_7_), channel_id=1, source_target_pairs={{0,2},{1,3},{2,0},{3,1},{4,6},{5,7},{6,4},{7,5},{8,10},{9,11},{10,... | collective-permute-start | bytes 251912 | tf_op jit(solution)/shard_map/ppermute | solution.py:363
  41.8 2.8 %collective-permute-start.8 = (bf16[2,2,328,128]{3,2,1,0:T(8,128)(2,1)S(1)}, bf16[2,2,328,128]{3,2,1,0:T(8,128)(2,1)S(1)}, u32[]{:S(2)}, u32[]{:S(2)}) collective-permute-start(bf16[2,2,328,128]{3,2,1,0:T(8,128)(2,1)S(1)} %get-tuple-element.47), channel_id=1, source_target_pairs={{0,8},{4,12},{8,0},{12,4},{16,24},{20,28},{24,16},{28,20},{1,9},{5... | collective-permute-start | bytes 1007624 | tf_op jit(solution)/shard_map/ppermute | solution.py:363
  44.9 2.4 %collective-permute-done.12.refs_1_.refs_2_ = bf16[328,128]{1,0:T(8,128)(2,1)S(1)} collective-permute-done((bf16[328,128]{1,0:T(8,128)(2,1)S(1)}, bf16[328,128]{1,0:T(8,128)(2,1)S(1)}, u32[]{:S(2)}, u32[]{:S(2)}) %collective-permute-start.12) | collective-permute-done | bytes 84000 | tf_op jit(solution)/shard_map/ppermute | solution.py:363
  47.3 1.6 %collective-permute-start.9 = (bf16[2,2,328,128]{3,2,1,0:T(8,128)(2,1)S(1)}, bf16[2,2,328,128]{3,2,1,0:T(8,128)(2,1)S(1)}, u32[]{:S(2)}, u32[]{:S(2)}) collective-permute-start(bf16[2,2,328,128]{3,2,1,0:T(8,128)(2,1)S(1)} %get-tuple-element.48), channel_id=1, source_target_pairs={{0,16},{4,20},{8,24},{12,28},{16,0},{20,4},{24,8},{28,12},{1,17},{... | collective-permute-start | bytes 1007624 | tf_op jit(solution)/shard_map/ppermute | solution.py:363
  52.7 1.6 %couple.4 = (bf16[2,1,328,128]{3,2,1,0:T(8,128)(2,1)S(1)}, bf16[2,1,328,128]{3,2,1,0:T(8,128)(2,1)S(1)}, bf16[2,1,328,128]{3,2,1,0:T(8,128)(2,1)S(1)}, bf16[2,1,328,128]{3,2,1,0:T(8,128)(2,1)S(1)}) custom-call(bf16[328,128]{1,0:T(8,128)(2,1)S(1)} %get-tuple-element.50.refs_0_, bf16[328,128]{1,0:T(8,128)(2,1)S(1)} %collective-permute-done.11.refs_0_.refs_1_, ...), custom_call_target="tpu_custom_call" | custom-call | flops 30000001024 | bytes 1 | tf_op jit(solution)/shard_map/couple/pallas_call | solution.py:453
  54.3 1.4 %collective-permute-start.19 = (bf16[2,1,328,128]{3,2,1,0:T(8,128)(2,1)S(1)}, bf16[2,1,328,128]{3,2,1,0:T(8,128)(2,1)S(1)}, u32[]{:S(2)}, u32[]{:S(2)}) collective-permute-start(bf16[2,1,328,128]{3,2,1,0:T(8,128)(2,1)S(1)} %get-tuple-element.58), channel_id=1, source_target_pairs={{0,8},{4,12},{8,0},{12,4},{16,24},{20,28},{24,16},{28,20},{1,9},{5... | collective-permute-start | bytes 503816 | tf_op jit(solution)/shard_map/ppermute | solution.py:363
  55.7 1.5 %collective-permute-start.20 = (bf16[2,1,328,128]{3,2,1,0:T(8,128)(2,1)S(1)}, bf16[2,1,328,128]{3,2,1,0:T(8,128)(2,1)S(1)}, u32[]{:S(2)}, u32[]{:S(2)}) collective-permute-start(bf16[2,1,328,128]{3,2,1,0:T(8,128)(2,1)S(1)} %get-tuple-element.59), channel_id=1, source_target_pairs={{0,16},{4,20},{8,24},{12,28},{16,0},{20,4},{24,8},{28,12},{1,17},{... | collective-permute-start | bytes 503816 | tf_op jit(solution)/shard_map/ppermute | solution.py:363
  57.3 4.7 %collective-permute-done.23.refs_2_ = bf16[328,256]{1,0:T(8,128)(2,1)S(1)} collective-permute-done((bf16[328,256]{1,0:T(8,128)(2,1)S(1)}, bf16[328,256]{1,0:T(8,128)(2,1)S(1)}, u32[]{:S(2)}, u32[]{:S(2)}) %collective-permute-start.23) | collective-permute-done | bytes 167968 | tf_op jit(solution)/shard_map/ppermute | solution.py:363
  62.0 1.9 %collective-permute-start.21 = (bf16[2,1,328,128]{3,2,1,0:T(8,128)(2,1)S(1)}, bf16[2,1,328,128]{3,2,1,0:T(8,128)(2,1)S(1)}, u32[]{:S(2)}, u32[]{:S(2)}) collective-permute-start(bf16[2,1,328,128]{3,2,1,0:T(8,128)(2,1)S(1)} %get-tuple-element.60), channel_id=1, source_target_pairs={{0,24},{4,28},{8,16},{12,20},{16,8},{20,12},{24,0},{28,4},{1,25},{... | collective-permute-start | bytes 503816 | tf_op jit(solution)/shard_map/ppermute | solution.py:363
  63.9 2.1 %couple.5 = (bf16[2,1,328,128]{3,2,1,0:T(8,128)(2,1)S(1)}, bf16[2,1,328,128]{3,2,1,0:T(8,128)(2,1)S(1)}, bf16[2,1,328,128]{3,2,1,0:T(8,128)(2,1)S(1)}, bf16[2,1,328,128]{3,2,1,0:T(8,128)(2,1)S(1)}) custom-call(bf16[328,256]{1,0:T(8,128)(2,1)S(1)} %get-tuple-element.61.refs_0_, bf16[328,256]{1,0:T(8,128)(2,1)S(1)} %collective-permute-done.22.refs_1_, ...), custom_call_target="tpu_custom_call" | custom-call | flops 30000001024 | bytes 1 | tf_op jit(solution)/shard_map/couple/pallas_call | solution.py:453
  66.1 2.2 %collective-permute-done.21.refs_3_.refs_10_ = bf16[2,1,328,128]{3,2,1,0:T(8,128)(2,1)S(1)} collective-permute-done((bf16[2,1,328,128]{3,2,1,0:T(8,128)(2,1)S(1)}, bf16[2,1,328,128]{3,2,1,0:T(8,128)(2,1)S(1)}, u32[]{:S(2)}, u32[]{:S(2)}) %collective-permute-start.21) | collective-permute-done | bytes 167968 | tf_op jit(solution)/shard_map/ppermute | solution.py:363
  68.3 1.7 %place.2.refs_6_ = bf16[1296,1024]{1,0:T(8,128)(2,1)} custom-call(bf16[2,2,328,128]{3,2,1,0:T(8,128)(2,1)S(1)} %get-tuple-element.46.refs_3_.refs_0_, bf16[2,1,328,128]{3,2,1,0:T(8,128)(2,1)S(1)} %get-tuple-element.57.refs_4_.refs_0_.refs_1_, bf16[2,1,328,128]{3,2,1,0:T(8,128)(2,1)S(1)} %get-tuple-element.63.refs_4_.refs_2_, ...), custom_call_target="tpu_custom_call" | custom-call | flops 1 | bytes 1 | tf_op jit(solution)/shard_map/place/pallas_call | solution.py:300
  70.0 1.7 %place.3 = bf16[1296,1024]{1,0:T(8,128)(2,1)} custom-call(bf16[4,2,328,128]{3,2,1,0:T(8,128)(2,1)S(1)} %collective-permute-done.18.refs_0_, bf16[4,1,328,128]{3,2,1,0:T(8,128)(2,1)S(1)} %collective-permute-done.25.refs_1_, bf16[2,1,328,128]{3,2,1,0:T(8,128)(2,1)S(1)} %get-tuple-element.63.refs_4_.refs_2_, ...), custom_call_target="tpu_custom_call", output_to_operand_aliasing={{}: (6, {})} | custom-call | flops 1 | bytes 1 | tf_op jit(solution)/shard_map/place/pallas_call | solution.py:300
  (65 shorter events, 13.5 us)
Async XLA Ops:
  1.8 7.5 %collective-permute-start.1 = (bf16[324,512]{1,0:T(8,128)(2,1)S(1)}, bf16[324,512]{1,0:T(8,128)(2,1)S(1)}, u32[]{:S(2)}, u32[]{:S(2)}) collective-permute-start(bf16[324,512]{1,0:T(8,128)(2,1)S(1)} %get-tuple-element.69), channel_id=1, source_target_pairs={{0,4},{4,0},{8,12},{12,8},{16,20},{20,16},{24,28},{28,24},{1,5},{5... | collective-permute-start | bytes 995336 | tf_op jit(solution)/shard_map/ppermute | solution.py:363
  2.3 12.5 %collective-permute-start = (bf16[324,512]{1,0:T(8,128)(2,1)S(1)}, bf16[324,512]{1,0:T(8,128)(2,1)S(1)}, u32[]{:S(2)}, u32[]{:S(2)}) collective-permute-start(bf16[324,512]{1,0:T(8,128)(2,1)S(1)} %get-tuple-element.70), channel_id=1, source_target_pairs={{4,8},{12,16},{20,24},{8,4},{16,12},{24,20},{5,9},{13,17},{21,25},... | collective-permute-start | bytes 995336 | tf_op jit(solution)/shard_map/ppermute | solution.py:390
  3.0 7.9 %collective-permute-start.4 = (s32[1,512]{1,0:T(1,128)S(1)}, s32[1,512]{1,0:T(1,128)S(1)}, u32[]{:S(2)}, u32[]{:S(2)}) collective-permute-start(s32[1,512]{1,0:T(1,128)S(1)} %bitcast.19), channel_id=1, source_target_pairs={{0,3},{1,2},{2,1},{3,0},{4,7},{5,6},{6,5},{7,4},{8,11},{9,10},{10,... | collective-permute-start | bytes 6152 | tf_op jit(solution)/shard_map/ppermute | solution.py:363
  7.7 4.5 %collective-permute-start.3 = (s32[1,512]{1,0:T(1,128)S(1)}, s32[1,512]{1,0:T(1,128)S(1)}, u32[]{:S(2)}, u32[]{:S(2)}) collective-permute-start(s32[1,512]{1,0:T(1,128)S(1)} %bitcast.20), channel_id=1, source_target_pairs={{0,2},{1,3},{2,0},{3,1},{4,6},{5,7},{6,4},{7,5},{8,10},{9,11},{10,... | collective-permute-start | bytes 6152 | tf_op jit(solution)/shard_map/ppermute | solution.py:363
  16.5 10.5 %collective-permute-start.5 = (bf16[328,256]{1,0:T(8,128)(2,1)S(1)}, bf16[328,256]{1,0:T(8,128)(2,1)S(1)}, u32[]{:S(2)}, u32[]{:S(2)}) collective-permute-start(bf16[328,256]{1,0:T(8,128)(2,1)S(1)} %get-tuple-element.39), channel_id=1, source_target_pairs={{0,1},{1,0},{2,3},{3,2},{4,5},{5,4},{6,7},{7,6},{8,9},{9,8},{10,11... | collective-permute-start | bytes 503816 | tf_op jit(solution)/shard_map/ppermute | solution.py:363
  16.7 11.6 %collective-permute-start.6 = (bf16[328,256]{1,0:T(8,128)(2,1)S(1)}, bf16[328,256]{1,0:T(8,128)(2,1)S(1)}, u32[]{:S(2)}, u32[]{:S(2)}) collective-permute-start(bf16[328,256]{1,0:T(8,128)(2,1)S(1)} %get-tuple-element.40), channel_id=1, source_target_pairs={{0,2},{1,3},{2,0},{3,1},{4,6},{5,7},{6,4},{7,5},{8,10},{9,11},{10,... | collective-permute-start | bytes 503816 | tf_op jit(solution)/shard_map/ppermute | solution.py:363
  19.6 8.7 %collective-permute-start.14 = (bf16[2,1,328,128]{3,2,1,0:T(8,128)(2,1)S(1)}, bf16[2,1,328,128]{3,2,1,0:T(8,128)(2,1)S(1)}, u32[]{:S(2)}, u32[]{:S(2)}) collective-permute-start(bf16[2,1,328,128]{3,2,1,0:T(8,128)(2,1)S(1)} %get-tuple-element.52), channel_id=1, source_target_pairs={{0,8},{4,12},{8,0},{12,4},{16,24},{20,28},{24,16},{28,20},{1,9},{5... | collective-permute-start | bytes 503816 | tf_op jit(solution)/shard_map/ppermute | solution.py:363
  23.0 9.6 %collective-permute-start.15 = (bf16[2,1,328,128]{3,2,1,0:T(8,128)(2,1)S(1)}, bf16[2,1,328,128]{3,2,1,0:T(8,128)(2,1)S(1)}, u32[]{:S(2)}, u32[]{:S(2)}) collective-permute-start(bf16[2,1,328,128]{3,2,1,0:T(8,128)(2,1)S(1)} %get-tuple-element.53), channel_id=1, source_target_pairs={{0,16},{4,20},{8,24},{12,28},{16,0},{20,4},{24,8},{28,12},{1,17},{... | collective-permute-start | bytes 503816 | tf_op jit(solution)/shard_map/ppermute | solution.py:363
  24.5 8.1 %collective-permute-start.16 = (bf16[2,1,328,128]{3,2,1,0:T(8,128)(2,1)S(1)}, bf16[2,1,328,128]{3,2,1,0:T(8,128)(2,1)S(1)}, u32[]{:S(2)}, u32[]{:S(2)}) collective-permute-start(bf16[2,1,328,128]{3,2,1,0:T(8,128)(2,1)S(1)} %get-tuple-element.54), channel_id=1, source_target_pairs={{0,24},{4,28},{8,16},{12,20},{16,8},{20,12},{24,0},{28,4},{1,25},{... | collective-permute-start | bytes 503816 | tf_op jit(solution)/shard_map/ppermute | solution.py:363
  27.0 8.6 %collective-permute-start.7 = (bf16[328,256]{1,0:T(8,128)(2,1)S(1)}, bf16[328,256]{1,0:T(8,128)(2,1)S(1)}, u32[]{:S(2)}, u32[]{:S(2)}) collective-permute-start(bf16[328,256]{1,0:T(8,128)(2,1)S(1)} %get-tuple-element.41), channel_id=1, source_target_pairs={{0,3},{1,2},{2,1},{3,0},{4,7},{5,6},{6,5},{7,4},{8,11},{9,10},{10,... | collective-permute-start | bytes 503816 | tf_op jit(solution)/shard_map/ppermute | solution.py:363
  32.6 9.2 %collective-permute-start.17 = (bf16[4,1,328,128]{3,2,1,0:T(8,128)(2,1)S(1)}, bf16[4,1,328,128]{3,2,1,0:T(8,128)(2,1)S(1)}, u32[]{:S(2)}, u32[]{:S(2)}) collective-permute-start(bf16[4,1,328,128]{3,2,1,0:T(8,128)(2,1)S(1)} %stack.3), channel_id=1, source_target_pairs={{0,4},{4,0},{8,12},{12,8},{16,20},{20,16},{24,28},{28,24},{1,5},{5... | collective-permute-start | bytes 1007624 | tf_op jit(solution)/shard_map/ppermute | solution.py:363
  37.5 13.9 %collective-permute-start.10 = (bf16[2,2,328,128]{3,2,1,0:T(8,128)(2,1)S(1)}, bf16[2,2,328,128]{3,2,1,0:T(8,128)(2,1)S(1)}, u32[]{:S(2)}, u32[]{:S(2)}) collective-permute-start(bf16[2,2,328,128]{3,2,1,0:T(8,128)(2,1)S(1)} %get-tuple-element.49), channel_id=1, source_target_pairs={{0,24},{4,28},{8,16},{12,20},{16,8},{20,12},{24,0},{28,4},{1,25},{... | collective-permute-start | bytes 1007624 | tf_op jit(solution)/shard_map/ppermute | solution.py:363
  37.6 9.7 %collective-permute-start.12 = (bf16[328,128]{1,0:T(8,128)(2,1)S(1)}, bf16[328,128]{1,0:T(8,128)(2,1)S(1)}, u32[]{:S(2)}, u32[]{:S(2)}) collective-permute-start(bf16[328,128]{1,0:T(8,128)(2,1)S(1)} %gate.7.refs_7_), channel_id=1, source_target_pairs={{0,2},{1,3},{2,0},{3,1},{4,6},{5,7},{6,4},{7,5},{8,10},{9,11},{10,... | collective-permute-start | bytes 251912 | tf_op jit(solution)/shard_map/ppermute | solution.py:363
  40.8 8.1 %collective-permute-start.13 = (bf16[328,128]{1,0:T(8,128)(2,1)S(1)}, bf16[328,128]{1,0:T(8,128)(2,1)S(1)}, u32[]{:S(2)}, u32[]{:S(2)}) collective-permute-start(bf16[328,128]{1,0:T(8,128)(2,1)S(1)} %gate.8.refs_8_), channel_id=1, source_target_pairs={{0,3},{1,2},{2,1},{3,0},{4,7},{5,6},{6,5},{7,4},{8,11},{9,10},{10,... | collective-permute-start | bytes 251912 | tf_op jit(solution)/shard_map/ppermute | solution.py:363
  41.7 7.2 %collective-permute-start.11 = (bf16[328,128]{1,0:T(8,128)(2,1)S(1)}, bf16[328,128]{1,0:T(8,128)(2,1)S(1)}, u32[]{:S(2)}, u32[]{:S(2)}) collective-permute-start(bf16[328,128]{1,0:T(8,128)(2,1)S(1)} %gate.6.refs_6_), channel_id=1, source_target_pairs={{0,1},{1,0},{2,3},{3,2},{4,5},{5,4},{6,7},{7,6},{8,9},{9,8},{10,11... | collective-permute-start | bytes 251912 | tf_op jit(solution)/shard_map/ppermute | solution.py:363
  41.8 12.6 %collective-permute-start.8 = (bf16[2,2,328,128]{3,2,1,0:T(8,128)(2,1)S(1)}, bf16[2,2,328,128]{3,2,1,0:T(8,128)(2,1)S(1)}, u32[]{:S(2)}, u32[]{:S(2)}) collective-permute-start(bf16[2,2,328,128]{3,2,1,0:T(8,128)(2,1)S(1)} %get-tuple-element.47), channel_id=1, source_target_pairs={{0,8},{4,12},{8,0},{12,4},{16,24},{20,28},{24,16},{28,20},{1,9},{5... | collective-permute-start | bytes 1007624 | tf_op jit(solution)/shard_map/ppermute | solution.py:363
  47.3 8.4 %collective-permute-start.9 = (bf16[2,2,328,128]{3,2,1,0:T(8,128)(2,1)S(1)}, bf16[2,2,328,128]{3,2,1,0:T(8,128)(2,1)S(1)}, u32[]{:S(2)}, u32[]{:S(2)}) collective-permute-start(bf16[2,2,328,128]{3,2,1,0:T(8,128)(2,1)S(1)} %get-tuple-element.48), channel_id=1, source_target_pairs={{0,16},{4,20},{8,24},{12,28},{16,0},{20,4},{24,8},{28,12},{1,17},{... | collective-permute-start | bytes 1007624 | tf_op jit(solution)/shard_map/ppermute | solution.py:363
  49.0 13.0 %collective-permute-start.23 = (bf16[328,256]{1,0:T(8,128)(2,1)S(1)}, bf16[328,256]{1,0:T(8,128)(2,1)S(1)}, u32[]{:S(2)}, u32[]{:S(2)}) collective-permute-start(bf16[328,256]{1,0:T(8,128)(2,1)S(1)} %gate.9.refs_6_), channel_id=1, source_target_pairs={{0,2},{1,3},{2,0},{3,1},{4,6},{5,7},{6,4},{7,5},{8,10},{9,11},{10,... | collective-permute-start | bytes 503816 | tf_op jit(solution)/shard_map/ppermute | solution.py:363
  50.1 13.8 %collective-permute-start.24 = (bf16[328,256]{1,0:T(8,128)(2,1)S(1)}, bf16[328,256]{1,0:T(8,128)(2,1)S(1)}, u32[]{:S(2)}, u32[]{:S(2)}) collective-permute-start(bf16[328,256]{1,0:T(8,128)(2,1)S(1)} %gate.10.refs_7_), channel_id=1, source_target_pairs={{0,3},{1,2},{2,1},{3,0},{4,7},{5,6},{6,5},{7,4},{8,11},{9,10},{10,... | collective-permute-start | bytes 503816 | tf_op jit(solution)/shard_map/ppermute | solution.py:363
  51.4 12.5 %collective-permute-start.22 = (bf16[328,256]{1,0:T(8,128)(2,1)S(1)}, bf16[328,256]{1,0:T(8,128)(2,1)S(1)}, u32[]{:S(2)}, u32[]{:S(2)}) collective-permute-start(bf16[328,256]{1,0:T(8,128)(2,1)S(1)} %gate.11), channel_id=1, source_target_pairs={{0,1},{1,0},{2,3},{3,2},{4,5},{5,4},{6,7},{7,6},{8,9},{9,8},{10,11... | collective-permute-start | bytes 503816 | tf_op jit(solution)/shard_map/ppermute | solution.py:363
  54.3 11.7 %collective-permute-start.19 = (bf16[2,1,328,128]{3,2,1,0:T(8,128)(2,1)S(1)}, bf16[2,1,328,128]{3,2,1,0:T(8,128)(2,1)S(1)}, u32[]{:S(2)}, u32[]{:S(2)}) collective-permute-start(bf16[2,1,328,128]{3,2,1,0:T(8,128)(2,1)S(1)} %get-tuple-element.58), channel_id=1, source_target_pairs={{0,8},{4,12},{8,0},{12,4},{16,24},{20,28},{24,16},{28,20},{1,9},{5... | collective-permute-start | bytes 503816 | tf_op jit(solution)/shard_map/ppermute | solution.py:363
  55.7 10.3 %collective-permute-start.20 = (bf16[2,1,328,128]{3,2,1,0:T(8,128)(2,1)S(1)}, bf16[2,1,328,128]{3,2,1,0:T(8,128)(2,1)S(1)}, u32[]{:S(2)}, u32[]{:S(2)}) collective-permute-start(bf16[2,1,328,128]{3,2,1,0:T(8,128)(2,1)S(1)} %get-tuple-element.59), channel_id=1, source_target_pairs={{0,16},{4,20},{8,24},{12,28},{16,0},{20,4},{24,8},{28,12},{1,17},{... | collective-permute-start | bytes 503816 | tf_op jit(solution)/shard_map/ppermute | solution.py:363
  62.0 6.3 %collective-permute-start.21 = (bf16[2,1,328,128]{3,2,1,0:T(8,128)(2,1)S(1)}, bf16[2,1,328,128]{3,2,1,0:T(8,128)(2,1)S(1)}, u32[]{:S(2)}, u32[]{:S(2)}) collective-permute-start(bf16[2,1,328,128]{3,2,1,0:T(8,128)(2,1)S(1)} %get-tuple-element.60), channel_id=1, source_target_pairs={{0,24},{4,28},{8,16},{12,20},{16,8},{20,12},{24,0},{28,4},{1,25},{... | collective-permute-start | bytes 503816 | tf_op jit(solution)/shard_map/ppermute | solution.py:363
  63.9 6.1 %collective-permute-start.18 = (bf16[4,2,328,128]{3,2,1,0:T(8,128)(2,1)S(1)}, bf16[4,2,328,128]{3,2,1,0:T(8,128)(2,1)S(1)}, u32[]{:S(2)}, u32[]{:S(2)}) collective-permute-start(bf16[4,2,328,128]{3,2,1,0:T(8,128)(2,1)S(1)} %stack.4), channel_id=1, source_target_pairs={{0,4},{4,0},{8,12},{12,8},{16,20},{20,16},{24,28},{28,24},{1,5},{5... | collective-permute-start | bytes 2015240 | tf_op jit(solution)/shard_map/ppermute | solution.py:363
  (6 other events, 29.8 us)

commit v9 on v8

--- a/solution.py
+++ b/solution.py
@@ -81,10 +81,11 @@
         tile(pl.ds(full, 16), end)
 
 
-def order_kernel(bins_axis, owners_count, width, slots, *refs):
+def order_kernel(blocks, owners_count, width, slots, *refs):
     inner, sea = refs[:2]
-    owner = refs[2 : 2 + bins_axis]
-    part, far_order, meta, order = refs[2 + bins_axis :]
+    owner = refs[2 : 2 + len(blocks)]
+    part, far_order = refs[2 + len(blocks) : 4 + len(blocks)]
+    order = refs[-1]
     lon_rows, rows = inner.shape[0] + 1, inner.shape[1]
     points = lon_rows * LANES
     me = lax.axis_index("bins")
@@ -94,7 +95,7 @@
     near_at = pl.ds(pl.multiple_of(jnp.where(even, last, 0), LANES), LANES)
     far_at = pl.ds(pl.multiple_of(jnp.where(even, 0, last), LANES), LANES)
     owners_id = iota((owners_count, points), 0)
-    hot = [(owner[m][...] == owners_id).astype(F32) for m in range(bins_axis)]
+    hot = [(owner[m][...] == owners_id).astype(F32) for m in range(len(blocks))]
     earlier = (iota((points, points), 0) < iota((points, points), 1)).astype(F32).astype(BF16)
     before = jnp.dot(
         jnp.concatenate(hot, axis=0).astype(BF16), earlier, preferred_element_type=F32
@@ -102,7 +103,7 @@
     main = (CHUNKS - 1) * width
     place_id = iota(order.shape, 0)
     none = [jnp.zeros((1, points), F32)]
-    for m in range(bins_axis):
+    for m, offset_of in enumerate(blocks):
         own = owner[m][...]
         count = jnp.sum(hot[m], axis=1, keepdims=True)
         offset = jnp.sum(jnp.where(owners_id < own, count, 0.0), axis=0, keepdims=True)
@@ -112,7 +113,7 @@
         quarter = key & (CHUNKS - 1)
         slot = (key - first - ((quarter - first) & (CHUNKS - 1))) // CHUNKS
         towards = own ^ me_pts
-        block = me ^ m
+        block = me ^ offset_of
         group = (towards & (CHUNKS - 1)) ^ block
         spread = main + towards // CHUNKS * LANES + group * slots + slot
         place = jnp.where(quarter < CHUNKS - 1, quarter * width + key // CHUNKS, spread)
@@ -127,14 +128,15 @@
         end = slice(rows - 16, rows)
         spare = part[m, end, main:].astype(F32) + dot_nt(facts, order[main:, :])
         part[m, end, main:] = spare.astype(BF16)
-        if m == 0:
+        if offset_of == 0:
             facts = [slot.astype(F32), towards.astype(F32), rank, weight] + none * 4
-            meta[...] = dot_nt(jnp.concatenate(facts, axis=0).astype(BF16), order[:main, :])
+            refs[-2][...] = dot_nt(jnp.concatenate(facts, axis=0).astype(BF16), order[:main, :])
 
 
 def pack_kernel(rows_out, bins_axis, width, pairs, *refs):
-    planes, far, speed, side, sea, part, far_order = refs[:7]
-    chunks, moved = refs[7:-1], refs[-1]
+    planes, far, speed, side, sea = refs[:5]
+    parts, far_orders = refs[5:7], refs[7:9]
+    chunks, moved = refs[9:-1], refs[-1]
     direct = chunks[len(MAIN) * bins_axis :]
     lon_rows, rows, _ = planes.shape
     top = lon_rows - 1
@@ -155,7 +157,9 @@
     spread = []
     for m in range(bins_axis):
         at = pl.ds(pl.multiple_of((me ^ m) * LANES, LANES), LANES)
-        ordered = dot_nt(moved[:, at], far_order[m]) + part[m].astype(F32)
+        late = m == bins_axis - 1
+        index = 0 if late else m
+        ordered = dot_nt(moved[:, at], far_orders[late][index]) + parts[late][index].astype(F32)
         ordered = ordered[:rows_out]
         ordered = jnp.where((me & 1) == 1, pltpu.roll(ordered, 4, 0), ordered).astype(BF16)
         for c, quarters in enumerate(MAIN):
@@ -418,20 +422,27 @@
         cost_estimate=cost(1, 1),
         name="inner",
     )(planes, near, speed, side, sea)
-    part, far_order, meta = pl.pallas_call(
-        functools.partial(order_kernel, bins_axis, owners_count, width, slots),
-        out_shape=[
-            jax.ShapeDtypeStruct((bins_axis, tall, order_columns), BF16),
-            jax.ShapeDtypeStruct((bins_axis, order_columns, LANES), BF16),
-            jax.ShapeDtypeStruct((8, (CHUNKS - 1) * width), F32),
-        ],
-        in_specs=vmem(2 + bins_axis),
-        out_specs=vmem(3),
-        scratch_shapes=[pltpu.VMEM((order_columns, points), BF16)],
-        compiler_params=params(16),
-        cost_estimate=cost(1, 1),
-        name="order",
-    )(inner, sea, *owners)
+    ordered = []
+    for group in (tuple(range(bins_axis - 1)), (bins_axis - 1,)):
+        shapes = [
+            jax.ShapeDtypeStruct((len(group), tall, order_columns), BF16),
+            jax.ShapeDtypeStruct((len(group), order_columns, LANES), BF16),
+        ]
+        if group[0] == 0:
+            shapes.append(jax.ShapeDtypeStruct((8, (CHUNKS - 1) * width), F32))
+        ordered.append(
+            pl.pallas_call(
+                functools.partial(order_kernel, group, owners_count, width, slots),
+                out_shape=shapes,
+                in_specs=vmem(2 + len(group)),
+                out_specs=vmem(len(shapes)),
+                scratch_shapes=[pltpu.VMEM((order_columns, points), BF16)],
+                compiler_params=params(16),
+                cost_estimate=cost(1, 1),
+                name="order",
+            )(inner, sea, *[owners[m] for m in group])
+        )
+    meta = ordered[0][2]
     packed = pl.pallas_call(
         functools.partial(pack_kernel, rows, bins_axis, width, pairs),
         out_shape=[
@@ -440,13 +451,13 @@
             for _ in range(bins_axis)
         ]
         + [jax.ShapeDtypeStruct((2, 1, rows, LANES), BF16)] * pairs,
-        in_specs=vmem(7),
+        in_specs=vmem(9),
         out_specs=vmem(len(MAIN) * bins_axis + pairs),
         scratch_shapes=[pltpu.VMEM((tall, lats), BF16)],
         compiler_params=params(16),
         cost_estimate=cost(1, 1),
         name="pack",
-    )(planes, far, speed, side, sea, part, far_order)
+    )(planes, far, speed, side, sea, *[o[0] for o in ordered], *[o[1] for o in ordered])
 
     def couple(quarters, blocks, ready):
         shape = (2, len(quarters), quarter_rows, LANES)

time: 72.2 us -> 72.4 us (level)
  waiting for transfers between devices: 19.4 us -> 11.5 us
  starting transfers between devices: 32.6 us -> 39.6 us
    ppermute x25, waiting for transfers between devices: 19.4 us -> 11.5 us  [exchange(): lax.ppermute(array, axis, [(i, i ^ offset) for i in range(lax.axis_size(a...]
    ppermute x25, starting transfers between devices: 32 us -> 38.9 us  [exchange(): lax.ppermute(array, axis, [(i, i ^ offset) for i in range(lax.axis_size(a...]
    pallas_call x1 -> x2, Pallas kernels: 2.61 us -> 3.06 us  [chunked(): pl.pallas_call(functools.partial(order_kernel, group, owners_count, width...]
  transfers between devices with their start and end apart: 26 -> 26, of which waited for: 7 -> 6; matrix products, arithmetic and copies ran while one was open for 2% -> 2% of each run, Pallas kernels for 18% -> 19%
where the time goes in v9:
time: 72.4 us; the launch traced here: 71.4 us
  starting transfers between devices  39.6 us (55%)
  Pallas kernels  16.8 us (23%)
  waiting for transfers between devices  11.5 us (16%)
  local copies, waits for them, and re-layouts  2.11 us (3%)
  other arithmetic  0.93 us (1%)
    ppermute x25, starting transfers between devices, exchange(): lax.ppermute(array, axis, [(i, i ^ offset) for i in range(lax.axis_size(a...  38.9 us
    ppermute x25, waiting for transfers between devices, exchange(): lax.ppermute(array, axis, [(i, i ^ offset) for i in range(lax.axis_size(a...  11.5 us
    pallas_call x3, Pallas kernels, couple(): pl.pallas_call(functools.partial(couple_kernel, quarters, bins_axis, loca...  5.69 us
    pallas_call x2, Pallas kernels, place(): pl.pallas_call(functools.partial(place_kernel, all_bins // CHUNKS, tuple(...  3.35 us
    pallas_call x2, Pallas kernels, chunked(): pl.pallas_call(functools.partial(order_kernel, group, owners_count, width...  3.06 us
    pallas_call x1, Pallas kernels, chunked(): pl.pallas_call(functools.partial(pack_kernel, rows, bins_axis, width, pai...  1.7 us
    unnamed x9, local copies, waits for them, and re-layouts  1.62 us
  transfers between devices with their start and end apart: 26, of which 6 were waited for; matrix products, arithmetic and copies ran while one was open for 2% of the time, Pallas kernels for 19%

profile of v9, /device:TPU:0, one launch (start us, length us, event | category | flops | bytes accessed | tf_op | source)
XLA Modules:
  0.0 71.4 jit_solution(11699894239041609743)
XLA Ops:
  0.0 1.6 %copy.10 = bf16[324,4,512]{2,0,1:T(8,128)(2,1)S(1)} copy(bf16[324,4,512]{2,1,0:T(4,128)(2,1)} %param.6) | data formatting | bytes 2654208 | tf_op args[0]
  3.0 4.7 %collective-permute-start.4 = (s32[1,512]{1,0:T(1,128)S(1)}, s32[1,512]{1,0:T(1,128)S(1)}, u32[]{:S(2)}, u32[]{:S(2)}) collective-permute-start(s32[1,512]{1,0:T(1,128)S(1)} %bitcast.19), channel_id=1, source_target_pairs={{0,3},{1,2},{2,1},{3,0},{4,7},{5,6},{6,5},{7,4},{8,11},{9,10},{10,... | collective-permute-start | bytes 6152 | tf_op jit(solution)/shard_map/ppermute | solution.py:367
  12.2 2.0 %order.2 = (bf16[3,336,640]{2,1,0:T(8,128)(2,1)S(1)}, bf16[3,640,128]{2,1,0:T(8,128)(2,1)S(1)}, f32[8,384]{1,0:T(8,128)S(1)}) custom-call(bf16[3,336,512]{2,1,0:T(8,128)(2,1)S(1)} %inner.1.refs_0_, s32[4,512]{1,0:T(4,128)S(1)} %copy-done.2, s32[1,512]{1,0:T(1,128)S(1)} %bitcast.22, s32[1,512]{1,0:T(1,128)S(1)} %collective-permute-done.2.refs_3_, ...), custom_call_target="tpu_custom_call" | custom-call | flops 1 | bytes 1 | tf_op jit(solution)/shard_map/order/pallas_call | solution.py:434
  14.3 1.7 %pack.1 = (bf16[328,256]{1,0:T(8,128)(2,1)S(1)}, bf16[328,256]{1,0:T(8,128)(2,1)S(1)}, bf16[328,256]{1,0:T(8,128)(2,1)S(1)}, bf16[328,256]{1,0:T(8,128)(2,1)S(1)...) custom-call(bf16[4,336,512]{2,1,0:T(8,128)(2,1)S(1)} %pad.12.planes., ...), custom_call_target="tpu_custom_call" | custom-call | flops 1 | bytes 1 | tf_op jit(solution)/shard_map/pack/pallas_call | solution.py:446
  17.2 2.9 %collective-permute-start.6 = (bf16[328,256]{1,0:T(8,128)(2,1)S(1)}, bf16[328,256]{1,0:T(8,128)(2,1)S(1)}, u32[]{:S(2)}, u32[]{:S(2)}) collective-permute-start(bf16[328,256]{1,0:T(8,128)(2,1)S(1)} %get-tuple-element.44), channel_id=1, source_target_pairs={{0,2},{1,3},{2,0},{3,1},{4,6},{5,7},{6,4},{7,5},{8,10},{9,11},{10,... | collective-permute-start | bytes 503816 | tf_op jit(solution)/shard_map/ppermute | solution.py:367
  20.1 3.3 %collective-permute-start.14 = (bf16[2,1,328,128]{3,2,1,0:T(8,128)(2,1)S(1)}, bf16[2,1,328,128]{3,2,1,0:T(8,128)(2,1)S(1)}, u32[]{:S(2)}, u32[]{:S(2)}) collective-permute-start(bf16[2,1,328,128]{3,2,1,0:T(8,128)(2,1)S(1)} %get-tuple-element.56), channel_id=1, source_target_pairs={{0,8},{4,12},{8,0},{12,4},{16,24},{20,28},{24,16},{28,20},{1,9},{5... | collective-permute-start | bytes 503816 | tf_op jit(solution)/shard_map/ppermute | solution.py:367
  23.4 1.5 %collective-permute-start.15 = (bf16[2,1,328,128]{3,2,1,0:T(8,128)(2,1)S(1)}, bf16[2,1,328,128]{3,2,1,0:T(8,128)(2,1)S(1)}, u32[]{:S(2)}, u32[]{:S(2)}) collective-permute-start(bf16[2,1,328,128]{3,2,1,0:T(8,128)(2,1)S(1)} %get-tuple-element.57), channel_id=1, source_target_pairs={{0,16},{4,20},{8,24},{12,28},{16,0},{20,4},{24,8},{28,12},{1,17},{... | collective-permute-start | bytes 503816 | tf_op jit(solution)/shard_map/ppermute | solution.py:367
  25.8 2.0 %collective-permute-start.7 = (bf16[328,256]{1,0:T(8,128)(2,1)S(1)}, bf16[328,256]{1,0:T(8,128)(2,1)S(1)}, u32[]{:S(2)}, u32[]{:S(2)}) collective-permute-start(bf16[328,256]{1,0:T(8,128)(2,1)S(1)} %get-tuple-element.45), channel_id=1, source_target_pairs={{0,3},{1,2},{2,1},{3,0},{4,7},{5,6},{6,5},{7,4},{8,11},{9,10},{10,... | collective-permute-start | bytes 503816 | tf_op jit(solution)/shard_map/ppermute | solution.py:367
  29.1 3.5 %collective-permute-done.15.refs_2_ = bf16[2,1,328,128]{3,2,1,0:T(8,128)(2,1)S(1)} collective-permute-done((bf16[2,1,328,128]{3,2,1,0:T(8,128)(2,1)S(1)}, bf16[2,1,328,128]{3,2,1,0:T(8,128)(2,1)S(1)}, u32[]{:S(2)}, u32[]{:S(2)}) %collective-permute-start.15) | collective-permute-done | bytes 167968 | tf_op jit(solution)/shard_map/ppermute | solution.py:367
  32.7 1.8 %collective-permute-done.7.refs_2_.refs_3_ = bf16[328,256]{1,0:T(8,128)(2,1)S(1)} collective-permute-done((bf16[328,256]{1,0:T(8,128)(2,1)S(1)}, bf16[328,256]{1,0:T(8,128)(2,1)S(1)}, u32[]{:S(2)}, u32[]{:S(2)}) %collective-permute-start.7) | collective-permute-done | bytes 167968 | tf_op jit(solution)/shard_map/ppermute | solution.py:367
  34.5 1.9 %couple.3 = (bf16[2,2,328,128]{3,2,1,0:T(8,128)(2,1)S(1)}, bf16[2,2,328,128]{3,2,1,0:T(8,128)(2,1)S(1)}, bf16[2,2,328,128]{3,2,1,0:T(8,128)(2,1)S(1)}, bf16[2,2,328,128]{3,2,1,0:T(8,128)(2,1)S(1)}) custom-call(bf16[328,256]{1,0:T(8,128)(2,1)S(1)} %get-tuple-element.42.refs_0_, bf16[328,256]{1,0:T(8,128)(2,1)S(1)} %collective-permute-done.5.refs_0_.refs_1_.refs_4_, ...), custom_call_target="tpu_custom_call" | custom-call | flops 3000000000 | bytes 1 | tf_op jit(solution)/shard_map/couple/pallas_call | solution.py:464
  37.2 3.6 %collective-permute-start.12 = (bf16[328,128]{1,0:T(8,128)(2,1)S(1)}, bf16[328,128]{1,0:T(8,128)(2,1)S(1)}, u32[]{:S(2)}, u32[]{:S(2)}) collective-permute-start(bf16[328,128]{1,0:T(8,128)(2,1)S(1)} %gate.7.refs_7_), channel_id=1, source_target_pairs={{0,2},{1,3},{2,0},{3,1},{4,6},{5,7},{6,4},{7,5},{8,10},{9,11},{10,... | collective-permute-start | bytes 251912 | tf_op jit(solution)/shard_map/ppermute | solution.py:367
  42.1 2.9 %collective-permute-start.8 = (bf16[2,2,328,128]{3,2,1,0:T(8,128)(2,1)S(1)}, bf16[2,2,328,128]{3,2,1,0:T(8,128)(2,1)S(1)}, u32[]{:S(2)}, u32[]{:S(2)}) collective-permute-start(bf16[2,2,328,128]{3,2,1,0:T(8,128)(2,1)S(1)} %get-tuple-element.51), channel_id=1, source_target_pairs={{0,8},{4,12},{8,0},{12,4},{16,24},{20,28},{24,16},{28,20},{1,9},{5... | collective-permute-start | bytes 1007624 | tf_op jit(solution)/shard_map/ppermute | solution.py:367
  46.0 3.2 %collective-permute-start.9 = (bf16[2,2,328,128]{3,2,1,0:T(8,128)(2,1)S(1)}, bf16[2,2,328,128]{3,2,1,0:T(8,128)(2,1)S(1)}, u32[]{:S(2)}, u32[]{:S(2)}) collective-permute-start(bf16[2,2,328,128]{3,2,1,0:T(8,128)(2,1)S(1)} %get-tuple-element.52), channel_id=1, source_target_pairs={{0,16},{4,20},{8,24},{12,28},{16,0},{20,4},{24,8},{28,12},{1,17},{... | collective-permute-start | bytes 1007624 | tf_op jit(solution)/shard_map/ppermute | solution.py:367
  51.2 1.7 %collective-permute-start.22 = (bf16[328,256]{1,0:T(8,128)(2,1)S(1)}, bf16[328,256]{1,0:T(8,128)(2,1)S(1)}, u32[]{:S(2)}, u32[]{:S(2)}) collective-permute-start(bf16[328,256]{1,0:T(8,128)(2,1)S(1)} %gate.11), channel_id=1, source_target_pairs={{0,1},{1,0},{2,3},{3,2},{4,5},{5,4},{6,7},{7,6},{8,9},{9,8},{10,11... | collective-permute-start | bytes 503816 | tf_op jit(solution)/shard_map/ppermute | solution.py:367
  53.0 1.6 %couple.4 = (bf16[2,1,328,128]{3,2,1,0:T(8,128)(2,1)S(1)}, bf16[2,1,328,128]{3,2,1,0:T(8,128)(2,1)S(1)}, bf16[2,1,328,128]{3,2,1,0:T(8,128)(2,1)S(1)}, bf16[2,1,328,128]{3,2,1,0:T(8,128)(2,1)S(1)}) custom-call(bf16[328,128]{1,0:T(8,128)(2,1)S(1)} %get-tuple-element.54.refs_0_, bf16[328,128]{1,0:T(8,128)(2,1)S(1)} %collective-permute-done.11.refs_0_.refs_1_, ...), custom_call_target="tpu_custom_call" | custom-call | flops 30000001024 | bytes 1 | tf_op jit(solution)/shard_map/couple/pallas_call | solution.py:464
  54.6 1.8 %collective-permute-start.19 = (bf16[2,1,328,128]{3,2,1,0:T(8,128)(2,1)S(1)}, bf16[2,1,328,128]{3,2,1,0:T(8,128)(2,1)S(1)}, u32[]{:S(2)}, u32[]{:S(2)}) collective-permute-start(bf16[2,1,328,128]{3,2,1,0:T(8,128)(2,1)S(1)} %get-tuple-element.62), channel_id=1, source_target_pairs={{0,8},{4,12},{8,0},{12,4},{16,24},{20,28},{24,16},{28,20},{1,9},{5... | collective-permute-start | bytes 503816 | tf_op jit(solution)/shard_map/ppermute | solution.py:367
  56.4 1.5 %collective-permute-start.20 = (bf16[2,1,328,128]{3,2,1,0:T(8,128)(2,1)S(1)}, bf16[2,1,328,128]{3,2,1,0:T(8,128)(2,1)S(1)}, u32[]{:S(2)}, u32[]{:S(2)}) collective-permute-start(bf16[2,1,328,128]{3,2,1,0:T(8,128)(2,1)S(1)} %get-tuple-element.63), channel_id=1, source_target_pairs={{0,16},{4,20},{8,24},{12,28},{16,0},{20,4},{24,8},{28,12},{1,17},{... | collective-permute-start | bytes 503816 | tf_op jit(solution)/shard_map/ppermute | solution.py:367
  57.9 3.6 %collective-permute-done.23.refs_2_ = bf16[328,256]{1,0:T(8,128)(2,1)S(1)} collective-permute-done((bf16[328,256]{1,0:T(8,128)(2,1)S(1)}, bf16[328,256]{1,0:T(8,128)(2,1)S(1)}, u32[]{:S(2)}, u32[]{:S(2)}) %collective-permute-start.23) | collective-permute-done | bytes 167968 | tf_op jit(solution)/shard_map/ppermute | solution.py:367
  61.5 2.4 %collective-permute-start.21 = (bf16[2,1,328,128]{3,2,1,0:T(8,128)(2,1)S(1)}, bf16[2,1,328,128]{3,2,1,0:T(8,128)(2,1)S(1)}, u32[]{:S(2)}, u32[]{:S(2)}) collective-permute-start(bf16[2,1,328,128]{3,2,1,0:T(8,128)(2,1)S(1)} %get-tuple-element.64), channel_id=1, source_target_pairs={{0,24},{4,28},{8,16},{12,20},{16,8},{20,12},{24,0},{28,4},{1,25},{... | collective-permute-start | bytes 503816 | tf_op jit(solution)/shard_map/ppermute | solution.py:367
  63.9 2.1 %couple.5 = (bf16[2,1,328,128]{3,2,1,0:T(8,128)(2,1)S(1)}, bf16[2,1,328,128]{3,2,1,0:T(8,128)(2,1)S(1)}, bf16[2,1,328,128]{3,2,1,0:T(8,128)(2,1)S(1)}, bf16[2,1,328,128]{3,2,1,0:T(8,128)(2,1)S(1)}) custom-call(bf16[328,256]{1,0:T(8,128)(2,1)S(1)} %get-tuple-element.65.refs_0_, bf16[328,256]{1,0:T(8,128)(2,1)S(1)} %collective-permute-done.22.refs_1_, ...), custom_call_target="tpu_custom_call" | custom-call | flops 30000001024 | bytes 1 | tf_op jit(solution)/shard_map/couple/pallas_call | solution.py:464
  66.0 1.7 %collective-permute-done.21.refs_3_.refs_10_ = bf16[2,1,328,128]{3,2,1,0:T(8,128)(2,1)S(1)} collective-permute-done((bf16[2,1,328,128]{3,2,1,0:T(8,128)(2,1)S(1)}, bf16[2,1,328,128]{3,2,1,0:T(8,128)(2,1)S(1)}, u32[]{:S(2)}, u32[]{:S(2)}) %collective-permute-start.21) | collective-permute-done | bytes 167968 | tf_op jit(solution)/shard_map/ppermute | solution.py:367
  67.8 1.7 %place.2.refs_6_ = bf16[1296,1024]{1,0:T(8,128)(2,1)} custom-call(bf16[2,2,328,128]{3,2,1,0:T(8,128)(2,1)S(1)} %get-tuple-element.50.refs_3_.refs_0_, bf16[2,1,328,128]{3,2,1,0:T(8,128)(2,1)S(1)} %get-tuple-element.61.refs_4_.refs_0_.refs_1_, bf16[2,1,328,128]{3,2,1,0:T(8,128)(2,1)S(1)} %get-tuple-element.67.refs_4_.refs_2_, ...), custom_call_target="tpu_custom_call" | custom-call | flops 1 | bytes 1 | tf_op jit(solution)/shard_map/place/pallas_call | solution.py:304
  69.5 1.7 %place.3 = bf16[1296,1024]{1,0:T(8,128)(2,1)} custom-call(bf16[4,2,328,128]{3,2,1,0:T(8,128)(2,1)S(1)} %collective-permute-done.18.refs_0_, bf16[4,1,328,128]{3,2,1,0:T(8,128)(2,1)S(1)} %collective-permute-done.25.refs_1_, bf16[2,1,328,128]{3,2,1,0:T(8,128)(2,1)S(1)} %get-tuple-element.67.refs_4_.refs_2_, ...), custom_call_target="tpu_custom_call", output_to_operand_aliasing={{}: (6, {})} | custom-call | flops 1 | bytes 1 | tf_op jit(solution)/shard_map/place/pallas_call | solution.py:304
  (66 shorter events, 14.5 us)
Async XLA Ops:
  1.8 7.5 %collective-permute-start.1 = (bf16[324,512]{1,0:T(8,128)(2,1)S(1)}, bf16[324,512]{1,0:T(8,128)(2,1)S(1)}, u32[]{:S(2)}, u32[]{:S(2)}) collective-permute-start(bf16[324,512]{1,0:T(8,128)(2,1)S(1)} %get-tuple-element.73), channel_id=1, source_target_pairs={{0,4},{4,0},{8,12},{12,8},{16,20},{20,16},{24,28},{28,24},{1,5},{5... | collective-permute-start | bytes 995336 | tf_op jit(solution)/shard_map/ppermute | solution.py:367
  2.3 11.9 %collective-permute-start = (bf16[324,512]{1,0:T(8,128)(2,1)S(1)}, bf16[324,512]{1,0:T(8,128)(2,1)S(1)}, u32[]{:S(2)}, u32[]{:S(2)}) collective-permute-start(bf16[324,512]{1,0:T(8,128)(2,1)S(1)} %get-tuple-element.74), channel_id=1, source_target_pairs={{4,8},{12,16},{20,24},{8,4},{16,12},{24,20},{5,9},{13,17},{21,25},... | collective-permute-start | bytes 995336 | tf_op jit(solution)/shard_map/ppermute | solution.py:394
  3.0 7.9 %collective-permute-start.4 = (s32[1,512]{1,0:T(1,128)S(1)}, s32[1,512]{1,0:T(1,128)S(1)}, u32[]{:S(2)}, u32[]{:S(2)}) collective-permute-start(s32[1,512]{1,0:T(1,128)S(1)} %bitcast.19), channel_id=1, source_target_pairs={{0,3},{1,2},{2,1},{3,0},{4,7},{5,6},{6,5},{7,4},{8,11},{9,10},{10,... | collective-permute-start | bytes 6152 | tf_op jit(solution)/shard_map/ppermute | solution.py:367
  7.7 4.5 %collective-permute-start.2 = (s32[1,512]{1,0:T(1,128)S(1)}, s32[1,512]{1,0:T(1,128)S(1)}, u32[]{:S(2)}, u32[]{:S(2)}) collective-permute-start(s32[1,512]{1,0:T(1,128)S(1)} %bitcast.21), channel_id=1, source_target_pairs={{0,1},{1,0},{2,3},{3,2},{4,5},{5,4},{6,7},{7,6},{8,9},{9,8},{10,11... | collective-permute-start | bytes 6152 | tf_op jit(solution)/shard_map/ppermute | solution.py:367
  16.0 9.9 %collective-permute-start.5 = (bf16[328,256]{1,0:T(8,128)(2,1)S(1)}, bf16[328,256]{1,0:T(8,128)(2,1)S(1)}, u32[]{:S(2)}, u32[]{:S(2)}) collective-permute-start(bf16[328,256]{1,0:T(8,128)(2,1)S(1)} %get-tuple-element.43), channel_id=1, source_target_pairs={{0,1},{1,0},{2,3},{3,2},{4,5},{5,4},{6,7},{7,6},{8,9},{9,8},{10,11... | collective-permute-start | bytes 503816 | tf_op jit(solution)/shard_map/ppermute | solution.py:367
  17.2 11.9 %collective-permute-start.6 = (bf16[328,256]{1,0:T(8,128)(2,1)S(1)}, bf16[328,256]{1,0:T(8,128)(2,1)S(1)}, u32[]{:S(2)}, u32[]{:S(2)}) collective-permute-start(bf16[328,256]{1,0:T(8,128)(2,1)S(1)} %get-tuple-element.44), channel_id=1, source_target_pairs={{0,2},{1,3},{2,0},{3,1},{4,6},{5,7},{6,4},{7,5},{8,10},{9,11},{10,... | collective-permute-start | bytes 503816 | tf_op jit(solution)/shard_map/ppermute | solution.py:367
  20.1 9.0 %collective-permute-start.14 = (bf16[2,1,328,128]{3,2,1,0:T(8,128)(2,1)S(1)}, bf16[2,1,328,128]{3,2,1,0:T(8,128)(2,1)S(1)}, u32[]{:S(2)}, u32[]{:S(2)}) collective-permute-start(bf16[2,1,328,128]{3,2,1,0:T(8,128)(2,1)S(1)} %get-tuple-element.56), channel_id=1, source_target_pairs={{0,8},{4,12},{8,0},{12,4},{16,24},{20,28},{24,16},{28,20},{1,9},{5... | collective-permute-start | bytes 503816 | tf_op jit(solution)/shard_map/ppermute | solution.py:367
  23.4 9.1 %collective-permute-start.15 = (bf16[2,1,328,128]{3,2,1,0:T(8,128)(2,1)S(1)}, bf16[2,1,328,128]{3,2,1,0:T(8,128)(2,1)S(1)}, u32[]{:S(2)}, u32[]{:S(2)}) collective-permute-start(bf16[2,1,328,128]{3,2,1,0:T(8,128)(2,1)S(1)} %get-tuple-element.57), channel_id=1, source_target_pairs={{0,16},{4,20},{8,24},{12,28},{16,0},{20,4},{24,8},{28,12},{1,17},{... | collective-permute-start | bytes 503816 | tf_op jit(solution)/shard_map/ppermute | solution.py:367
  24.9 7.6 %collective-permute-start.16 = (bf16[2,1,328,128]{3,2,1,0:T(8,128)(2,1)S(1)}, bf16[2,1,328,128]{3,2,1,0:T(8,128)(2,1)S(1)}, u32[]{:S(2)}, u32[]{:S(2)}) collective-permute-start(bf16[2,1,328,128]{3,2,1,0:T(8,128)(2,1)S(1)} %get-tuple-element.58), channel_id=1, source_target_pairs={{0,24},{4,28},{8,16},{12,20},{16,8},{20,12},{24,0},{28,4},{1,25},{... | collective-permute-start | bytes 503816 | tf_op jit(solution)/shard_map/ppermute | solution.py:367
  25.8 8.7 %collective-permute-start.7 = (bf16[328,256]{1,0:T(8,128)(2,1)S(1)}, bf16[328,256]{1,0:T(8,128)(2,1)S(1)}, u32[]{:S(2)}, u32[]{:S(2)}) collective-permute-start(bf16[328,256]{1,0:T(8,128)(2,1)S(1)} %get-tuple-element.45), channel_id=1, source_target_pairs={{0,3},{1,2},{2,1},{3,0},{4,7},{5,6},{6,5},{7,4},{8,11},{9,10},{10,... | collective-permute-start | bytes 503816 | tf_op jit(solution)/shard_map/ppermute | solution.py:367
  32.6 9.6 %collective-permute-start.17 = (bf16[4,1,328,128]{3,2,1,0:T(8,128)(2,1)S(1)}, bf16[4,1,328,128]{3,2,1,0:T(8,128)(2,1)S(1)}, u32[]{:S(2)}, u32[]{:S(2)}) collective-permute-start(bf16[4,1,328,128]{3,2,1,0:T(8,128)(2,1)S(1)} %stack.3), channel_id=1, source_target_pairs={{0,4},{4,0},{8,12},{12,8},{16,20},{20,16},{24,28},{28,24},{1,5},{5... | collective-permute-start | bytes 1007624 | tf_op jit(solution)/shard_map/ppermute | solution.py:367
  36.5 14.8 %collective-permute-start.10 = (bf16[2,2,328,128]{3,2,1,0:T(8,128)(2,1)S(1)}, bf16[2,2,328,128]{3,2,1,0:T(8,128)(2,1)S(1)}, u32[]{:S(2)}, u32[]{:S(2)}) collective-permute-start(bf16[2,2,328,128]{3,2,1,0:T(8,128)(2,1)S(1)} %get-tuple-element.53), channel_id=1, source_target_pairs={{0,24},{4,28},{8,16},{12,20},{16,8},{20,12},{24,0},{28,4},{1,25},{... | collective-permute-start | bytes 1007624 | tf_op jit(solution)/shard_map/ppermute | solution.py:367
  37.2 8.8 %collective-permute-start.12 = (bf16[328,128]{1,0:T(8,128)(2,1)S(1)}, bf16[328,128]{1,0:T(8,128)(2,1)S(1)}, u32[]{:S(2)}, u32[]{:S(2)}) collective-permute-start(bf16[328,128]{1,0:T(8,128)(2,1)S(1)} %gate.7.refs_7_), channel_id=1, source_target_pairs={{0,2},{1,3},{2,0},{3,1},{4,6},{5,7},{6,4},{7,5},{8,10},{9,11},{10,... | collective-permute-start | bytes 251912 | tf_op jit(solution)/shard_map/ppermute | solution.py:367
  40.8 8.4 %collective-permute-start.13 = (bf16[328,128]{1,0:T(8,128)(2,1)S(1)}, bf16[328,128]{1,0:T(8,128)(2,1)S(1)}, u32[]{:S(2)}, u32[]{:S(2)}) collective-permute-start(bf16[328,128]{1,0:T(8,128)(2,1)S(1)} %gate.8.refs_8_), channel_id=1, source_target_pairs={{0,3},{1,2},{2,1},{3,0},{4,7},{5,6},{6,5},{7,4},{8,11},{9,10},{10,... | collective-permute-start | bytes 251912 | tf_op jit(solution)/shard_map/ppermute | solution.py:367
  42.1 7.1 %collective-permute-start.11 = (bf16[328,128]{1,0:T(8,128)(2,1)S(1)}, bf16[328,128]{1,0:T(8,128)(2,1)S(1)}, u32[]{:S(2)}, u32[]{:S(2)}) collective-permute-start(bf16[328,128]{1,0:T(8,128)(2,1)S(1)} %gate.6.refs_6_), channel_id=1, source_target_pairs={{0,1},{1,0},{2,3},{3,2},{4,5},{5,4},{6,7},{7,6},{8,9},{9,8},{10,11... | collective-permute-start | bytes 251912 | tf_op jit(solution)/shard_map/ppermute | solution.py:367
  42.1 12.5 %collective-permute-start.8 = (bf16[2,2,328,128]{3,2,1,0:T(8,128)(2,1)S(1)}, bf16[2,2,328,128]{3,2,1,0:T(8,128)(2,1)S(1)}, u32[]{:S(2)}, u32[]{:S(2)}) collective-permute-start(bf16[2,2,328,128]{3,2,1,0:T(8,128)(2,1)S(1)} %get-tuple-element.51), channel_id=1, source_target_pairs={{0,8},{4,12},{8,0},{12,4},{16,24},{20,28},{24,16},{28,20},{1,9},{5... | collective-permute-start | bytes 1007624 | tf_op jit(solution)/shard_map/ppermute | solution.py:367
  46.0 10.4 %collective-permute-start.9 = (bf16[2,2,328,128]{3,2,1,0:T(8,128)(2,1)S(1)}, bf16[2,2,328,128]{3,2,1,0:T(8,128)(2,1)S(1)}, u32[]{:S(2)}, u32[]{:S(2)}) collective-permute-start(bf16[2,2,328,128]{3,2,1,0:T(8,128)(2,1)S(1)} %get-tuple-element.52), channel_id=1, source_target_pairs={{0,16},{4,20},{8,24},{12,28},{16,0},{20,4},{24,8},{28,12},{1,17},{... | collective-permute-start | bytes 1007624 | tf_op jit(solution)/shard_map/ppermute | solution.py:367
  49.2 12.2 %collective-permute-start.23 = (bf16[328,256]{1,0:T(8,128)(2,1)S(1)}, bf16[328,256]{1,0:T(8,128)(2,1)S(1)}, u32[]{:S(2)}, u32[]{:S(2)}) collective-permute-start(bf16[328,256]{1,0:T(8,128)(2,1)S(1)} %gate.9.refs_6_), channel_id=1, source_target_pairs={{0,2},{1,3},{2,0},{3,1},{4,6},{5,7},{6,4},{7,5},{8,10},{9,11},{10,... | collective-permute-start | bytes 503816 | tf_op jit(solution)/shard_map/ppermute | solution.py:367
  50.0 13.9 %collective-permute-start.24 = (bf16[328,256]{1,0:T(8,128)(2,1)S(1)}, bf16[328,256]{1,0:T(8,128)(2,1)S(1)}, u32[]{:S(2)}, u32[]{:S(2)}) collective-permute-start(bf16[328,256]{1,0:T(8,128)(2,1)S(1)} %gate.10.refs_7_), channel_id=1, source_target_pairs={{0,3},{1,2},{2,1},{3,0},{4,7},{5,6},{6,5},{7,4},{8,11},{9,10},{10,... | collective-permute-start | bytes 503816 | tf_op jit(solution)/shard_map/ppermute | solution.py:367
  51.2 12.6 %collective-permute-start.22 = (bf16[328,256]{1,0:T(8,128)(2,1)S(1)}, bf16[328,256]{1,0:T(8,128)(2,1)S(1)}, u32[]{:S(2)}, u32[]{:S(2)}) collective-permute-start(bf16[328,256]{1,0:T(8,128)(2,1)S(1)} %gate.11), channel_id=1, source_target_pairs={{0,1},{1,0},{2,3},{3,2},{4,5},{5,4},{6,7},{7,6},{8,9},{9,8},{10,11... | collective-permute-start | bytes 503816 | tf_op jit(solution)/shard_map/ppermute | solution.py:367
  54.6 11.4 %collective-permute-start.19 = (bf16[2,1,328,128]{3,2,1,0:T(8,128)(2,1)S(1)}, bf16[2,1,328,128]{3,2,1,0:T(8,128)(2,1)S(1)}, u32[]{:S(2)}, u32[]{:S(2)}) collective-permute-start(bf16[2,1,328,128]{3,2,1,0:T(8,128)(2,1)S(1)} %get-tuple-element.62), channel_id=1, source_target_pairs={{0,8},{4,12},{8,0},{12,4},{16,24},{20,28},{24,16},{28,20},{1,9},{5... | collective-permute-start | bytes 503816 | tf_op jit(solution)/shard_map/ppermute | solution.py:367
  56.4 9.6 %collective-permute-start.20 = (bf16[2,1,328,128]{3,2,1,0:T(8,128)(2,1)S(1)}, bf16[2,1,328,128]{3,2,1,0:T(8,128)(2,1)S(1)}, u32[]{:S(2)}, u32[]{:S(2)}) collective-permute-start(bf16[2,1,328,128]{3,2,1,0:T(8,128)(2,1)S(1)} %get-tuple-element.63), channel_id=1, source_target_pairs={{0,16},{4,20},{8,24},{12,28},{16,0},{20,4},{24,8},{28,12},{1,17},{... | collective-permute-start | bytes 503816 | tf_op jit(solution)/shard_map/ppermute | solution.py:367
  61.5 6.3 %collective-permute-start.21 = (bf16[2,1,328,128]{3,2,1,0:T(8,128)(2,1)S(1)}, bf16[2,1,328,128]{3,2,1,0:T(8,128)(2,1)S(1)}, u32[]{:S(2)}, u32[]{:S(2)}) collective-permute-start(bf16[2,1,328,128]{3,2,1,0:T(8,128)(2,1)S(1)} %get-tuple-element.64), channel_id=1, source_target_pairs={{0,24},{4,28},{8,16},{12,20},{16,8},{20,12},{24,0},{28,4},{1,25},{... | collective-permute-start | bytes 503816 | tf_op jit(solution)/shard_map/ppermute | solution.py:367
  63.9 5.7 %collective-permute-start.18 = (bf16[4,2,328,128]{3,2,1,0:T(8,128)(2,1)S(1)}, bf16[4,2,328,128]{3,2,1,0:T(8,128)(2,1)S(1)}, u32[]{:S(2)}, u32[]{:S(2)}) collective-permute-start(bf16[4,2,328,128]{3,2,1,0:T(8,128)(2,1)S(1)} %stack.4), channel_id=1, source_target_pairs={{0,4},{4,0},{8,12},{12,8},{16,20},{20,16},{24,28},{28,24},{1,5},{5... | collective-permute-start | bytes 2015240 | tf_op jit(solution)/shard_map/ppermute | solution.py:367
  (6 other events, 31.1 us)

commit v10 on v9

--- a/solution.py
+++ b/solution.py
@@ -503,7 +503,7 @@
     regrouped = [
         regrouped[0],
         gate(regrouped[1], *second[1:], came[0][0], came[0][pairs - 1]),
-        *[gate(b, *second[1:], came[0][0]) for b in regrouped[2:]],
+        *[gate(b, *second[2:], came[0][0]) for b in regrouped[2:]],
     ]
     third = over_bins(regrouped)
     came.append(over_pts(couple(MAIN[1], second, regrouped[2:])))

time: 72.4 us -> 71.8 us (level)
  waiting for transfers between devices: 11.5 us -> 10 us
  starting transfers between devices: 39.6 us -> 40.5 us
    ppermute x25, waiting for transfers between devices: 11.5 us -> 10 us  [exchange(): lax.ppermute(array, axis, [(i, i ^ offset) for i in range(lax.axis_size(a...]
    ppermute x25, starting transfers between devices: 38.9 us -> 39.9 us  [exchange(): lax.ppermute(array, axis, [(i, i ^ offset) for i in range(lax.axis_size(a...]
where the time goes in v10:
time: 71.8 us; the launch traced here: 70.8 us
  starting transfers between devices  40.5 us (56%)
  Pallas kernels  16.8 us (23%)
  waiting for transfers between devices  10 us (14%)
  local copies, waits for them, and re-layouts  2.11 us (3%)
  other arithmetic  0.93 us (1%)
    ppermute x25, starting transfers between devices, exchange(): lax.ppermute(array, axis, [(i, i ^ offset) for i in range(lax.axis_size(a...  39.9 us
    ppermute x25, waiting for transfers between devices, exchange(): lax.ppermute(array, axis, [(i, i ^ offset) for i in range(lax.axis_size(a...  10 us
    pallas_call x3, Pallas kernels, couple(): pl.pallas_call(functools.partial(couple_kernel, quarters, bins_axis, loca...  5.69 us
    pallas_call x2, Pallas kernels, place(): pl.pallas_call(functools.partial(place_kernel, all_bins // CHUNKS, tuple(...  3.34 us
    pallas_call x2, Pallas kernels, chunked(): pl.pallas_call(functools.partial(order_kernel, group, owners_count, width...  3.06 us
    pallas_call x1, Pallas kernels, chunked(): pl.pallas_call(functools.partial(pack_kernel, rows, bins_axis, width, pai...  1.7 us
    unnamed x9, local copies, waits for them, and re-layouts  1.62 us
  transfers between devices with their start and end apart: 26, of which 6 were waited for; matrix products, arithmetic and copies ran while one was open for 2% of the time, Pallas kernels for 19%

profile of v10, /device:TPU:0, one launch (start us, length us, event | category | flops | bytes accessed | tf_op | source)
XLA Modules:
  0.0 70.8 jit_solution(2043126598521650612)
XLA Ops:
  0.0 1.6 %copy.10 = bf16[324,4,512]{2,0,1:T(8,128)(2,1)S(1)} copy(bf16[324,4,512]{2,1,0:T(4,128)(2,1)} %param.6) | data formatting | bytes 2654208 | tf_op args[0]
  3.0 4.7 %collective-permute-start.4 = (s32[1,512]{1,0:T(1,128)S(1)}, s32[1,512]{1,0:T(1,128)S(1)}, u32[]{:S(2)}, u32[]{:S(2)}) collective-permute-start(s32[1,512]{1,0:T(1,128)S(1)} %bitcast.19), channel_id=1, source_target_pairs={{0,3},{1,2},{2,1},{3,0},{4,7},{5,6},{6,5},{7,4},{8,11},{9,10},{10,... | collective-permute-start | bytes 6152 | tf_op jit(solution)/shard_map/ppermute | solution.py:367
  12.2 2.0 %order.2 = (bf16[3,336,640]{2,1,0:T(8,128)(2,1)S(1)}, bf16[3,640,128]{2,1,0:T(8,128)(2,1)S(1)}, f32[8,384]{1,0:T(8,128)S(1)}) custom-call(bf16[3,336,512]{2,1,0:T(8,128)(2,1)S(1)} %inner.1.refs_0_, s32[4,512]{1,0:T(4,128)S(1)} %copy-done.2, s32[1,512]{1,0:T(1,128)S(1)} %bitcast.22, s32[1,512]{1,0:T(1,128)S(1)} %collective-permute-done.2.refs_3_, ...), custom_call_target="tpu_custom_call" | custom-call | flops 1 | bytes 1 | tf_op jit(solution)/shard_map/order/pallas_call | solution.py:434
  14.3 1.7 %pack.1 = (bf16[328,256]{1,0:T(8,128)(2,1)S(1)}, bf16[328,256]{1,0:T(8,128)(2,1)S(1)}, bf16[328,256]{1,0:T(8,128)(2,1)S(1)}, bf16[328,256]{1,0:T(8,128)(2,1)S(1)...) custom-call(bf16[4,336,512]{2,1,0:T(8,128)(2,1)S(1)} %pad.12.planes., ...), custom_call_target="tpu_custom_call" | custom-call | flops 1 | bytes 1 | tf_op jit(solution)/shard_map/pack/pallas_call | solution.py:446
  17.2 2.9 %collective-permute-start.6 = (bf16[328,256]{1,0:T(8,128)(2,1)S(1)}, bf16[328,256]{1,0:T(8,128)(2,1)S(1)}, u32[]{:S(2)}, u32[]{:S(2)}) collective-permute-start(bf16[328,256]{1,0:T(8,128)(2,1)S(1)} %get-tuple-element.44), channel_id=1, source_target_pairs={{0,2},{1,3},{2,0},{3,1},{4,6},{5,7},{6,4},{7,5},{8,10},{9,11},{10,... | collective-permute-start | bytes 503816 | tf_op jit(solution)/shard_map/ppermute | solution.py:367
  20.1 3.3 %collective-permute-start.14 = (bf16[2,1,328,128]{3,2,1,0:T(8,128)(2,1)S(1)}, bf16[2,1,328,128]{3,2,1,0:T(8,128)(2,1)S(1)}, u32[]{:S(2)}, u32[]{:S(2)}) collective-permute-start(bf16[2,1,328,128]{3,2,1,0:T(8,128)(2,1)S(1)} %get-tuple-element.56), channel_id=1, source_target_pairs={{0,8},{4,12},{8,0},{12,4},{16,24},{20,28},{24,16},{28,20},{1,9},{5... | collective-permute-start | bytes 503816 | tf_op jit(solution)/shard_map/ppermute | solution.py:367
  23.4 1.5 %collective-permute-start.15 = (bf16[2,1,328,128]{3,2,1,0:T(8,128)(2,1)S(1)}, bf16[2,1,328,128]{3,2,1,0:T(8,128)(2,1)S(1)}, u32[]{:S(2)}, u32[]{:S(2)}) collective-permute-start(bf16[2,1,328,128]{3,2,1,0:T(8,128)(2,1)S(1)} %get-tuple-element.57), channel_id=1, source_target_pairs={{0,16},{4,20},{8,24},{12,28},{16,0},{20,4},{24,8},{28,12},{1,17},{... | collective-permute-start | bytes 503816 | tf_op jit(solution)/shard_map/ppermute | solution.py:367
  25.8 2.0 %collective-permute-start.7 = (bf16[328,256]{1,0:T(8,128)(2,1)S(1)}, bf16[328,256]{1,0:T(8,128)(2,1)S(1)}, u32[]{:S(2)}, u32[]{:S(2)}) collective-permute-start(bf16[328,256]{1,0:T(8,128)(2,1)S(1)} %get-tuple-element.45), channel_id=1, source_target_pairs={{0,3},{1,2},{2,1},{3,0},{4,7},{5,6},{6,5},{7,4},{8,11},{9,10},{10,... | collective-permute-start | bytes 503816 | tf_op jit(solution)/shard_map/ppermute | solution.py:367
  29.1 3.5 %collective-permute-done.15.refs_2_ = bf16[2,1,328,128]{3,2,1,0:T(8,128)(2,1)S(1)} collective-permute-done((bf16[2,1,328,128]{3,2,1,0:T(8,128)(2,1)S(1)}, bf16[2,1,328,128]{3,2,1,0:T(8,128)(2,1)S(1)}, u32[]{:S(2)}, u32[]{:S(2)}) %collective-permute-start.15) | collective-permute-done | bytes 167968 | tf_op jit(solution)/shard_map/ppermute | solution.py:367
  32.7 1.8 %collective-permute-done.7.refs_2_.refs_3_ = bf16[328,256]{1,0:T(8,128)(2,1)S(1)} collective-permute-done((bf16[328,256]{1,0:T(8,128)(2,1)S(1)}, bf16[328,256]{1,0:T(8,128)(2,1)S(1)}, u32[]{:S(2)}, u32[]{:S(2)}) %collective-permute-start.7) | collective-permute-done | bytes 167968 | tf_op jit(solution)/shard_map/ppermute | solution.py:367
  34.5 1.9 %couple.3 = (bf16[2,2,328,128]{3,2,1,0:T(8,128)(2,1)S(1)}, bf16[2,2,328,128]{3,2,1,0:T(8,128)(2,1)S(1)}, bf16[2,2,328,128]{3,2,1,0:T(8,128)(2,1)S(1)}, bf16[2,2,328,128]{3,2,1,0:T(8,128)(2,1)S(1)}) custom-call(bf16[328,256]{1,0:T(8,128)(2,1)S(1)} %get-tuple-element.42.refs_0_, bf16[328,256]{1,0:T(8,128)(2,1)S(1)} %collective-permute-done.5.refs_0_.refs_1_.refs_4_, ...), custom_call_target="tpu_custom_call" | custom-call | flops 3000000000 | bytes 1 | tf_op jit(solution)/shard_map/couple/pallas_call | solution.py:464
  37.2 3.6 %collective-permute-start.12 = (bf16[328,128]{1,0:T(8,128)(2,1)S(1)}, bf16[328,128]{1,0:T(8,128)(2,1)S(1)}, u32[]{:S(2)}, u32[]{:S(2)}) collective-permute-start(bf16[328,128]{1,0:T(8,128)(2,1)S(1)} %gate.7.refs_7_), channel_id=1, source_target_pairs={{0,2},{1,3},{2,0},{3,1},{4,6},{5,7},{6,4},{7,5},{8,10},{9,11},{10,... | collective-permute-start | bytes 251912 | tf_op jit(solution)/shard_map/ppermute | solution.py:367
  40.8 1.3 %collective-permute-start.13 = (bf16[328,128]{1,0:T(8,128)(2,1)S(1)}, bf16[328,128]{1,0:T(8,128)(2,1)S(1)}, u32[]{:S(2)}, u32[]{:S(2)}) collective-permute-start(bf16[328,128]{1,0:T(8,128)(2,1)S(1)} %gate.8.refs_8_), channel_id=1, source_target_pairs={{0,3},{1,2},{2,1},{3,0},{4,7},{5,6},{6,5},{7,4},{8,11},{9,10},{10,... | collective-permute-start | bytes 251912 | tf_op jit(solution)/shard_map/ppermute | solution.py:367
  42.1 2.9 %collective-permute-start.8 = (bf16[2,2,328,128]{3,2,1,0:T(8,128)(2,1)S(1)}, bf16[2,2,328,128]{3,2,1,0:T(8,128)(2,1)S(1)}, u32[]{:S(2)}, u32[]{:S(2)}) collective-permute-start(bf16[2,2,328,128]{3,2,1,0:T(8,128)(2,1)S(1)} %get-tuple-element.51), channel_id=1, source_target_pairs={{0,8},{4,12},{8,0},{12,4},{16,24},{20,28},{24,16},{28,20},{1,9},{5... | collective-permute-start | bytes 1007624 | tf_op jit(solution)/shard_map/ppermute | solution.py:367
  46.0 3.2 %collective-permute-start.9 = (bf16[2,2,328,128]{3,2,1,0:T(8,128)(2,1)S(1)}, bf16[2,2,328,128]{3,2,1,0:T(8,128)(2,1)S(1)}, u32[]{:S(2)}, u32[]{:S(2)}) collective-permute-start(bf16[2,2,328,128]{3,2,1,0:T(8,128)(2,1)S(1)} %get-tuple-element.52), channel_id=1, source_target_pairs={{0,16},{4,20},{8,24},{12,28},{16,0},{20,4},{24,8},{28,12},{1,17},{... | collective-permute-start | bytes 1007624 | tf_op jit(solution)/shard_map/ppermute | solution.py:367
  51.2 1.7 %collective-permute-start.22 = (bf16[328,256]{1,0:T(8,128)(2,1)S(1)}, bf16[328,256]{1,0:T(8,128)(2,1)S(1)}, u32[]{:S(2)}, u32[]{:S(2)}) collective-permute-start(bf16[328,256]{1,0:T(8,128)(2,1)S(1)} %gate.11), channel_id=1, source_target_pairs={{0,1},{1,0},{2,3},{3,2},{4,5},{5,4},{6,7},{7,6},{8,9},{9,8},{10,11... | collective-permute-start | bytes 503816 | tf_op jit(solution)/shard_map/ppermute | solution.py:367
  53.0 1.6 %couple.4 = (bf16[2,1,328,128]{3,2,1,0:T(8,128)(2,1)S(1)}, bf16[2,1,328,128]{3,2,1,0:T(8,128)(2,1)S(1)}, bf16[2,1,328,128]{3,2,1,0:T(8,128)(2,1)S(1)}, bf16[2,1,328,128]{3,2,1,0:T(8,128)(2,1)S(1)}) custom-call(bf16[328,128]{1,0:T(8,128)(2,1)S(1)} %get-tuple-element.54.refs_0_, bf16[328,128]{1,0:T(8,128)(2,1)S(1)} %collective-permute-done.11.refs_1_.refs_0_, ...), custom_call_target="tpu_custom_call" | custom-call | flops 30000001024 | bytes 1 | tf_op jit(solution)/shard_map/couple/pallas_call | solution.py:464
  54.6 1.5 %collective-permute-start.19 = (bf16[2,1,328,128]{3,2,1,0:T(8,128)(2,1)S(1)}, bf16[2,1,328,128]{3,2,1,0:T(8,128)(2,1)S(1)}, u32[]{:S(2)}, u32[]{:S(2)}) collective-permute-start(bf16[2,1,328,128]{3,2,1,0:T(8,128)(2,1)S(1)} %get-tuple-element.62), channel_id=1, source_target_pairs={{0,8},{4,12},{8,0},{12,4},{16,24},{20,28},{24,16},{28,20},{1,9},{5... | collective-permute-start | bytes 503816 | tf_op jit(solution)/shard_map/ppermute | solution.py:367
  56.1 1.7 %collective-permute-start.20 = (bf16[2,1,328,128]{3,2,1,0:T(8,128)(2,1)S(1)}, bf16[2,1,328,128]{3,2,1,0:T(8,128)(2,1)S(1)}, u32[]{:S(2)}, u32[]{:S(2)}) collective-permute-start(bf16[2,1,328,128]{3,2,1,0:T(8,128)(2,1)S(1)} %get-tuple-element.63), channel_id=1, source_target_pairs={{0,16},{4,20},{8,24},{12,28},{16,0},{20,4},{24,8},{28,12},{1,17},{... | collective-permute-start | bytes 503816 | tf_op jit(solution)/shard_map/ppermute | solution.py:367
  57.9 2.6 %collective-permute-done.23.refs_2_ = bf16[328,256]{1,0:T(8,128)(2,1)S(1)} collective-permute-done((bf16[328,256]{1,0:T(8,128)(2,1)S(1)}, bf16[328,256]{1,0:T(8,128)(2,1)S(1)}, u32[]{:S(2)}, u32[]{:S(2)}) %collective-permute-start.23) | collective-permute-done | bytes 167968 | tf_op jit(solution)/shard_map/ppermute | solution.py:367
  60.5 3.3 %collective-permute-start.21 = (bf16[2,1,328,128]{3,2,1,0:T(8,128)(2,1)S(1)}, bf16[2,1,328,128]{3,2,1,0:T(8,128)(2,1)S(1)}, u32[]{:S(2)}, u32[]{:S(2)}) collective-permute-start(bf16[2,1,328,128]{3,2,1,0:T(8,128)(2,1)S(1)} %get-tuple-element.64), channel_id=1, source_target_pairs={{0,24},{4,28},{8,16},{12,20},{16,8},{20,12},{24,0},{28,4},{1,25},{... | collective-permute-start | bytes 503816 | tf_op jit(solution)/shard_map/ppermute | solution.py:367
  63.9 2.1 %couple.5 = (bf16[2,1,328,128]{3,2,1,0:T(8,128)(2,1)S(1)}, bf16[2,1,328,128]{3,2,1,0:T(8,128)(2,1)S(1)}, bf16[2,1,328,128]{3,2,1,0:T(8,128)(2,1)S(1)}, bf16[2,1,328,128]{3,2,1,0:T(8,128)(2,1)S(1)}) custom-call(bf16[328,256]{1,0:T(8,128)(2,1)S(1)} %get-tuple-element.65.refs_0_, bf16[328,256]{1,0:T(8,128)(2,1)S(1)} %collective-permute-done.22.refs_1_, ...), custom_call_target="tpu_custom_call" | custom-call | flops 30000001024 | bytes 1 | tf_op jit(solution)/shard_map/couple/pallas_call | solution.py:464
  67.3 1.7 %place.2.refs_6_ = bf16[1296,1024]{1,0:T(8,128)(2,1)} custom-call(bf16[2,2,328,128]{3,2,1,0:T(8,128)(2,1)S(1)} %get-tuple-element.50.refs_2_.refs_0_.refs_3_, bf16[2,1,328,128]{3,2,1,0:T(8,128)(2,1)S(1)} %get-tuple-element.61.refs_4_.refs_0_.refs_1_, bf16[2,1,328,128]{3,2,1,0:T(8,128)(2,1)S(1)} %get-tuple-element.67.refs_4_.refs_2_, ...), custom_call_target="tpu_custom_call" | custom-call | flops 1 | bytes 1 | tf_op jit(solution)/shard_map/place/pallas_call | solution.py:304
  69.0 1.7 %place.3 = bf16[1296,1024]{1,0:T(8,128)(2,1)} custom-call(bf16[4,2,328,128]{3,2,1,0:T(8,128)(2,1)S(1)} %collective-permute-done.18.refs_0_, bf16[4,1,328,128]{3,2,1,0:T(8,128)(2,1)S(1)} %collective-permute-done.25.refs_1_, bf16[2,1,328,128]{3,2,1,0:T(8,128)(2,1)S(1)} %get-tuple-element.67.refs_4_.refs_2_, ...), custom_call_target="tpu_custom_call", output_to_operand_aliasing={{}: (6, {})} | custom-call | flops 1 | bytes 1 | tf_op jit(solution)/shard_map/place/pallas_call | solution.py:304
  (66 shorter events, 14.3 us)
Async XLA Ops:
  1.8 7.5 %collective-permute-start.1 = (bf16[324,512]{1,0:T(8,128)(2,1)S(1)}, bf16[324,512]{1,0:T(8,128)(2,1)S(1)}, u32[]{:S(2)}, u32[]{:S(2)}) collective-permute-start(bf16[324,512]{1,0:T(8,128)(2,1)S(1)} %get-tuple-element.73), channel_id=1, source_target_pairs={{0,4},{4,0},{8,12},{12,8},{16,20},{20,16},{24,28},{28,24},{1,5},{5... | collective-permute-start | bytes 995336 | tf_op jit(solution)/shard_map/ppermute | solution.py:367
  2.3 11.9 %collective-permute-start = (bf16[324,512]{1,0:T(8,128)(2,1)S(1)}, bf16[324,512]{1,0:T(8,128)(2,1)S(1)}, u32[]{:S(2)}, u32[]{:S(2)}) collective-permute-start(bf16[324,512]{1,0:T(8,128)(2,1)S(1)} %get-tuple-element.74), channel_id=1, source_target_pairs={{4,8},{12,16},{20,24},{8,4},{16,12},{24,20},{5,9},{13,17},{21,25},... | collective-permute-start | bytes 995336 | tf_op jit(solution)/shard_map/ppermute | solution.py:394
  3.0 7.9 %collective-permute-start.4 = (s32[1,512]{1,0:T(1,128)S(1)}, s32[1,512]{1,0:T(1,128)S(1)}, u32[]{:S(2)}, u32[]{:S(2)}) collective-permute-start(s32[1,512]{1,0:T(1,128)S(1)} %bitcast.19), channel_id=1, source_target_pairs={{0,3},{1,2},{2,1},{3,0},{4,7},{5,6},{6,5},{7,4},{8,11},{9,10},{10,... | collective-permute-start | bytes 6152 | tf_op jit(solution)/shard_map/ppermute | solution.py:367
  7.7 4.5 %collective-permute-start.3 = (s32[1,512]{1,0:T(1,128)S(1)}, s32[1,512]{1,0:T(1,128)S(1)}, u32[]{:S(2)}, u32[]{:S(2)}) collective-permute-start(s32[1,512]{1,0:T(1,128)S(1)} %bitcast.20), channel_id=1, source_target_pairs={{0,2},{1,3},{2,0},{3,1},{4,6},{5,7},{6,4},{7,5},{8,10},{9,11},{10,... | collective-permute-start | bytes 6152 | tf_op jit(solution)/shard_map/ppermute | solution.py:367
  16.0 9.9 %collective-permute-start.5 = (bf16[328,256]{1,0:T(8,128)(2,1)S(1)}, bf16[328,256]{1,0:T(8,128)(2,1)S(1)}, u32[]{:S(2)}, u32[]{:S(2)}) collective-permute-start(bf16[328,256]{1,0:T(8,128)(2,1)S(1)} %get-tuple-element.43), channel_id=1, source_target_pairs={{0,1},{1,0},{2,3},{3,2},{4,5},{5,4},{6,7},{7,6},{8,9},{9,8},{10,11... | collective-permute-start | bytes 503816 | tf_op jit(solution)/shard_map/ppermute | solution.py:367
  17.2 11.9 %collective-permute-start.6 = (bf16[328,256]{1,0:T(8,128)(2,1)S(1)}, bf16[328,256]{1,0:T(8,128)(2,1)S(1)}, u32[]{:S(2)}, u32[]{:S(2)}) collective-permute-start(bf16[328,256]{1,0:T(8,128)(2,1)S(1)} %get-tuple-element.44), channel_id=1, source_target_pairs={{0,2},{1,3},{2,0},{3,1},{4,6},{5,7},{6,4},{7,5},{8,10},{9,11},{10,... | collective-permute-start | bytes 503816 | tf_op jit(solution)/shard_map/ppermute | solution.py:367
  20.1 9.0 %collective-permute-start.14 = (bf16[2,1,328,128]{3,2,1,0:T(8,128)(2,1)S(1)}, bf16[2,1,328,128]{3,2,1,0:T(8,128)(2,1)S(1)}, u32[]{:S(2)}, u32[]{:S(2)}) collective-permute-start(bf16[2,1,328,128]{3,2,1,0:T(8,128)(2,1)S(1)} %get-tuple-element.56), channel_id=1, source_target_pairs={{0,8},{4,12},{8,0},{12,4},{16,24},{20,28},{24,16},{28,20},{1,9},{5... | collective-permute-start | bytes 503816 | tf_op jit(solution)/shard_map/ppermute | solution.py:367
  23.4 9.1 %collective-permute-start.15 = (bf16[2,1,328,128]{3,2,1,0:T(8,128)(2,1)S(1)}, bf16[2,1,328,128]{3,2,1,0:T(8,128)(2,1)S(1)}, u32[]{:S(2)}, u32[]{:S(2)}) collective-permute-start(bf16[2,1,328,128]{3,2,1,0:T(8,128)(2,1)S(1)} %get-tuple-element.57), channel_id=1, source_target_pairs={{0,16},{4,20},{8,24},{12,28},{16,0},{20,4},{24,8},{28,12},{1,17},{... | collective-permute-start | bytes 503816 | tf_op jit(solution)/shard_map/ppermute | solution.py:367
  24.9 7.6 %collective-permute-start.16 = (bf16[2,1,328,128]{3,2,1,0:T(8,128)(2,1)S(1)}, bf16[2,1,328,128]{3,2,1,0:T(8,128)(2,1)S(1)}, u32[]{:S(2)}, u32[]{:S(2)}) collective-permute-start(bf16[2,1,328,128]{3,2,1,0:T(8,128)(2,1)S(1)} %get-tuple-element.58), channel_id=1, source_target_pairs={{0,24},{4,28},{8,16},{12,20},{16,8},{20,12},{24,0},{28,4},{1,25},{... | collective-permute-start | bytes 503816 | tf_op jit(solution)/shard_map/ppermute | solution.py:367
  25.8 8.7 %collective-permute-start.7 = (bf16[328,256]{1,0:T(8,128)(2,1)S(1)}, bf16[328,256]{1,0:T(8,128)(2,1)S(1)}, u32[]{:S(2)}, u32[]{:S(2)}) collective-permute-start(bf16[328,256]{1,0:T(8,128)(2,1)S(1)} %get-tuple-element.45), channel_id=1, source_target_pairs={{0,3},{1,2},{2,1},{3,0},{4,7},{5,6},{6,5},{7,4},{8,11},{9,10},{10,... | collective-permute-start | bytes 503816 | tf_op jit(solution)/shard_map/ppermute | solution.py:367
  32.6 9.6 %collective-permute-start.17 = (bf16[4,1,328,128]{3,2,1,0:T(8,128)(2,1)S(1)}, bf16[4,1,328,128]{3,2,1,0:T(8,128)(2,1)S(1)}, u32[]{:S(2)}, u32[]{:S(2)}) collective-permute-start(bf16[4,1,328,128]{3,2,1,0:T(8,128)(2,1)S(1)} %stack.3), channel_id=1, source_target_pairs={{0,4},{4,0},{8,12},{12,8},{16,20},{20,16},{24,28},{28,24},{1,5},{5... | collective-permute-start | bytes 1007624 | tf_op jit(solution)/shard_map/ppermute | solution.py:367
  36.5 14.8 %collective-permute-start.10 = (bf16[2,2,328,128]{3,2,1,0:T(8,128)(2,1)S(1)}, bf16[2,2,328,128]{3,2,1,0:T(8,128)(2,1)S(1)}, u32[]{:S(2)}, u32[]{:S(2)}) collective-permute-start(bf16[2,2,328,128]{3,2,1,0:T(8,128)(2,1)S(1)} %get-tuple-element.53), channel_id=1, source_target_pairs={{0,24},{4,28},{8,16},{12,20},{16,8},{20,12},{24,0},{28,4},{1,25},{... | collective-permute-start | bytes 1007624 | tf_op jit(solution)/shard_map/ppermute | solution.py:367
  37.2 8.8 %collective-permute-start.12 = (bf16[328,128]{1,0:T(8,128)(2,1)S(1)}, bf16[328,128]{1,0:T(8,128)(2,1)S(1)}, u32[]{:S(2)}, u32[]{:S(2)}) collective-permute-start(bf16[328,128]{1,0:T(8,128)(2,1)S(1)} %gate.7.refs_7_), channel_id=1, source_target_pairs={{0,2},{1,3},{2,0},{3,1},{4,6},{5,7},{6,4},{7,5},{8,10},{9,11},{10,... | collective-permute-start | bytes 251912 | tf_op jit(solution)/shard_map/ppermute | solution.py:367
  40.8 8.4 %collective-permute-start.13 = (bf16[328,128]{1,0:T(8,128)(2,1)S(1)}, bf16[328,128]{1,0:T(8,128)(2,1)S(1)}, u32[]{:S(2)}, u32[]{:S(2)}) collective-permute-start(bf16[328,128]{1,0:T(8,128)(2,1)S(1)} %gate.8.refs_8_), channel_id=1, source_target_pairs={{0,3},{1,2},{2,1},{3,0},{4,7},{5,6},{6,5},{7,4},{8,11},{9,10},{10,... | collective-permute-start | bytes 251912 | tf_op jit(solution)/shard_map/ppermute | solution.py:367
  42.1 7.9 %collective-permute-start.11 = (bf16[328,128]{1,0:T(8,128)(2,1)S(1)}, bf16[328,128]{1,0:T(8,128)(2,1)S(1)}, u32[]{:S(2)}, u32[]{:S(2)}) collective-permute-start(bf16[328,128]{1,0:T(8,128)(2,1)S(1)} %gate.6.refs_6_), channel_id=1, source_target_pairs={{0,1},{1,0},{2,3},{3,2},{4,5},{5,4},{6,7},{7,6},{8,9},{9,8},{10,11... | collective-permute-start | bytes 251912 | tf_op jit(solution)/shard_map/ppermute | solution.py:367
  42.1 12.5 %collective-permute-start.8 = (bf16[2,2,328,128]{3,2,1,0:T(8,128)(2,1)S(1)}, bf16[2,2,328,128]{3,2,1,0:T(8,128)(2,1)S(1)}, u32[]{:S(2)}, u32[]{:S(2)}) collective-permute-start(bf16[2,2,328,128]{3,2,1,0:T(8,128)(2,1)S(1)} %get-tuple-element.51), channel_id=1, source_target_pairs={{0,8},{4,12},{8,0},{12,4},{16,24},{20,28},{24,16},{28,20},{1,9},{5... | collective-permute-start | bytes 1007624 | tf_op jit(solution)/shard_map/ppermute | solution.py:367
  46.0 10.1 %collective-permute-start.9 = (bf16[2,2,328,128]{3,2,1,0:T(8,128)(2,1)S(1)}, bf16[2,2,328,128]{3,2,1,0:T(8,128)(2,1)S(1)}, u32[]{:S(2)}, u32[]{:S(2)}) collective-permute-start(bf16[2,2,328,128]{3,2,1,0:T(8,128)(2,1)S(1)} %get-tuple-element.52), channel_id=1, source_target_pairs={{0,16},{4,20},{8,24},{12,28},{16,0},{20,4},{24,8},{28,12},{1,17},{... | collective-permute-start | bytes 1007624 | tf_op jit(solution)/shard_map/ppermute | solution.py:367
  49.2 11.3 %collective-permute-start.23 = (bf16[328,256]{1,0:T(8,128)(2,1)S(1)}, bf16[328,256]{1,0:T(8,128)(2,1)S(1)}, u32[]{:S(2)}, u32[]{:S(2)}) collective-permute-start(bf16[328,256]{1,0:T(8,128)(2,1)S(1)} %gate.9.refs_6_), channel_id=1, source_target_pairs={{0,2},{1,3},{2,0},{3,1},{4,6},{5,7},{6,4},{7,5},{8,10},{9,11},{10,... | collective-permute-start | bytes 503816 | tf_op jit(solution)/shard_map/ppermute | solution.py:367
  50.0 13.8 %collective-permute-start.24 = (bf16[328,256]{1,0:T(8,128)(2,1)S(1)}, bf16[328,256]{1,0:T(8,128)(2,1)S(1)}, u32[]{:S(2)}, u32[]{:S(2)}) collective-permute-start(bf16[328,256]{1,0:T(8,128)(2,1)S(1)} %gate.10.refs_7_), channel_id=1, source_target_pairs={{0,3},{1,2},{2,1},{3,0},{4,7},{5,6},{6,5},{7,4},{8,11},{9,10},{10,... | collective-permute-start | bytes 503816 | tf_op jit(solution)/shard_map/ppermute | solution.py:367
  51.2 12.6 %collective-permute-start.22 = (bf16[328,256]{1,0:T(8,128)(2,1)S(1)}, bf16[328,256]{1,0:T(8,128)(2,1)S(1)}, u32[]{:S(2)}, u32[]{:S(2)}) collective-permute-start(bf16[328,256]{1,0:T(8,128)(2,1)S(1)} %gate.11), channel_id=1, source_target_pairs={{0,1},{1,0},{2,3},{3,2},{4,5},{5,4},{6,7},{7,6},{8,9},{9,8},{10,11... | collective-permute-start | bytes 503816 | tf_op jit(solution)/shard_map/ppermute | solution.py:367
  54.6 11.4 %collective-permute-start.19 = (bf16[2,1,328,128]{3,2,1,0:T(8,128)(2,1)S(1)}, bf16[2,1,328,128]{3,2,1,0:T(8,128)(2,1)S(1)}, u32[]{:S(2)}, u32[]{:S(2)}) collective-permute-start(bf16[2,1,328,128]{3,2,1,0:T(8,128)(2,1)S(1)} %get-tuple-element.62), channel_id=1, source_target_pairs={{0,8},{4,12},{8,0},{12,4},{16,24},{20,28},{24,16},{28,20},{1,9},{5... | collective-permute-start | bytes 503816 | tf_op jit(solution)/shard_map/ppermute | solution.py:367
  56.1 9.9 %collective-permute-start.20 = (bf16[2,1,328,128]{3,2,1,0:T(8,128)(2,1)S(1)}, bf16[2,1,328,128]{3,2,1,0:T(8,128)(2,1)S(1)}, u32[]{:S(2)}, u32[]{:S(2)}) collective-permute-start(bf16[2,1,328,128]{3,2,1,0:T(8,128)(2,1)S(1)} %get-tuple-element.63), channel_id=1, source_target_pairs={{0,16},{4,20},{8,24},{12,28},{16,0},{20,4},{24,8},{28,12},{1,17},{... | collective-permute-start | bytes 503816 | tf_op jit(solution)/shard_map/ppermute | solution.py:367
  60.5 6.7 %collective-permute-start.21 = (bf16[2,1,328,128]{3,2,1,0:T(8,128)(2,1)S(1)}, bf16[2,1,328,128]{3,2,1,0:T(8,128)(2,1)S(1)}, u32[]{:S(2)}, u32[]{:S(2)}) collective-permute-start(bf16[2,1,328,128]{3,2,1,0:T(8,128)(2,1)S(1)} %get-tuple-element.64), channel_id=1, source_target_pairs={{0,24},{4,28},{8,16},{12,20},{16,8},{20,12},{24,0},{28,4},{1,25},{... | collective-permute-start | bytes 503816 | tf_op jit(solution)/shard_map/ppermute | solution.py:367
  63.9 5.1 %collective-permute-start.18 = (bf16[4,2,328,128]{3,2,1,0:T(8,128)(2,1)S(1)}, bf16[4,2,328,128]{3,2,1,0:T(8,128)(2,1)S(1)}, u32[]{:S(2)}, u32[]{:S(2)}) collective-permute-start(bf16[4,2,328,128]{3,2,1,0:T(8,128)(2,1)S(1)} %stack.4), channel_id=1, source_target_pairs={{0,4},{4,0},{8,12},{12,8},{16,20},{20,16},{24,28},{28,24},{1,5},{5... | collective-permute-start | bytes 2015240 | tf_op jit(solution)/shard_map/ppermute | solution.py:367
  (6 other events, 31.1 us)

commit v11 on v10

--- a/solution.py
+++ b/solution.py
@@ -254,9 +254,9 @@
             start = (v ^ quarter) * held
             lead = start % 8
             updated = values[start - lead : start - lead + tall, cut]
-            if lead:
-                updated = pltpu.roll(updated, tall - lead, 0)
-            updated = jnp.where(row_id < held, updated, jnp.where(row_id == held, rank[:, cut], 0.0))
+            spare = row_id == (0 if lead else held)
+            mine = row_id >= lead if lead else row_id < held
+            updated = jnp.where(spare, rank[:, cut], jnp.where(mine, updated, 0.0))
             group = (towards[:, cut] & (CHUNKS - 1)) ^ v
             column = towards[:, cut] // CHUNKS * LANES + group * slots + slot[:, cut]
             route = (slot_id == column).astype(F32).astype(BF16)
@@ -271,15 +271,23 @@
     me = lax.axis_index("pts")
     tall = refs[0].shape[-2]
     slot_id = iota((LANES, LANES), 0)
+    is_first = iota((8, LANES), 0) < 4
     copies = []
     for number, x in enumerate(sources):
         blocks = [refs[n][index] for n, index in picks[number]]
-        pieces = []
+        groups = []
         for g in range(CHUNKS):
             lhs = lane_groups(blocks, (x % CHUNKS) ^ g)
-            rank = lhs[tall - 8 :, :].astype(F32)[held - tall + 8 : held - tall + 9, :].astype(I32)
+            if g * held % 8:
+                rank = lhs[0:8, :].astype(F32)[0:1, :].astype(I32)
+            else:
+                rank = lhs[tall - 8 :, :].astype(F32)[held - tall + 8 : held - tall + 9, :].astype(I32)
             spots = (slot_id == rank).astype(F32).astype(BF16)
-            pieces.append(dot_nt(lhs, spots)[:held])
+            groups.append(dot_nt(lhs, spots))
+        pieces = []
+        for g in range(0, CHUNKS, 2):
+            seam = jnp.where(is_first, groups[g][tall - 8 :], groups[g + 1][:8])
+            pieces += [groups[g][: tall - 8], seam, groups[g + 1][8:]]
         staged[number] = jnp.concatenate(pieces, axis=0).astype(BF16)
         at = pl.ds(pl.multiple_of((me ^ x) * LANES, LANES), LANES)
         copy = pltpu.make_async_copy(staged.at[number], out.at[:, at], sems.at[number])

time: 71.8 us -> 71.8 us (level)
  no operation moved by 1% of the time
where the time goes in v11:
time: 71.8 us; the launch traced here: 70.8 us
  starting transfers between devices  40.5 us (56%)
  Pallas kernels  16.7 us (23%)
  waiting for transfers between devices  10.1 us (14%)
  local copies, waits for them, and re-layouts  2.11 us (3%)
  other arithmetic  0.93 us (1%)
    ppermute x25, starting transfers between devices, exchange(): lax.ppermute(array, axis, [(i, i ^ offset) for i in range(lax.axis_size(a...  39.9 us
    ppermute x25, waiting for transfers between devices, exchange(): lax.ppermute(array, axis, [(i, i ^ offset) for i in range(lax.axis_size(a...  10 us
    pallas_call x3, Pallas kernels, couple(): pl.pallas_call(functools.partial(couple_kernel, quarters, bins_axis, loca...  5.68 us
    pallas_call x2, Pallas kernels, place(): pl.pallas_call(functools.partial(place_kernel, all_bins // CHUNKS, tuple(...  3.33 us
    pallas_call x2, Pallas kernels, chunked(): pl.pallas_call(functools.partial(order_kernel, group, owners_count, width...  3.06 us
    pallas_call x1, Pallas kernels, chunked(): pl.pallas_call(functools.partial(pack_kernel, rows, bins_axis, width, pai...  1.7 us
    unnamed x9, local copies, waits for them, and re-layouts  1.62 us
  transfers between devices with their start and end apart: 26, of which 6 were waited for; matrix products, arithmetic and copies ran while one was open for 2% of the time, Pallas kernels for 19%

profile of v11, /device:TPU:0, one launch (start us, length us, event | category | flops | bytes accessed | tf_op | source)
XLA Modules:
  0.0 70.8 jit_solution(17839958188541270762)
XLA Ops:
  0.0 1.6 %copy.10 = bf16[324,4,512]{2,0,1:T(8,128)(2,1)S(1)} copy(bf16[324,4,512]{2,1,0:T(4,128)(2,1)} %param.6) | data formatting | bytes 2654208 | tf_op args[0]
  3.0 4.7 %collective-permute-start.4 = (s32[1,512]{1,0:T(1,128)S(1)}, s32[1,512]{1,0:T(1,128)S(1)}, u32[]{:S(2)}, u32[]{:S(2)}) collective-permute-start(s32[1,512]{1,0:T(1,128)S(1)} %bitcast.19), channel_id=1, source_target_pairs={{0,3},{1,2},{2,1},{3,0},{4,7},{5,6},{6,5},{7,4},{8,11},{9,10},{10,... | collective-permute-start | bytes 6152 | tf_op jit(solution)/shard_map/ppermute | solution.py:375
  12.2 2.0 %order.2 = (bf16[3,336,640]{2,1,0:T(8,128)(2,1)S(1)}, bf16[3,640,128]{2,1,0:T(8,128)(2,1)S(1)}, f32[8,384]{1,0:T(8,128)S(1)}) custom-call(bf16[3,336,512]{2,1,0:T(8,128)(2,1)S(1)} %inner.1.refs_0_, s32[4,512]{1,0:T(4,128)S(1)} %copy-done.2, s32[1,512]{1,0:T(1,128)S(1)} %bitcast.22, s32[1,512]{1,0:T(1,128)S(1)} %collective-permute-done.2.refs_3_, ...), custom_call_target="tpu_custom_call" | custom-call | flops 1 | bytes 1 | tf_op jit(solution)/shard_map/order/pallas_call | solution.py:442
  14.3 1.7 %pack.1 = (bf16[328,256]{1,0:T(8,128)(2,1)S(1)}, bf16[328,256]{1,0:T(8,128)(2,1)S(1)}, bf16[328,256]{1,0:T(8,128)(2,1)S(1)}, bf16[328,256]{1,0:T(8,128)(2,1)S(1)...) custom-call(bf16[4,336,512]{2,1,0:T(8,128)(2,1)S(1)} %pad.12.planes., ...), custom_call_target="tpu_custom_call" | custom-call | flops 1 | bytes 1 | tf_op jit(solution)/shard_map/pack/pallas_call | solution.py:454
  17.2 2.9 %collective-permute-start.6 = (bf16[328,256]{1,0:T(8,128)(2,1)S(1)}, bf16[328,256]{1,0:T(8,128)(2,1)S(1)}, u32[]{:S(2)}, u32[]{:S(2)}) collective-permute-start(bf16[328,256]{1,0:T(8,128)(2,1)S(1)} %get-tuple-element.44), channel_id=1, source_target_pairs={{0,2},{1,3},{2,0},{3,1},{4,6},{5,7},{6,4},{7,5},{8,10},{9,11},{10,... | collective-permute-start | bytes 503816 | tf_op jit(solution)/shard_map/ppermute | solution.py:375
  20.1 3.3 %collective-permute-start.14 = (bf16[2,1,328,128]{3,2,1,0:T(8,128)(2,1)S(1)}, bf16[2,1,328,128]{3,2,1,0:T(8,128)(2,1)S(1)}, u32[]{:S(2)}, u32[]{:S(2)}) collective-permute-start(bf16[2,1,328,128]{3,2,1,0:T(8,128)(2,1)S(1)} %get-tuple-element.56), channel_id=1, source_target_pairs={{0,8},{4,12},{8,0},{12,4},{16,24},{20,28},{24,16},{28,20},{1,9},{5... | collective-permute-start | bytes 503816 | tf_op jit(solution)/shard_map/ppermute | solution.py:375
  23.4 1.5 %collective-permute-start.15 = (bf16[2,1,328,128]{3,2,1,0:T(8,128)(2,1)S(1)}, bf16[2,1,328,128]{3,2,1,0:T(8,128)(2,1)S(1)}, u32[]{:S(2)}, u32[]{:S(2)}) collective-permute-start(bf16[2,1,328,128]{3,2,1,0:T(8,128)(2,1)S(1)} %get-tuple-element.57), channel_id=1, source_target_pairs={{0,16},{4,20},{8,24},{12,28},{16,0},{20,4},{24,8},{28,12},{1,17},{... | collective-permute-start | bytes 503816 | tf_op jit(solution)/shard_map/ppermute | solution.py:375
  25.8 2.0 %collective-permute-start.7 = (bf16[328,256]{1,0:T(8,128)(2,1)S(1)}, bf16[328,256]{1,0:T(8,128)(2,1)S(1)}, u32[]{:S(2)}, u32[]{:S(2)}) collective-permute-start(bf16[328,256]{1,0:T(8,128)(2,1)S(1)} %get-tuple-element.45), channel_id=1, source_target_pairs={{0,3},{1,2},{2,1},{3,0},{4,7},{5,6},{6,5},{7,4},{8,11},{9,10},{10,... | collective-permute-start | bytes 503816 | tf_op jit(solution)/shard_map/ppermute | solution.py:375
  29.1 3.5 %collective-permute-done.15.refs_2_ = bf16[2,1,328,128]{3,2,1,0:T(8,128)(2,1)S(1)} collective-permute-done((bf16[2,1,328,128]{3,2,1,0:T(8,128)(2,1)S(1)}, bf16[2,1,328,128]{3,2,1,0:T(8,128)(2,1)S(1)}, u32[]{:S(2)}, u32[]{:S(2)}) %collective-permute-start.15) | collective-permute-done | bytes 167968 | tf_op jit(solution)/shard_map/ppermute | solution.py:375
  32.7 1.8 %collective-permute-done.7.refs_2_.refs_3_ = bf16[328,256]{1,0:T(8,128)(2,1)S(1)} collective-permute-done((bf16[328,256]{1,0:T(8,128)(2,1)S(1)}, bf16[328,256]{1,0:T(8,128)(2,1)S(1)}, u32[]{:S(2)}, u32[]{:S(2)}) %collective-permute-start.7) | collective-permute-done | bytes 167968 | tf_op jit(solution)/shard_map/ppermute | solution.py:375
  34.5 1.9 %couple.3 = (bf16[2,2,328,128]{3,2,1,0:T(8,128)(2,1)S(1)}, bf16[2,2,328,128]{3,2,1,0:T(8,128)(2,1)S(1)}, bf16[2,2,328,128]{3,2,1,0:T(8,128)(2,1)S(1)}, bf16[2,2,328,128]{3,2,1,0:T(8,128)(2,1)S(1)}) custom-call(bf16[328,256]{1,0:T(8,128)(2,1)S(1)} %get-tuple-element.42.refs_0_, bf16[328,256]{1,0:T(8,128)(2,1)S(1)} %collective-permute-done.5.refs_0_.refs_1_.refs_4_, ...), custom_call_target="tpu_custom_call" | custom-call | flops 3000000000 | bytes 1 | tf_op jit(solution)/shard_map/couple/pallas_call | solution.py:472
  37.2 3.6 %collective-permute-start.12 = (bf16[328,128]{1,0:T(8,128)(2,1)S(1)}, bf16[328,128]{1,0:T(8,128)(2,1)S(1)}, u32[]{:S(2)}, u32[]{:S(2)}) collective-permute-start(bf16[328,128]{1,0:T(8,128)(2,1)S(1)} %gate.7.refs_7_), channel_id=1, source_target_pairs={{0,2},{1,3},{2,0},{3,1},{4,6},{5,7},{6,4},{7,5},{8,10},{9,11},{10,... | collective-permute-start | bytes 251912 | tf_op jit(solution)/shard_map/ppermute | solution.py:375
  40.8 1.3 %collective-permute-start.13 = (bf16[328,128]{1,0:T(8,128)(2,1)S(1)}, bf16[328,128]{1,0:T(8,128)(2,1)S(1)}, u32[]{:S(2)}, u32[]{:S(2)}) collective-permute-start(bf16[328,128]{1,0:T(8,128)(2,1)S(1)} %gate.8.refs_8_), channel_id=1, source_target_pairs={{0,3},{1,2},{2,1},{3,0},{4,7},{5,6},{6,5},{7,4},{8,11},{9,10},{10,... | collective-permute-start | bytes 251912 | tf_op jit(solution)/shard_map/ppermute | solution.py:375
  42.1 2.9 %collective-permute-start.8 = (bf16[2,2,328,128]{3,2,1,0:T(8,128)(2,1)S(1)}, bf16[2,2,328,128]{3,2,1,0:T(8,128)(2,1)S(1)}, u32[]{:S(2)}, u32[]{:S(2)}) collective-permute-start(bf16[2,2,328,128]{3,2,1,0:T(8,128)(2,1)S(1)} %get-tuple-element.51), channel_id=1, source_target_pairs={{0,8},{4,12},{8,0},{12,4},{16,24},{20,28},{24,16},{28,20},{1,9},{5... | collective-permute-start | bytes 1007624 | tf_op jit(solution)/shard_map/ppermute | solution.py:375
  46.0 3.2 %collective-permute-start.9 = (bf16[2,2,328,128]{3,2,1,0:T(8,128)(2,1)S(1)}, bf16[2,2,328,128]{3,2,1,0:T(8,128)(2,1)S(1)}, u32[]{:S(2)}, u32[]{:S(2)}) collective-permute-start(bf16[2,2,328,128]{3,2,1,0:T(8,128)(2,1)S(1)} %get-tuple-element.52), channel_id=1, source_target_pairs={{0,16},{4,20},{8,24},{12,28},{16,0},{20,4},{24,8},{28,12},{1,17},{... | collective-permute-start | bytes 1007624 | tf_op jit(solution)/shard_map/ppermute | solution.py:375
  51.2 1.7 %collective-permute-start.22 = (bf16[328,256]{1,0:T(8,128)(2,1)S(1)}, bf16[328,256]{1,0:T(8,128)(2,1)S(1)}, u32[]{:S(2)}, u32[]{:S(2)}) collective-permute-start(bf16[328,256]{1,0:T(8,128)(2,1)S(1)} %gate.11), channel_id=1, source_target_pairs={{0,1},{1,0},{2,3},{3,2},{4,5},{5,4},{6,7},{7,6},{8,9},{9,8},{10,11... | collective-permute-start | bytes 503816 | tf_op jit(solution)/shard_map/ppermute | solution.py:375
  53.0 1.6 %couple.4 = (bf16[2,1,328,128]{3,2,1,0:T(8,128)(2,1)S(1)}, bf16[2,1,328,128]{3,2,1,0:T(8,128)(2,1)S(1)}, bf16[2,1,328,128]{3,2,1,0:T(8,128)(2,1)S(1)}, bf16[2,1,328,128]{3,2,1,0:T(8,128)(2,1)S(1)}) custom-call(bf16[328,128]{1,0:T(8,128)(2,1)S(1)} %get-tuple-element.54.refs_0_, bf16[328,128]{1,0:T(8,128)(2,1)S(1)} %collective-permute-done.11.refs_1_.refs_0_, ...), custom_call_target="tpu_custom_call" | custom-call | flops 30000001024 | bytes 1 | tf_op jit(solution)/shard_map/couple/pallas_call | solution.py:472
  54.6 1.5 %collective-permute-start.19 = (bf16[2,1,328,128]{3,2,1,0:T(8,128)(2,1)S(1)}, bf16[2,1,328,128]{3,2,1,0:T(8,128)(2,1)S(1)}, u32[]{:S(2)}, u32[]{:S(2)}) collective-permute-start(bf16[2,1,328,128]{3,2,1,0:T(8,128)(2,1)S(1)} %get-tuple-element.62), channel_id=1, source_target_pairs={{0,8},{4,12},{8,0},{12,4},{16,24},{20,28},{24,16},{28,20},{1,9},{5... | collective-permute-start | bytes 503816 | tf_op jit(solution)/shard_map/ppermute | solution.py:375
  56.1 1.7 %collective-permute-start.20 = (bf16[2,1,328,128]{3,2,1,0:T(8,128)(2,1)S(1)}, bf16[2,1,328,128]{3,2,1,0:T(8,128)(2,1)S(1)}, u32[]{:S(2)}, u32[]{:S(2)}) collective-permute-start(bf16[2,1,328,128]{3,2,1,0:T(8,128)(2,1)S(1)} %get-tuple-element.63), channel_id=1, source_target_pairs={{0,16},{4,20},{8,24},{12,28},{16,0},{20,4},{24,8},{28,12},{1,17},{... | collective-permute-start | bytes 503816 | tf_op jit(solution)/shard_map/ppermute | solution.py:375
  57.9 2.6 %collective-permute-done.23.refs_2_ = bf16[328,256]{1,0:T(8,128)(2,1)S(1)} collective-permute-done((bf16[328,256]{1,0:T(8,128)(2,1)S(1)}, bf16[328,256]{1,0:T(8,128)(2,1)S(1)}, u32[]{:S(2)}, u32[]{:S(2)}) %collective-permute-start.23) | collective-permute-done | bytes 167968 | tf_op jit(solution)/shard_map/ppermute | solution.py:375
  60.5 3.3 %collective-permute-start.21 = (bf16[2,1,328,128]{3,2,1,0:T(8,128)(2,1)S(1)}, bf16[2,1,328,128]{3,2,1,0:T(8,128)(2,1)S(1)}, u32[]{:S(2)}, u32[]{:S(2)}) collective-permute-start(bf16[2,1,328,128]{3,2,1,0:T(8,128)(2,1)S(1)} %get-tuple-element.64), channel_id=1, source_target_pairs={{0,24},{4,28},{8,16},{12,20},{16,8},{20,12},{24,0},{28,4},{1,25},{... | collective-permute-start | bytes 503816 | tf_op jit(solution)/shard_map/ppermute | solution.py:375
  63.9 2.1 %couple.5 = (bf16[2,1,328,128]{3,2,1,0:T(8,128)(2,1)S(1)}, bf16[2,1,328,128]{3,2,1,0:T(8,128)(2,1)S(1)}, bf16[2,1,328,128]{3,2,1,0:T(8,128)(2,1)S(1)}, bf16[2,1,328,128]{3,2,1,0:T(8,128)(2,1)S(1)}) custom-call(bf16[328,256]{1,0:T(8,128)(2,1)S(1)} %get-tuple-element.65.refs_0_, bf16[328,256]{1,0:T(8,128)(2,1)S(1)} %collective-permute-done.22.refs_1_, ...), custom_call_target="tpu_custom_call" | custom-call | flops 30000001024 | bytes 1 | tf_op jit(solution)/shard_map/couple/pallas_call | solution.py:472
  67.3 1.7 %place.2.refs_6_ = bf16[1296,1024]{1,0:T(8,128)(2,1)} custom-call(bf16[2,2,328,128]{3,2,1,0:T(8,128)(2,1)S(1)} %get-tuple-element.50.refs_2_.refs_0_.refs_3_, bf16[2,1,328,128]{3,2,1,0:T(8,128)(2,1)S(1)} %get-tuple-element.61.refs_4_.refs_0_.refs_1_, bf16[2,1,328,128]{3,2,1,0:T(8,128)(2,1)S(1)} %get-tuple-element.67.refs_4_.refs_2_, ...), custom_call_target="tpu_custom_call" | custom-call | flops 1 | bytes 1 | tf_op jit(solution)/shard_map/place/pallas_call | solution.py:312
  69.0 1.7 %place.3 = bf16[1296,1024]{1,0:T(8,128)(2,1)} custom-call(bf16[4,2,328,128]{3,2,1,0:T(8,128)(2,1)S(1)} %collective-permute-done.18.refs_0_, bf16[4,1,328,128]{3,2,1,0:T(8,128)(2,1)S(1)} %collective-permute-done.25.refs_1_, bf16[2,1,328,128]{3,2,1,0:T(8,128)(2,1)S(1)} %get-tuple-element.67.refs_4_.refs_2_, ...), custom_call_target="tpu_custom_call", output_to_operand_aliasing={{}: (6, {})} | custom-call | flops 1 | bytes 1 | tf_op jit(solution)/shard_map/place/pallas_call | solution.py:312
  (66 shorter events, 14.3 us)
Async XLA Ops:
  1.8 7.5 %collective-permute-start.1 = (bf16[324,512]{1,0:T(8,128)(2,1)S(1)}, bf16[324,512]{1,0:T(8,128)(2,1)S(1)}, u32[]{:S(2)}, u32[]{:S(2)}) collective-permute-start(bf16[324,512]{1,0:T(8,128)(2,1)S(1)} %get-tuple-element.73), channel_id=1, source_target_pairs={{0,4},{4,0},{8,12},{12,8},{16,20},{20,16},{24,28},{28,24},{1,5},{5... | collective-permute-start | bytes 995336 | tf_op jit(solution)/shard_map/ppermute | solution.py:375
  2.3 11.9 %collective-permute-start = (bf16[324,512]{1,0:T(8,128)(2,1)S(1)}, bf16[324,512]{1,0:T(8,128)(2,1)S(1)}, u32[]{:S(2)}, u32[]{:S(2)}) collective-permute-start(bf16[324,512]{1,0:T(8,128)(2,1)S(1)} %get-tuple-element.74), channel_id=1, source_target_pairs={{4,8},{12,16},{20,24},{8,4},{16,12},{24,20},{5,9},{13,17},{21,25},... | collective-permute-start | bytes 995336 | tf_op jit(solution)/shard_map/ppermute | solution.py:402
  3.0 7.9 %collective-permute-start.4 = (s32[1,512]{1,0:T(1,128)S(1)}, s32[1,512]{1,0:T(1,128)S(1)}, u32[]{:S(2)}, u32[]{:S(2)}) collective-permute-start(s32[1,512]{1,0:T(1,128)S(1)} %bitcast.19), channel_id=1, source_target_pairs={{0,3},{1,2},{2,1},{3,0},{4,7},{5,6},{6,5},{7,4},{8,11},{9,10},{10,... | collective-permute-start | bytes 6152 | tf_op jit(solution)/shard_map/ppermute | solution.py:375
  7.7 4.5 %collective-permute-start.3 = (s32[1,512]{1,0:T(1,128)S(1)}, s32[1,512]{1,0:T(1,128)S(1)}, u32[]{:S(2)}, u32[]{:S(2)}) collective-permute-start(s32[1,512]{1,0:T(1,128)S(1)} %bitcast.20), channel_id=1, source_target_pairs={{0,2},{1,3},{2,0},{3,1},{4,6},{5,7},{6,4},{7,5},{8,10},{9,11},{10,... | collective-permute-start | bytes 6152 | tf_op jit(solution)/shard_map/ppermute | solution.py:375
  16.0 9.9 %collective-permute-start.5 = (bf16[328,256]{1,0:T(8,128)(2,1)S(1)}, bf16[328,256]{1,0:T(8,128)(2,1)S(1)}, u32[]{:S(2)}, u32[]{:S(2)}) collective-permute-start(bf16[328,256]{1,0:T(8,128)(2,1)S(1)} %get-tuple-element.43), channel_id=1, source_target_pairs={{0,1},{1,0},{2,3},{3,2},{4,5},{5,4},{6,7},{7,6},{8,9},{9,8},{10,11... | collective-permute-start | bytes 503816 | tf_op jit(solution)/shard_map/ppermute | solution.py:375
  17.2 11.9 %collective-permute-start.6 = (bf16[328,256]{1,0:T(8,128)(2,1)S(1)}, bf16[328,256]{1,0:T(8,128)(2,1)S(1)}, u32[]{:S(2)}, u32[]{:S(2)}) collective-permute-start(bf16[328,256]{1,0:T(8,128)(2,1)S(1)} %get-tuple-element.44), channel_id=1, source_target_pairs={{0,2},{1,3},{2,0},{3,1},{4,6},{5,7},{6,4},{7,5},{8,10},{9,11},{10,... | collective-permute-start | bytes 503816 | tf_op jit(solution)/shard_map/ppermute | solution.py:375
  20.1 9.0 %collective-permute-start.14 = (bf16[2,1,328,128]{3,2,1,0:T(8,128)(2,1)S(1)}, bf16[2,1,328,128]{3,2,1,0:T(8,128)(2,1)S(1)}, u32[]{:S(2)}, u32[]{:S(2)}) collective-permute-start(bf16[2,1,328,128]{3,2,1,0:T(8,128)(2,1)S(1)} %get-tuple-element.56), channel_id=1, source_target_pairs={{0,8},{4,12},{8,0},{12,4},{16,24},{20,28},{24,16},{28,20},{1,9},{5... | collective-permute-start | bytes 503816 | tf_op jit(solution)/shard_map/ppermute | solution.py:375
  23.4 9.1 %collective-permute-start.15 = (bf16[2,1,328,128]{3,2,1,0:T(8,128)(2,1)S(1)}, bf16[2,1,328,128]{3,2,1,0:T(8,128)(2,1)S(1)}, u32[]{:S(2)}, u32[]{:S(2)}) collective-permute-start(bf16[2,1,328,128]{3,2,1,0:T(8,128)(2,1)S(1)} %get-tuple-element.57), channel_id=1, source_target_pairs={{0,16},{4,20},{8,24},{12,28},{16,0},{20,4},{24,8},{28,12},{1,17},{... | collective-permute-start | bytes 503816 | tf_op jit(solution)/shard_map/ppermute | solution.py:375
  24.9 7.6 %collective-permute-start.16 = (bf16[2,1,328,128]{3,2,1,0:T(8,128)(2,1)S(1)}, bf16[2,1,328,128]{3,2,1,0:T(8,128)(2,1)S(1)}, u32[]{:S(2)}, u32[]{:S(2)}) collective-permute-start(bf16[2,1,328,128]{3,2,1,0:T(8,128)(2,1)S(1)} %get-tuple-element.58), channel_id=1, source_target_pairs={{0,24},{4,28},{8,16},{12,20},{16,8},{20,12},{24,0},{28,4},{1,25},{... | collective-permute-start | bytes 503816 | tf_op jit(solution)/shard_map/ppermute | solution.py:375
  25.8 8.7 %collective-permute-start.7 = (bf16[328,256]{1,0:T(8,128)(2,1)S(1)}, bf16[328,256]{1,0:T(8,128)(2,1)S(1)}, u32[]{:S(2)}, u32[]{:S(2)}) collective-permute-start(bf16[328,256]{1,0:T(8,128)(2,1)S(1)} %get-tuple-element.45), channel_id=1, source_target_pairs={{0,3},{1,2},{2,1},{3,0},{4,7},{5,6},{6,5},{7,4},{8,11},{9,10},{10,... | collective-permute-start | bytes 503816 | tf_op jit(solution)/shard_map/ppermute | solution.py:375
  32.6 9.5 %collective-permute-start.17 = (bf16[4,1,328,128]{3,2,1,0:T(8,128)(2,1)S(1)}, bf16[4,1,328,128]{3,2,1,0:T(8,128)(2,1)S(1)}, u32[]{:S(2)}, u32[]{:S(2)}) collective-permute-start(bf16[4,1,328,128]{3,2,1,0:T(8,128)(2,1)S(1)} %stack.3), channel_id=1, source_target_pairs={{0,4},{4,0},{8,12},{12,8},{16,20},{20,16},{24,28},{28,24},{1,5},{5... | collective-permute-start | bytes 1007624 | tf_op jit(solution)/shard_map/ppermute | solution.py:375
  36.4 14.8 %collective-permute-start.10 = (bf16[2,2,328,128]{3,2,1,0:T(8,128)(2,1)S(1)}, bf16[2,2,328,128]{3,2,1,0:T(8,128)(2,1)S(1)}, u32[]{:S(2)}, u32[]{:S(2)}) collective-permute-start(bf16[2,2,328,128]{3,2,1,0:T(8,128)(2,1)S(1)} %get-tuple-element.53), channel_id=1, source_target_pairs={{0,24},{4,28},{8,16},{12,20},{16,8},{20,12},{24,0},{28,4},{1,25},{... | collective-permute-start | bytes 1007624 | tf_op jit(solution)/shard_map/ppermute | solution.py:375
  37.2 8.8 %collective-permute-start.12 = (bf16[328,128]{1,0:T(8,128)(2,1)S(1)}, bf16[328,128]{1,0:T(8,128)(2,1)S(1)}, u32[]{:S(2)}, u32[]{:S(2)}) collective-permute-start(bf16[328,128]{1,0:T(8,128)(2,1)S(1)} %gate.7.refs_7_), channel_id=1, source_target_pairs={{0,2},{1,3},{2,0},{3,1},{4,6},{5,7},{6,4},{7,5},{8,10},{9,11},{10,... | collective-permute-start | bytes 251912 | tf_op jit(solution)/shard_map/ppermute | solution.py:375
  40.8 8.4 %collective-permute-start.13 = (bf16[328,128]{1,0:T(8,128)(2,1)S(1)}, bf16[328,128]{1,0:T(8,128)(2,1)S(1)}, u32[]{:S(2)}, u32[]{:S(2)}) collective-permute-start(bf16[328,128]{1,0:T(8,128)(2,1)S(1)} %gate.8.refs_8_), channel_id=1, source_target_pairs={{0,3},{1,2},{2,1},{3,0},{4,7},{5,6},{6,5},{7,4},{8,11},{9,10},{10,... | collective-permute-start | bytes 251912 | tf_op jit(solution)/shard_map/ppermute | solution.py:375
  42.1 7.9 %collective-permute-start.11 = (bf16[328,128]{1,0:T(8,128)(2,1)S(1)}, bf16[328,128]{1,0:T(8,128)(2,1)S(1)}, u32[]{:S(2)}, u32[]{:S(2)}) collective-permute-start(bf16[328,128]{1,0:T(8,128)(2,1)S(1)} %gate.6.refs_6_), channel_id=1, source_target_pairs={{0,1},{1,0},{2,3},{3,2},{4,5},{5,4},{6,7},{7,6},{8,9},{9,8},{10,11... | collective-permute-start | bytes 251912 | tf_op jit(solution)/shard_map/ppermute | solution.py:375
  42.1 12.5 %collective-permute-start.8 = (bf16[2,2,328,128]{3,2,1,0:T(8,128)(2,1)S(1)}, bf16[2,2,328,128]{3,2,1,0:T(8,128)(2,1)S(1)}, u32[]{:S(2)}, u32[]{:S(2)}) collective-permute-start(bf16[2,2,328,128]{3,2,1,0:T(8,128)(2,1)S(1)} %get-tuple-element.51), channel_id=1, source_target_pairs={{0,8},{4,12},{8,0},{12,4},{16,24},{20,28},{24,16},{28,20},{1,9},{5... | collective-permute-start | bytes 1007624 | tf_op jit(solution)/shard_map/ppermute | solution.py:375
  46.0 10.1 %collective-permute-start.9 = (bf16[2,2,328,128]{3,2,1,0:T(8,128)(2,1)S(1)}, bf16[2,2,328,128]{3,2,1,0:T(8,128)(2,1)S(1)}, u32[]{:S(2)}, u32[]{:S(2)}) collective-permute-start(bf16[2,2,328,128]{3,2,1,0:T(8,128)(2,1)S(1)} %get-tuple-element.52), channel_id=1, source_target_pairs={{0,16},{4,20},{8,24},{12,28},{16,0},{20,4},{24,8},{28,12},{1,17},{... | collective-permute-start | bytes 1007624 | tf_op jit(solution)/shard_map/ppermute | solution.py:375
  49.2 11.3 %collective-permute-start.23 = (bf16[328,256]{1,0:T(8,128)(2,1)S(1)}, bf16[328,256]{1,0:T(8,128)(2,1)S(1)}, u32[]{:S(2)}, u32[]{:S(2)}) collective-permute-start(bf16[328,256]{1,0:T(8,128)(2,1)S(1)} %gate.9.refs_6_), channel_id=1, source_target_pairs={{0,2},{1,3},{2,0},{3,1},{4,6},{5,7},{6,4},{7,5},{8,10},{9,11},{10,... | collective-permute-start | bytes 503816 | tf_op jit(solution)/shard_map/ppermute | solution.py:375
  50.0 13.8 %collective-permute-start.24 = (bf16[328,256]{1,0:T(8,128)(2,1)S(1)}, bf16[328,256]{1,0:T(8,128)(2,1)S(1)}, u32[]{:S(2)}, u32[]{:S(2)}) collective-permute-start(bf16[328,256]{1,0:T(8,128)(2,1)S(1)} %gate.10.refs_7_), channel_id=1, source_target_pairs={{0,3},{1,2},{2,1},{3,0},{4,7},{5,6},{6,5},{7,4},{8,11},{9,10},{10,... | collective-permute-start | bytes 503816 | tf_op jit(solution)/shard_map/ppermute | solution.py:375
  51.2 12.6 %collective-permute-start.22 = (bf16[328,256]{1,0:T(8,128)(2,1)S(1)}, bf16[328,256]{1,0:T(8,128)(2,1)S(1)}, u32[]{:S(2)}, u32[]{:S(2)}) collective-permute-start(bf16[328,256]{1,0:T(8,128)(2,1)S(1)} %gate.11), channel_id=1, source_target_pairs={{0,1},{1,0},{2,3},{3,2},{4,5},{5,4},{6,7},{7,6},{8,9},{9,8},{10,11... | collective-permute-start | bytes 503816 | tf_op jit(solution)/shard_map/ppermute | solution.py:375
  54.6 11.4 %collective-permute-start.19 = (bf16[2,1,328,128]{3,2,1,0:T(8,128)(2,1)S(1)}, bf16[2,1,328,128]{3,2,1,0:T(8,128)(2,1)S(1)}, u32[]{:S(2)}, u32[]{:S(2)}) collective-permute-start(bf16[2,1,328,128]{3,2,1,0:T(8,128)(2,1)S(1)} %get-tuple-element.62), channel_id=1, source_target_pairs={{0,8},{4,12},{8,0},{12,4},{16,24},{20,28},{24,16},{28,20},{1,9},{5... | collective-permute-start | bytes 503816 | tf_op jit(solution)/shard_map/ppermute | solution.py:375
  56.1 9.9 %collective-permute-start.20 = (bf16[2,1,328,128]{3,2,1,0:T(8,128)(2,1)S(1)}, bf16[2,1,328,128]{3,2,1,0:T(8,128)(2,1)S(1)}, u32[]{:S(2)}, u32[]{:S(2)}) collective-permute-start(bf16[2,1,328,128]{3,2,1,0:T(8,128)(2,1)S(1)} %get-tuple-element.63), channel_id=1, source_target_pairs={{0,16},{4,20},{8,24},{12,28},{16,0},{20,4},{24,8},{28,12},{1,17},{... | collective-permute-start | bytes 503816 | tf_op jit(solution)/shard_map/ppermute | solution.py:375
  60.5 6.7 %collective-permute-start.21 = (bf16[2,1,328,128]{3,2,1,0:T(8,128)(2,1)S(1)}, bf16[2,1,328,128]{3,2,1,0:T(8,128)(2,1)S(1)}, u32[]{:S(2)}, u32[]{:S(2)}) collective-permute-start(bf16[2,1,328,128]{3,2,1,0:T(8,128)(2,1)S(1)} %get-tuple-element.64), channel_id=1, source_target_pairs={{0,24},{4,28},{8,16},{12,20},{16,8},{20,12},{24,0},{28,4},{1,25},{... | collective-permute-start | bytes 503816 | tf_op jit(solution)/shard_map/ppermute | solution.py:375
  63.9 5.1 %collective-permute-start.18 = (bf16[4,2,328,128]{3,2,1,0:T(8,128)(2,1)S(1)}, bf16[4,2,328,128]{3,2,1,0:T(8,128)(2,1)S(1)}, u32[]{:S(2)}, u32[]{:S(2)}) collective-permute-start(bf16[4,2,328,128]{3,2,1,0:T(8,128)(2,1)S(1)} %stack.4), channel_id=1, source_target_pairs={{0,4},{4,0},{8,12},{12,8},{16,20},{20,16},{24,28},{28,24},{1,5},{5... | collective-permute-start | bytes 2015240 | tf_op jit(solution)/shard_map/ppermute | solution.py:375
  (6 other events, 31.1 us)
